TPU v7x, 32 devices: a whole 2x2x4 slice. The times are simulated.
32 devices in a mesh: group: 2 (over y), inst: 4 (over x, core), tp: 4 (over z).
Axes of the slice: x: 2, y: 2, z: 4, core: 2. Of those that a mesh axis runs over, the one named last changes fastest.
Arguments:
- mig_hidden: bfloat16 [8, 64, 2, 5120], P(('group', 'inst'), None, None, 'tp'), parts along dimension 0, may hold values from -6 to 6
- mig_dest: int32 [8, 2], P('group'), parts along dimension 0, may hold values from 0 to 3, as said below
- mig_count: int32 [8, 2], P('group'), parts along dimension 0, may hold values from 48 to 64
- attn_gain: bfloat16 [5120], P('tp'), may hold values from 0.099609375 to 1.8984375
- kv_weight: bfloat16 [5120, 2048], P('tp'), may hold values from -0.078125 to 0.078125
- k_gain: bfloat16 [128], replicated, may hold values from 0.099609375 to 1.8984375
- query: bfloat16 [8, 5, 8192], P(('group', 'inst')), parts along dimension 0, may hold values from -113.137085 to 113.137085
- new_kv: bfloat16 [8, 5, 2048], P(('group', 'inst')), parts along dimension 0, may hold values from -5 to 5
- k_cache: bfloat16 [8, 3, 4096, 1024], P(('group', 'inst'), None, 'tp'), parts along dimension 0, may hold values from -4 to 4
- v_cache: bfloat16 [8, 3, 4096, 1024], P(('group', 'inst'), None, 'tp'), parts along dimension 0, may hold values from -5 to 5
- lengths: int32 [8, 3], P(('group', 'inst')), parts along dimension 0, may hold values from 256 to 4096
Outputs:
- attn_out: bfloat16 [8, 5, 8192], P(('group', 'inst'), None, 'tp'), parts along dimension 0
There are 2 independent parts, one for each index of `group`. A program takes and returns all parts, laid end to end along the dimension named above; an argument that names none is the same for every part. Nothing has to cross between parts.
Inputs may be any that keep to these rules, and one draw needn't show every extreme that they name: `mig_dest`: each instance receives exactly 2 requests, never its own, and each instance sends its 2 requests to different instances.
All inputs are finite; a program needn't handle non-finite values.
Results may differ from a plain program's by a relative error of at most 0.02.
Values may be sent and summed in bfloat16 or wider, within the bound.
No kernel may reach another device: no remote copies, remote signals or barrier semaphores. Data moves between devices by JAX's collectives and lax.ppermute only.
A program may use at most 64 MiB of HBM per device.

v0:
```python
import jax
import jax.numpy as jnp
from jax import lax
from jax.sharding import PartitionSpec as P

D = 5120


EPS = 1e-06
THETA = 1000000.0


def rotate(keys, positions):
    half = keys.shape[-1] // 2
    freq = THETA ** (-jnp.arange(half, dtype=jnp.float32) * 2.0 / keys.shape[-1])
    angle = positions[..., None] * freq
    first = keys[..., :half]
    second = keys[..., half:]
    cosine = jnp.cos(angle)
    sine = jnp.sin(angle)
    return jnp.concatenate(
        [first * cosine - second * sine, second * cosine + first * sine], axis=-1
    )


def rebuild(hidden, attn_gain, kv_weight, k_gain, rank):
    wide = hidden.astype(jnp.float32)
    squares = lax.psum(jnp.sum(wide * wide, axis=-1), "tp")
    scale = lax.rsqrt(squares / D + EPS)
    normed = (wide * scale[..., None] * attn_gain.astype(jnp.float32)).astype(jnp.bfloat16)
    slot_total, requests, feats = normed.shape
    count = lax.axis_size("tp") * (slot_total // lax.axis_size("tp"))
    product = jnp.dot(
        normed.reshape(count * requests, feats), kv_weight, preferred_element_type=jnp.float32
    )
    summed = lax.psum_scatter(
        product.reshape(count, requests, -1).astype(jnp.bfloat16),
        "tp",
        scatter_dimension=0,
        tiled=True,
    ).astype(jnp.float32)
    local_rows = summed.shape[0]
    width = summed.shape[2] // 2
    head_size = k_gain.shape[0]
    keys = summed[..., :width].reshape(local_rows, requests, -1, head_size)
    keys = (
        keys
        * lax.rsqrt(jnp.mean(keys * keys, axis=-1, keepdims=True) + EPS)
        * k_gain.astype(jnp.float32)
    )
    positions = (rank * local_rows + jnp.arange(local_rows)).astype(jnp.float32)
    keys = rotate(keys, positions[:, None, None])
    return (
        keys.reshape(local_rows, requests, width).astype(jnp.bfloat16),
        summed[..., width:].astype(jnp.bfloat16),
    )


def partial_softmax(queries, keys, values, valid, kv_heads, head_size):
    rows, positions = valid.shape
    heads_q = queries.reshape(rows, kv_heads, -1, head_size)
    heads_k = keys.reshape(rows, positions, kv_heads, head_size)
    heads_v = values.reshape(rows, positions, kv_heads, head_size)
    scores = jnp.einsum("rgqd,rpgd->rgqp", heads_q, heads_k, preferred_element_type=jnp.float32)
    scores = scores / jnp.sqrt(jnp.float32(head_size))
    mask = valid[:, None, None, :]
    scores = jnp.where(mask, scores, -1e30)
    peak = jnp.max(scores, axis=-1)
    weights = jnp.where(mask, jnp.exp(scores - peak[..., None]), 0.0)
    total = jnp.sum(weights, axis=-1)
    summed = jnp.einsum(
        "rgqp,rpgd->rgqd", weights.astype(jnp.bfloat16), heads_v, preferred_element_type=jnp.float32
    )
    return (peak.reshape(rows, -1), total.reshape(rows, -1), summed.reshape(rows, -1, head_size))


def per_device(
    mig_hidden,
    mig_dest,
    mig_count,
    attn_gain,
    kv_weight,
    k_gain,
    query,
    new_kv,
    k_cache,
    v_cache,
    lengths,
):
    inst_count = lax.axis_size("inst")
    here = lax.axis_index("inst")
    tp_count = lax.axis_size("tp")
    rank = lax.axis_index("tp")
    head_size = k_gain.shape[0]
    width = kv_weight.shape[1] // 2
    kv_heads = width // head_size
    requests = mig_dest.shape[1]
    resident = k_cache.shape[1]
    incoming = (mig_dest == here).astype(jnp.int32)
    has_one = jnp.sum(incoming, axis=1)
    order = jnp.cumsum(has_one) - has_one
    picker = (order[None, :] == jnp.arange(requests)[:, None]) & (has_one[None, :] > 0)
    counts_in = jnp.sum(
        picker.astype(jnp.int32) * jnp.sum(incoming * mig_count, axis=1)[None, :], axis=1
    )
    pick_rows = picker.astype(jnp.bfloat16)
    own_dest = lax.dynamic_index_in_dim(mig_dest, here, 0, keepdims=False)
    outgoing = (own_dest[None, :] == jnp.arange(inst_count)[:, None]).astype(jnp.bfloat16)
    buffer = jnp.einsum(
        "dj,cjf->dcf", outgoing, mig_hidden[0], preferred_element_type=jnp.float32
    ).astype(jnp.bfloat16)
    arrived = lax.all_to_all(buffer, "inst", split_axis=0, concat_axis=0, tiled=True)
    hidden_in = jnp.einsum(
        "ks,scf->ckf", pick_rows, arrived, preferred_element_type=jnp.float32
    ).astype(jnp.bfloat16)
    moved_keys, moved_values = rebuild(hidden_in, attn_gain, kv_weight, k_gain, rank)
    queries = query[0]
    cache_rows = k_cache.shape[2]
    cache_pos = rank * cache_rows + jnp.arange(cache_rows)
    cache_valid = cache_pos[None, :] < lengths[0][:, None]
    peak_r, total_r, summed_r = partial_softmax(
        queries[:resident], k_cache[0], v_cache[0], cache_valid, kv_heads, head_size
    )
    moved_rows = moved_keys.shape[0]
    moved_pos = rank * moved_rows + jnp.arange(moved_rows)
    moved_valid = moved_pos[None, :] < counts_in[:, None]
    peak_m, total_m, summed_m = partial_softmax(
        queries[resident:],
        jnp.transpose(moved_keys, (1, 0, 2)),
        jnp.transpose(moved_values, (1, 0, 2)),
        moved_valid,
        kv_heads,
        head_size,
    )
    peak = jnp.concatenate([peak_r, peak_m], axis=0)
    total = jnp.concatenate([total_r, total_m], axis=0)
    summed = jnp.concatenate([summed_r, summed_m], axis=0)
    heads_all = peak.shape[1]
    heads_mine = heads_all // tp_count
    first_head = rank * heads_mine
    peak_all, total_all, summed_all = (
        lax.all_to_all(
            peak[None].astype(jnp.bfloat16), "tp", split_axis=2, concat_axis=0, tiled=True
        ).astype(jnp.float32),
        lax.all_to_all(
            total[None].astype(jnp.bfloat16), "tp", split_axis=2, concat_axis=0, tiled=True
        ).astype(jnp.float32),
        lax.all_to_all(
            summed[None].astype(jnp.bfloat16), "tp", split_axis=2, concat_axis=0, tiled=True
        ).astype(jnp.float32),
    )
    peak = jnp.max(peak_all, axis=0)
    factor = jnp.exp(peak_all - peak[None])
    total = jnp.sum(total_all * factor, axis=0)
    summed = jnp.sum(summed_all * factor[..., None], axis=0)
    decoded = queries.shape[0]
    group = heads_all // kv_heads
    own = new_kv[0]
    own_keys = jnp.repeat(own[:, :width].reshape(decoded, kv_heads, head_size), group, axis=1)
    own_values = jnp.repeat(own[:, width:].reshape(decoded, kv_heads, head_size), group, axis=1)
    own_keys = lax.dynamic_slice_in_dim(own_keys, first_head, heads_mine, 1).astype(jnp.float32)
    own_values = lax.dynamic_slice_in_dim(own_values, first_head, heads_mine, 1).astype(jnp.float32)
    my_queries = lax.dynamic_slice_in_dim(
        queries.reshape(decoded, heads_all, head_size), first_head, heads_mine, 1
    ).astype(jnp.float32)
    own_score = jnp.sum(my_queries * own_keys, axis=-1) / jnp.sqrt(jnp.float32(head_size))
    top = jnp.maximum(peak, own_score)
    keep = jnp.exp(peak - top)
    own_weight = jnp.exp(own_score - top)
    denom = total * keep + own_weight
    numer = (
        summed * keep[..., None]
        + own_weight.astype(jnp.bfloat16).astype(jnp.float32)[..., None] * own_values
    )
    result = (numer / denom[..., None]).astype(jnp.bfloat16)
    return result.reshape(1, decoded, heads_mine * head_size)


def solution(mesh):
    placed = (
        P(("group", "inst"), None, None, "tp"),
        P("group", None),
        P("group", None),
        P("tp"),
        P("tp", None),
        P(),
        P(("group", "inst"), None, None),
        P(("group", "inst"), None, None),
        P(("group", "inst"), None, "tp", None),
        P(("group", "inst"), None, "tp", None),
        P(("group", "inst"), None),
    )
    return jax.shard_map(
        per_device,
        mesh=mesh,
        in_specs=placed,
        out_specs=P(("group", "inst"), None, "tp"),
        check_vma=False,
    )
```

profile of v0, /device:TPU:0, one launch (start us, length us, event | category | flops | bytes accessed | tf_op | source)
XLA Modules:
  0.0 103.3 jit_solution(10821263281761743072)
XLA Ops:
  6.5 0.0 copy-start
  6.5 0.9 dynamic-slice_reduce_fusion
  7.4 0.1 copy-done
  7.5 0.7 convolution_convert_fusion
  8.2 0.9 copy.111
  9.1 4.2 %all-to-all-start = ((bf16[4,64,1280]{2,1,0:T(8,128)(2,1)}), bf16[4,64,1280]{2,1,0:T(8,128)(2,1)S(1)}, u32[]{:S(2)}, u32[]{:S(2)}) async-start(bf16[4,64,1280]{2,1,0:T(8,128)(2,1)} %copy.111), calls=%async_computation | async-start | bytes 1310720 | tf_op jit(solution)/shard_map/all_to_all | solution.py:112
  13.3 0.0 reduce-scatter.2.cloned.1.call-start
  13.3 0.7 select_reduce_fusion.1
  14.0 0.2 reduce-window.8
  14.2 0.0 copy-start.4
  14.2 4.4 %copy.132 = bf16[384,8,8,128]{3,2,1,0:T(8,128)(2,1)S(1)} copy(bf16[384,8,8,128]{3,1,2,0:T(8,128)(2,1)} %bitcast.124) | data formatting | bytes 12582912
  18.7 0.0 copy-done.1
  18.7 0.0 copy-start.3
  18.8 0.1 broadcast_compare_fusion
  18.9 1.8 %fusion.66 = (f32[3,8,8]{2,1,0:T(8,128)S(1)}, f32[3,8,8,1024]{3,2,1,0:T(8,128)S(1)}) fusion(bf16[3,1024,8,128]{3,2,1,0:T(8,128)(2,1)S(1)} %bitcast.123, bf16[1,3,64,128]{3,1,2,0:T(4,128)(2,1)S(1)} %slice_bitcast_fusion.1, pred[3,1024]{1,0:T(4,128)(4,1)S(1)} %broadcast_compare_fusion), kind=kOutput, calls=%fused_computation.107 | convolution fusion | flops 50921280 | bytes 7130880 | tf_op jit(solution)/shard_map/rgqd,rpgd->rgqp/dot_general | solution.py:64
  20.7 0.3 fusion.26
  21.0 0.0 copy-done.3
  21.0 4.4 %copy.133 = bf16[384,8,8,128]{3,2,1,0:T(8,128)(2,1)S(1)} copy(bf16[384,8,8,128]{3,1,2,0:T(8,128)(2,1)} %bitcast.125) | data formatting | bytes 12582912
  25.5 1.4 %fusion.21 = bf16[1,3,64,128]{3,2,1,0:T(8,128)(2,1)S(1)} fusion(bf16[3,1024,8,128]{3,2,1,0:T(8,128)(2,1)S(1)} %bitcast.122, f32[3,8,8,1024]{3,2,1,0:T(8,128)S(1)} %get-tuple-element.25, f32[3,8,8]{2,1,0:T(8,128)S(1)} %get-tuple-element.24, pred[3,1024]{1,0:T(4,128)(4,1)S(1)} %broadcast_compare_fusion), kind=kOutput, calls=%fused_computation.16 | convolution fusion | flops 50946048 | bytes 7130880 | tf_op jit(solution)/shard_map/rgqp,rpgd->rgqd/dot_general | solution.py:71
  26.9 0.0 all-to-all-done
  26.9 0.8 multiply_reduce_fusion
  27.7 0.1 copy.113
  27.8 12.7 %psum.7 = f32[64,2]{0,1:T(2,128)S(1)} all-reduce(f32[64,2]{0,1:T(2,128)S(1)} %copy.113), channel_id=1, replica_groups=mesh['group'=2,'inst'=4,'tp'=4] {'tp'}, use_global_device_ids=true, to_apply=%region_6.7 | all-reduce | flops 128 | bytes 1024 | tf_op jit(solution)/shard_map/psum | solution.py:28
  40.5 0.1 copy.114
  40.6 0.4 fusion.32
  41.0 4.1 %fusion.6 = bf16[64,2,2048]{2,0,1:T(8,128)(2,1)} fusion(bf16[1280,2048]{1,0:T(8,128)(2,1)} %param.15, bf16[64,2,1280]{2,1,0:T(2,128)(2,1)S(1)} %fusion.32), kind=kOutput, calls=%fused_computation.7 | convolution fusion | flops 671350784 | bytes 6094848 | tf_op jit(solution)/shard_map/dot_general | solution.py:33
  45.1 0.0 reduce-scatter.2.cloned.1.call-update
  45.2 0.0 copy-done.5
  45.3 0.1 concatenate.56
  45.3 0.1 concatenate.53
  45.5 0.1 multiply_reduce_fusion.2
  45.6 0.1 select_reduce_fusion
  45.7 0.1 broadcast_compare_fusion.2
  45.8 0.1 multiply_cosine_fusion
  45.9 19.7 %reduce-scatter.2.cloned.1.call-done = bf16[16,2,2048]{2,0,1:T(8,128)(2,1)} async-done(((bf16[64,2,2048]{2,0,1:T(8,128)(2,1)}), bf16[16,2,2048]{2,0,1:T(8,128)(2,1)}) %reduce-scatter.2.cloned.1.call-update) | async-done | bytes 131088 | tf_op jit(solution)/shard_map/reduce_scatter | solution.py:36
  65.6 0.9 slice_bitcast_fusion
  66.5 0.1 multiply_reduce_fusion.1
  66.7 0.1 multiply_multiply_fusion
  66.8 0.1 subtract_convert_fusion
  66.9 0.1 pad_maximum_fusion.1
  67.0 0.2 fusion.65
  67.3 0.2 fusion.40
  67.4 0.2 fusion.24
  67.7 0.1 concatenate.57
  67.8 0.7 copy.126
  68.5 3.3 %all-to-all-start.3 = ((bf16[1,5,64]{1,0,2:T(2,128)(2,1)}), bf16[1,5,64]{1,0,2:T(2,128)(2,1)S(1)}, u32[]{:S(2)}, u32[]{:S(2)}) async-start(bf16[1,5,64]{1,0,2:T(2,128)(2,1)} %copy.126), calls=%async_computation.4 | async-start | bytes 65536 | tf_op jit(solution)/shard_map/all_to_all | solution.py:145
  71.8 0.1 concatenate.54
  71.9 0.7 pad_maximum_fusion
  72.6 0.7 copy.120
  73.3 4.1 %all-to-all-done.3 = bf16[1,5,64]{1,0,2:T(2,128)(2,1)S(1)} async-done(((bf16[1,5,64]{1,0,2:T(2,128)(2,1)}), bf16[1,5,64]{1,0,2:T(2,128)(2,1)S(1)}, u32[]{:S(2)}, u32[]{:S(2)}) %all-to-all-start.3) | async-done | bytes 672 | tf_op jit(solution)/shard_map/all_to_all | solution.py:145
  77.4 3.3 %all-to-all-start.2 = ((bf16[1,5,64]{1,0,2:T(2,128)(2,1)}), bf16[1,5,64]{1,0,2:T(2,128)(2,1)S(1)}, u32[]{:S(2)}, u32[]{:S(2)}) async-start(bf16[1,5,64]{1,0,2:T(2,128)(2,1)} %copy.120), calls=%async_computation.3 | async-start | bytes 65536 | tf_op jit(solution)/shard_map/all_to_all | solution.py:142
  80.7 0.1 copy.127
  80.8 0.1 reshape.388
  80.9 5.4 %all-to-all-done.2 = bf16[1,5,64]{1,0,2:T(2,128)(2,1)S(1)} async-done(((bf16[1,5,64]{1,0,2:T(2,128)(2,1)}), bf16[1,5,64]{1,0,2:T(2,128)(2,1)S(1)}, u32[]{:S(2)}, u32[]{:S(2)}) %all-to-all-start.2) | async-done | bytes 672 | tf_op jit(solution)/shard_map/all_to_all | solution.py:142
  86.3 3.3 %all-to-all-start.1 = ((bf16[1,5,64,128]{3,1,0,2:T(8,128)(2,1)}), bf16[1,5,64,128]{3,1,0,2:T(8,128)(2,1)S(1)}, u32[]{:S(2)}, u32[]{:S(2)}) async-start(bf16[1,5,64,128]{3,1,0,2:T(8,128)(2,1)} %pad_maximum_fusion), calls=%async_computation.2 | async-start | bytes 262144 | tf_op jit(solution)/shard_map/all_to_all | solution.py:148
  89.7 0.1 copy.121
  89.7 0.1 all_to_all.15
  89.9 0.1 copy.122
  90.0 0.1 copy.123
  90.1 0.1 copy.124
  90.2 0.1 copy.128
  90.3 5.3 %all-to-all-done.1 = bf16[1,5,64,128]{3,1,0,2:T(8,128)(2,1)S(1)} async-done(((bf16[1,5,64,128]{3,1,0,2:T(8,128)(2,1)}), bf16[1,5,64,128]{3,1,0,2:T(8,128)(2,1)S(1)}, u32[]{:S(2)}, u32[]{:S(2)}) %all-to-all-start.1) | async-done | bytes 81952 | tf_op jit(solution)/shard_map/all_to_all | solution.py:148
  95.5 0.1 fusion.35
  95.7 0.7 fusion.49
  (35 shorter events, 0.5 us)
Async XLA Ops:
  6.5 1.0 copy-start
  9.1 17.8 %all-to-all-start = ((bf16[4,64,1280]{2,1,0:T(8,128)(2,1)}), bf16[4,64,1280]{2,1,0:T(8,128)(2,1)S(1)}, u32[]{:S(2)}, u32[]{:S(2)}) async-start(bf16[4,64,1280]{2,1,0:T(8,128)(2,1)} %copy.111), calls=%async_computation | async-start | bytes 1310720 | tf_op jit(solution)/shard_map/all_to_all | solution.py:112
  13.3 52.3 %reduce-scatter.2.cloned.1.call-start = ((), (), s32[]{:S(2)}) async-start(), calls=%async_computation.5 | async-start | bytes 655360 | tf_op jit(solution)/shard_map/reduce_scatter | solution.py:36
  14.2 4.5 %copy-start.1 = (bf16[1,5,8192]{2,1,0:T(8,128)(2,1)S(1)}, bf16[1,5,8192]{2,1,0:T(8,128)(2,1)}, u32[]{:S(2)}) copy-start(bf16[1,5,8192]{2,1,0:T(8,128)(2,1)} %param.17) | copy-start | bytes 245764
  14.2 4.5 %copy-start.2 = (bf16[1,5,2048]{2,1,0:T(8,128)(2,1)S(1)}, bf16[1,5,2048]{2,1,0:T(8,128)(2,1)}, u32[]{:S(2)}) copy-start(bf16[1,5,2048]{2,1,0:T(8,128)(2,1)} %param.18) | copy-start | bytes 61444
  14.2 4.6 %copy-start.4 = (s32[1,3]{1,0:T(1,128)S(1)}, s32[1,3]{1,0:T(1,128)}, u32[]{:S(2)}) copy-start(s32[1,3]{1,0:T(1,128)} %param.21) | copy-start | bytes 40
  18.7 2.3 %copy-start.3 = (bf16[1280]{0:T(1024)(128)(2,1)S(1)}, bf16[1280]{0:T(1024)(128)(2,1)}, u32[]{:S(2)}) copy-start(bf16[1280]{0:T(1024)(128)(2,1)} %param.14) | copy-start | bytes 7684
  26.9 18.3 %copy-start.5 = (bf16[128]{0:T(256)(128)(2,1)S(1)}, bf16[128]{0:T(256)(128)(2,1)}, u32[]{:S(2)}) copy-start(bf16[128]{0:T(256)(128)(2,1)} %param.16) | copy-start | bytes 772
  68.5 8.9 %all-to-all-start.3 = ((bf16[1,5,64]{1,0,2:T(2,128)(2,1)}), bf16[1,5,64]{1,0,2:T(2,128)(2,1)S(1)}, u32[]{:S(2)}, u32[]{:S(2)}) async-start(bf16[1,5,64]{1,0,2:T(2,128)(2,1)} %copy.126), calls=%async_computation.4 | async-start | bytes 65536 | tf_op jit(solution)/shard_map/all_to_all | solution.py:145
  77.4 8.9 %all-to-all-start.2 = ((bf16[1,5,64]{1,0,2:T(2,128)(2,1)}), bf16[1,5,64]{1,0,2:T(2,128)(2,1)S(1)}, u32[]{:S(2)}, u32[]{:S(2)}) async-start(bf16[1,5,64]{1,0,2:T(2,128)(2,1)} %copy.120), calls=%async_computation.3 | async-start | bytes 65536 | tf_op jit(solution)/shard_map/all_to_all | solution.py:142
  86.3 9.2 %all-to-all-start.1 = ((bf16[1,5,64,128]{3,1,0,2:T(8,128)(2,1)}), bf16[1,5,64,128]{3,1,0,2:T(8,128)(2,1)S(1)}, u32[]{:S(2)}, u32[]{:S(2)}) async-start(bf16[1,5,64,128]{3,1,0,2:T(8,128)(2,1)} %pad_maximum_fusion), calls=%async_computation.2 | async-start | bytes 262144 | tf_op jit(solution)/shard_map/all_to_all | solution.py:148
Sparse Core Ops, SparseCore 0:
  45.3 20.2 reduce-scatter.1
where the time goes:
time: 104 us; the launch traced here: 103 us
  waiting for transfers between devices  34.5 us (33%)
  starting transfers between devices  14.1 us (14%)
  between operations  13.8 us (13%)
  local copies, waits for them, and re-layouts  13.7 us (13%)
  blocking collectives  12.7 us (12%)
  matrix products  9.31 us (9%)
  other arithmetic  5.28 us (5%)
    reduce_scatter x1, waiting for transfers between devices, rebuild(): lax.psum_scatter(product.reshape(count, requests, -1).astype(jnp.bfloat16...  19.7 us
    psum x1, blocking collectives, rebuild(): squares = lax.psum(jnp.sum(wide * wide, axis=-1), 'tp')  12.7 us
    unnamed x19, local copies, waits for them, and re-layouts  9.07 us
    all_to_all x1, waiting for transfers between devices, per_device(): lax.all_to_all(peak[None].astype(jnp.bfloat16), 'tp', split_axis=2, conca...  5.42 us
    all_to_all x1, waiting for transfers between devices, per_device(): lax.all_to_all(summed[None].astype(jnp.bfloat16), 'tp', split_axis=2, con...  5.27 us
    all_to_all x1, starting transfers between devices, per_device(): lax.all_to_all(buffer, 'inst', split_axis=0, concat_axis=0, tiled=True)  4.21 us
    dot_general x1, matrix products, rebuild(): jnp.dot(normed.reshape(count * requests, feats), kv_weight, preferred_ele...  4.13 us
    all_to_all x1, waiting for transfers between devices, per_device(): lax.all_to_all(total[None].astype(jnp.bfloat16), 'tp', split_axis=2, conc...  4.08 us
  transfers between devices with their start and end apart: 5, of which 4 were waited for; matrix products, arithmetic and copies ran while one was open for 16% of the time, Pallas kernels for 0%

commit v1 on v0

v1 whole, which is shorter than its diff:
```python
import functools

import jax
import jax.numpy as jnp
import numpy as np
from jax import lax
from jax.experimental import pallas as pl
from jax.experimental.pallas import tpu as pltpu
from jax.sharding import PartitionSpec as P

EPS = 1e-06
THETA = 1000000.0
ABSENT = -1e30
F32 = jnp.float32
BF16 = jnp.bfloat16
VMEM_LIMIT = 56 * 1024 * 1024

VMEM = pl.BlockSpec(memory_space=pltpu.VMEM)
SMEM = pl.BlockSpec(memory_space=pltpu.SMEM)
ANYWHERE = pl.BlockSpec(memory_space=pl.ANY)


def iota(shape, dim):
    return lax.broadcasted_iota(jnp.int32, shape, dim)


def column_to_row(column, period):
    n = column.shape[0]
    spread = jnp.where(iota((n, 128), 0) % period == iota((n, 128), 1), column, 0.0)
    return jnp.sum(spread.reshape(n // period, period, 128), axis=1)


def row_to_column(row, n):
    return jnp.sum(
        jnp.where(iota((n, 128), 0) == iota((n, 128), 1), row, 0.0), axis=1, keepdims=True
    )


def split_bf16(x):
    high = x.astype(BF16)
    return high, (x - high.astype(F32)).astype(BF16)


def project_kernel(ranks, rank_ref, x_ref, gain_ref, wk_ref, wv_ref, *rest):
    outs, sq_ref, xg_ref = rest[:ranks], rest[ranks], rest[ranks + 1]
    step = pl.program_id(0)
    slots, requests, _ = x_ref.shape

    @pl.when(step == 0)
    def _():
        gain = gain_ref[...].astype(F32)
        for r in range(requests):
            x = x_ref[:, r, :].astype(F32)
            xg_ref[r * slots : (r + 1) * slots, :] = (x * gain).astype(BF16)
            sq_ref[r : r + 1, :] = column_to_row(jnp.sum(x * x, axis=1, keepdims=True), slots)

    width = wk_ref.shape[1]
    keys = jnp.dot(xg_ref[...], wk_ref[...], preferred_element_type=F32).astype(BF16)
    values = jnp.dot(xg_ref[...], wv_ref[...], preferred_element_type=F32).astype(BF16)
    for j in range(ranks):

        @pl.when(step == j)
        def _():
            outs[j][:, :width] = keys
            outs[j][:, width:] = values


def project(rank, x, gain, weight, ranks, heads_mine, group, kv_mine):
    slots, requests, feats = x.shape
    width = weight.shape[1] // 2
    kv_heads = width // 128
    piece = kv_mine * 128

    def column(j, rank_ref):
        return lax.rem(rank_ref[0] + j, ranks) * heads_mine // group // kv_mine

    spec = pltpu.PrefetchScalarGridSpec(
        num_scalar_prefetch=1,
        grid=(ranks,),
        in_specs=[
            pl.BlockSpec((slots, requests, feats), lambda j, s: (0, 0, 0)),
            pl.BlockSpec((1, feats), lambda j, s: (0, 0)),
            pl.BlockSpec((feats, piece), lambda j, s: (0, column(j, s))),
            pl.BlockSpec((feats, piece), lambda j, s: (0, kv_heads // kv_mine + column(j, s))),
        ],
        out_specs=[pl.BlockSpec((requests * slots, 2 * piece), lambda j, s: (0, 0))] * ranks
        + [pl.BlockSpec((requests, 128), lambda j, s: (0, 0))],
        scratch_shapes=[pltpu.VMEM((requests * slots, feats), BF16)],
    )
    outs = pl.pallas_call(
        functools.partial(project_kernel, ranks),
        grid_spec=spec,
        out_shape=[jax.ShapeDtypeStruct((requests * slots, 2 * piece), BF16)] * ranks
        + [jax.ShapeDtypeStruct((requests, 128), F32)],
        compiler_params=pltpu.CompilerParams(vmem_limit_bytes=VMEM_LIMIT),
        cost_estimate=pl.CostEstimate(
            flops=2 * requests * slots * feats * 2 * width,
            bytes_accessed=2 * feats * 2 * width,
            transcendentals=0,
        ),
        name="project",
    )(rank, x, gain, weight, weight)
    return outs[:ranks], outs[ranks]


def resident_kernel(ranks, rank_ref, len_ref, q_ref, sq_ref, k_hbm, v_hbm, *rest):
    outs = rest[:ranks]
    k_buf, v_buf, o_all, m_all, l_all, sems = rest[ranks:]
    residents, positions, width = k_buf.shape
    copies = []
    for r in range(residents):
        copies.append(
            (
                pltpu.make_async_copy(k_hbm.at[r], k_buf.at[r], sems.at[0, r]),
                pltpu.make_async_copy(v_hbm.at[r], v_buf.at[r], sems.at[1, r]),
            )
        )
    for pair in copies:
        for copy in pair:
            copy.start()
    heads = q_ref.shape[1]
    kv_heads = width // 128
    group = heads // kv_heads
    pair_rows = 2 * group
    heads_mine = heads // ranks
    rank = rank_ref[0]
    top_half = iota((pair_rows, 128), 0) < group
    scale = F32(1.0) / jnp.sqrt(F32(128.0))
    for r in range(residents):
        copies[r][0].wait()
        valid = rank * positions + iota((pair_rows, positions), 1) < len_ref[0, r]
        weights = []
        for p in range(kv_heads // 2):
            rows = slice(p * pair_rows, (p + 1) * pair_rows)
            q = q_ref[r, rows, :]
            zero = jnp.zeros_like(q)
            lhs = jnp.concatenate(
                [jnp.where(top_half, q, zero), jnp.where(top_half, zero, q)], axis=1
            )
            scores = lax.dot_general(
                lhs,
                k_buf[r, :, p * 256 : (p + 1) * 256],
                (((1,), (1,)), ((), ())),
                preferred_element_type=F32,
            )
            scores = jnp.where(valid, scores * scale, ABSENT)
            peak = jnp.max(scores, axis=1, keepdims=True).astype(BF16).astype(F32)
            weight = jnp.where(valid, jnp.exp(scores - peak), 0.0)
            m_all[r, rows, :] = peak
            l_all[r, rows, :] = jnp.sum(weight, axis=1, keepdims=True)
            weights.append(weight.astype(BF16))
        copies[r][1].wait()
        for p in range(kv_heads // 2):
            rows = slice(p * pair_rows, (p + 1) * pair_rows)
            both = jnp.dot(
                weights[p], v_buf[r, :, p * 256 : (p + 1) * 256], preferred_element_type=F32
            )
            o_all[r, rows, :] = jnp.where(top_half, both[:, :128], both[:, 128:])
    stats = []
    for r in range(residents):
        peak = column_to_row(m_all[r], heads_mine)
        high, low = split_bf16(column_to_row(l_all[r], heads_mine))
        stats.append((peak, high.astype(F32), low.astype(F32)))
    for t in range(ranks):
        for r in range(residents):
            for i in range(3):
                o_all[residents + i, t * residents + r : t * residents + r + 1, :] = stats[r][i][
                    t : t + 1
                ]
    sq_high, sq_low = split_bf16(sq_ref[...])
    requests = sq_ref.shape[0]
    for j in range(ranks):
        target = lax.rem(rank + j, ranks)
        parts = [
            o_all[r, pl.ds(target * heads_mine, heads_mine), :] for r in range(residents)
        ] + [
            o_all[residents + i, pl.ds(target * residents, residents), :] for i in range(3)
        ]
        parts += [sq_high.astype(F32), sq_low.astype(F32)]
        filled = residents * (heads_mine + 3) + 2 * requests
        rest_rows = outs[j].shape[0] - filled
        if rest_rows:
            parts.append(jnp.zeros((rest_rows, 128), F32))
        outs[j][...] = jnp.concatenate(parts, axis=0).astype(BF16)


def attend_resident(rank, lengths, queries, squares, k_cache, v_cache, ranks):
    residents, positions, width = k_cache.shape
    heads = queries.shape[1]
    heads_mine = heads // ranks
    requests = squares.shape[0]
    rows = -(-(residents * (heads_mine + 3) + 2 * requests) // 16) * 16
    return pl.pallas_call(
        functools.partial(resident_kernel, ranks),
        in_specs=[SMEM, SMEM, VMEM, VMEM, ANYWHERE, ANYWHERE],
        out_specs=[VMEM] * ranks,
        out_shape=[jax.ShapeDtypeStruct((rows, 128), BF16)] * ranks,
        scratch_shapes=[
            pltpu.VMEM((residents, positions, width), BF16),
            pltpu.VMEM((residents, positions, width), BF16),
            pltpu.VMEM((residents + 3, heads, 128), F32),
            pltpu.VMEM((residents, heads, 1), F32),
            pltpu.VMEM((residents, heads, 1), F32),
            pltpu.SemaphoreType.DMA((2, residents)),
        ],
        compiler_params=pltpu.CompilerParams(vmem_limit_bytes=VMEM_LIMIT),
        cost_estimate=pl.CostEstimate(
            flops=4 * residents * heads * positions * 128,
            bytes_accessed=4 * residents * positions * width,
            transcendentals=residents * heads * positions,
        ),
        name="attend_resident",
    )(rank, lengths, queries, squares, k_cache, v_cache)


def expand(own, rows):
    per = rows // own.shape[0]
    which = iota((rows, 128), 0) // per
    out = jnp.broadcast_to(own[0:1], (rows, 128))
    for h in range(1, own.shape[0]):
        out = jnp.where(which == h, own[h : h + 1], out)
    return out


def moved_kernel(
    insts, ranks, features, at_sq, here_ref, dest_ref, count_ref, gain_ref, cos_ref, sin_ref, *rest
):
    pieces, rest = rest[:ranks], rest[ranks:]
    payloads, rest = rest[:ranks], rest[ranks:]
    asks, rest = rest[: insts - 1], rest[insts - 1 :]
    out_ref, ask_ref, line_ref = rest
    here = here_ref[0]
    requests = dest_ref.shape[1]
    slots = pieces[0].shape[0] // requests
    piece = pieces[0].shape[1] // 2
    kv_mine = piece // 128
    heads_mine = line_ref.shape[1] // 128
    which = iota((heads_mine, 128), 0) // (heads_mine // kv_mine)
    which_slots = iota((heads_mine, slots), 0) // (heads_mine // kv_mine)
    lane = iota((heads_mine, slots), 1)
    scale = F32(1.0) / jnp.sqrt(F32(128.0))
    gain = gain_ref[...].astype(F32)
    squares = None
    for t in range(ranks):
        high = payloads[t][at_sq : at_sq + requests, :].astype(F32)
        low = payloads[t][at_sq + requests : at_sq + 2 * requests, :].astype(F32)
        squares = high + low if squares is None else squares + high + low
    for r in range(requests):
        dest = dest_ref[here, r]
        count = count_ref[here, r]
        place = jnp.int32(0)
        for s in range(insts):
            for c in range(requests):
                place += jnp.where((dest_ref[s, c] == dest) & (here > s), 1, 0).astype(jnp.int32)
        shift = lax.rem(here - dest + insts, insts)
        for j in range(1, insts):

            @pl.when(shift == j)
            def _():
                ask_ref[...] = asks[j - 1][place]

        ask = ask_ref[...]
        q = ask[:heads_mine]
        own_k = expand(ask[heads_mine : heads_mine + kv_mine].astype(F32), heads_mine)
        own_v = expand(ask[heads_mine + kv_mine : heads_mine + 2 * kv_mine].astype(F32), heads_mine)
        rows = slice(r * slots, (r + 1) * slots)
        kv = pieces[0][rows, :].astype(F32)
        for t in range(1, ranks):
            kv = kv + pieces[t][rows, :].astype(F32)
        kv = kv * lax.rsqrt(row_to_column(squares[r : r + 1], slots) / features + EPS)
        scores = None
        values = []
        for h in range(kv_mine):
            key = kv[:, h * 128 : (h + 1) * 128]
            key = key * lax.rsqrt(jnp.mean(key * key, axis=1, keepdims=True) + EPS) * gain
            key = key * cos_ref[...] + pltpu.roll(key, 64, 1) * sin_ref[...]
            part = lax.dot_general(
                q, key.astype(BF16), (((1,), (1,)), ((), ())), preferred_element_type=F32
            )
            scores = part if scores is None else jnp.where(which_slots == h, part, scores)
            values.append(kv[:, piece + h * 128 : piece + (h + 1) * 128].astype(BF16))
        valid = lane < count
        scores = jnp.where(valid, scores * scale, ABSENT)
        own_score = jnp.sum(q.astype(F32) * own_k, axis=1, keepdims=True) * scale
        top = jnp.maximum(jnp.max(scores, axis=1, keepdims=True), own_score)
        weights = jnp.where(valid, jnp.exp(scores - top), 0.0)
        own_weight = jnp.exp(own_score - top)
        total = jnp.sum(weights, axis=1, keepdims=True) + own_weight
        weights = weights.astype(BF16)
        summed = None
        for h in range(kv_mine):
            part = jnp.dot(weights, values[h], preferred_element_type=F32)
            summed = part if summed is None else jnp.where(which == h, part, summed)
        summed = summed + own_weight.astype(BF16).astype(F32) * own_v
        result = summed / total
        for h in range(heads_mine):
            line_ref[r : r + 1, h * 128 : (h + 1) * 128] = result[h : h + 1, :]
    out_ref[...] = line_ref[...].astype(BF16)


def attend_moved(here, dest, count, k_gain, cos, sin, pieces, payloads, asks, heads_mine, at_sq, features):
    requests = dest.shape[1]
    insts, ranks = len(asks) + 1, len(pieces)
    return pl.pallas_call(
        functools.partial(moved_kernel, insts, ranks, features, at_sq),
        in_specs=[SMEM] * 3 + [VMEM] * (3 + 2 * ranks + insts - 1),
        out_specs=VMEM,
        out_shape=jax.ShapeDtypeStruct((requests, heads_mine * 128), BF16),
        scratch_shapes=[
            pltpu.VMEM(asks[0].shape[1:], BF16),
            pltpu.VMEM((requests, heads_mine * 128), F32),
        ],
        compiler_params=pltpu.CompilerParams(vmem_limit_bytes=VMEM_LIMIT),
        name="attend_moved",
    )(here, dest, count, k_gain, cos, sin, *pieces, *payloads, *asks)


def combine_kernel(ranks, residents, ask_ref, *rest):
    payloads = rest[:ranks]
    out_ref, line_ref = rest[ranks:]
    heads_mine = line_ref.shape[1] // 128
    kv_mine = (ask_ref.shape[1] - heads_mine) // 2
    scale = F32(1.0) / jnp.sqrt(F32(128.0))
    at = residents * heads_mine
    for r in range(residents):
        q = ask_ref[r, :heads_mine, :].astype(F32)
        own_k = expand(ask_ref[r, heads_mine : heads_mine + kv_mine, :].astype(F32), heads_mine)
        own_v = expand(
            ask_ref[r, heads_mine + kv_mine : heads_mine + 2 * kv_mine, :].astype(F32), heads_mine
        )
        own_score = jnp.sum(q * own_k, axis=1, keepdims=True) * scale
        peaks, totals = [], []
        for t in range(ranks):
            stat = payloads[t][at : at + 3 * residents, :].astype(F32)
            peaks.append(row_to_column(stat[r : r + 1], heads_mine))
            total = stat[residents + r : residents + r + 1]
            total = total + stat[2 * residents + r : 2 * residents + r + 1]
            totals.append(row_to_column(total, heads_mine))
        top = own_score
        for t in range(ranks):
            top = jnp.maximum(top, peaks[t])
        own_weight = jnp.exp(own_score - top)
        denom = own_weight
        numer = own_weight.astype(BF16).astype(F32) * own_v
        for t in range(ranks):
            keep = jnp.exp(peaks[t] - top)
            denom = denom + keep * totals[t]
            numer = numer + keep * payloads[t][r * heads_mine : (r + 1) * heads_mine, :].astype(F32)
        result = numer / denom
        for h in range(heads_mine):
            line_ref[r : r + 1, h * 128 : (h + 1) * 128] = result[h : h + 1, :]
    out_ref[...] = line_ref[...].astype(BF16)


def combine_resident(asks, payloads, residents, heads_mine):
    return pl.pallas_call(
        functools.partial(combine_kernel, len(payloads), residents),
        in_specs=[VMEM] * (1 + len(payloads)),
        out_specs=VMEM,
        out_shape=jax.ShapeDtypeStruct((residents, heads_mine * 128), BF16),
        scratch_shapes=[pltpu.VMEM((residents, heads_mine * 128), F32)],
        compiler_params=pltpu.CompilerParams(vmem_limit_bytes=VMEM_LIMIT),
        name="combine_resident",
    )(asks, *payloads)


def finish_kernel(insts, here_ref, dest_ref, kept_ref, *rest):
    moved = rest[: insts - 1]
    out_ref, line_ref = rest[insts - 1 :]
    residents = kept_ref.shape[0]
    requests = dest_ref.shape[1]
    here = here_ref[0]
    line_ref[:residents, :] = kept_ref[...].astype(F32)
    place = jnp.int32(residents)
    for s in range(insts):
        for c in range(requests):
            mine = dest_ref[s, c] == here
            shift = lax.rem(here - s + insts, insts)
            for j in range(1, insts):

                @pl.when(mine & (shift == j))
                def _():
                    line_ref[pl.ds(place, 1), :] = moved[j - 1][c : c + 1, :].astype(F32)

            place += jnp.where(mine, 1, 0).astype(jnp.int32)
    out_ref[...] = line_ref[...].astype(BF16)


def finish(here, dest, kept, moved):
    residents, width = kept.shape
    rows = residents + dest.shape[1]
    return pl.pallas_call(
        functools.partial(finish_kernel, len(moved) + 1),
        in_specs=[SMEM, SMEM, VMEM] + [VMEM] * len(moved),
        out_specs=VMEM,
        out_shape=jax.ShapeDtypeStruct((rows, width), BF16),
        scratch_shapes=[pltpu.VMEM((rows, width), F32)],
        compiler_params=pltpu.CompilerParams(vmem_limit_bytes=VMEM_LIMIT),
        name="finish",
    )(here, dest, kept, *moved)


def shifted(x, axis, j, n):
    return lax.ppermute(x, axis, [(i, (i + j) % n) for i in range(n)])


def rotation(slots, head_size):
    half = head_size // 2
    freq = THETA ** (-np.arange(half) * 2.0 / head_size)
    angle = np.arange(slots)[:, None] * freq[None, :]
    cos, sin = np.cos(angle), np.sin(angle)
    return (
        np.concatenate([cos, cos], axis=1).astype(np.float32),
        np.concatenate([-sin, sin], axis=1).astype(np.float32),
    )


def per_device(
    mig_hidden,
    mig_dest,
    mig_count,
    attn_gain,
    kv_weight,
    k_gain,
    query,
    new_kv,
    k_cache,
    v_cache,
    lengths,
):
    insts = lax.axis_size("inst")
    ranks = lax.axis_size("tp")
    here = lax.axis_index("inst").astype(jnp.int32).reshape(1)
    rank = lax.axis_index("tp").astype(jnp.int32).reshape(1)
    head_size = k_gain.shape[0]
    slots, requests, feats = mig_hidden.shape[1:]
    residents = k_cache.shape[1]
    decoded = query.shape[1]
    heads = query.shape[2] // head_size
    kv_heads = kv_weight.shape[1] // 2 // head_size
    heads_mine = heads // ranks
    group = heads // kv_heads
    kv_mine = max(1, heads_mine // group)

    queries = query[0].reshape(decoded, heads, head_size)
    own = new_kv[0].reshape(decoded, 2, kv_heads, head_size)
    my_queries = lax.dynamic_slice_in_dim(queries, rank[0] * heads_mine, heads_mine, 1)
    my_own = lax.dynamic_slice_in_dim(own, rank[0] * heads_mine // group, kv_mine, 2)
    asks = jnp.concatenate(
        [my_queries, my_own.reshape(decoded, 2 * kv_mine, head_size)], axis=1
    )
    asked = [shifted(asks[residents:], "inst", j, insts) for j in range(1, insts)]

    pieces, squares = project(
        rank, mig_hidden[0], attn_gain.reshape(1, feats), kv_weight, ranks, heads_mine, group, kv_mine
    )
    pieces = [pieces[0]] + [shifted(pieces[j], "tp", j, ranks) for j in range(1, ranks)]
    payloads = attend_resident(rank, lengths, queries, squares, k_cache[0], v_cache[0], ranks)
    payloads = [payloads[0]] + [shifted(payloads[j], "tp", j, ranks) for j in range(1, ranks)]
    kept = combine_resident(asks, payloads, residents, heads_mine)
    cos, sin = rotation(slots, head_size)
    moved = attend_moved(
        here,
        mig_dest,
        mig_count,
        k_gain.reshape(1, head_size),
        cos,
        sin,
        pieces,
        payloads,
        asked,
        heads_mine,
        residents * (heads_mine + 3),
        feats * ranks,
    )
    moved = [shifted(moved, "inst", j, insts) for j in range(1, insts)]
    return finish(here, mig_dest, kept, moved)[None]


def solution(mesh):
    placed = (
        P(("group", "inst"), None, None, "tp"),
        P("group", None),
        P("group", None),
        P("tp"),
        P("tp", None),
        P(),
        P(("group", "inst"), None, None),
        P(("group", "inst"), None, None),
        P(("group", "inst"), None, "tp", None),
        P(("group", "inst"), None, "tp", None),
        P(("group", "inst"), None),
    )
    return jax.shard_map(
        per_device,
        mesh=mesh,
        in_specs=placed,
        out_specs=P(("group", "inst"), None, "tp"),
        check_vma=False,
    )
```

time: 104 us -> 43.3 us (0.42)
  waiting for transfers between devices: 34.5 us -> 5.59 us
  Pallas kernels: 0 us -> 18.5 us
  between operations: 13.8 us -> 0.22 us
  blocking collectives: 12.7 us -> 0 us
  matrix products: 9.31 us -> 0 us
  local copies, waits for them, and re-layouts: 13.7 us -> 4.58 us
  other arithmetic: 5.28 us -> 0.62 us
    reduce_scatter x1 -> x0, waiting for transfers between devices: 19.7 us -> none  [rebuild(): lax.psum_scatter(product.reshape(count, requests, -1).astype(jnp.bfloat16...]
    pallas_call x0 -> x5, Pallas kernels: none -> 18.5 us  [the longest x1 6.92 us: attend_resident(): pl.pallas_call(functools.partial(resident_kernel, ranks), in_specs=[SMEM,...]
    all_to_all x4 -> x0, waiting for transfers between devices: 14.8 us -> none  [the longest x1 5.42 us: per_device(): lax.all_to_all(peak[None].astype(jnp.bfloat16), 'tp', split_axis=2, conca...]
    all_to_all x4 -> x0, starting transfers between devices: 14.1 us -> none  [the longest x1 4.21 us: per_device(): lax.all_to_all(buffer, 'inst', split_axis=0, concat_axis=0, tiled=True)]
    ppermute x0 -> x12, starting transfers between devices: none -> 13.4 us  [shifted(): return lax.ppermute(x, axis, [(i, (i + j) % n) for i in range(n)])]
    psum x1 -> x0, blocking collectives: 12.7 us -> none  [rebuild(): squares = lax.psum(jnp.sum(wide * wide, axis=-1), 'tp')]
    dot_general x7 -> x0, matrix products: 9.31 us -> none  [the longest x1 4.13 us: rebuild(): jnp.dot(normed.reshape(count * requests, feats), kv_weight, preferred_ele...]
    unnamed x19 -> x38, local copies, waits for them, and re-layouts: 9.07 us -> 3.24 us
  transfers between devices with their start and end apart: 5 -> 12, of which waited for: 4 -> 4; matrix products, arithmetic and copies ran while one was open for 16% -> 5% of each run, Pallas kernels for 0% -> 20%
where the time goes in v1:
time: 43.3 us; the launch traced here: 42.9 us
  Pallas kernels  18.5 us (43%)
  starting transfers between devices  13.4 us (31%)
  waiting for transfers between devices  5.59 us (13%)
  local copies, waits for them, and re-layouts  4.58 us (11%)
  other arithmetic  0.62 us (1%)
    ppermute x12, starting transfers between devices, shifted(): return lax.ppermute(x, axis, [(i, (i + j) % n) for i in range(n)])  13.4 us
    pallas_call x1, Pallas kernels, attend_resident(): pl.pallas_call(functools.partial(resident_kernel, ranks), in_specs=[SMEM,...  6.92 us
    ppermute x12, waiting for transfers between devices, shifted(): return lax.ppermute(x, axis, [(i, (i + j) % n) for i in range(n)])  5.59 us
    pallas_call x1, Pallas kernels, project(): pl.pallas_call(functools.partial(project_kernel, ranks), grid_spec=spec,...  5.36 us
    unnamed x38, local copies, waits for them, and re-layouts  3.24 us
    pallas_call x1, Pallas kernels, attend_moved(): pl.pallas_call(functools.partial(moved_kernel, insts, ranks, features, at...  3.03 us
    pallas_call x1, Pallas kernels, finish(): pl.pallas_call(functools.partial(finish_kernel, len(moved) + 1), in_specs...  1.62 us
    pallas_call x1, Pallas kernels, combine_resident(): pl.pallas_call(functools.partial(combine_kernel, len(payloads), residents...  1.55 us
  transfers between devices with their start and end apart: 12, of which 4 were waited for; matrix products, arithmetic and copies ran while one was open for 5% of the time, Pallas kernels for 20%

profile of v1, /device:TPU:0, one launch (start us, length us, event | category | flops | bytes accessed | tf_op | source)
XLA Modules:
  0.0 42.9 jit_solution(13164094676181856383)
XLA Ops:
  0.0 0.0 copy-start.8
  0.0 0.0 copy-start.1
  0.0 1.3 %reshape.18.gain_ref = bf16[1,1280]{1,0:T(2,128)(2,1)} reshape(bf16[1280]{0:T(1024)(128)(2,1)} %param.16) | data formatting | bytes 5120 | tf_op jit(solution)/shard_map/reshape | solution.py:455
  1.3 5.4 %project.1 = (bf16[128,512]{1,0:T(8,128)(2,1)}, bf16[128,512]{1,0:T(8,128)(2,1)}, bf16[128,512]{1,0:T(8,128)(2,1)}, bf16[128,512]{1,0:T(8,128)(2,1)}, f32[2,128]{1,0:T(2,128)}) custom-call(s32[1]{0:T(128)} %bitcast.2.rank_ref, bf16[64,2,1280]{2,1,0:T(2,128)(2,1)} %bitcast.23, bf16[1,1280]{1,0:T(2,128)(2,1)} %reshape.18.gain_ref, bf16[1280,2048]{1,0:T(8,128)(2,1)} %wv_ref.1, ...), custom_call_target="tpu_custom_call" | custom-call | flops 671088640 | bytes 5242880 | tf_op jit(solution)/shard_map/project/pallas_call | solution.py:90
  6.7 3.0 %collective-permute-start.3 = (bf16[128,512]{1,0:T(8,128)(2,1)}, bf16[128,512]{1,0:T(8,128)(2,1)S(1)}, u32[]{:S(2)}, u32[]{:S(2)}) collective-permute-start(bf16[128,512]{1,0:T(8,128)(2,1)} %get-tuple-element.20), channel_id=1, source_target_pairs={{0,1},{1,2},{2,3},{3,0},{4,5},{5,6},{6,7},{7,4},{8,9},{9,10},{10,1... | collective-permute-start | bytes 393224 | tf_op jit(solution)/shard_map/ppermute | solution.py:404
  9.7 2.6 %collective-permute-start.4 = (bf16[128,512]{1,0:T(8,128)(2,1)}, bf16[128,512]{1,0:T(8,128)(2,1)S(1)}, u32[]{:S(2)}, u32[]{:S(2)}) collective-permute-start(bf16[128,512]{1,0:T(8,128)(2,1)} %get-tuple-element.21), channel_id=1, source_target_pairs={{0,2},{1,3},{2,0},{3,1},{4,6},{5,7},{6,4},{7,5},{8,10},{9,11},{10,... | collective-permute-start | bytes 393224 | tf_op jit(solution)/shard_map/ppermute | solution.py:404
  12.3 1.3 %collective-permute-start.5 = (bf16[128,512]{1,0:T(8,128)(2,1)}, bf16[128,512]{1,0:T(8,128)(2,1)S(1)}, u32[]{:S(2)}, u32[]{:S(2)}) collective-permute-start(bf16[128,512]{1,0:T(8,128)(2,1)} %get-tuple-element.22), channel_id=1, source_target_pairs={{0,3},{1,0},{2,1},{3,2},{4,7},{5,4},{6,5},{7,6},{8,11},{9,8},{10,9... | collective-permute-start | bytes 393224 | tf_op jit(solution)/shard_map/ppermute | solution.py:404
  13.6 0.0 copy-done.8
  13.7 0.0 copy-done.1
  13.7 0.0 copy-start
  13.8 0.1 collective-permute-start.6
  13.8 1.6 %collective-permute-start.7 = (bf16[2,20,128]{2,1,0:T(8,128)(2,1)S(1)}, bf16[2,20,128]{2,1,0:T(8,128)(2,1)S(1)}, u32[]{:S(2)}, u32[]{:S(2)}) collective-permute-start(bf16[2,20,128]{2,1,0:T(8,128)(2,1)S(1)} %fusion), channel_id=1, source_target_pairs={{0,8},{4,12},{8,0},{12,4},{1,9},{5,13},{9,1},{13,5},{2,10},{6,14},... | collective-permute-start | bytes 30728 | tf_op jit(solution)/shard_map/ppermute | solution.py:404
  15.4 0.0 copy-done
  15.4 0.0 copy-start.15
  15.4 6.9 %attend_resident.1 = (bf16[64,128]{1,0:T(8,128)(2,1)}, bf16[64,128]{1,0:T(8,128)(2,1)}, bf16[64,128]{1,0:T(8,128)(2,1)}, bf16[64,128]{1,0:T(8,128)(2,1)}) custom-call(s32[1]{0:T(128)} %bitcast.2.rank_ref, s32[1,3]{1,0:T(1,128)} %len_ref.1, bf16[5,64,128]{2,1,0:T(8,128)(2,1)} %bitcast.22, f32[2,128]{1,0:T(2,128)} %get-tuple-element.14.sq_ref, ...), custom_call_target="tpu_custom_call" | custom-call | flops 100663296 | bytes 12582912 | tf_op jit(solution)/shard_map/attend_resident/pallas_call | solution.py:193
  22.3 0.0 collective-permute-done.6.rest_8_
  22.3 0.0 copy-start.9
  22.4 0.7 %collective-permute-start = (bf16[64,128]{1,0:T(8,128)(2,1)}, bf16[64,128]{1,0:T(8,128)(2,1)S(1)}, u32[]{:S(2)}, u32[]{:S(2)}) collective-permute-start(bf16[64,128]{1,0:T(8,128)(2,1)} %get-tuple-element.16), channel_id=1, source_target_pairs={{0,1},{1,2},{2,3},{3,0},{4,5},{5,6},{6,7},{7,4},{8,9},{9,10},{10,1... | collective-permute-start | bytes 49160 | tf_op jit(solution)/shard_map/ppermute | solution.py:404
  23.1 0.0 collective-permute-done.7.rest_9_
  23.1 0.0 copy-start.10
  23.1 1.1 %collective-permute-start.8 = (bf16[2,20,128]{2,1,0:T(8,128)(2,1)S(1)}, bf16[2,20,128]{2,1,0:T(8,128)(2,1)S(1)}, u32[]{:S(2)}, u32[]{:S(2)}) collective-permute-start(bf16[2,20,128]{2,1,0:T(8,128)(2,1)S(1)} %fusion), channel_id=1, source_target_pairs={{0,12},{4,0},{8,4},{12,8},{1,13},{5,1},{9,5},{13,9},{2,14},{6,2},{... | collective-permute-start | bytes 30728 | tf_op jit(solution)/shard_map/ppermute | solution.py:404
  24.2 1.4 %collective-permute-done.8.rest_10_ = bf16[2,20,128]{2,1,0:T(8,128)(2,1)S(1)} collective-permute-done((bf16[2,20,128]{2,1,0:T(8,128)(2,1)S(1)}, bf16[2,20,128]{2,1,0:T(8,128)(2,1)S(1)}, u32[]{:S(2)}, u32[]{:S(2)}) %collective-permute-start.8) | collective-permute-done | bytes 10272 | tf_op jit(solution)/shard_map/ppermute | solution.py:404
  25.6 0.0 copy-start.11
  25.6 0.3 collective-permute-start.1
  26.0 2.2 %collective-permute-done.rest_1_.rest_5_ = bf16[64,128]{1,0:T(8,128)(2,1)S(1)} collective-permute-done((bf16[64,128]{1,0:T(8,128)(2,1)}, bf16[64,128]{1,0:T(8,128)(2,1)S(1)}, u32[]{:S(2)}, u32[]{:S(2)}) %collective-permute-start) | collective-permute-done | bytes 16416 | tf_op jit(solution)/shard_map/ppermute | solution.py:404
  28.2 0.0 copy-start.5
  28.2 0.7 %collective-permute-start.2 = (bf16[64,128]{1,0:T(8,128)(2,1)}, bf16[64,128]{1,0:T(8,128)(2,1)S(1)}, u32[]{:S(2)}, u32[]{:S(2)}) collective-permute-start(bf16[64,128]{1,0:T(8,128)(2,1)} %get-tuple-element.18), channel_id=1, source_target_pairs={{0,3},{1,0},{2,1},{3,2},{4,7},{5,4},{6,5},{7,6},{8,11},{9,8},{10,9... | collective-permute-start | bytes 49160 | tf_op jit(solution)/shard_map/ppermute | solution.py:404
  28.8 0.0 copy-done.15
  28.8 0.7 %copy.16.dest_ref = s32[4,2]{1,0:T(4,128)} copy(s32[4,2]{0,1:T(2,128)S(1)} %copy-done.15) | data formatting | bytes 64 | tf_op args[1]
  29.5 0.0 copy-done.16
  29.5 0.7 %copy.15.count_ref = s32[4,2]{1,0:T(4,128)} copy(s32[4,2]{0,1:T(2,128)S(1)} %copy-done.16) | data formatting | bytes 64 | tf_op args[2]
  30.1 0.3 collective-permute-done.1.rest_2_.rest_6_
  30.5 0.0 copy-start.6
  30.5 1.6 %collective-permute-done.2.rest_3_.rest_7_ = bf16[64,128]{1,0:T(8,128)(2,1)S(1)} collective-permute-done((bf16[64,128]{1,0:T(8,128)(2,1)}, bf16[64,128]{1,0:T(8,128)(2,1)S(1)}, u32[]{:S(2)}, u32[]{:S(2)}) %collective-permute-start.2) | collective-permute-done | bytes 16416 | tf_op jit(solution)/shard_map/ppermute | solution.py:404
  32.1 0.0 copy-start.7
  32.1 0.0 collective-permute-done.3.rest_1_
  32.1 0.0 copy-start.2
  32.1 0.0 collective-permute-done.4.rest_2_
  32.1 0.0 copy-start.3
  32.1 0.0 collective-permute-done.5.rest_3_
  32.1 0.0 copy-start.4
  32.2 0.0 copy-done.9
  32.2 0.0 copy-done.10
  32.2 0.0 copy-done.11
  32.2 0.0 copy-done.5
  32.2 0.0 copy-done.6
  32.2 0.5 %copy-done.7 = bf16[64,128]{1,0:T(8,128)(2,1)} copy-done((bf16[64,128]{1,0:T(8,128)(2,1)}, bf16[64,128]{1,0:T(8,128)(2,1)S(1)}, u32[]{:S(2)}) %copy-start.7) | copy-done | bytes 16408
  32.7 0.1 copy-done.2
  32.8 0.1 copy-done.3
  32.8 0.0 copy-done.4
  32.9 3.0 %attend_moved.1 = bf16[2,2048]{1,0:T(2,128)(2,1)} custom-call(s32[1]{0:T(128)} %bitcast.here_ref, s32[4,2]{1,0:T(4,128)} %copy.16.dest_ref, s32[4,2]{1,0:T(4,128)} %copy.15.count_ref, bf16[1,128]{1,0:T(2,128)(2,1)} %bitcast.29, f32[64,128]{1,0:T(8,128)} %constant.33.clone.cos_ref, f32[64,128]{1,0:T(8,128)} %constant.34.clone.sin_ref, ...), custom_call_target="tpu_custom_call" | custom-call | tf_op jit(solution)/shard_map/attend_moved/pallas_call | solution.py:304
  35.9 0.0 collective-permute-start.9
  35.9 0.6 %collective-permute-start.10 = (bf16[2,2048]{1,0:T(2,128)(2,1)}, bf16[2,2048]{1,0:T(2,128)(2,1)S(1)}, u32[]{:S(2)}, u32[]{:S(2)}) collective-permute-start(bf16[2,2048]{1,0:T(2,128)(2,1)} %attend_moved.1), channel_id=1, source_target_pairs={{0,8},{4,12},{8,0},{12,4},{1,9},{5,13},{9,1},{13,5},{2,10},{6,14},... | collective-permute-start | bytes 24584 | tf_op jit(solution)/shard_map/ppermute | solution.py:404
  36.5 1.4 %collective-permute-start.11 = (bf16[2,2048]{1,0:T(2,128)(2,1)}, bf16[2,2048]{1,0:T(2,128)(2,1)S(1)}, u32[]{:S(2)}, u32[]{:S(2)}) collective-permute-start(bf16[2,2048]{1,0:T(2,128)(2,1)} %attend_moved.1), channel_id=1, source_target_pairs={{0,12},{4,0},{8,4},{12,8},{1,13},{5,1},{9,5},{13,9},{2,14},{6,2},{... | collective-permute-start | bytes 24584 | tf_op jit(solution)/shard_map/ppermute | solution.py:404
  37.9 0.6 %pad_maximum_fusion.ask_ref = bf16[5,20,128]{2,1,0:T(8,128)(2,1)} fusion(bf16[5,4,128]{2,1,0:T(4,128)(2,1)S(1)} %bitcast.26, bf16[5,16,128]{2,1,0:T(8,128)(2,1)S(1)} %constant_dynamic-slice_fusion.1), kind=kLoop, calls=%fused_computation.2 | loop fusion | flops 51200 | bytes 51200 | tf_op jit(solution)/shard_map/concatenate | solution.py:449
  38.5 1.6 %combine_resident.1.kept_ref = bf16[3,2048]{1,0:T(4,128)(2,1)} custom-call(bf16[5,20,128]{2,1,0:T(8,128)(2,1)} %pad_maximum_fusion.ask_ref, bf16[64,128]{1,0:T(8,128)(2,1)} %get-tuple-element.15.rest_0_.rest_4_, bf16[64,128]{1,0:T(8,128)(2,1)} %copy-done.5, bf16[64,128]{1,0:T(8,128)(2,1)} %copy-done.6, bf16[64,128]{1,0:T(8,128)(2,1)} %copy-done.7), custom_call_target="tpu_custom_call" | custom-call | tf_op jit(solution)/shard_map/combine_resident/pallas_call | solution.py:356
  40.1 0.0 collective-permute-done.9.rest_0_
  40.1 0.0 collective-permute-done.10.rest_1_
  40.1 0.0 copy-start.13
  40.1 0.0 collective-permute-done.11.rest_2_
  40.1 0.6 %copy-done.12 = bf16[2,2048]{1,0:T(2,128)(2,1)} copy-done((bf16[2,2048]{1,0:T(2,128)(2,1)}, bf16[2,2048]{1,0:T(2,128)(2,1)S(1)}, u32[]{:S(2)}) %copy-start.12) | copy-done | bytes 8216
  40.7 0.0 copy-done.13
  40.7 0.6 %copy-done.14 = bf16[2,2048]{1,0:T(2,128)(2,1)} copy-done((bf16[2,2048]{1,0:T(2,128)(2,1)}, bf16[2,2048]{1,0:T(2,128)(2,1)S(1)}, u32[]{:S(2)}) %copy-start.14) | copy-done | bytes 8216
  41.3 1.6 %finish.1 = bf16[5,2048]{1,0:T(8,128)(2,1)} custom-call(s32[1]{0:T(128)} %bitcast.here_ref, s32[4,2]{1,0:T(4,128)} %copy.16.dest_ref, bf16[3,2048]{1,0:T(4,128)(2,1)} %combine_resident.1.kept_ref, bf16[2,2048]{1,0:T(2,128)(2,1)} %copy-done.12, bf16[2,2048]{1,0:T(2,128)(2,1)} %copy-done.13, bf16[2,2048]{1,0:T(2,128)(2,1)} %copy-done.14), custom_call_target="tpu_custom_call" | custom-call | tf_op jit(solution)/shard_map/finish/pallas_call | solution.py:392
  (8 shorter events, 0.1 us)
Async XLA Ops:
  0.0 13.6 %copy-start.8 = (bf16[1,5,2048]{2,1,0:T(8,128)(2,1)S(1)}, bf16[1,5,2048]{2,1,0:T(8,128)(2,1)}, u32[]{:S(2)}) copy-start(bf16[1,5,2048]{2,1,0:T(8,128)(2,1)} %param.20) | copy-start | bytes 61444
  0.0 13.7 %copy-start.1 = (bf16[1,5,8192]{2,1,0:T(8,128)(2,1)S(1)}, bf16[1,5,8192]{2,1,0:T(8,128)(2,1)}, u32[]{:S(2)}) copy-start(bf16[1,5,8192]{2,1,0:T(8,128)(2,1)} %param.19) | copy-start | bytes 245764
  6.7 25.4 %collective-permute-start.3 = (bf16[128,512]{1,0:T(8,128)(2,1)}, bf16[128,512]{1,0:T(8,128)(2,1)S(1)}, u32[]{:S(2)}, u32[]{:S(2)}) collective-permute-start(bf16[128,512]{1,0:T(8,128)(2,1)} %get-tuple-element.20), channel_id=1, source_target_pairs={{0,1},{1,2},{2,3},{3,0},{4,5},{5,6},{6,7},{7,4},{8,9},{9,10},{10,1... | collective-permute-start | bytes 393224 | tf_op jit(solution)/shard_map/ppermute | solution.py:404
  9.7 22.4 %collective-permute-start.4 = (bf16[128,512]{1,0:T(8,128)(2,1)}, bf16[128,512]{1,0:T(8,128)(2,1)S(1)}, u32[]{:S(2)}, u32[]{:S(2)}) collective-permute-start(bf16[128,512]{1,0:T(8,128)(2,1)} %get-tuple-element.21), channel_id=1, source_target_pairs={{0,2},{1,3},{2,0},{3,1},{4,6},{5,7},{6,4},{7,5},{8,10},{9,11},{10,... | collective-permute-start | bytes 393224 | tf_op jit(solution)/shard_map/ppermute | solution.py:404
  12.3 19.8 %collective-permute-start.5 = (bf16[128,512]{1,0:T(8,128)(2,1)}, bf16[128,512]{1,0:T(8,128)(2,1)S(1)}, u32[]{:S(2)}, u32[]{:S(2)}) collective-permute-start(bf16[128,512]{1,0:T(8,128)(2,1)} %get-tuple-element.22), channel_id=1, source_target_pairs={{0,3},{1,0},{2,1},{3,2},{4,7},{5,4},{6,5},{7,6},{8,11},{9,8},{10,9... | collective-permute-start | bytes 393224 | tf_op jit(solution)/shard_map/ppermute | solution.py:404
  13.7 1.7 %copy-start = (bf16[1,5,64,128]{3,2,1,0:T(8,128)(2,1)}, bf16[1,5,64,128]{3,2,1,0:T(8,128)(2,1)S(1)}, u32[]{:S(2)}) copy-start(bf16[1,5,64,128]{3,2,1,0:T(8,128)(2,1)S(1)} %copy.21) | copy-start | bytes 245764
  13.8 8.6 %collective-permute-start.6 = (bf16[2,20,128]{2,1,0:T(8,128)(2,1)S(1)}, bf16[2,20,128]{2,1,0:T(8,128)(2,1)S(1)}, u32[]{:S(2)}, u32[]{:S(2)}) collective-permute-start(bf16[2,20,128]{2,1,0:T(8,128)(2,1)S(1)} %fusion), channel_id=1, source_target_pairs={{0,4},{4,8},{8,12},{12,0},{1,5},{5,9},{9,13},{13,1},{2,6},{6,10},{... | collective-permute-start | bytes 30728 | tf_op jit(solution)/shard_map/ppermute | solution.py:404
  13.8 9.2 %collective-permute-start.7 = (bf16[2,20,128]{2,1,0:T(8,128)(2,1)S(1)}, bf16[2,20,128]{2,1,0:T(8,128)(2,1)S(1)}, u32[]{:S(2)}, u32[]{:S(2)}) collective-permute-start(bf16[2,20,128]{2,1,0:T(8,128)(2,1)S(1)} %fusion), channel_id=1, source_target_pairs={{0,8},{4,12},{8,0},{12,4},{1,9},{5,13},{9,1},{13,5},{2,10},{6,14},... | collective-permute-start | bytes 30728 | tf_op jit(solution)/shard_map/ppermute | solution.py:404
  15.4 13.4 %copy-start.15 = (s32[4,2]{0,1:T(2,128)S(1)}, s32[4,2]{0,1:T(2,128)}, u32[]{:S(2)}) copy-start(s32[4,2]{0,1:T(2,128)} %param.14) | copy-start | bytes 100
  15.4 14.1 %copy-start.16 = (s32[4,2]{0,1:T(2,128)S(1)}, s32[4,2]{0,1:T(2,128)}, u32[]{:S(2)}) copy-start(s32[4,2]{0,1:T(2,128)} %param.15) | copy-start | bytes 100
  22.3 9.8 %copy-start.9 = (bf16[2,20,128]{2,1,0:T(8,128)(2,1)}, bf16[2,20,128]{2,1,0:T(8,128)(2,1)S(1)}, u32[]{:S(2)}) copy-start(bf16[2,20,128]{2,1,0:T(8,128)(2,1)S(1)} %collective-permute-done.6.rest_8_) | copy-start | bytes 30724
  22.4 5.8 %collective-permute-start = (bf16[64,128]{1,0:T(8,128)(2,1)}, bf16[64,128]{1,0:T(8,128)(2,1)S(1)}, u32[]{:S(2)}, u32[]{:S(2)}) collective-permute-start(bf16[64,128]{1,0:T(8,128)(2,1)} %get-tuple-element.16), channel_id=1, source_target_pairs={{0,1},{1,2},{2,3},{3,0},{4,5},{5,6},{6,7},{7,4},{8,9},{9,10},{10,1... | collective-permute-start | bytes 49160 | tf_op jit(solution)/shard_map/ppermute | solution.py:404
  23.1 9.1 %copy-start.10 = (bf16[2,20,128]{2,1,0:T(8,128)(2,1)}, bf16[2,20,128]{2,1,0:T(8,128)(2,1)S(1)}, u32[]{:S(2)}) copy-start(bf16[2,20,128]{2,1,0:T(8,128)(2,1)S(1)} %collective-permute-done.7.rest_9_) | copy-start | bytes 30724
  23.1 2.5 %collective-permute-start.8 = (bf16[2,20,128]{2,1,0:T(8,128)(2,1)S(1)}, bf16[2,20,128]{2,1,0:T(8,128)(2,1)S(1)}, u32[]{:S(2)}, u32[]{:S(2)}) collective-permute-start(bf16[2,20,128]{2,1,0:T(8,128)(2,1)S(1)} %fusion), channel_id=1, source_target_pairs={{0,12},{4,0},{8,4},{12,8},{1,13},{5,1},{9,5},{13,9},{2,14},{6,2},{... | collective-permute-start | bytes 30728 | tf_op jit(solution)/shard_map/ppermute | solution.py:404
  25.6 6.6 %copy-start.11 = (bf16[2,20,128]{2,1,0:T(8,128)(2,1)}, bf16[2,20,128]{2,1,0:T(8,128)(2,1)S(1)}, u32[]{:S(2)}) copy-start(bf16[2,20,128]{2,1,0:T(8,128)(2,1)S(1)} %collective-permute-done.8.rest_10_) | copy-start | bytes 30724
  25.6 4.9 %collective-permute-start.1 = (bf16[64,128]{1,0:T(8,128)(2,1)}, bf16[64,128]{1,0:T(8,128)(2,1)S(1)}, u32[]{:S(2)}, u32[]{:S(2)}) collective-permute-start(bf16[64,128]{1,0:T(8,128)(2,1)} %get-tuple-element.17), channel_id=1, source_target_pairs={{0,2},{1,3},{2,0},{3,1},{4,6},{5,7},{6,4},{7,5},{8,10},{9,11},{10,... | collective-permute-start | bytes 49160 | tf_op jit(solution)/shard_map/ppermute | solution.py:404
  28.2 4.0 %copy-start.5 = (bf16[64,128]{1,0:T(8,128)(2,1)}, bf16[64,128]{1,0:T(8,128)(2,1)S(1)}, u32[]{:S(2)}) copy-start(bf16[64,128]{1,0:T(8,128)(2,1)S(1)} %collective-permute-done.rest_1_.rest_5_) | copy-start | bytes 49156
  28.2 3.9 %collective-permute-start.2 = (bf16[64,128]{1,0:T(8,128)(2,1)}, bf16[64,128]{1,0:T(8,128)(2,1)S(1)}, u32[]{:S(2)}, u32[]{:S(2)}) collective-permute-start(bf16[64,128]{1,0:T(8,128)(2,1)} %get-tuple-element.18), channel_id=1, source_target_pairs={{0,3},{1,0},{2,1},{3,2},{4,7},{5,4},{6,5},{7,6},{8,11},{9,8},{10,9... | collective-permute-start | bytes 49160 | tf_op jit(solution)/shard_map/ppermute | solution.py:404
  30.5 1.7 %copy-start.6 = (bf16[64,128]{1,0:T(8,128)(2,1)}, bf16[64,128]{1,0:T(8,128)(2,1)S(1)}, u32[]{:S(2)}) copy-start(bf16[64,128]{1,0:T(8,128)(2,1)S(1)} %collective-permute-done.1.rest_2_.rest_6_) | copy-start | bytes 49156
  32.1 0.6 %copy-start.7 = (bf16[64,128]{1,0:T(8,128)(2,1)}, bf16[64,128]{1,0:T(8,128)(2,1)S(1)}, u32[]{:S(2)}) copy-start(bf16[64,128]{1,0:T(8,128)(2,1)S(1)} %collective-permute-done.2.rest_3_.rest_7_) | copy-start | bytes 49156
  32.1 0.7 %copy-start.2 = (bf16[128,512]{1,0:T(8,128)(2,1)}, bf16[128,512]{1,0:T(8,128)(2,1)S(1)}, u32[]{:S(2)}) copy-start(bf16[128,512]{1,0:T(8,128)(2,1)S(1)} %collective-permute-done.3.rest_1_) | copy-start | bytes 393220
  32.1 0.7 %copy-start.3 = (bf16[128,512]{1,0:T(8,128)(2,1)}, bf16[128,512]{1,0:T(8,128)(2,1)S(1)}, u32[]{:S(2)}) copy-start(bf16[128,512]{1,0:T(8,128)(2,1)S(1)} %collective-permute-done.4.rest_2_) | copy-start | bytes 393220
  32.1 0.7 %copy-start.4 = (bf16[128,512]{1,0:T(8,128)(2,1)}, bf16[128,512]{1,0:T(8,128)(2,1)S(1)}, u32[]{:S(2)}) copy-start(bf16[128,512]{1,0:T(8,128)(2,1)S(1)} %collective-permute-done.5.rest_3_) | copy-start | bytes 393220
  35.9 4.2 %collective-permute-start.9 = (bf16[2,2048]{1,0:T(2,128)(2,1)}, bf16[2,2048]{1,0:T(2,128)(2,1)S(1)}, u32[]{:S(2)}, u32[]{:S(2)}) collective-permute-start(bf16[2,2048]{1,0:T(2,128)(2,1)} %attend_moved.1), channel_id=1, source_target_pairs={{0,4},{4,8},{8,12},{12,0},{1,5},{5,9},{9,13},{13,1},{2,6},{6,10},{... | collective-permute-start | bytes 24584 | tf_op jit(solution)/shard_map/ppermute | solution.py:404
  35.9 4.2 %collective-permute-start.10 = (bf16[2,2048]{1,0:T(2,128)(2,1)}, bf16[2,2048]{1,0:T(2,128)(2,1)S(1)}, u32[]{:S(2)}, u32[]{:S(2)}) collective-permute-start(bf16[2,2048]{1,0:T(2,128)(2,1)} %attend_moved.1), channel_id=1, source_target_pairs={{0,8},{4,12},{8,0},{12,4},{1,9},{5,13},{9,1},{13,5},{2,10},{6,14},... | collective-permute-start | bytes 24584 | tf_op jit(solution)/shard_map/ppermute | solution.py:404
  36.5 3.6 %collective-permute-start.11 = (bf16[2,2048]{1,0:T(2,128)(2,1)}, bf16[2,2048]{1,0:T(2,128)(2,1)S(1)}, u32[]{:S(2)}, u32[]{:S(2)}) collective-permute-start(bf16[2,2048]{1,0:T(2,128)(2,1)} %attend_moved.1), channel_id=1, source_target_pairs={{0,12},{4,0},{8,4},{12,8},{1,13},{5,1},{9,5},{13,9},{2,14},{6,2},{... | collective-permute-start | bytes 24584 | tf_op jit(solution)/shard_map/ppermute | solution.py:404
  40.1 0.6 %copy-start.12 = (bf16[2,2048]{1,0:T(2,128)(2,1)}, bf16[2,2048]{1,0:T(2,128)(2,1)S(1)}, u32[]{:S(2)}) copy-start(bf16[2,2048]{1,0:T(2,128)(2,1)S(1)} %collective-permute-done.9.rest_0_) | copy-start | bytes 24580
  40.1 0.6 %copy-start.13 = (bf16[2,2048]{1,0:T(2,128)(2,1)}, bf16[2,2048]{1,0:T(2,128)(2,1)S(1)}, u32[]{:S(2)}) copy-start(bf16[2,2048]{1,0:T(2,128)(2,1)S(1)} %collective-permute-done.10.rest_1_) | copy-start | bytes 24580
  40.7 0.6 %copy-start.14 = (bf16[2,2048]{1,0:T(2,128)(2,1)}, bf16[2,2048]{1,0:T(2,128)(2,1)S(1)}, u32[]{:S(2)}) copy-start(bf16[2,2048]{1,0:T(2,128)(2,1)S(1)} %collective-permute-done.11.rest_2_) | copy-start | bytes 24580

commit v2 on v1

v2 whole, which is shorter than its diff:
```python
import functools

import jax
import jax.numpy as jnp
import numpy as np
from jax import lax
from jax.experimental import pallas as pl
from jax.experimental.pallas import tpu as pltpu
from jax.sharding import PartitionSpec as P

EPS = 1e-06
THETA = 1000000.0
ABSENT = -1e30
F32 = jnp.float32
BF16 = jnp.bfloat16
MIB = 1024 * 1024

VMEM = pl.BlockSpec(memory_space=pltpu.VMEM)
SMEM = pl.BlockSpec(memory_space=pltpu.SMEM)
HBM = pl.BlockSpec(memory_space=pltpu.HBM)


def iota(shape, dim):
    return lax.broadcasted_iota(jnp.int32, shape, dim)


def column_to_row(column, period):
    n = column.shape[0]
    spread = jnp.where(iota((n, 128), 0) % period == iota((n, 128), 1), column, 0.0)
    return jnp.sum(spread.reshape(n // period, period, 128), axis=1)


def row_to_column(row, n):
    return jnp.sum(
        jnp.where(iota((n, 128), 0) == iota((n, 128), 1), row, 0.0), axis=1, keepdims=True
    )


def split_bf16(x):
    high = x.astype(BF16)
    return high, (x - high.astype(F32)).astype(BF16)


def project_kernel(ranks, group, rank_ref, gain_ref, x_hbm, w_hbm, *rest):
    outs, sq_ref = rest[:ranks], rest[ranks]
    x_ref, w_ref, xg_ref, x_sem, w_sems = rest[ranks + 1 :]
    slots, requests, feats = x_ref.shape
    piece = w_ref.shape[2] // 2
    kv_width = w_hbm.shape[1] // 2
    heads_mine = kv_width // 128 * group // ranks
    rank = rank_ref[0]
    x_copy = pltpu.make_async_copy(x_hbm, x_ref, x_sem)
    x_copy.start()
    copies = []
    for j in range(ranks):
        first = lax.rem(rank + j, ranks) * heads_mine // group * 128
        first = pl.multiple_of(first, 128)
        pair = (
            pltpu.make_async_copy(
                w_hbm.at[:, pl.ds(first, piece)], w_ref.at[j, :, :piece], w_sems.at[0, j]
            ),
            pltpu.make_async_copy(
                w_hbm.at[:, pl.ds(kv_width + first, piece)], w_ref.at[j, :, piece:], w_sems.at[1, j]
            ),
        )
        copies.append(pair)
        for copy in pair:
            copy.start()
    x_copy.wait()
    rows = slots * requests
    squares = jnp.zeros((rows, 128), F32)
    for c in range(0, feats, 128):
        width = min(128, feats - c)
        x = x_ref[:, :, c : c + width].astype(F32).reshape(rows, width)
        gain = gain_ref[c : c + width].astype(F32).reshape(1, width)
        xg_ref[:, c : c + width] = (x * gain).astype(BF16)
        x = x * x
        if width < 128:
            x = jnp.concatenate([x, jnp.zeros((rows, 128 - width), F32)], axis=1)
        squares = squares + x
    sq_ref[...] = column_to_row(jnp.sum(squares, axis=1, keepdims=True), 128)
    for j in range(ranks):
        for copy in copies[j]:
            copy.wait()
        outs[j][...] = jnp.dot(xg_ref[...], w_ref[j], preferred_element_type=F32).astype(BF16)


def project(rank, x, gain, weight, ranks, group, kv_mine):
    slots, requests, feats = x.shape
    rows = slots * requests
    piece = kv_mine * 128
    outs = pl.pallas_call(
        functools.partial(project_kernel, ranks, group),
        in_specs=[SMEM, VMEM, HBM, HBM],
        out_specs=[VMEM] * (ranks + 1),
        out_shape=[jax.ShapeDtypeStruct((rows, 2 * piece), BF16)] * ranks
        + [jax.ShapeDtypeStruct((rows // 128, 128), F32)],
        scratch_shapes=[
            pltpu.VMEM((slots, requests, feats), BF16),
            pltpu.VMEM((ranks, feats, 2 * piece), BF16),
            pltpu.VMEM((rows, feats), BF16),
            pltpu.SemaphoreType.DMA,
            pltpu.SemaphoreType.DMA((2, ranks)),
        ],
        compiler_params=pltpu.CompilerParams(vmem_limit_bytes=16 * MIB),
        cost_estimate=pl.CostEstimate(
            flops=4 * rows * feats * piece * ranks,
            bytes_accessed=4 * feats * piece * ranks,
            transcendentals=0,
        ),
        name="project",
    )(rank, gain, x, weight)
    return outs[:ranks], outs[ranks]


def resident_kernel(ranks, rank_ref, len_ref, q_ref, sq_ref, k_hbm, v_hbm, *rest):
    outs = rest[:ranks]
    k_buf, v_buf, o_all, s_all, sems = rest[ranks:]
    residents, positions, width = k_buf.shape
    copies = []
    for r in range(residents):
        copies.append(
            (
                pltpu.make_async_copy(k_hbm.at[r], k_buf.at[r], sems.at[0, r]),
                pltpu.make_async_copy(v_hbm.at[r], v_buf.at[r], sems.at[1, r]),
            )
        )
    for pair in copies:
        for copy in pair:
            copy.start()
    heads = q_ref.shape[1]
    kv_heads = width // 128
    group = heads // kv_heads
    pair_rows = 2 * group
    heads_mine = heads // ranks
    rank = rank_ref[0]
    top_half = iota((pair_rows, 128), 0) < group
    own_block = iota((heads, width), 0) // group == iota((heads, width), 1) // 128
    scale = F32(1.0) / jnp.sqrt(F32(128.0))
    for r in range(residents):
        wide = jnp.concatenate([q_ref[r]] * kv_heads, axis=1)
        wide = jnp.where(own_block, wide, jnp.zeros_like(wide))
        if heads < 128:
            wide = jnp.concatenate([wide, jnp.zeros((128 - heads, width), BF16)], axis=0)
        copies[r][0].wait()
        scores = lax.dot_general(
            k_buf[r], wide, (((1,), (1,)), ((), ())), preferred_element_type=F32
        )
        scores = jnp.transpose(scores)[:heads]
        valid = rank * positions + iota((heads, positions), 1) < len_ref[0, r]
        scores = jnp.where(valid, scores * scale, ABSENT)
        peak = jnp.max(scores, axis=1, keepdims=True).astype(BF16).astype(F32)
        weights = jnp.where(valid, jnp.exp(scores - peak), 0.0)
        high, low = split_bf16(jnp.sum(weights, axis=1, keepdims=True))
        s_all[r, 0] = column_to_row(peak, heads_mine)
        s_all[r, 1] = column_to_row(high.astype(F32), heads_mine)
        s_all[r, 2] = column_to_row(low.astype(F32), heads_mine)
        weights = weights.astype(BF16)
        copies[r][1].wait()
        for p in range(kv_heads // 2):
            rows = slice(p * pair_rows, (p + 1) * pair_rows)
            both = jnp.dot(
                weights[rows], v_buf[r, :, p * 256 : (p + 1) * 256], preferred_element_type=F32
            )
            o_all[r, rows, :] = jnp.where(top_half, both[:, :128], both[:, 128:])
    sq_high, sq_low = split_bf16(sq_ref[...])
    sq_rows = sq_ref.shape[0]
    filled = residents * (heads_mine + 3) + 2 * sq_rows
    for j in range(ranks):
        target = lax.rem(rank + j, ranks)
        first = pl.multiple_of(target * heads_mine, heads_mine)
        parts = [o_all[r, pl.ds(first, heads_mine), :] for r in range(residents)]
        parts += [s_all[r, i, pl.ds(target, 1), :] for i in range(3) for r in range(residents)]
        parts += [sq_high.astype(F32), sq_low.astype(F32)]
        if outs[j].shape[0] > filled:
            parts.append(jnp.zeros((outs[j].shape[0] - filled, 128), F32))
        outs[j][...] = jnp.concatenate(parts, axis=0).astype(BF16)


def attend_resident(rank, lengths, queries, squares, k_cache, v_cache, ranks):
    residents, positions, width = k_cache.shape
    heads = queries.shape[1]
    heads_mine = heads // ranks
    rows = -(-(residents * (heads_mine + 3) + 2 * squares.shape[0]) // 16) * 16
    return pl.pallas_call(
        functools.partial(resident_kernel, ranks),
        in_specs=[SMEM, SMEM, VMEM, VMEM, HBM, HBM],
        out_specs=[VMEM] * ranks,
        out_shape=[jax.ShapeDtypeStruct((rows, 128), BF16)] * ranks,
        scratch_shapes=[
            pltpu.VMEM((residents, positions, width), BF16),
            pltpu.VMEM((residents, positions, width), BF16),
            pltpu.VMEM((residents, heads, 128), F32),
            pltpu.VMEM((residents, 3, ranks, 128), F32),
            pltpu.SemaphoreType.DMA((2, residents)),
        ],
        compiler_params=pltpu.CompilerParams(vmem_limit_bytes=32 * MIB),
        cost_estimate=pl.CostEstimate(
            flops=4 * residents * heads * positions * 128,
            bytes_accessed=4 * residents * positions * width,
            transcendentals=residents * heads * positions,
        ),
        name="attend_resident",
    )(rank, lengths, queries, squares, k_cache, v_cache)


def expand(own, rows):
    per = rows // own.shape[0]
    which = iota((rows, 128), 0) // per
    out = jnp.broadcast_to(own[0:1], (rows, 128))
    for h in range(1, own.shape[0]):
        out = jnp.where(which == h, own[h : h + 1], out)
    return out


def moved_kernel(
    insts, ranks, features, at_sq, here_ref, dest_ref, count_ref, gain_ref, cos_ref, sin_ref, *rest
):
    pieces, rest = rest[:ranks], rest[ranks:]
    payloads, rest = rest[:ranks], rest[ranks:]
    asks, rest = rest[: insts - 1], rest[insts - 1 :]
    out_ref, q_ref, own_ref, line_ref = rest
    here = here_ref[0]
    requests = dest_ref.shape[0]
    tokens = pieces[0].shape[0]
    piece = pieces[0].shape[1] // 2
    kv_mine = piece // 128
    heads_mine = line_ref.shape[1] // 128
    rows = requests * heads_mine
    scale = F32(1.0) / jnp.sqrt(F32(128.0))
    gain = gain_ref[...].astype(F32)

    row_request = iota((rows, tokens), 0) // heads_mine
    limit = jnp.zeros((rows, tokens), jnp.int32)
    for r in range(requests):
        dest = dest_ref[r, here]
        limit = jnp.where(row_request == r, count_ref[r, here], limit)
        place = jnp.int32(0)
        for s in range(insts):
            for c in range(requests):
                place += jnp.where((dest_ref[c, s] == dest) & (here > s), 1, 0).astype(jnp.int32)
        shift = lax.rem(here - dest + insts, insts)
        for j in range(1, insts):

            @pl.when(shift == j)
            def _():
                ask = asks[j - 1][place].astype(F32)
                at = slice(r * heads_mine, (r + 1) * heads_mine)
                q_ref[at, :] = ask[:heads_mine]
                own_ref[0, at, :] = expand(ask[heads_mine : heads_mine + kv_mine], heads_mine)
                own_ref[1, at, :] = expand(
                    ask[heads_mine + kv_mine : heads_mine + 2 * kv_mine], heads_mine
                )

    squares = None
    blocks = tokens // 128
    for t in range(ranks):
        both = payloads[t][at_sq : at_sq + 2 * blocks, :].astype(F32)
        both = both[:blocks] + both[blocks:]
        squares = both if squares is None else squares + both
    squares = jnp.concatenate(
        [row_to_column(squares[b : b + 1], 128) for b in range(blocks)], axis=0
    )
    kv = pieces[0][...].astype(F32)
    for t in range(1, ranks):
        kv = kv + pieces[t][...].astype(F32)
    kv = kv * lax.rsqrt(squares / features + EPS)

    q = q_ref[...]
    q16 = q.astype(BF16)
    which = iota((rows, tokens), 0) % heads_mine // (heads_mine // kv_mine)
    scores = None
    for h in range(kv_mine):
        key = kv[:, h * 128 : (h + 1) * 128]
        key = key * lax.rsqrt(jnp.mean(key * key, axis=1, keepdims=True) + EPS) * gain
        key = key * cos_ref[...] + pltpu.roll(key, 64, 1) * sin_ref[...]
        part = lax.dot_general(
            q16, key.astype(BF16), (((1,), (1,)), ((), ())), preferred_element_type=F32
        )
        scores = part if scores is None else jnp.where(which == h, part, scores)
    token = iota((rows, tokens), 1)
    valid = (token % requests == row_request) & (token // requests < limit)
    scores = jnp.where(valid, scores * scale, ABSENT)
    own_score = jnp.sum(q * own_ref[0], axis=1, keepdims=True) * scale
    top = jnp.maximum(jnp.max(scores, axis=1, keepdims=True), own_score)
    weights = jnp.where(valid, jnp.exp(scores - top), 0.0)
    own_weight = jnp.exp(own_score - top)
    total = jnp.sum(weights, axis=1, keepdims=True) + own_weight
    weights = weights.astype(BF16)
    summed = None
    for h in range(kv_mine):
        value = kv[:, piece + h * 128 : piece + (h + 1) * 128].astype(BF16)
        part = jnp.dot(weights, value, preferred_element_type=F32)
        summed = part if summed is None else jnp.where(which[:, :128] == h, part, summed)
    summed = summed + own_weight.astype(BF16).astype(F32) * own_ref[1]
    result = summed / total
    for r in range(requests):
        for h in range(heads_mine):
            at = r * heads_mine + h
            line_ref[r : r + 1, h * 128 : (h + 1) * 128] = result[at : at + 1, :]
    out_ref[...] = line_ref[...].astype(BF16)


def attend_moved(here, dest, count, k_gain, cos, sin, pieces, payloads, asks, heads_mine, at_sq, features):
    requests = dest.shape[0]
    insts, ranks = len(asks) + 1, len(pieces)
    rows = requests * heads_mine
    return pl.pallas_call(
        functools.partial(moved_kernel, insts, ranks, features, at_sq),
        in_specs=[SMEM] * 3 + [VMEM] * (3 + 2 * ranks + insts - 1),
        out_specs=VMEM,
        out_shape=jax.ShapeDtypeStruct((requests, heads_mine * 128), BF16),
        scratch_shapes=[
            pltpu.VMEM((rows, 128), F32),
            pltpu.VMEM((2, rows, 128), F32),
            pltpu.VMEM((requests, heads_mine * 128), F32),
        ],
        compiler_params=pltpu.CompilerParams(vmem_limit_bytes=16 * MIB),
        name="attend_moved",
    )(here, dest, count, k_gain, cos, sin, *pieces, *payloads, *asks)


def combine_kernel(ranks, residents, ask_ref, *rest):
    payloads = rest[:ranks]
    out_ref, line_ref = rest[ranks:]
    heads_mine = line_ref.shape[1] // 128
    kv_mine = (ask_ref.shape[1] - heads_mine) // 2
    scale = F32(1.0) / jnp.sqrt(F32(128.0))
    at = residents * heads_mine
    for r in range(residents):
        q = ask_ref[r, :heads_mine, :].astype(F32)
        own_k = expand(ask_ref[r, heads_mine : heads_mine + kv_mine, :].astype(F32), heads_mine)
        own_v = expand(
            ask_ref[r, heads_mine + kv_mine : heads_mine + 2 * kv_mine, :].astype(F32), heads_mine
        )
        own_score = jnp.sum(q * own_k, axis=1, keepdims=True) * scale
        peaks, totals = [], []
        for t in range(ranks):
            stat = payloads[t][at : at + 3 * residents, :].astype(F32)
            peaks.append(row_to_column(stat[r : r + 1], heads_mine))
            total = stat[residents + r : residents + r + 1]
            total = total + stat[2 * residents + r : 2 * residents + r + 1]
            totals.append(row_to_column(total, heads_mine))
        top = own_score
        for t in range(ranks):
            top = jnp.maximum(top, peaks[t])
        own_weight = jnp.exp(own_score - top)
        denom = own_weight
        numer = own_weight.astype(BF16).astype(F32) * own_v
        for t in range(ranks):
            keep = jnp.exp(peaks[t] - top)
            denom = denom + keep * totals[t]
            numer = numer + keep * payloads[t][r * heads_mine : (r + 1) * heads_mine, :].astype(F32)
        result = numer / denom
        for h in range(heads_mine):
            line_ref[r : r + 1, h * 128 : (h + 1) * 128] = result[h : h + 1, :]
    out_ref[...] = line_ref[...].astype(BF16)


def combine_resident(asks, payloads, residents, heads_mine):
    return pl.pallas_call(
        functools.partial(combine_kernel, len(payloads), residents),
        in_specs=[VMEM] * (1 + len(payloads)),
        out_specs=VMEM,
        out_shape=jax.ShapeDtypeStruct((residents, heads_mine * 128), BF16),
        scratch_shapes=[pltpu.VMEM((residents, heads_mine * 128), F32)],
        compiler_params=pltpu.CompilerParams(vmem_limit_bytes=8 * MIB),
        name="combine_resident",
    )(asks, *payloads)


def finish_kernel(insts, here_ref, dest_ref, kept_ref, *rest):
    moved = rest[: insts - 1]
    out_ref, line_ref = rest[insts - 1 :]
    residents = kept_ref.shape[0]
    requests = dest_ref.shape[0]
    here = here_ref[0]
    line_ref[:residents, :] = kept_ref[...].astype(F32)
    place = jnp.int32(residents)
    for s in range(insts):
        for c in range(requests):
            mine = dest_ref[c, s] == here
            shift = lax.rem(here - s + insts, insts)
            for j in range(1, insts):

                @pl.when(mine & (shift == j))
                def _():
                    line_ref[pl.ds(place, 1), :] = moved[j - 1][c : c + 1, :].astype(F32)

            place += jnp.where(mine, 1, 0).astype(jnp.int32)
    out_ref[...] = line_ref[...].astype(BF16)


def finish(here, dest, kept, moved):
    residents, width = kept.shape
    rows = residents + dest.shape[0]
    return pl.pallas_call(
        functools.partial(finish_kernel, len(moved) + 1),
        in_specs=[SMEM, SMEM, VMEM] + [VMEM] * len(moved),
        out_specs=VMEM,
        out_shape=jax.ShapeDtypeStruct((rows, width), BF16),
        scratch_shapes=[pltpu.VMEM((rows, width), F32)],
        compiler_params=pltpu.CompilerParams(vmem_limit_bytes=8 * MIB),
        name="finish",
    )(here, dest, kept, *moved)


def shifted(x, axis, j, n):
    return lax.ppermute(x, axis, [(i, (i + j) % n) for i in range(n)])


def rotation(slots, requests, head_size):
    half = head_size // 2
    freq = THETA ** (-np.arange(half) * 2.0 / head_size)
    angle = np.repeat(np.arange(slots), requests)[:, None] * freq[None, :]
    cos, sin = np.cos(angle), np.sin(angle)
    return (
        np.concatenate([cos, cos], axis=1).astype(np.float32),
        np.concatenate([-sin, sin], axis=1).astype(np.float32),
    )


def per_device(
    mig_hidden,
    mig_dest,
    mig_count,
    attn_gain,
    kv_weight,
    k_gain,
    query,
    new_kv,
    k_cache,
    v_cache,
    lengths,
):
    insts = lax.axis_size("inst")
    ranks = lax.axis_size("tp")
    here = lax.axis_index("inst").astype(jnp.int32).reshape(1)
    rank = lax.axis_index("tp").astype(jnp.int32).reshape(1)
    head_size = k_gain.shape[0]
    slots, requests, feats = mig_hidden.shape[1:]
    residents = k_cache.shape[1]
    decoded = query.shape[1]
    heads = query.shape[2] // head_size
    kv_heads = kv_weight.shape[1] // 2 // head_size
    heads_mine = heads // ranks
    group = heads // kv_heads
    kv_mine = max(1, heads_mine // group)

    queries = query[0].reshape(decoded, heads, head_size)
    own = new_kv[0].reshape(decoded, 2, kv_heads, head_size)
    my_queries = lax.dynamic_slice_in_dim(queries, rank[0] * heads_mine, heads_mine, 1)
    my_own = lax.dynamic_slice_in_dim(own, rank[0] * heads_mine // group, kv_mine, 2)
    asks = jnp.concatenate(
        [my_queries, my_own.reshape(decoded, 2 * kv_mine, head_size)], axis=1
    )
    asked = [shifted(asks[residents:], "inst", j, insts) for j in range(1, insts)]

    pieces, squares = project(
        rank, mig_hidden[0], attn_gain, kv_weight, ranks, group, kv_mine
    )
    pieces = [pieces[0]] + [shifted(pieces[j], "tp", j, ranks) for j in range(1, ranks)]
    payloads = attend_resident(rank, lengths, queries, squares, k_cache[0], v_cache[0], ranks)
    payloads = [payloads[0]] + [shifted(payloads[j], "tp", j, ranks) for j in range(1, ranks)]
    kept = combine_resident(asks, payloads, residents, heads_mine)
    dest, count = mig_dest.T, mig_count.T
    cos, sin = rotation(slots, requests, head_size)
    moved = attend_moved(
        here,
        dest,
        count,
        k_gain.reshape(1, head_size),
        cos,
        sin,
        pieces,
        payloads,
        asked,
        heads_mine,
        residents * (heads_mine + 3),
        feats * ranks,
    )
    moved = [shifted(moved, "inst", j, insts) for j in range(1, insts)]
    return finish(here, dest, kept, moved)[None]


def solution(mesh):
    placed = (
        P(("group", "inst"), None, None, "tp"),
        P("group", None),
        P("group", None),
        P("tp"),
        P("tp", None),
        P(),
        P(("group", "inst"), None, None),
        P(("group", "inst"), None, None),
        P(("group", "inst"), None, "tp", None),
        P(("group", "inst"), None, "tp", None),
        P(("group", "inst"), None),
    )
    return jax.shard_map(
        per_device,
        mesh=mesh,
        in_specs=placed,
        out_specs=P(("group", "inst"), None, "tp"),
        check_vma=False,
    )
```

time: 43.3 us -> 48.2 us (1.11)
  the two profiles are of different devices: /device:TPU:0 before, /device:TPU:1 now
where the time goes in v2:
time: 48.2 us; the launch traced here: 47.9 us
  starting transfers between devices  14.6 us (30%)
  Pallas kernels  13.3 us (28%)
  local copies, waits for them, and re-layouts  12.1 us (25%)
  waiting for transfers between devices  7.7 us (16%)
    ppermute x12, starting transfers between devices, shifted(): return lax.ppermute(x, axis, [(i, (i + j) % n) for i in range(n)])  14.6 us
    unnamed x24, local copies, waits for them, and re-layouts  12.1 us
    ppermute x12, waiting for transfers between devices, shifted(): return lax.ppermute(x, axis, [(i, (i + j) % n) for i in range(n)])  7.7 us
    pallas_call x1, Pallas kernels, attend_resident(): pl.pallas_call(functools.partial(resident_kernel, ranks), in_specs=[SMEM,...  7.61 us
    pallas_call x1, Pallas kernels, project(): pl.pallas_call(functools.partial(project_kernel, ranks, group), in_specs=...  2.91 us
    pallas_call x1, Pallas kernels, finish(): pl.pallas_call(functools.partial(finish_kernel, len(moved) + 1), in_specs...  1.34 us
    pallas_call x1, Pallas kernels, attend_moved(): pl.pallas_call(functools.partial(moved_kernel, insts, ranks, features, at...  1.28 us
  transfers between devices with their start and end apart: 12, of which 6 were waited for; matrix products, arithmetic and copies ran while one was open for 4% of the time, Pallas kernels for 16%

profile of v2, /device:TPU:1, one launch (start us, length us, event | category | flops | bytes accessed | tf_op | source)
XLA Modules:
  0.0 47.9 jit_solution(17964589704884219145)
XLA Ops:
  0.0 0.0 copy-start.2
  0.0 2.5 %copy-done.2 = bf16[1280,2048]{1,0:T(8,128)(2,1)S(1)} copy-done((bf16[1280,2048]{1,0:T(8,128)(2,1)S(1)}, bf16[1280,2048]{1,0:T(8,128)(2,1)}, u32[]{:S(2)}) %copy-start.2) | copy-done | bytes 5242904
  2.5 0.0 copy-start.3
  2.5 1.0 %copy-done.3 = bf16[1,64,2,1280]{3,2,1,0:T(2,128)(2,1)S(1)} copy-done((bf16[1,64,2,1280]{3,2,1,0:T(2,128)(2,1)S(1)}, bf16[1,64,2,1280]{3,2,1,0:T(2,128)(2,1)}, u32[]{:S(2)}) %copy-start.3) | copy-done | bytes 327704
  3.5 0.0 copy-start.6
  3.5 0.7 %copy-done.6 = bf16[1280]{0:T(1024)(128)(2,1)S(1)} copy-done((bf16[1280]{0:T(1024)(128)(2,1)S(1)}, bf16[1280]{0:T(1024)(128)(2,1)}, u32[]{:S(2)}) %copy-start.6) | copy-done | bytes 2584
  4.1 2.9 %project.1 = (bf16[128,512]{1,0:T(8,128)(2,1)S(1)}, bf16[128,512]{1,0:T(8,128)(2,1)S(1)}, bf16[128,512]{1,0:T(8,128)(2,1)S(1)}, bf16[128,512]{1,0:T(8,128)(2,1)S(1)}, f32[1,128]{1,0:T(1,128)S(1)}) custom-call(s32[1]{0:T(128)} %bitcast.3.rank_ref, bf16[1280]{0:T(1024)(128)(2,1)S(1)} %copy-done.6, bf16[64,2,1280]{2,1,0:T(2,128)(2,1)S(1)} %bitcast.25, ...), custom_call_target="tpu_custom_call" | custom-call | flops 671088640 | bytes 5242880 | tf_op jit(solution)/shard_map/project/pallas_call | solution.py:92
  7.1 2.2 %collective-permute-start.3 = (bf16[128,512]{1,0:T(8,128)(2,1)S(1)}, bf16[128,512]{1,0:T(8,128)(2,1)S(1)}, u32[]{:S(2)}, u32[]{:S(2)}) collective-permute-start(bf16[128,512]{1,0:T(8,128)(2,1)S(1)} %get-tuple-element.20), channel_id=1, source_target_pairs={{0,1},{1,2},{2,3},{3,0},{4,5},{5,6},{6,7},{7,4},{8,9},{9,10},{10,1... | collective-permute-start | bytes 393224 | tf_op jit(solution)/shard_map/ppermute | solution.py:409
  9.2 2.3 %collective-permute-start.4 = (bf16[128,512]{1,0:T(8,128)(2,1)S(1)}, bf16[128,512]{1,0:T(8,128)(2,1)S(1)}, u32[]{:S(2)}, u32[]{:S(2)}) collective-permute-start(bf16[128,512]{1,0:T(8,128)(2,1)S(1)} %get-tuple-element.21), channel_id=1, source_target_pairs={{0,2},{1,3},{2,0},{3,1},{4,6},{5,7},{6,4},{7,5},{8,10},{9,11},{10,... | collective-permute-start | bytes 393224 | tf_op jit(solution)/shard_map/ppermute | solution.py:409
  11.5 1.1 %collective-permute-start.5 = (bf16[128,512]{1,0:T(8,128)(2,1)S(1)}, bf16[128,512]{1,0:T(8,128)(2,1)S(1)}, u32[]{:S(2)}, u32[]{:S(2)}) collective-permute-start(bf16[128,512]{1,0:T(8,128)(2,1)S(1)} %get-tuple-element.22), channel_id=1, source_target_pairs={{0,3},{1,0},{2,1},{3,2},{4,7},{5,4},{6,5},{7,6},{8,11},{9,8},{10,9... | collective-permute-start | bytes 393224 | tf_op jit(solution)/shard_map/ppermute | solution.py:409
  12.6 0.8 %copy.19 = bf16[1,5,16,128]{3,2,1,0:T(8,128)(2,1)S(1)} copy(bf16[1,5,16,128]{3,1,2,0:T(8,128)(2,1)} %bitcast.33) | data formatting | bytes 40960
  13.4 0.9 %copy.18 = bf16[1,5,64,128]{3,2,1,0:T(8,128)(2,1)S(1)} copy(bf16[1,5,64,128]{3,1,2,0:T(8,128)(2,1)} %bitcast.30) | data formatting | bytes 163840
  14.4 2.7 %collective-permute-start.6 = (bf16[2,20,128]{2,1,0:T(8,128)(2,1)S(1)}, bf16[2,20,128]{2,1,0:T(8,128)(2,1)S(1)}, u32[]{:S(2)}, u32[]{:S(2)}) collective-permute-start(bf16[2,20,128]{2,1,0:T(8,128)(2,1)S(1)} %fusion), channel_id=1, source_target_pairs={{0,4},{4,8},{8,12},{12,0},{1,5},{5,9},{9,13},{13,1},{2,6},{6,10},{... | collective-permute-start | bytes 30728 | tf_op jit(solution)/shard_map/ppermute | solution.py:409
  17.0 0.3 collective-permute-start.7
  17.3 0.0 copy-start
  17.3 2.8 %copy-done = bf16[1,3,1024,1024]{3,2,1,0:T(8,128)(2,1)S(1)} copy-done((bf16[1,3,1024,1024]{3,2,1,0:T(8,128)(2,1)S(1)}, bf16[1,3,1024,1024]{3,2,1,0:T(8,128)(2,1)}, u32[]{:S(2)}) %copy-start) | copy-done | bytes 6291480
  20.1 0.0 copy-start.1
  20.1 2.8 %copy-done.1 = bf16[1,3,1024,1024]{3,2,1,0:T(8,128)(2,1)S(1)} copy-done((bf16[1,3,1024,1024]{3,2,1,0:T(8,128)(2,1)S(1)}, bf16[1,3,1024,1024]{3,2,1,0:T(8,128)(2,1)}, u32[]{:S(2)}) %copy-start.1) | copy-done | bytes 6291480
  22.8 0.0 copy-start.9
  22.8 0.7 %copy-done.9 = s32[1,3]{1,0:T(1,128)S(1)} copy-done((s32[1,3]{1,0:T(1,128)S(1)}, s32[1,3]{1,0:T(1,128)}, u32[]{:S(2)}) %copy-start.9) | copy-done | bytes 36
  23.5 0.0 copy-start.4
  23.5 0.0 copy-start.5
  23.5 0.0 copy-start.7
  23.5 0.0 copy-start.8
  23.5 0.0 copy-start.10
  23.5 7.6 %attend_resident.1 = (bf16[64,128]{1,0:T(8,128)(2,1)S(1)}, bf16[64,128]{1,0:T(8,128)(2,1)S(1)}, bf16[64,128]{1,0:T(8,128)(2,1)S(1)}, bf16[64,128]{1,0:T(8,128)(2,1)S(1)}) custom-call(s32[1]{0:T(128)} %bitcast.3.rank_ref, s32[1,3]{1,0:T(1,128)S(1)} %copy-done.9, bf16[5,64,128]{2,1,0:T(8,128)(2,1)S(1)} %bitcast.24, f32[1,128]{1,0:T(1,128)S(1)} %get-tuple-element.14.sq_ref, ...), custom_call_target="tpu_custom_call" | custom-call | flops 100663296 | bytes 12582912 | tf_op jit(solution)/shard_map/attend_resident/pallas_call | solution.py:185
  31.1 0.0 collective-permute-done.6.rest_8_
  31.2 0.5 collective-permute-start
  31.6 0.0 collective-permute-done.7.rest_9_
  31.6 0.5 %collective-permute-start.8 = (bf16[2,20,128]{2,1,0:T(8,128)(2,1)S(1)}, bf16[2,20,128]{2,1,0:T(8,128)(2,1)S(1)}, u32[]{:S(2)}, u32[]{:S(2)}) collective-permute-start(bf16[2,20,128]{2,1,0:T(8,128)(2,1)S(1)} %fusion), channel_id=1, source_target_pairs={{0,12},{4,0},{8,4},{12,8},{1,13},{5,1},{9,5},{13,9},{2,14},{6,2},{... | collective-permute-start | bytes 30728 | tf_op jit(solution)/shard_map/ppermute | solution.py:409
  32.1 2.6 %collective-permute-done.8.rest_10_ = bf16[2,20,128]{2,1,0:T(8,128)(2,1)S(1)} collective-permute-done((bf16[2,20,128]{2,1,0:T(8,128)(2,1)S(1)}, bf16[2,20,128]{2,1,0:T(8,128)(2,1)S(1)}, u32[]{:S(2)}, u32[]{:S(2)}) %collective-permute-start.8) | collective-permute-done | bytes 10272 | tf_op jit(solution)/shard_map/ppermute | solution.py:409
  34.7 0.1 collective-permute-start.1
  34.8 0.8 %collective-permute-done.rest_1_.rest_5_ = bf16[64,128]{1,0:T(8,128)(2,1)S(1)} collective-permute-done((bf16[64,128]{1,0:T(8,128)(2,1)S(1)}, bf16[64,128]{1,0:T(8,128)(2,1)S(1)}, u32[]{:S(2)}, u32[]{:S(2)}) %collective-permute-start) | collective-permute-done | bytes 16416 | tf_op jit(solution)/shard_map/ppermute | solution.py:409
  35.6 2.0 %collective-permute-start.2 = (bf16[64,128]{1,0:T(8,128)(2,1)S(1)}, bf16[64,128]{1,0:T(8,128)(2,1)S(1)}, u32[]{:S(2)}, u32[]{:S(2)}) collective-permute-start(bf16[64,128]{1,0:T(8,128)(2,1)S(1)} %get-tuple-element.18), channel_id=1, source_target_pairs={{0,3},{1,0},{2,1},{3,2},{4,7},{5,4},{6,5},{7,6},{8,11},{9,8},{10,9... | collective-permute-start | bytes 49160 | tf_op jit(solution)/shard_map/ppermute | solution.py:409
  37.6 0.6 %collective-permute-done.1.rest_2_.rest_6_ = bf16[64,128]{1,0:T(8,128)(2,1)S(1)} collective-permute-done((bf16[64,128]{1,0:T(8,128)(2,1)S(1)}, bf16[64,128]{1,0:T(8,128)(2,1)S(1)}, u32[]{:S(2)}, u32[]{:S(2)}) %collective-permute-start.1) | collective-permute-done | bytes 16416 | tf_op jit(solution)/shard_map/ppermute | solution.py:409
  38.2 0.8 %collective-permute-done.2.rest_3_.rest_7_ = bf16[64,128]{1,0:T(8,128)(2,1)S(1)} collective-permute-done((bf16[64,128]{1,0:T(8,128)(2,1)S(1)}, bf16[64,128]{1,0:T(8,128)(2,1)S(1)}, u32[]{:S(2)}, u32[]{:S(2)}) %collective-permute-start.2) | collective-permute-done | bytes 16416 | tf_op jit(solution)/shard_map/ppermute | solution.py:409
  39.0 0.0 collective-permute-done.3.rest_1_
  39.0 0.0 collective-permute-done.4.rest_2_
  39.0 0.0 collective-permute-done.5.rest_3_
  39.0 0.0 copy-done.4
  39.0 0.0 copy-done.5
  39.0 0.0 copy-done.7
  39.1 0.0 copy-done.8
  39.1 0.0 copy-done.10
  39.1 1.3 %attend_moved.1 = bf16[2,2048]{1,0:T(2,128)(2,1)S(1)} custom-call(s32[1]{0:T(128)} %bitcast.here_ref, s32[2,4]{1,0:T(2,128)S(1)} %bitcast.26, s32[2,4]{1,0:T(2,128)S(1)} %bitcast.28, bf16[1,128]{1,0:T(2,128)(2,1)S(1)} %bitcast.29, f32[128,128]{1,0:T(8,128)S(1)} %copy-done.4, f32[128,128]{1,0:T(8,128)S(1)} %copy-done.5, ...), custom_call_target="tpu_custom_call" | custom-call | tf_op jit(solution)/shard_map/attend_moved/pallas_call | solution.py:308
  40.4 2.0 %collective-permute-start.9 = (bf16[2,2048]{1,0:T(2,128)(2,1)S(1)}, bf16[2,2048]{1,0:T(2,128)(2,1)S(1)}, u32[]{:S(2)}, u32[]{:S(2)}) collective-permute-start(bf16[2,2048]{1,0:T(2,128)(2,1)S(1)} %attend_moved.1), channel_id=1, source_target_pairs={{0,4},{4,8},{8,12},{12,0},{1,5},{5,9},{9,13},{13,1},{2,6},{6,10},{... | collective-permute-start | bytes 24584 | tf_op jit(solution)/shard_map/ppermute | solution.py:409
  42.4 1.1 %collective-permute-start.10 = (bf16[2,2048]{1,0:T(2,128)(2,1)S(1)}, bf16[2,2048]{1,0:T(2,128)(2,1)S(1)}, u32[]{:S(2)}, u32[]{:S(2)}) collective-permute-start(bf16[2,2048]{1,0:T(2,128)(2,1)S(1)} %attend_moved.1), channel_id=1, source_target_pairs={{0,8},{4,12},{8,0},{12,4},{1,9},{5,13},{9,1},{13,5},{2,10},{6,14},... | collective-permute-start | bytes 24584 | tf_op jit(solution)/shard_map/ppermute | solution.py:409
  43.5 0.0 collective-permute-start.11
  43.5 0.2 combine_resident.1.kept_ref
  43.6 0.0 collective-permute-done.9.rest_0_
  43.6 1.2 %collective-permute-done.10.rest_1_ = bf16[2,2048]{1,0:T(2,128)(2,1)S(1)} collective-permute-done((bf16[2,2048]{1,0:T(2,128)(2,1)S(1)}, bf16[2,2048]{1,0:T(2,128)(2,1)S(1)}, u32[]{:S(2)}, u32[]{:S(2)}) %collective-permute-start.10) | collective-permute-done | bytes 8224 | tf_op jit(solution)/shard_map/ppermute | solution.py:409
  44.9 1.7 %collective-permute-done.11.rest_2_ = bf16[2,2048]{1,0:T(2,128)(2,1)S(1)} collective-permute-done((bf16[2,2048]{1,0:T(2,128)(2,1)S(1)}, bf16[2,2048]{1,0:T(2,128)(2,1)S(1)}, u32[]{:S(2)}, u32[]{:S(2)}) %collective-permute-start.11) | collective-permute-done | bytes 8224 | tf_op jit(solution)/shard_map/ppermute | solution.py:409
  46.5 1.3 %finish.1 = bf16[5,2048]{1,0:T(8,128)(2,1)} custom-call(s32[1]{0:T(128)} %bitcast.here_ref, s32[2,4]{1,0:T(2,128)S(1)} %bitcast.27, bf16[3,2048]{1,0:T(4,128)(2,1)S(1)} %combine_resident.1.kept_ref, bf16[2,2048]{1,0:T(2,128)(2,1)S(1)} %collective-permute-done.9.rest_0_, bf16[2,2048]{1,0:T(2,128)(2,1)S(1)} %collective-permute-done.10.rest_1_, ...), custom_call_target="tpu_custom_call" | custom-call | tf_op jit(solution)/shard_map/finish/pallas_call | solution.py:397
  (4 shorter events, 0.0 us)
Async XLA Ops:
  0.0 2.5 %copy-start.2 = (bf16[1280,2048]{1,0:T(8,128)(2,1)S(1)}, bf16[1280,2048]{1,0:T(8,128)(2,1)}, u32[]{:S(2)}) copy-start(bf16[1280,2048]{1,0:T(8,128)(2,1)} %w_hbm.1) | copy-start | bytes 15728644
  2.5 1.0 %copy-start.3 = (bf16[1,64,2,1280]{3,2,1,0:T(2,128)(2,1)S(1)}, bf16[1,64,2,1280]{3,2,1,0:T(2,128)(2,1)}, u32[]{:S(2)}) copy-start(bf16[1,64,2,1280]{3,2,1,0:T(2,128)(2,1)} %param.13) | copy-start | bytes 983044
  3.5 0.7 %copy-start.6 = (bf16[1280]{0:T(1024)(128)(2,1)S(1)}, bf16[1280]{0:T(1024)(128)(2,1)}, u32[]{:S(2)}) copy-start(bf16[1280]{0:T(1024)(128)(2,1)} %gain_ref.1) | copy-start | bytes 7684
  7.1 31.9 %collective-permute-start.3 = (bf16[128,512]{1,0:T(8,128)(2,1)S(1)}, bf16[128,512]{1,0:T(8,128)(2,1)S(1)}, u32[]{:S(2)}, u32[]{:S(2)}) collective-permute-start(bf16[128,512]{1,0:T(8,128)(2,1)S(1)} %get-tuple-element.20), channel_id=1, source_target_pairs={{0,1},{1,2},{2,3},{3,0},{4,5},{5,6},{6,7},{7,4},{8,9},{9,10},{10,1... | collective-permute-start | bytes 393224 | tf_op jit(solution)/shard_map/ppermute | solution.py:409
  9.2 29.8 %collective-permute-start.4 = (bf16[128,512]{1,0:T(8,128)(2,1)S(1)}, bf16[128,512]{1,0:T(8,128)(2,1)S(1)}, u32[]{:S(2)}, u32[]{:S(2)}) collective-permute-start(bf16[128,512]{1,0:T(8,128)(2,1)S(1)} %get-tuple-element.21), channel_id=1, source_target_pairs={{0,2},{1,3},{2,0},{3,1},{4,6},{5,7},{6,4},{7,5},{8,10},{9,11},{10,... | collective-permute-start | bytes 393224 | tf_op jit(solution)/shard_map/ppermute | solution.py:409
  11.5 27.5 %collective-permute-start.5 = (bf16[128,512]{1,0:T(8,128)(2,1)S(1)}, bf16[128,512]{1,0:T(8,128)(2,1)S(1)}, u32[]{:S(2)}, u32[]{:S(2)}) collective-permute-start(bf16[128,512]{1,0:T(8,128)(2,1)S(1)} %get-tuple-element.22), channel_id=1, source_target_pairs={{0,3},{1,0},{2,1},{3,2},{4,7},{5,4},{6,5},{7,6},{8,11},{9,8},{10,9... | collective-permute-start | bytes 393224 | tf_op jit(solution)/shard_map/ppermute | solution.py:409
  14.4 16.8 %collective-permute-start.6 = (bf16[2,20,128]{2,1,0:T(8,128)(2,1)S(1)}, bf16[2,20,128]{2,1,0:T(8,128)(2,1)S(1)}, u32[]{:S(2)}, u32[]{:S(2)}) collective-permute-start(bf16[2,20,128]{2,1,0:T(8,128)(2,1)S(1)} %fusion), channel_id=1, source_target_pairs={{0,4},{4,8},{8,12},{12,0},{1,5},{5,9},{9,13},{13,1},{2,6},{6,10},{... | collective-permute-start | bytes 30728 | tf_op jit(solution)/shard_map/ppermute | solution.py:409
  17.0 14.6 %collective-permute-start.7 = (bf16[2,20,128]{2,1,0:T(8,128)(2,1)S(1)}, bf16[2,20,128]{2,1,0:T(8,128)(2,1)S(1)}, u32[]{:S(2)}, u32[]{:S(2)}) collective-permute-start(bf16[2,20,128]{2,1,0:T(8,128)(2,1)S(1)} %fusion), channel_id=1, source_target_pairs={{0,8},{4,12},{8,0},{12,4},{1,9},{5,13},{9,1},{13,5},{2,10},{6,14},... | collective-permute-start | bytes 30728 | tf_op jit(solution)/shard_map/ppermute | solution.py:409
  17.3 2.8 %copy-start = (bf16[1,3,1024,1024]{3,2,1,0:T(8,128)(2,1)S(1)}, bf16[1,3,1024,1024]{3,2,1,0:T(8,128)(2,1)}, u32[]{:S(2)}) copy-start(bf16[1,3,1024,1024]{3,2,1,0:T(8,128)(2,1)} %param.21) | copy-start | bytes 18874372
  20.1 2.8 %copy-start.1 = (bf16[1,3,1024,1024]{3,2,1,0:T(8,128)(2,1)S(1)}, bf16[1,3,1024,1024]{3,2,1,0:T(8,128)(2,1)}, u32[]{:S(2)}) copy-start(bf16[1,3,1024,1024]{3,2,1,0:T(8,128)(2,1)} %param.22) | copy-start | bytes 18874372
  22.8 0.7 %copy-start.9 = (s32[1,3]{1,0:T(1,128)S(1)}, s32[1,3]{1,0:T(1,128)}, u32[]{:S(2)}) copy-start(s32[1,3]{1,0:T(1,128)} %len_ref.1) | copy-start | bytes 40
  23.5 15.5 %copy-start.4 = (f32[128,128]{1,0:T(8,128)S(1)}, f32[128,128]{1,0:T(8,128)}, u32[]{:S(2)}) copy-start(f32[128,128]{1,0:T(8,128)} %constant.33.clone.cos_ref) | copy-start | bytes 196612
  23.5 15.5 %copy-start.5 = (f32[128,128]{1,0:T(8,128)S(1)}, f32[128,128]{1,0:T(8,128)}, u32[]{:S(2)}) copy-start(f32[128,128]{1,0:T(8,128)} %constant.34.clone.sin_ref) | copy-start | bytes 196612
  23.5 15.5 %copy-start.7 = (s32[4,2]{0,1:T(2,128)S(1)}, s32[4,2]{0,1:T(2,128)}, u32[]{:S(2)}) copy-start(s32[4,2]{0,1:T(2,128)} %param.14) | copy-start | bytes 100
  23.5 15.5 %copy-start.8 = (s32[4,2]{0,1:T(2,128)S(1)}, s32[4,2]{0,1:T(2,128)}, u32[]{:S(2)}) copy-start(s32[4,2]{0,1:T(2,128)} %param.15) | copy-start | bytes 100
  23.5 15.6 %copy-start.10 = (bf16[128]{0:T(256)(128)(2,1)S(1)}, bf16[128]{0:T(256)(128)(2,1)}, u32[]{:S(2)}) copy-start(bf16[128]{0:T(256)(128)(2,1)} %param.18) | copy-start | bytes 772
  31.2 4.4 %collective-permute-start = (bf16[64,128]{1,0:T(8,128)(2,1)S(1)}, bf16[64,128]{1,0:T(8,128)(2,1)S(1)}, u32[]{:S(2)}, u32[]{:S(2)}) collective-permute-start(bf16[64,128]{1,0:T(8,128)(2,1)S(1)} %get-tuple-element.16), channel_id=1, source_target_pairs={{0,1},{1,2},{2,3},{3,0},{4,5},{5,6},{6,7},{7,4},{8,9},{9,10},{10,1... | collective-permute-start | bytes 49160 | tf_op jit(solution)/shard_map/ppermute | solution.py:409
  31.6 3.1 %collective-permute-start.8 = (bf16[2,20,128]{2,1,0:T(8,128)(2,1)S(1)}, bf16[2,20,128]{2,1,0:T(8,128)(2,1)S(1)}, u32[]{:S(2)}, u32[]{:S(2)}) collective-permute-start(bf16[2,20,128]{2,1,0:T(8,128)(2,1)S(1)} %fusion), channel_id=1, source_target_pairs={{0,12},{4,0},{8,4},{12,8},{1,13},{5,1},{9,5},{13,9},{2,14},{6,2},{... | collective-permute-start | bytes 30728 | tf_op jit(solution)/shard_map/ppermute | solution.py:409
  34.7 3.5 %collective-permute-start.1 = (bf16[64,128]{1,0:T(8,128)(2,1)S(1)}, bf16[64,128]{1,0:T(8,128)(2,1)S(1)}, u32[]{:S(2)}, u32[]{:S(2)}) collective-permute-start(bf16[64,128]{1,0:T(8,128)(2,1)S(1)} %get-tuple-element.17), channel_id=1, source_target_pairs={{0,2},{1,3},{2,0},{3,1},{4,6},{5,7},{6,4},{7,5},{8,10},{9,11},{10,... | collective-permute-start | bytes 49160 | tf_op jit(solution)/shard_map/ppermute | solution.py:409
  35.6 3.4 %collective-permute-start.2 = (bf16[64,128]{1,0:T(8,128)(2,1)S(1)}, bf16[64,128]{1,0:T(8,128)(2,1)S(1)}, u32[]{:S(2)}, u32[]{:S(2)}) collective-permute-start(bf16[64,128]{1,0:T(8,128)(2,1)S(1)} %get-tuple-element.18), channel_id=1, source_target_pairs={{0,3},{1,0},{2,1},{3,2},{4,7},{5,4},{6,5},{7,6},{8,11},{9,8},{10,9... | collective-permute-start | bytes 49160 | tf_op jit(solution)/shard_map/ppermute | solution.py:409
  40.4 3.3 %collective-permute-start.9 = (bf16[2,2048]{1,0:T(2,128)(2,1)S(1)}, bf16[2,2048]{1,0:T(2,128)(2,1)S(1)}, u32[]{:S(2)}, u32[]{:S(2)}) collective-permute-start(bf16[2,2048]{1,0:T(2,128)(2,1)S(1)} %attend_moved.1), channel_id=1, source_target_pairs={{0,4},{4,8},{8,12},{12,0},{1,5},{5,9},{9,13},{13,1},{2,6},{6,10},{... | collective-permute-start | bytes 24584 | tf_op jit(solution)/shard_map/ppermute | solution.py:409
  42.4 2.5 %collective-permute-start.10 = (bf16[2,2048]{1,0:T(2,128)(2,1)S(1)}, bf16[2,2048]{1,0:T(2,128)(2,1)S(1)}, u32[]{:S(2)}, u32[]{:S(2)}) collective-permute-start(bf16[2,2048]{1,0:T(2,128)(2,1)S(1)} %attend_moved.1), channel_id=1, source_target_pairs={{0,8},{4,12},{8,0},{12,4},{1,9},{5,13},{9,1},{13,5},{2,10},{6,14},... | collective-permute-start | bytes 24584 | tf_op jit(solution)/shard_map/ppermute | solution.py:409
  43.5 3.1 %collective-permute-start.11 = (bf16[2,2048]{1,0:T(2,128)(2,1)S(1)}, bf16[2,2048]{1,0:T(2,128)(2,1)S(1)}, u32[]{:S(2)}, u32[]{:S(2)}) collective-permute-start(bf16[2,2048]{1,0:T(2,128)(2,1)S(1)} %attend_moved.1), channel_id=1, source_target_pairs={{0,12},{4,0},{8,4},{12,8},{1,13},{5,1},{9,5},{13,9},{2,14},{6,2},{... | collective-permute-start | bytes 24584 | tf_op jit(solution)/shard_map/ppermute | solution.py:409

commit v3 on v2

--- a/solution.py
+++ b/solution.py
@@ -41,15 +41,17 @@
     return high, (x - high.astype(F32)).astype(BF16)
 
 
-def project_kernel(ranks, group, rank_ref, gain_ref, x_hbm, w_hbm, *rest):
+def project_kernel(ranks, group, gain_hbm, x_hbm, w_hbm, *rest):
     outs, sq_ref = rest[:ranks], rest[ranks]
-    x_ref, w_ref, xg_ref, x_sem, w_sems = rest[ranks + 1 :]
+    gain_ref, x_ref, w_ref, xg_ref, in_sems, w_sems = rest[ranks + 1 :]
     slots, requests, feats = x_ref.shape
     piece = w_ref.shape[2] // 2
     kv_width = w_hbm.shape[1] // 2
     heads_mine = kv_width // 128 * group // ranks
-    rank = rank_ref[0]
-    x_copy = pltpu.make_async_copy(x_hbm, x_ref, x_sem)
+    rank = lax.axis_index("tp")
+    gain_copy = pltpu.make_async_copy(gain_hbm, gain_ref, in_sems.at[0])
+    gain_copy.start()
+    x_copy = pltpu.make_async_copy(x_hbm, x_ref, in_sems.at[1])
     x_copy.start()
     copies = []
     for j in range(ranks):
@@ -66,6 +68,7 @@
         copies.append(pair)
         for copy in pair:
             copy.start()
+    gain_copy.wait()
     x_copy.wait()
     rows = slots * requests
     squares = jnp.zeros((rows, 128), F32)
@@ -79,41 +82,42 @@
             x = jnp.concatenate([x, jnp.zeros((rows, 128 - width), F32)], axis=1)
         squares = squares + x
     sq_ref[...] = column_to_row(jnp.sum(squares, axis=1, keepdims=True), 128)
-    for j in range(ranks):
+    for j in list(range(1, ranks)) + [0]:
         for copy in copies[j]:
             copy.wait()
         outs[j][...] = jnp.dot(xg_ref[...], w_ref[j], preferred_element_type=F32).astype(BF16)
 
 
-def project(rank, x, gain, weight, ranks, group, kv_mine):
+def project(x, gain, weight, ranks, group, kv_mine):
     slots, requests, feats = x.shape
     rows = slots * requests
     piece = kv_mine * 128
     outs = pl.pallas_call(
         functools.partial(project_kernel, ranks, group),
-        in_specs=[SMEM, VMEM, HBM, HBM],
+        in_specs=[HBM, HBM, HBM],
         out_specs=[VMEM] * (ranks + 1),
         out_shape=[jax.ShapeDtypeStruct((rows, 2 * piece), BF16)] * ranks
         + [jax.ShapeDtypeStruct((rows // 128, 128), F32)],
         scratch_shapes=[
+            pltpu.VMEM((feats,), BF16),
             pltpu.VMEM((slots, requests, feats), BF16),
             pltpu.VMEM((ranks, feats, 2 * piece), BF16),
             pltpu.VMEM((rows, feats), BF16),
-            pltpu.SemaphoreType.DMA,
+            pltpu.SemaphoreType.DMA((2,)),
             pltpu.SemaphoreType.DMA((2, ranks)),
         ],
-        compiler_params=pltpu.CompilerParams(vmem_limit_bytes=16 * MIB),
+        compiler_params=pltpu.CompilerParams(vmem_limit_bytes=55889100),
         cost_estimate=pl.CostEstimate(
             flops=4 * rows * feats * piece * ranks,
             bytes_accessed=4 * feats * piece * ranks,
             transcendentals=0,
         ),
         name="project",
-    )(rank, gain, x, weight)
+    )(gain, x, weight)
     return outs[:ranks], outs[ranks]
 
 
-def resident_kernel(ranks, rank_ref, len_ref, q_ref, sq_ref, k_hbm, v_hbm, *rest):
+def resident_kernel(ranks, valid_ref, q_ref, sq_ref, k_hbm, v_hbm, *rest):
     outs = rest[:ranks]
     k_buf, v_buf, o_all, s_all, sems = rest[ranks:]
     residents, positions, width = k_buf.shape
@@ -122,18 +126,23 @@
         copies.append(
             (
                 pltpu.make_async_copy(k_hbm.at[r], k_buf.at[r], sems.at[0, r]),
-                pltpu.make_async_copy(v_hbm.at[r], v_buf.at[r], sems.at[1, r]),
+                pltpu.make_async_copy(
+                    v_hbm.at[r, :, : width // 2], v_buf.at[r, :, : width // 2], sems.at[1, r]
+                ),
+                pltpu.make_async_copy(
+                    v_hbm.at[r, :, width // 2 :], v_buf.at[r, :, width // 2 :], sems.at[2, r]
+                ),
             )
         )
-    for pair in copies:
-        for copy in pair:
+    for trio in copies:
+        for copy in trio:
             copy.start()
     heads = q_ref.shape[1]
     kv_heads = width // 128
     group = heads // kv_heads
     pair_rows = 2 * group
     heads_mine = heads // ranks
-    rank = rank_ref[0]
+    rank = lax.axis_index("tp")
     top_half = iota((pair_rows, 128), 0) < group
     own_block = iota((heads, width), 0) // group == iota((heads, width), 1) // 128
     scale = F32(1.0) / jnp.sqrt(F32(128.0))
@@ -147,7 +156,7 @@
             k_buf[r], wide, (((1,), (1,)), ((), ())), preferred_element_type=F32
         )
         scores = jnp.transpose(scores)[:heads]
-        valid = rank * positions + iota((heads, positions), 1) < len_ref[0, r]
+        valid = iota((heads, positions), 1) < valid_ref[r]
         scores = jnp.where(valid, scores * scale, ABSENT)
         peak = jnp.max(scores, axis=1, keepdims=True).astype(BF16).astype(F32)
         weights = jnp.where(valid, jnp.exp(scores - peak), 0.0)
@@ -156,8 +165,9 @@
         s_all[r, 1] = column_to_row(high.astype(F32), heads_mine)
         s_all[r, 2] = column_to_row(low.astype(F32), heads_mine)
         weights = weights.astype(BF16)
-        copies[r][1].wait()
         for p in range(kv_heads // 2):
+            if p * 4 % kv_heads == 0:
+                copies[r][1 + p * 4 // kv_heads].wait()
             rows = slice(p * pair_rows, (p + 1) * pair_rows)
             both = jnp.dot(
                 weights[rows], v_buf[r, :, p * 256 : (p + 1) * 256], preferred_element_type=F32
@@ -177,14 +187,14 @@
         outs[j][...] = jnp.concatenate(parts, axis=0).astype(BF16)
 
 
-def attend_resident(rank, lengths, queries, squares, k_cache, v_cache, ranks):
+def attend_resident(valid, queries, squares, k_cache, v_cache, ranks):
     residents, positions, width = k_cache.shape
     heads = queries.shape[1]
     heads_mine = heads // ranks
     rows = -(-(residents * (heads_mine + 3) + 2 * squares.shape[0]) // 16) * 16
     return pl.pallas_call(
         functools.partial(resident_kernel, ranks),
-        in_specs=[SMEM, SMEM, VMEM, VMEM, HBM, HBM],
+        in_specs=[SMEM, VMEM, VMEM, HBM, HBM],
         out_specs=[VMEM] * ranks,
         out_shape=[jax.ShapeDtypeStruct((rows, 128), BF16)] * ranks,
         scratch_shapes=[
@@ -192,16 +202,16 @@
             pltpu.VMEM((residents, positions, width), BF16),
             pltpu.VMEM((residents, heads, 128), F32),
             pltpu.VMEM((residents, 3, ranks, 128), F32),
-            pltpu.SemaphoreType.DMA((2, residents)),
+            pltpu.SemaphoreType.DMA((3, residents)),
         ],
-        compiler_params=pltpu.CompilerParams(vmem_limit_bytes=32 * MIB),
+        compiler_params=pltpu.CompilerParams(vmem_limit_bytes=52 * MIB),
         cost_estimate=pl.CostEstimate(
             flops=4 * residents * heads * positions * 128,
             bytes_accessed=4 * residents * positions * width,
             transcendentals=residents * heads * positions,
         ),
         name="attend_resident",
-    )(rank, lengths, queries, squares, k_cache, v_cache)
+    )(valid, queries, squares, k_cache, v_cache)
 
 
 def expand(own, rows):
@@ -218,8 +228,7 @@
 ):
     pieces, rest = rest[:ranks], rest[ranks:]
     payloads, rest = rest[:ranks], rest[ranks:]
-    asks, rest = rest[: insts - 1], rest[insts - 1 :]
-    out_ref, q_ref, own_ref, line_ref = rest
+    asks, out_ref, q_ref, own_ref, line_ref = rest
     here = here_ref[0]
     requests = dest_ref.shape[0]
     tokens = pieces[0].shape[0]
@@ -239,18 +248,11 @@
         for s in range(insts):
             for c in range(requests):
                 place += jnp.where((dest_ref[c, s] == dest) & (here > s), 1, 0).astype(jnp.int32)
-        shift = lax.rem(here - dest + insts, insts)
-        for j in range(1, insts):
-
-            @pl.when(shift == j)
-            def _():
-                ask = asks[j - 1][place].astype(F32)
-                at = slice(r * heads_mine, (r + 1) * heads_mine)
-                q_ref[at, :] = ask[:heads_mine]
-                own_ref[0, at, :] = expand(ask[heads_mine : heads_mine + kv_mine], heads_mine)
-                own_ref[1, at, :] = expand(
-                    ask[heads_mine + kv_mine : heads_mine + 2 * kv_mine], heads_mine
-                )
+        ask = asks[dest, place].astype(F32)
+        at = slice(r * heads_mine, (r + 1) * heads_mine)
+        q_ref[at, :] = ask[:heads_mine]
+        own_ref[0, at, :] = expand(ask[heads_mine : heads_mine + kv_mine], heads_mine)
+        own_ref[1, at, :] = expand(ask[heads_mine + kv_mine : heads_mine + 2 * kv_mine], heads_mine)
 
     squares = None
     blocks = tokens // 128
@@ -303,11 +305,11 @@
 
 def attend_moved(here, dest, count, k_gain, cos, sin, pieces, payloads, asks, heads_mine, at_sq, features):
     requests = dest.shape[0]
-    insts, ranks = len(asks) + 1, len(pieces)
+    insts, ranks = asks.shape[0], len(pieces)
     rows = requests * heads_mine
     return pl.pallas_call(
         functools.partial(moved_kernel, insts, ranks, features, at_sq),
-        in_specs=[SMEM] * 3 + [VMEM] * (3 + 2 * ranks + insts - 1),
+        in_specs=[SMEM] * 3 + [VMEM] * (4 + 2 * ranks),
         out_specs=VMEM,
         out_shape=jax.ShapeDtypeStruct((requests, heads_mine * 128), BF16),
         scratch_shapes=[
@@ -317,7 +319,7 @@
         ],
         compiler_params=pltpu.CompilerParams(vmem_limit_bytes=16 * MIB),
         name="attend_moved",
-    )(here, dest, count, k_gain, cos, sin, *pieces, *payloads, *asks)
+    )(here, dest, count, k_gain, cos, sin, *pieces, *payloads, asks)
 
 
 def combine_kernel(ranks, residents, ask_ref, *rest):
@@ -436,7 +438,7 @@
     insts = lax.axis_size("inst")
     ranks = lax.axis_size("tp")
     here = lax.axis_index("inst").astype(jnp.int32).reshape(1)
-    rank = lax.axis_index("tp").astype(jnp.int32).reshape(1)
+    rank = lax.axis_index("tp")
     head_size = k_gain.shape[0]
     slots, requests, feats = mig_hidden.shape[1:]
     residents = k_cache.shape[1]
@@ -449,18 +451,20 @@
 
     queries = query[0].reshape(decoded, heads, head_size)
     own = new_kv[0].reshape(decoded, 2, kv_heads, head_size)
-    my_queries = lax.dynamic_slice_in_dim(queries, rank[0] * heads_mine, heads_mine, 1)
-    my_own = lax.dynamic_slice_in_dim(own, rank[0] * heads_mine // group, kv_mine, 2)
+    my_queries = lax.dynamic_slice_in_dim(queries, rank * heads_mine, heads_mine, 1)
+    my_own = lax.dynamic_slice_in_dim(own, rank * heads_mine // group, kv_mine, 2)
     asks = jnp.concatenate(
         [my_queries, my_own.reshape(decoded, 2 * kv_mine, head_size)], axis=1
     )
-    asked = [shifted(asks[residents:], "inst", j, insts) for j in range(1, insts)]
+    asked = jnp.broadcast_to(asks[residents:], (insts,) + asks[residents:].shape)
+    asked = lax.all_to_all(asked, "inst", 0, 0, tiled=True)
 
     pieces, squares = project(
-        rank, mig_hidden[0], attn_gain, kv_weight, ranks, group, kv_mine
+        mig_hidden[0], attn_gain, kv_weight, ranks, group, kv_mine
     )
     pieces = [pieces[0]] + [shifted(pieces[j], "tp", j, ranks) for j in range(1, ranks)]
-    payloads = attend_resident(rank, lengths, queries, squares, k_cache[0], v_cache[0], ranks)
+    valid = lengths[0] - rank * k_cache.shape[2]
+    payloads = attend_resident(valid, queries, squares, k_cache[0], v_cache[0], ranks)
     payloads = [payloads[0]] + [shifted(payloads[j], "tp", j, ranks) for j in range(1, ranks)]
     kept = combine_resident(asks, payloads, residents, heads_mine)
     dest, count = mig_dest.T, mig_count.T

time: 48.2 us -> 41.8 us (0.87)
  the two profiles are of different devices: /device:TPU:1 before, /device:TPU:0 now
where the time goes in v3:
time: 41.8 us; the launch traced here: 41.4 us
  starting transfers between devices  16.5 us (39%)
  Pallas kernels  15.6 us (37%)
  waiting for transfers between devices  6.02 us (14%)
  local copies, waits for them, and re-layouts  2.32 us (6%)
  other arithmetic  0.68 us (2%)
    ppermute x9, starting transfers between devices, shifted(): return lax.ppermute(x, axis, [(i, (i + j) % n) for i in range(n)])  13.2 us
    pallas_call x1, Pallas kernels, attend_resident(): pl.pallas_call(functools.partial(resident_kernel, ranks), in_specs=[SMEM,...  8.72 us
    pallas_call x1, Pallas kernels, project(): pl.pallas_call(functools.partial(project_kernel, ranks, group), in_specs=...  4.24 us
    ppermute x9, waiting for transfers between devices, shifted(): return lax.ppermute(x, axis, [(i, (i + j) % n) for i in range(n)])  3.66 us
    all_to_all x1, starting transfers between devices, per_device(): asked = lax.all_to_all(asked, 'inst', 0, 0, tiled=True)  3.27 us
    all_to_all x1, waiting for transfers between devices, per_device(): asked = lax.all_to_all(asked, 'inst', 0, 0, tiled=True)  2.36 us
    unnamed x16, local copies, waits for them, and re-layouts  1.65 us
    pallas_call x1, Pallas kernels, finish(): pl.pallas_call(functools.partial(finish_kernel, len(moved) + 1), in_specs...  1.34 us
  transfers between devices with their start and end apart: 10, of which 4 were waited for; matrix products, arithmetic and copies ran while one was open for 2% of the time, Pallas kernels for 0%

profile of v3, /device:TPU:0, one launch (start us, length us, event | category | flops | bytes accessed | tf_op | source)
XLA Modules:
  0.0 41.4 jit_solution(427474994633820064)
XLA Ops:
  0.0 0.9 %copy.20 = bf16[1,5,64,128]{3,2,1,0:T(8,128)(2,1)S(1)} copy(bf16[1,5,64,128]{3,1,2,0:T(8,128)(2,1)} %bitcast.31) | data formatting | bytes 163840
  0.9 0.7 %subtract_bitcast_fusion.valid_ref = s32[3]{0:T(128)S(1)} fusion(s32[1,3]{1,0:T(1,128)} %param.23, s32[]{:T(128)S(6)} %mul.8), kind=kLoop, calls=%fused_computation.6 | loop fusion | flops 3 | bytes 28 | tf_op jit(solution)/shard_map/sub | solution.py:466
  1.6 0.0 copy-start.2
  1.6 0.7 %copy-done.2 = bf16[1280]{0:T(1024)(128)(2,1)S(1)} copy-done((bf16[1280]{0:T(1024)(128)(2,1)S(1)}, bf16[1280]{0:T(1024)(128)(2,1)}, u32[]{:S(2)}) %copy-start.2) | copy-done | bytes 2584
  2.3 4.2 %project.1 = (bf16[128,512]{1,0:T(8,128)(2,1)S(1)}, bf16[128,512]{1,0:T(8,128)(2,1)S(1)}, bf16[128,512]{1,0:T(8,128)(2,1)S(1)}, bf16[128,512]{1,0:T(8,128)(2,1)S(1)}, f32[1,128]{1,0:T(1,128)S(1)}) custom-call(bf16[1280]{0:T(1024)(128)(2,1)S(1)} %copy-done.2, bf16[64,2,1280]{2,1,0:T(2,128)(2,1)} %bitcast.30, bf16[1280,2048]{1,0:T(8,128)(2,1)} %w_hbm.1), custom_call_target="tpu_custom_call" | custom-call | flops 671088640 | bytes 5242880 | tf_op jit(solution)/shard_map/project/pallas_call | solution.py:95
  6.5 0.0 copy-start.6
  6.5 0.0 copy-start
  6.5 0.0 copy-start.1
  6.6 0.0 copy-start.3
  6.6 0.0 copy-start.4
  6.6 0.0 copy-start.5
  6.6 8.7 %attend_resident.1 = (bf16[64,128]{1,0:T(8,128)(2,1)S(1)}, bf16[64,128]{1,0:T(8,128)(2,1)S(1)}, bf16[64,128]{1,0:T(8,128)(2,1)S(1)}, bf16[64,128]{1,0:T(8,128)(2,1)S(1)}) custom-call(s32[3]{0:T(128)S(1)} %subtract_bitcast_fusion.valid_ref, bf16[5,64,128]{2,1,0:T(8,128)(2,1)S(1)} %bitcast.22, f32[1,128]{1,0:T(1,128)S(1)} %get-tuple-element.14.sq_ref, ...), custom_call_target="tpu_custom_call" | custom-call | flops 100663296 | bytes 12582912 | tf_op jit(solution)/shard_map/attend_resident/pallas_call | solution.py:195
  15.3 3.1 %collective-permute-start = (bf16[64,128]{1,0:T(8,128)(2,1)S(1)}, bf16[64,128]{1,0:T(8,128)(2,1)S(1)}, u32[]{:S(2)}, u32[]{:S(2)}) collective-permute-start(bf16[64,128]{1,0:T(8,128)(2,1)S(1)} %get-tuple-element.16), channel_id=1, source_target_pairs={{0,1},{1,2},{2,3},{3,0},{4,5},{5,6},{6,7},{7,4},{8,9},{9,10},{10,1... | collective-permute-start | bytes 49160 | tf_op jit(solution)/shard_map/ppermute | solution.py:411
  18.4 1.6 %collective-permute-start.3 = (bf16[128,512]{1,0:T(8,128)(2,1)S(1)}, bf16[128,512]{1,0:T(8,128)(2,1)S(1)}, u32[]{:S(2)}, u32[]{:S(2)}) collective-permute-start(bf16[128,512]{1,0:T(8,128)(2,1)S(1)} %get-tuple-element.20), channel_id=1, source_target_pairs={{0,1},{1,2},{2,3},{3,0},{4,5},{5,6},{6,7},{7,4},{8,9},{9,10},{10,1... | collective-permute-start | bytes 393224 | tf_op jit(solution)/shard_map/ppermute | solution.py:411
  20.0 1.1 %collective-permute-start.4 = (bf16[128,512]{1,0:T(8,128)(2,1)S(1)}, bf16[128,512]{1,0:T(8,128)(2,1)S(1)}, u32[]{:S(2)}, u32[]{:S(2)}) collective-permute-start(bf16[128,512]{1,0:T(8,128)(2,1)S(1)} %get-tuple-element.21), channel_id=1, source_target_pairs={{0,2},{1,3},{2,0},{3,1},{4,6},{5,7},{6,4},{7,5},{8,10},{9,11},{10,... | collective-permute-start | bytes 393224 | tf_op jit(solution)/shard_map/ppermute | solution.py:411
  21.1 2.9 %collective-permute-start.5 = (bf16[128,512]{1,0:T(8,128)(2,1)S(1)}, bf16[128,512]{1,0:T(8,128)(2,1)S(1)}, u32[]{:S(2)}, u32[]{:S(2)}) collective-permute-start(bf16[128,512]{1,0:T(8,128)(2,1)S(1)} %get-tuple-element.22), channel_id=1, source_target_pairs={{0,3},{1,0},{2,1},{3,2},{4,7},{5,4},{6,5},{7,6},{8,11},{9,8},{10,9... | collective-permute-start | bytes 393224 | tf_op jit(solution)/shard_map/ppermute | solution.py:411
  23.9 0.0 copy-done.6
  24.0 0.6 %broadcast_in_dim.6 = bf16[4,2,20,128]{3,1,2,0:T(2,128)(2,1)} broadcast(bf16[2,20,128]{2,0,1:T(2,128)(2,1)S(1)} %copy.14), dimensions={1,2,3} | broadcast | bytes 51200 | tf_op jit(solution)/shard_map/broadcast_in_dim | solution.py:459
  24.7 3.3 %all-to-all-start = ((bf16[4,2,20,128]{3,1,2,0:T(2,128)(2,1)}), bf16[4,2,20,128]{3,1,2,0:T(2,128)(2,1)S(1)}, u32[]{:S(2)}, u32[]{:S(2)}) async-start(bf16[4,2,20,128]{3,1,2,0:T(2,128)(2,1)} %broadcast_in_dim.6), calls=%async_computation | async-start | bytes 81920 | tf_op jit(solution)/shard_map/all_to_all | solution.py:460
  27.9 0.4 collective-permute-start.1
  28.3 0.0 collective-permute-done.rest_1_.rest_5_
  28.3 1.2 %collective-permute-start.2 = (bf16[64,128]{1,0:T(8,128)(2,1)S(1)}, bf16[64,128]{1,0:T(8,128)(2,1)S(1)}, u32[]{:S(2)}, u32[]{:S(2)}) collective-permute-start(bf16[64,128]{1,0:T(8,128)(2,1)S(1)} %get-tuple-element.18), channel_id=1, source_target_pairs={{0,3},{1,0},{2,1},{3,2},{4,7},{5,4},{6,5},{7,6},{8,11},{9,8},{10,9... | collective-permute-start | bytes 49160 | tf_op jit(solution)/shard_map/ppermute | solution.py:411
  29.5 2.4 %all-to-all-done = bf16[4,2,20,128]{3,1,2,0:T(2,128)(2,1)S(1)} async-done(((bf16[4,2,20,128]{3,1,2,0:T(2,128)(2,1)}), bf16[4,2,20,128]{3,1,2,0:T(2,128)(2,1)S(1)}, u32[]{:S(2)}, u32[]{:S(2)}) %all-to-all-start) | async-done | bytes 40992 | tf_op jit(solution)/shard_map/all_to_all | solution.py:460
  31.9 2.5 %collective-permute-done.1.rest_2_.rest_6_ = bf16[64,128]{1,0:T(8,128)(2,1)S(1)} collective-permute-done((bf16[64,128]{1,0:T(8,128)(2,1)S(1)}, bf16[64,128]{1,0:T(8,128)(2,1)S(1)}, u32[]{:S(2)}, u32[]{:S(2)}) %collective-permute-start.1) | collective-permute-done | bytes 16416 | tf_op jit(solution)/shard_map/ppermute | solution.py:411
  34.4 0.0 collective-permute-done.2.rest_3_.rest_7_
  34.4 0.0 collective-permute-done.3.rest_1_
  34.4 0.0 collective-permute-done.4.rest_2_
  34.4 0.0 collective-permute-done.5.rest_3_
  34.4 0.0 copy-done
  34.4 0.0 copy-done.1
  34.4 0.0 copy-done.3
  34.4 0.0 copy-done.4
  34.4 0.0 copy-done.5
  34.4 1.2 %attend_moved.1 = bf16[2,2048]{1,0:T(2,128)(2,1)S(1)} custom-call(s32[1]{0:T(128)} %bitcast.here_ref, s32[2,4]{1,0:T(2,128)S(1)} %bitcast.24, s32[2,4]{1,0:T(2,128)S(1)} %bitcast.26, bf16[1,128]{1,0:T(2,128)(2,1)S(1)} %bitcast.27, f32[128,128]{1,0:T(8,128)S(1)} %copy-done, f32[128,128]{1,0:T(8,128)S(1)} %copy-done.1, ...), custom_call_target="tpu_custom_call" | custom-call | tf_op jit(solution)/shard_map/attend_moved/pallas_call | solution.py:310
  35.6 0.1 collective-permute-start.6
  35.7 1.6 %collective-permute-start.7 = (bf16[2,2048]{1,0:T(2,128)(2,1)S(1)}, bf16[2,2048]{1,0:T(2,128)(2,1)S(1)}, u32[]{:S(2)}, u32[]{:S(2)}) collective-permute-start(bf16[2,2048]{1,0:T(2,128)(2,1)S(1)} %attend_moved.1), channel_id=1, source_target_pairs={{0,8},{4,12},{8,0},{12,4},{1,9},{5,13},{9,1},{13,5},{2,10},{6,14},... | collective-permute-start | bytes 24584 | tf_op jit(solution)/shard_map/ppermute | solution.py:411
  37.3 1.4 %collective-permute-start.8 = (bf16[2,2048]{1,0:T(2,128)(2,1)S(1)}, bf16[2,2048]{1,0:T(2,128)(2,1)S(1)}, u32[]{:S(2)}, u32[]{:S(2)}) collective-permute-start(bf16[2,2048]{1,0:T(2,128)(2,1)S(1)} %attend_moved.1), channel_id=1, source_target_pairs={{0,12},{4,0},{8,4},{12,8},{1,13},{5,1},{9,5},{13,9},{2,14},{6,2},{... | collective-permute-start | bytes 24584 | tf_op jit(solution)/shard_map/ppermute | solution.py:411
  38.7 0.2 combine_resident.1.kept_ref
  38.8 0.0 collective-permute-done.6.rest_0_
  38.9 0.6 %collective-permute-done.7.rest_1_ = bf16[2,2048]{1,0:T(2,128)(2,1)S(1)} collective-permute-done((bf16[2,2048]{1,0:T(2,128)(2,1)S(1)}, bf16[2,2048]{1,0:T(2,128)(2,1)S(1)}, u32[]{:S(2)}, u32[]{:S(2)}) %collective-permute-start.7) | collective-permute-done | bytes 8224 | tf_op jit(solution)/shard_map/ppermute | solution.py:411
  39.4 0.6 %collective-permute-done.8.rest_2_ = bf16[2,2048]{1,0:T(2,128)(2,1)S(1)} collective-permute-done((bf16[2,2048]{1,0:T(2,128)(2,1)S(1)}, bf16[2,2048]{1,0:T(2,128)(2,1)S(1)}, u32[]{:S(2)}, u32[]{:S(2)}) %collective-permute-start.8) | collective-permute-done | bytes 8224 | tf_op jit(solution)/shard_map/ppermute | solution.py:411
  40.0 1.3 %finish.1 = bf16[5,2048]{1,0:T(8,128)(2,1)} custom-call(s32[1]{0:T(128)} %bitcast.here_ref, s32[2,4]{1,0:T(2,128)S(1)} %bitcast.25, bf16[3,2048]{1,0:T(4,128)(2,1)S(1)} %combine_resident.1.kept_ref, bf16[2,2048]{1,0:T(2,128)(2,1)S(1)} %collective-permute-done.6.rest_0_, bf16[2,2048]{1,0:T(2,128)(2,1)S(1)} %collective-permute-done.7.rest_1_, ...), custom_call_target="tpu_custom_call" | custom-call | tf_op jit(solution)/shard_map/finish/pallas_call | solution.py:399
  (7 shorter events, 0.1 us)
Async XLA Ops:
  1.6 0.7 %copy-start.2 = (bf16[1280]{0:T(1024)(128)(2,1)S(1)}, bf16[1280]{0:T(1024)(128)(2,1)}, u32[]{:S(2)}) copy-start(bf16[1280]{0:T(1024)(128)(2,1)} %gain_hbm.1) | copy-start | bytes 7684
  6.5 17.4 %copy-start.6 = (bf16[1,5,2048]{2,1,0:T(8,128)(2,1)S(1)}, bf16[1,5,2048]{2,1,0:T(8,128)(2,1)}, u32[]{:S(2)}) copy-start(bf16[1,5,2048]{2,1,0:T(8,128)(2,1)} %param.20) | copy-start | bytes 61444
  6.5 27.9 %copy-start = (f32[128,128]{1,0:T(8,128)S(1)}, f32[128,128]{1,0:T(8,128)}, u32[]{:S(2)}) copy-start(f32[128,128]{1,0:T(8,128)} %constant.35.clone.cos_ref) | copy-start | bytes 196612
  6.5 27.9 %copy-start.1 = (f32[128,128]{1,0:T(8,128)S(1)}, f32[128,128]{1,0:T(8,128)}, u32[]{:S(2)}) copy-start(f32[128,128]{1,0:T(8,128)} %constant.36.clone.sin_ref) | copy-start | bytes 196612
  6.6 27.9 %copy-start.3 = (s32[4,2]{0,1:T(2,128)S(1)}, s32[4,2]{0,1:T(2,128)}, u32[]{:S(2)}) copy-start(s32[4,2]{0,1:T(2,128)} %param.14) | copy-start | bytes 100
  6.6 27.9 %copy-start.4 = (s32[4,2]{0,1:T(2,128)S(1)}, s32[4,2]{0,1:T(2,128)}, u32[]{:S(2)}) copy-start(s32[4,2]{0,1:T(2,128)} %param.15) | copy-start | bytes 100
  6.6 27.9 %copy-start.5 = (bf16[128]{0:T(256)(128)(2,1)S(1)}, bf16[128]{0:T(256)(128)(2,1)}, u32[]{:S(2)}) copy-start(bf16[128]{0:T(256)(128)(2,1)} %param.18) | copy-start | bytes 772
  15.3 13.0 %collective-permute-start = (bf16[64,128]{1,0:T(8,128)(2,1)S(1)}, bf16[64,128]{1,0:T(8,128)(2,1)S(1)}, u32[]{:S(2)}, u32[]{:S(2)}) collective-permute-start(bf16[64,128]{1,0:T(8,128)(2,1)S(1)} %get-tuple-element.16), channel_id=1, source_target_pairs={{0,1},{1,2},{2,3},{3,0},{4,5},{5,6},{6,7},{7,4},{8,9},{9,10},{10,1... | collective-permute-start | bytes 49160 | tf_op jit(solution)/shard_map/ppermute | solution.py:411
  18.4 16.0 %collective-permute-start.3 = (bf16[128,512]{1,0:T(8,128)(2,1)S(1)}, bf16[128,512]{1,0:T(8,128)(2,1)S(1)}, u32[]{:S(2)}, u32[]{:S(2)}) collective-permute-start(bf16[128,512]{1,0:T(8,128)(2,1)S(1)} %get-tuple-element.20), channel_id=1, source_target_pairs={{0,1},{1,2},{2,3},{3,0},{4,5},{5,6},{6,7},{7,4},{8,9},{9,10},{10,1... | collective-permute-start | bytes 393224 | tf_op jit(solution)/shard_map/ppermute | solution.py:411
  20.0 14.4 %collective-permute-start.4 = (bf16[128,512]{1,0:T(8,128)(2,1)S(1)}, bf16[128,512]{1,0:T(8,128)(2,1)S(1)}, u32[]{:S(2)}, u32[]{:S(2)}) collective-permute-start(bf16[128,512]{1,0:T(8,128)(2,1)S(1)} %get-tuple-element.21), channel_id=1, source_target_pairs={{0,2},{1,3},{2,0},{3,1},{4,6},{5,7},{6,4},{7,5},{8,10},{9,11},{10,... | collective-permute-start | bytes 393224 | tf_op jit(solution)/shard_map/ppermute | solution.py:411
  21.1 13.3 %collective-permute-start.5 = (bf16[128,512]{1,0:T(8,128)(2,1)S(1)}, bf16[128,512]{1,0:T(8,128)(2,1)S(1)}, u32[]{:S(2)}, u32[]{:S(2)}) collective-permute-start(bf16[128,512]{1,0:T(8,128)(2,1)S(1)} %get-tuple-element.22), channel_id=1, source_target_pairs={{0,3},{1,0},{2,1},{3,2},{4,7},{5,4},{6,5},{7,6},{8,11},{9,8},{10,9... | collective-permute-start | bytes 393224 | tf_op jit(solution)/shard_map/ppermute | solution.py:411
  24.7 7.2 %all-to-all-start = ((bf16[4,2,20,128]{3,1,2,0:T(2,128)(2,1)}), bf16[4,2,20,128]{3,1,2,0:T(2,128)(2,1)S(1)}, u32[]{:S(2)}, u32[]{:S(2)}) async-start(bf16[4,2,20,128]{3,1,2,0:T(2,128)(2,1)} %broadcast_in_dim.6), calls=%async_computation | async-start | bytes 81920 | tf_op jit(solution)/shard_map/all_to_all | solution.py:460
  27.9 6.4 %collective-permute-start.1 = (bf16[64,128]{1,0:T(8,128)(2,1)S(1)}, bf16[64,128]{1,0:T(8,128)(2,1)S(1)}, u32[]{:S(2)}, u32[]{:S(2)}) collective-permute-start(bf16[64,128]{1,0:T(8,128)(2,1)S(1)} %get-tuple-element.17), channel_id=1, source_target_pairs={{0,2},{1,3},{2,0},{3,1},{4,6},{5,7},{6,4},{7,5},{8,10},{9,11},{10,... | collective-permute-start | bytes 49160 | tf_op jit(solution)/shard_map/ppermute | solution.py:411
  28.3 6.0 %collective-permute-start.2 = (bf16[64,128]{1,0:T(8,128)(2,1)S(1)}, bf16[64,128]{1,0:T(8,128)(2,1)S(1)}, u32[]{:S(2)}, u32[]{:S(2)}) collective-permute-start(bf16[64,128]{1,0:T(8,128)(2,1)S(1)} %get-tuple-element.18), channel_id=1, source_target_pairs={{0,3},{1,0},{2,1},{3,2},{4,7},{5,4},{6,5},{7,6},{8,11},{9,8},{10,9... | collective-permute-start | bytes 49160 | tf_op jit(solution)/shard_map/ppermute | solution.py:411
  35.6 3.2 %collective-permute-start.6 = (bf16[2,2048]{1,0:T(2,128)(2,1)S(1)}, bf16[2,2048]{1,0:T(2,128)(2,1)S(1)}, u32[]{:S(2)}, u32[]{:S(2)}) collective-permute-start(bf16[2,2048]{1,0:T(2,128)(2,1)S(1)} %attend_moved.1), channel_id=1, source_target_pairs={{0,4},{4,8},{8,12},{12,0},{1,5},{5,9},{9,13},{13,1},{2,6},{6,10},{... | collective-permute-start | bytes 24584 | tf_op jit(solution)/shard_map/ppermute | solution.py:411
  35.7 3.7 %collective-permute-start.7 = (bf16[2,2048]{1,0:T(2,128)(2,1)S(1)}, bf16[2,2048]{1,0:T(2,128)(2,1)S(1)}, u32[]{:S(2)}, u32[]{:S(2)}) collective-permute-start(bf16[2,2048]{1,0:T(2,128)(2,1)S(1)} %attend_moved.1), channel_id=1, source_target_pairs={{0,8},{4,12},{8,0},{12,4},{1,9},{5,13},{9,1},{13,5},{2,10},{6,14},... | collective-permute-start | bytes 24584 | tf_op jit(solution)/shard_map/ppermute | solution.py:411
  37.3 2.8 %collective-permute-start.8 = (bf16[2,2048]{1,0:T(2,128)(2,1)S(1)}, bf16[2,2048]{1,0:T(2,128)(2,1)S(1)}, u32[]{:S(2)}, u32[]{:S(2)}) collective-permute-start(bf16[2,2048]{1,0:T(2,128)(2,1)S(1)} %attend_moved.1), channel_id=1, source_target_pairs={{0,12},{4,0},{8,4},{12,8},{1,13},{5,1},{9,5},{13,9},{2,14},{6,2},{... | collective-permute-start | bytes 24584 | tf_op jit(solution)/shard_map/ppermute | solution.py:411

commit v4 on v3

v4 whole, which is shorter than its diff:
```python
import functools

import jax
import jax.numpy as jnp
import numpy as np
from jax import lax
from jax.experimental import pallas as pl
from jax.experimental.pallas import tpu as pltpu
from jax.sharding import PartitionSpec as P

EPS = 1e-06
THETA = 1000000.0
ABSENT = -1e30
F32 = jnp.float32
BF16 = jnp.bfloat16
MIB = 1024 * 1024
CHUNK = 256

VMEM = pl.BlockSpec(memory_space=pltpu.VMEM)
SMEM = pl.BlockSpec(memory_space=pltpu.SMEM)
HBM = pl.BlockSpec(memory_space=pltpu.HBM)


def iota(shape, dim):
    return lax.broadcasted_iota(jnp.int32, shape, dim)


def column_to_row(column, period):
    n = column.shape[0]
    spread = jnp.where(iota((n, 128), 0) % period == iota((n, 128), 1), column, 0.0)
    return jnp.sum(spread.reshape(n // period, period, 128), axis=1)


def row_to_column(row, n):
    return jnp.sum(
        jnp.where(iota((n, 128), 0) == iota((n, 128), 1), row, 0.0), axis=1, keepdims=True
    )


def split_bf16(x):
    high = x.astype(BF16)
    return high, (x - high.astype(F32)).astype(BF16)


def project_kernel(ranks, group, gain_hbm, x_hbm, w_hbm, q_hbm, own_hbm, *rest):
    outs, ask_ref = rest[:ranks], rest[ranks]
    gain_ref, x_ref, w_ref, acc_ref, in_sems, w_sems = rest[ranks + 1 :]
    slots, requests, feats = x_ref.shape
    rows = slots * requests
    piece = outs[0].shape[1] // 2
    kv_width = w_hbm.shape[1] // 2
    heads_mine = kv_width // 128 * group // ranks
    rank = lax.axis_index("tp")

    def first_column(target):
        return pl.multiple_of(target * heads_mine // group * 128, 128)

    gain_copy = pltpu.make_async_copy(gain_hbm, gain_ref, in_sems.at[0])
    gain_copy.start()
    x_copy = pltpu.make_async_copy(x_hbm, x_ref, in_sems.at[1])
    x_copy.start()
    cuts = list(range(0, feats, CHUNK)) + [feats]
    chunks = list(zip(cuts[:-1], cuts[1:]))
    copies = []
    for i, (low, high) in enumerate(chunks):
        copies.append(
            pltpu.make_async_copy(
                w_hbm.at[low:high, :], w_ref.at[low:high, :], w_sems.at[i]
            )
        )
        copies[-1].start()
    mine = heads_mine * 128
    q_first = pl.multiple_of(rank * mine, 128)
    asking = [
        pltpu.make_async_copy(
            q_hbm.at[:, pl.ds(q_first, mine)], ask_ref.at[:, :mine], in_sems.at[2]
        )
    ]
    for i in range(2):
        asking.append(
            pltpu.make_async_copy(
                own_hbm.at[:, pl.ds(i * kv_width + first_column(rank), piece)],
                ask_ref.at[:, mine + i * piece : mine + (i + 1) * piece],
                in_sems.at[3 + i],
            )
        )
    for copy in asking:
        copy.start()
    gain_copy.wait()
    x_copy.wait()
    squares = jnp.zeros((rows, 128), F32)
    for i, (low, high) in enumerate(chunks):
        parts = []
        for c in range(low, high, 128):
            width = min(128, high - c)
            x = x_ref[:, :, c : c + width].astype(F32).reshape(rows, width)
            gain = gain_ref[c : c + width].astype(F32).reshape(1, width)
            parts.append((x * gain).astype(BF16))
            x = x * x
            if width < 128:
                x = jnp.concatenate([x, jnp.zeros((rows, 128 - width), F32)], axis=1)
            squares = squares + x
        xg = parts[0] if len(parts) == 1 else jnp.concatenate(parts, axis=1)
        copies[i].wait()
        for n in range(0, 2 * kv_width, 512):
            part = jnp.dot(xg, w_ref[low:high, n : n + 512], preferred_element_type=F32)
            if i == 0:
                acc_ref[:, n : n + 512] = part
            else:
                acc_ref[:, n : n + 512] += part
    sq = column_to_row(jnp.sum(squares, axis=1, keepdims=True), 128)
    high, low = split_bf16(sq)
    tail = jnp.concatenate([high.astype(F32), low.astype(F32)], axis=0)
    if outs[0].shape[0] - rows > tail.shape[0]:
        fill = outs[0].shape[0] - rows - tail.shape[0]
        tail = jnp.concatenate([tail, jnp.zeros((fill, 128), F32)], axis=0)
    extra = jnp.concatenate([tail.astype(BF16)] * (2 * piece // 128), axis=1)
    for j in range(ranks):
        first = first_column(rank ^ j)
        outs[j][:rows, :piece] = acc_ref[:, pl.ds(first, piece)].astype(BF16)
        outs[j][:rows, piece:] = acc_ref[:, pl.ds(kv_width + first, piece)].astype(BF16)
        outs[j][rows:, :] = extra
    for copy in asking:
        copy.wait()


def project(x, gain, weight, query, own, ranks, group, kv_mine):
    slots, requests, feats = x.shape
    rows = slots * requests
    piece = kv_mine * 128
    extra = -(-2 * (rows // 128) // 8) * 8
    decoded, q_width = query.shape
    outs = pl.pallas_call(
        functools.partial(project_kernel, ranks, group),
        in_specs=[HBM] * 5,
        out_specs=[VMEM] * (ranks + 1),
        out_shape=[jax.ShapeDtypeStruct((rows + extra, 2 * piece), BF16)] * ranks
        + [jax.ShapeDtypeStruct((decoded, q_width // ranks + 2 * piece), BF16)],
        scratch_shapes=[
            pltpu.VMEM((feats,), BF16),
            pltpu.VMEM((slots, requests, feats), BF16),
            pltpu.VMEM(weight.shape, BF16),
            pltpu.VMEM((rows, weight.shape[1]), F32),
            pltpu.SemaphoreType.DMA((5,)),
            pltpu.SemaphoreType.DMA((-(-feats // CHUNK),)),
        ],
        compiler_params=pltpu.CompilerParams(vmem_limit_bytes=60 * MIB),
        cost_estimate=pl.CostEstimate(
            flops=2 * rows * feats * weight.shape[1],
            bytes_accessed=2 * feats * weight.shape[1],
            transcendentals=0,
        ),
        name="project",
    )(gain, x, weight, query, own)
    return outs[:ranks], outs[ranks]


def resident_kernel(ranks, heads, len_hbm, q_hbm, k_hbm, v_hbm, *rest):
    outs = rest[:ranks]
    len_ref, q_ref, q_all, k_buf, v_buf, o_all, s_all, in_sems, sems = rest[ranks:]
    len_copy = pltpu.make_async_copy(len_hbm, len_ref, in_sems.at[0])
    len_copy.start()
    q_copy = pltpu.make_async_copy(q_hbm, q_ref, in_sems.at[1])
    q_copy.start()
    residents, positions, width = k_buf.shape
    half = width // 2
    copies = []
    for r in range(residents):
        trio = [pltpu.make_async_copy(k_hbm.at[r], k_buf.at[r], sems.at[0, r])]
        for i in range(2):
            at = slice(i * half, (i + 1) * half)
            trio.append(
                pltpu.make_async_copy(v_hbm.at[r, :, at], v_buf.at[r, :, at], sems.at[1 + i, r])
            )
        copies.append(trio)
    for trio in copies:
        for copy in trio:
            copy.start()
    kv_heads = width // 128
    group = heads // kv_heads
    pair_rows = 2 * group
    heads_mine = heads // ranks
    rank = lax.axis_index("tp")
    top_half = iota((pair_rows, 128), 0) < group
    scale = F32(1.0) / jnp.sqrt(F32(128.0))
    q_copy.wait()
    q_lines = q_ref[...].astype(F32)
    for r in range(residents):
        for h in range(heads):
            q_all[r, h : h + 1, :] = q_lines[r : r + 1, h * 128 : (h + 1) * 128]
    len_copy.wait()
    for r in range(residents):
        valid = rank * positions + iota((pair_rows, positions), 1) < len_ref[0, r]
        copies[r][0].wait()
        weights, peaks, totals = [], [], []
        for p in range(kv_heads // 2):
            q = q_all[r, p * pair_rows : (p + 1) * pair_rows, :]
            zero = jnp.zeros_like(q)
            lhs = jnp.concatenate(
                [jnp.where(top_half, q, zero), jnp.where(top_half, zero, q)], axis=1
            ).astype(BF16)
            scores = lax.dot_general(
                lhs,
                k_buf[r, :, p * 256 : (p + 1) * 256],
                (((1,), (1,)), ((), ())),
                preferred_element_type=F32,
            )
            scores = jnp.where(valid, scores * scale, ABSENT)
            peak = jnp.max(scores, axis=1, keepdims=True).astype(BF16).astype(F32)
            weight = jnp.where(valid, jnp.exp(scores - peak), 0.0)
            peaks.append(peak)
            totals.append(jnp.sum(weight, axis=1, keepdims=True))
            weights.append(weight.astype(BF16))
        high, low = split_bf16(jnp.concatenate(totals, axis=0))
        s_all[r, 0] = column_to_row(jnp.concatenate(peaks, axis=0), heads_mine)
        s_all[r, 1] = column_to_row(high.astype(F32), heads_mine)
        s_all[r, 2] = column_to_row(low.astype(F32), heads_mine)
        for p in range(kv_heads // 2):
            if p * 4 % kv_heads == 0:
                copies[r][1 + p * 4 // kv_heads].wait()
            both = jnp.dot(
                weights[p], v_buf[r, :, p * 256 : (p + 1) * 256], preferred_element_type=F32
            )
            o_all[r, p * pair_rows : (p + 1) * pair_rows, :] = jnp.where(
                top_half, both[:, :128], both[:, 128:]
            )
    filled = residents * (heads_mine + 3)
    for j in range(ranks):
        target = rank ^ j
        first = pl.multiple_of(target * heads_mine, heads_mine)
        parts = [o_all[r, pl.ds(first, heads_mine), :] for r in range(residents)]
        parts += [s_all[r, i, pl.ds(target, 1), :] for i in range(3) for r in range(residents)]
        if outs[j].shape[0] > filled:
            parts.append(jnp.zeros((outs[j].shape[0] - filled, 128), F32))
        outs[j][...] = jnp.concatenate(parts, axis=0).astype(BF16)


def attend_resident(lengths, query, k_cache, v_cache, ranks):
    residents, positions, width = k_cache.shape
    heads = query.shape[1] // 128
    heads_mine = heads // ranks
    rows = -(-(residents * (heads_mine + 3)) // 16) * 16
    return pl.pallas_call(
        functools.partial(resident_kernel, ranks, heads),
        in_specs=[HBM] * 4,
        out_specs=[VMEM] * ranks,
        out_shape=[jax.ShapeDtypeStruct((rows, 128), BF16)] * ranks,
        scratch_shapes=[
            pltpu.SMEM(lengths.shape, jnp.int32),
            pltpu.VMEM(query.shape, BF16),
            pltpu.VMEM((residents, heads, 128), F32),
            pltpu.VMEM((residents, positions, width), BF16),
            pltpu.VMEM((residents, positions, width), BF16),
            pltpu.VMEM((residents, heads, 128), F32),
            pltpu.VMEM((residents, 3, ranks, 128), F32),
            pltpu.SemaphoreType.DMA((2,)),
            pltpu.SemaphoreType.DMA((3, residents)),
        ],
        compiler_params=pltpu.CompilerParams(vmem_limit_bytes=60 * MIB),
        cost_estimate=pl.CostEstimate(
            flops=4 * residents * heads * positions * 128,
            bytes_accessed=4 * residents * positions * width,
            transcendentals=residents * heads * positions,
        ),
        name="attend_resident",
    )(lengths, query, k_cache, v_cache)


def block_of(blocks, b):
    step = b.bit_length() - 1
    array = blocks[step]
    return array if step == 0 else array.at[b - (1 << step)]


def prepare_kernel(insts, steps, residents, kv_mine, dest_ref, count_ref, gain_ref, cos_ref, sin_ref, *rest):
    asks, rest = rest[:steps], rest[steps:]
    q_out, own_out, limit_out, cos_out, sin_out, place_out, line_ref, q_ref, k_ref = rest
    requests = dest_ref.shape[0]
    rows = q_out.shape[0]
    heads_mine = rows // requests
    per = heads_mine // kv_mine
    decoded = asks[0].shape[0]
    here = lax.axis_index("inst")
    ask_row = iota((decoded, line_ref.shape[1]), 0)
    limit = jnp.zeros((rows, 128), jnp.int32)
    for r in range(requests):
        dest = dest_ref[r, here]
        limit = jnp.where(iota((rows, 128), 0) // heads_mine == r, count_ref[r, here], limit)
        place = jnp.int32(residents)
        for s in range(insts):
            for c in range(requests):
                place += jnp.where((dest_ref[c, s] == dest) & (here > s), 1, 0).astype(jnp.int32)
        for b in range(1, insts):

            @pl.when(here ^ b == dest)
            def _():
                ask = block_of(asks, b)[...].astype(F32)
                line_ref[r : r + 1, :] = jnp.sum(
                    jnp.where(ask_row == place, ask, 0.0), axis=0, keepdims=True
                )

        line = line_ref[r : r + 1, :]
        for h in range(heads_mine):
            at = r * heads_mine + h
            k_at = (heads_mine + h // per) * 128
            v_at = k_at + kv_mine * 128
            q_ref[at : at + 1, :] = line[:, h * 128 : (h + 1) * 128]
            k_ref[at : at + 1, :] = line[:, k_at : k_at + 128]
            own_out[0, at : at + 1, :] = line[:, v_at : v_at + 128]
    scale = F32(1.0) / jnp.sqrt(F32(128.0))
    q = q_ref[...]
    q_out[...] = q.astype(BF16)
    own_out[1] = jnp.broadcast_to(
        jnp.sum(q * k_ref[...], axis=1, keepdims=True) * scale, (rows, 128)
    )
    limit_out[...] = limit
    gain = gain_ref[...].astype(F32)
    cos_out[...] = cos_ref[...] * gain
    sin_out[...] = sin_ref[...] * pltpu.roll(jnp.broadcast_to(gain, (8, 128)), 64, 1)[:1]
    places = jnp.full(place_out.shape, -1, jnp.int32)
    row = iota(place_out.shape, 0)
    place = jnp.int32(residents)
    for s in range(insts):
        for c in range(requests):
            mine = dest_ref[c, s] == here
            places = jnp.where((row == (here ^ s) * requests + c) & mine, place, places)
            place += jnp.where(mine, 1, 0).astype(jnp.int32)
    place_out[...] = places


def prepare(dest, count, k_gain, cos, sin, asks, residents, heads_mine, kv_mine):
    requests, insts = dest.shape
    rows = requests * heads_mine
    return pl.pallas_call(
        functools.partial(prepare_kernel, insts, len(asks), residents, kv_mine),
        in_specs=[SMEM] * 2 + [VMEM] * (3 + len(asks)),
        out_specs=[VMEM] * 6,
        out_shape=[
            jax.ShapeDtypeStruct((rows, 128), BF16),
            jax.ShapeDtypeStruct((2, rows, 128), F32),
            jax.ShapeDtypeStruct((rows, 128), jnp.int32),
            jax.ShapeDtypeStruct(cos.shape, F32),
            jax.ShapeDtypeStruct(sin.shape, F32),
            jax.ShapeDtypeStruct((insts * requests, 128), jnp.int32),
        ],
        scratch_shapes=[
            pltpu.VMEM((requests, asks[0].shape[1]), F32),
            pltpu.VMEM((rows, 128), F32),
            pltpu.VMEM((rows, 128), F32),
        ],
        compiler_params=pltpu.CompilerParams(vmem_limit_bytes=16 * MIB),
        name="prepare",
    )(dest, count, k_gain, cos, sin, *asks)


def moved_kernel(ranks, features, q_ref, own_ref, limit_ref, cos_ref, sin_ref, *rest):
    pieces = rest[:ranks]
    _, out_ref, line_ref = rest[ranks:]
    requests = out_ref.shape[0]
    tokens = cos_ref.shape[0]
    piece = pieces[0].shape[1] // 2
    kv_mine = piece // 128
    rows = q_ref.shape[0]
    heads_mine = rows // requests
    scale = F32(1.0) / jnp.sqrt(F32(128.0))

    tail = pieces[0][tokens:, :].astype(F32)
    for t in range(1, ranks):
        tail = tail + pieces[t][tokens:, :].astype(F32)
    blocks = tokens // 128
    squares = tail[:blocks, :128] + tail[blocks : 2 * blocks, :128]
    squares = jnp.concatenate(
        [row_to_column(squares[b : b + 1], 128) for b in range(blocks)], axis=0
    )
    token_scale = lax.rsqrt(squares / features + EPS)

    def column_block(c):
        total = pieces[0][:tokens, c : c + 128].astype(F32)
        for t in range(1, ranks):
            total = total + pieces[t][:tokens, c : c + 128].astype(F32)
        return total * token_scale

    q = q_ref[...]
    which = iota((rows, tokens), 0) % heads_mine // (heads_mine // kv_mine)
    scores = None
    for h in range(kv_mine):
        key = column_block(h * 128)
        key = key * lax.rsqrt(jnp.mean(key * key, axis=1, keepdims=True) + EPS)
        key = key * cos_ref[...] + pltpu.roll(key, 64, 1) * sin_ref[...]
        part = lax.dot_general(
            q, key.astype(BF16), (((1,), (1,)), ((), ())), preferred_element_type=F32
        )
        scores = part if scores is None else jnp.where(which == h, part, scores)
    token = iota((rows, tokens), 1)
    limit = jnp.concatenate([limit_ref[...]] * (tokens // 128), axis=1)
    valid = (token % requests == iota((rows, tokens), 0) // heads_mine) & (
        token // requests < limit
    )
    scores = jnp.where(valid, scores * scale, ABSENT)
    own_score = own_ref[1]
    top = jnp.maximum(jnp.max(scores, axis=1, keepdims=True), own_score)
    weights = jnp.where(
        valid, jnp.exp(scores - jnp.concatenate([top] * (tokens // 128), axis=1)), 0.0
    )
    own_weight = jnp.exp(own_score - top)
    total = jnp.sum(weights, axis=1, keepdims=True) + own_weight
    weights = weights.astype(BF16)
    summed = None
    for h in range(kv_mine):
        value = column_block(piece + h * 128).astype(BF16)
        part = jnp.dot(weights, value, preferred_element_type=F32)
        summed = part if summed is None else jnp.where(which[:, :128] == h, part, summed)
    summed = summed + own_weight.astype(BF16).astype(F32) * own_ref[0]
    result = summed / total
    for r in range(requests):
        for h in range(heads_mine):
            at = r * heads_mine + h
            line_ref[r : r + 1, h * 128 : (h + 1) * 128] = result[at : at + 1, :]
    out_ref[...] = line_ref[...].astype(BF16)


def attend_moved(prepared, pieces, after, requests, features):
    rows = prepared[0].shape[0]
    width = rows // requests * 128
    return pl.pallas_call(
        functools.partial(moved_kernel, len(pieces), features),
        in_specs=[VMEM] * (len(prepared) + len(pieces) + 1),
        out_specs=VMEM,
        out_shape=jax.ShapeDtypeStruct((requests, width), BF16),
        scratch_shapes=[pltpu.VMEM((requests, width), F32)],
        compiler_params=pltpu.CompilerParams(vmem_limit_bytes=16 * MIB),
        name="attend_moved",
    )(*prepared, *pieces, after)


def combine_kernel(ranks, residents, kv_mine, ask_ref, *rest):
    payloads = rest[:ranks]
    out_ref, q_ref, own_ref = rest[ranks:]
    heads_mine = q_ref.shape[0]
    per = heads_mine // kv_mine
    scale = F32(1.0) / jnp.sqrt(F32(128.0))
    at = residents * heads_mine
    ask = ask_ref[...].astype(F32)
    for r in range(residents):
        for h in range(heads_mine):
            k_at = (heads_mine + h // per) * 128
            v_at = k_at + kv_mine * 128
            q_ref[h : h + 1, :] = ask[r : r + 1, h * 128 : (h + 1) * 128]
            own_ref[0, h : h + 1, :] = ask[r : r + 1, k_at : k_at + 128]
            own_ref[1, h : h + 1, :] = ask[r : r + 1, v_at : v_at + 128]
        own_score = jnp.sum(q_ref[...] * own_ref[0], axis=1, keepdims=True) * scale
        peaks, totals = [], []
        for t in range(ranks):
            stat = payloads[t][at : at + 3 * residents, :].astype(F32)
            peaks.append(row_to_column(stat[r : r + 1], heads_mine))
            total = stat[residents + r : residents + r + 1]
            total = total + stat[2 * residents + r : 2 * residents + r + 1]
            totals.append(row_to_column(total, heads_mine))
        top = own_score
        for t in range(ranks):
            top = jnp.maximum(top, peaks[t])
        own_weight = jnp.exp(own_score - top)
        denom = own_weight
        numer = own_weight.astype(BF16).astype(F32) * own_ref[1]
        for t in range(ranks):
            keep = jnp.exp(peaks[t] - top)
            denom = denom + keep * totals[t]
            numer = numer + keep * payloads[t][r * heads_mine : (r + 1) * heads_mine, :].astype(F32)
        result = numer / denom
        for h in range(heads_mine):
            out_ref[r : r + 1, h * 128 : (h + 1) * 128] = result[h : h + 1, :]


def combine_resident(asks, payloads, residents, heads_mine, kv_mine):
    return pl.pallas_call(
        functools.partial(combine_kernel, len(payloads), residents, kv_mine),
        in_specs=[VMEM] * (1 + len(payloads)),
        out_specs=VMEM,
        out_shape=jax.ShapeDtypeStruct((residents, heads_mine * 128), F32),
        scratch_shapes=[
            pltpu.VMEM((heads_mine, 128), F32),
            pltpu.VMEM((2, heads_mine, 128), F32),
        ],
        compiler_params=pltpu.CompilerParams(vmem_limit_bytes=8 * MIB),
        name="combine_resident",
    )(asks, *payloads)


def finish_kernel(insts, steps, kept_ref, place_ref, *rest):
    moved = rest[:steps]
    out_ref = rest[steps]
    residents = kept_ref.shape[0]
    decoded, width = out_ref.shape
    requests = decoded - residents
    row = iota((decoded, 128), 0)
    arrived = [block_of(moved, b)[...].astype(F32) for b in range(1, insts)]
    for c in range(0, width, 128):
        kept = kept_ref[:, c : c + 128]
        line = jnp.concatenate([kept, jnp.zeros((requests, 128), F32)], axis=0)
        for b in range(1, insts):
            for i in range(requests):
                at = b * requests + i
                line = jnp.where(
                    place_ref[at : at + 1, :] == row, arrived[b - 1][i : i + 1, c : c + 128], line
                )
        out_ref[:, c : c + 128] = line.astype(BF16)


def finish(kept, places, moved, insts, requests):
    residents, width = kept.shape
    return pl.pallas_call(
        functools.partial(finish_kernel, insts, len(moved)),
        in_specs=[VMEM] * (2 + len(moved)),
        out_specs=VMEM,
        out_shape=jax.ShapeDtypeStruct((residents + requests, width), BF16),
        compiler_params=pltpu.CompilerParams(vmem_limit_bytes=8 * MIB),
        name="finish",
    )(kept, places, *moved)


def swapped(x, axis, j, n):
    return lax.ppermute(x, axis, [(i, i ^ j) for i in range(n)])


def gather(x, axis, n):
    held, blocks = x, []
    for step in range(n.bit_length() - 1):
        blocks.append(swapped(held, axis, 1 << step, n))
        if 2 << step < n:
            one = blocks[-1]
            held = jnp.stack([held, one]) if step == 0 else jnp.concatenate([held, one])
    return blocks


def rotation(slots, requests, head_size):
    half = head_size // 2
    freq = THETA ** (-np.arange(half) * 2.0 / head_size)
    angle = np.repeat(np.arange(slots), requests)[:, None] * freq[None, :]
    cos, sin = np.cos(angle), np.sin(angle)
    return (
        np.concatenate([cos, cos], axis=1).astype(np.float32),
        np.concatenate([-sin, sin], axis=1).astype(np.float32),
    )


def per_device(
    mig_hidden,
    mig_dest,
    mig_count,
    attn_gain,
    kv_weight,
    k_gain,
    query,
    new_kv,
    k_cache,
    v_cache,
    lengths,
):
    insts = lax.axis_size("inst")
    ranks = lax.axis_size("tp")
    head_size = k_gain.shape[0]
    slots, requests, feats = mig_hidden.shape[1:]
    residents = k_cache.shape[1]
    heads = query.shape[2] // head_size
    kv_heads = kv_weight.shape[1] // 2 // head_size
    heads_mine = heads // ranks
    group = heads // kv_heads
    kv_mine = max(1, heads_mine // group)

    pieces, ask = project(
        mig_hidden[0], attn_gain, kv_weight, query[0], new_kv[0], ranks, group, kv_mine
    )
    pieces = [pieces[0]] + [swapped(pieces[j], "tp", j, ranks) for j in reversed(range(1, ranks))]
    asks = gather(ask, "inst", insts)
    payloads = attend_resident(lengths, query[0], k_cache[0], v_cache[0], ranks)
    payloads = [payloads[0]] + [swapped(payloads[j], "tp", j, ranks) for j in range(1, ranks)]
    kept = combine_resident(ask, payloads, residents, heads_mine, kv_mine)
    cos, sin = rotation(slots, requests, head_size)
    *prepared, places = prepare(
        mig_dest.T,
        mig_count.T,
        k_gain.reshape(1, head_size),
        cos,
        sin,
        asks,
        residents,
        heads_mine,
        kv_mine,
    )
    moved = attend_moved(prepared, pieces, kept, requests, feats * ranks)
    return finish(kept, places, gather(moved, "inst", insts), insts, requests)[None]


def solution(mesh):
    placed = (
        P(("group", "inst"), None, None, "tp"),
        P("group", None),
        P("group", None),
        P("tp"),
        P("tp", None),
        P(),
        P(("group", "inst"), None, None),
        P(("group", "inst"), None, None),
        P(("group", "inst"), None, "tp", None),
        P(("group", "inst"), None, "tp", None),
        P(("group", "inst"), None),
    )
    return jax.shard_map(
        per_device,
        mesh=mesh,
        in_specs=placed,
        out_specs=P(("group", "inst"), None, "tp"),
        check_vma=False,
    )
```

time: 41.8 us -> 45 us (1.077)
  waiting for transfers between devices: 6.02 us -> 12.1 us
  local copies, waits for them, and re-layouts: 2.32 us -> 0.75 us
  starting transfers between devices: 16.5 us -> 15.1 us
    ppermute x9 -> x10, waiting for transfers between devices: 3.66 us -> 12.1 us  [swapped(): return lax.ppermute(x, axis, [(i, i ^ j) for i in range(n)])]
    all_to_all x1 -> x0, starting transfers between devices: 3.27 us -> none  [per_device(): asked = lax.all_to_all(asked, 'inst', 0, 0, tiled=True)]
    all_to_all x1 -> x0, waiting for transfers between devices: 2.36 us -> none  [per_device(): asked = lax.all_to_all(asked, 'inst', 0, 0, tiled=True)]
    ppermute x9 -> x10, starting transfers between devices: 13.2 us -> 15.1 us  [swapped(): return lax.ppermute(x, axis, [(i, i ^ j) for i in range(n)])]
    unnamed x16, local copies, waits for them, and re-layouts: 1.65 us -> 0.75 us
    another operation x0 -> x2, other arithmetic: none -> 0.82 us  [gather(): held = jnp.stack([held, one]) if step == 0 else jnp.concatenate([held, one])]
    sub x1 -> x0, other arithmetic: 0.66 us -> none  [per_device(): valid = lengths[0] - rank * k_cache.shape[2]]
    broadcast_in_dim x1 -> x0, local copies, waits for them, and re-layouts: 0.64 us -> none  [per_device(): jnp.broadcast_to(asks[residents:], (insts,) + asks[residents:].shape)]
  transfers between devices with their start and end apart: 10 -> 10, of which waited for: 4 -> 5; matrix products, arithmetic and copies ran while one was open for 2% -> 2% of each run, Pallas kernels for 0% -> 23%
where the time goes in v4:
time: 45 us; the launch traced here: 44.7 us
  Pallas kernels  15.8 us (35%)
  starting transfers between devices  15.1 us (34%)
  waiting for transfers between devices  12.1 us (27%)
  other arithmetic  0.82 us (2%)
  local copies, waits for them, and re-layouts  0.75 us (2%)
    ppermute x10, starting transfers between devices, swapped(): return lax.ppermute(x, axis, [(i, i ^ j) for i in range(n)])  15.1 us
    ppermute x10, waiting for transfers between devices, swapped(): return lax.ppermute(x, axis, [(i, i ^ j) for i in range(n)])  12.1 us
    pallas_call x1, Pallas kernels, attend_resident(): pl.pallas_call(functools.partial(resident_kernel, ranks, heads), in_specs...  9.5 us
    pallas_call x1, Pallas kernels, project(): pl.pallas_call(functools.partial(project_kernel, ranks, group), in_specs=...  4.06 us
  transfers between devices with their start and end apart: 10, of which 5 were waited for; matrix products, arithmetic and copies ran while one was open for 2% of the time, Pallas kernels for 23%

profile of v4, /device:TPU:0, one launch (start us, length us, event | category | flops | bytes accessed | tf_op | source)
XLA Modules:
  0.0 44.7 jit_solution(14164489172816870890)
XLA Ops:
  0.0 4.1 %project.1 = (bf16[136,512]{1,0:T(8,128)(2,1)}, bf16[136,512]{1,0:T(8,128)(2,1)}, bf16[136,512]{1,0:T(8,128)(2,1)}, bf16[136,512]{1,0:T(8,128)(2,1)}, bf16[5,2560]{1,0:T(8,128)(2,1)}) custom-call(bf16[1280]{0:T(1024)(128)(2,1)} %gain_hbm.1, bf16[64,2,1280]{2,1,0:T(2,128)(2,1)} %bitcast.24, bf16[1280,2048]{1,0:T(8,128)(2,1)} %w_hbm.1, ...), custom_call_target="tpu_custom_call" | custom-call | flops 671088640 | bytes 5242880 | tf_op jit(solution)/shard_map/project/pallas_call | solution.py:133
  4.1 0.5 %collective-permute-start.3 = (bf16[5,2560]{1,0:T(8,128)(2,1)}, bf16[5,2560]{1,0:T(8,128)(2,1)S(1)}, u32[]{:S(2)}, u32[]{:S(2)}) collective-permute-start(bf16[5,2560]{1,0:T(8,128)(2,1)} %get-tuple-element.20.ask_ref), channel_id=1, source_target_pairs={{0,4},{4,0},{8,12},{12,8},{1,5},{5,1},{9,13},{13,9},{2,6},{6,2},{1... | collective-permute-start | bytes 76808 | tf_op jit(solution)/shard_map/ppermute | solution.py:522
  4.6 4.7 %collective-permute-start.5 = (bf16[136,512]{1,0:T(8,128)(2,1)}, bf16[136,512]{1,0:T(8,128)(2,1)S(1)}, u32[]{:S(2)}, u32[]{:S(2)}) collective-permute-start(bf16[136,512]{1,0:T(8,128)(2,1)} %get-tuple-element.32), channel_id=1, source_target_pairs={{0,3},{1,2},{2,1},{3,0},{4,7},{5,6},{6,5},{7,4},{8,11},{9,10},{10,... | collective-permute-start | bytes 417800 | tf_op jit(solution)/shard_map/ppermute | solution.py:522
  9.3 0.0 collective-permute-start.6
  9.3 0.7 %collective-permute-start.7 = (bf16[136,512]{1,0:T(8,128)(2,1)}, bf16[136,512]{1,0:T(8,128)(2,1)S(1)}, u32[]{:S(2)}, u32[]{:S(2)}) collective-permute-start(bf16[136,512]{1,0:T(8,128)(2,1)} %get-tuple-element.34), channel_id=1, source_target_pairs={{0,1},{1,0},{2,3},{3,2},{4,5},{5,4},{6,7},{7,6},{8,9},{9,8},{10,11... | collective-permute-start | bytes 417800 | tf_op jit(solution)/shard_map/ppermute | solution.py:522
  9.9 0.0 collective-permute-done.3.rest_0_
  9.9 0.8 %pad_maximum_fusion = bf16[2,5,2560]{2,1,0:T(8,128)(2,1)S(1)} fusion(bf16[1,5,2560]{2,1,0:T(8,128)(2,1)S(1)} %bitcast.13, bf16[1,5,2560]{2,1,0:T(8,128)(2,1)} %bitcast.14), kind=kLoop, calls=%fused_computation | loop fusion | flops 25600 | bytes 102400 | tf_op jit(solution)/shard_map/stack | solution.py:531
  10.7 1.7 %collective-permute-start.4 = (bf16[2,5,2560]{2,1,0:T(8,128)(2,1)S(1)}, bf16[2,5,2560]{2,1,0:T(8,128)(2,1)S(1)}, u32[]{:S(2)}, u32[]{:S(2)}) collective-permute-start(bf16[2,5,2560]{2,1,0:T(8,128)(2,1)S(1)} %pad_maximum_fusion), channel_id=1, source_target_pairs={{0,8},{4,12},{8,0},{12,4},{1,9},{5,13},{9,1},{13,5},{2,10},{6,14},... | collective-permute-start | bytes 153608 | tf_op jit(solution)/shard_map/ppermute | solution.py:522
  12.4 0.0 copy-start
  12.4 0.0 copy-start.2
  12.4 0.0 copy-start.3
  12.4 0.0 copy-start.5
  12.4 0.0 copy-start.6
  12.4 0.0 copy-start.7
  12.4 0.0 copy-start.1
  12.4 9.5 %attend_resident.1 = (bf16[64,128]{1,0:T(8,128)(2,1)}, bf16[64,128]{1,0:T(8,128)(2,1)}, bf16[64,128]{1,0:T(8,128)(2,1)}, bf16[64,128]{1,0:T(8,128)(2,1)}) custom-call(s32[1,3]{1,0:T(1,128)} %len_hbm.1, bf16[5,8192]{1,0:T(8,128)(2,1)} %bitcast.23, bf16[3,1024,1024]{2,1,0:T(8,128)(2,1)} %bitcast.20, bf16[3,1024,1024]{2,1,0:T(8,128)(2,1)} %bitcast.21), custom_call_target="tpu_custom_call" | custom-call | flops 100663296 | bytes 12582912 | tf_op jit(solution)/shard_map/attend_resident/pallas_call | solution.py:243
  22.0 1.3 %collective-permute-start = (bf16[64,128]{1,0:T(8,128)(2,1)}, bf16[64,128]{1,0:T(8,128)(2,1)S(1)}, u32[]{:S(2)}, u32[]{:S(2)}) collective-permute-start(bf16[64,128]{1,0:T(8,128)(2,1)} %get-tuple-element.22), channel_id=1, source_target_pairs={{0,1},{1,0},{2,3},{3,2},{4,5},{5,4},{6,7},{7,6},{8,9},{9,8},{10,11... | collective-permute-start | bytes 49160 | tf_op jit(solution)/shard_map/ppermute | solution.py:522
  23.3 2.7 %collective-permute-done.rest_1_ = bf16[64,128]{1,0:T(8,128)(2,1)S(1)} collective-permute-done((bf16[64,128]{1,0:T(8,128)(2,1)}, bf16[64,128]{1,0:T(8,128)(2,1)S(1)}, u32[]{:S(2)}, u32[]{:S(2)}) %collective-permute-start) | collective-permute-done | bytes 16416 | tf_op jit(solution)/shard_map/ppermute | solution.py:522
  26.0 2.1 %collective-permute-start.1 = (bf16[64,128]{1,0:T(8,128)(2,1)}, bf16[64,128]{1,0:T(8,128)(2,1)S(1)}, u32[]{:S(2)}, u32[]{:S(2)}) collective-permute-start(bf16[64,128]{1,0:T(8,128)(2,1)} %get-tuple-element.23), channel_id=1, source_target_pairs={{0,2},{1,3},{2,0},{3,1},{4,6},{5,7},{6,4},{7,5},{8,10},{9,11},{10,... | collective-permute-start | bytes 49160 | tf_op jit(solution)/shard_map/ppermute | solution.py:522
  28.1 2.7 %collective-permute-done.1.rest_2_ = bf16[64,128]{1,0:T(8,128)(2,1)S(1)} collective-permute-done((bf16[64,128]{1,0:T(8,128)(2,1)}, bf16[64,128]{1,0:T(8,128)(2,1)S(1)}, u32[]{:S(2)}, u32[]{:S(2)}) %collective-permute-start.1) | collective-permute-done | bytes 16416 | tf_op jit(solution)/shard_map/ppermute | solution.py:522
  30.8 3.6 %collective-permute-start.2 = (bf16[64,128]{1,0:T(8,128)(2,1)}, bf16[64,128]{1,0:T(8,128)(2,1)S(1)}, u32[]{:S(2)}, u32[]{:S(2)}) collective-permute-start(bf16[64,128]{1,0:T(8,128)(2,1)} %get-tuple-element.24), channel_id=1, source_target_pairs={{0,3},{1,2},{2,1},{3,0},{4,7},{5,6},{6,5},{7,4},{8,11},{9,10},{10,... | collective-permute-start | bytes 49160 | tf_op jit(solution)/shard_map/ppermute | solution.py:522
  34.4 2.1 %collective-permute-done.2.rest_3_ = bf16[64,128]{1,0:T(8,128)(2,1)S(1)} collective-permute-done((bf16[64,128]{1,0:T(8,128)(2,1)}, bf16[64,128]{1,0:T(8,128)(2,1)S(1)}, u32[]{:S(2)}, u32[]{:S(2)}) %collective-permute-start.2) | collective-permute-done | bytes 16416 | tf_op jit(solution)/shard_map/ppermute | solution.py:522
  36.6 0.0 copy-done
  36.6 0.0 copy-start.4
  36.6 0.7 %copy-done.4 = bf16[64,128]{1,0:T(8,128)(2,1)S(1)} copy-done((bf16[64,128]{1,0:T(8,128)(2,1)S(1)}, bf16[64,128]{1,0:T(8,128)(2,1)}, u32[]{:S(2)}) %copy-start.4) | copy-done | bytes 16408
  37.3 0.2 combine_resident.1.rest_4_.kept_ref
  37.5 0.0 collective-permute-done.4.rest_1_
  37.5 0.0 copy-done.2
  37.5 0.0 copy-done.3
  37.5 0.0 copy-done.5
  37.5 0.0 copy-done.6
  37.5 0.0 copy-done.7
  37.5 0.8 %prepare.1 = (bf16[32,128]{1,0:T(8,128)(2,1)S(1)}, f32[2,32,128]{2,1,0:T(8,128)S(1)}, s32[32,128]{1,0:T(8,128)S(1)}, f32[128,128]{1,0:T(8,128)S(1)}, f32[128,128]{1,0:T(8,128)S(1)}, /*index=5*/s32[8,128]{1,0:T(8,128)S(1)}) custom-call(s32[2,4]{1,0:T(2,128)S(1)} %bitcast.17, s32[2,4]{1,0:T(2,128)S(1)} %bitcast.18, bf16[1,128]{1,0:T(2,128)(2,1)S(1)} %bitcast.19, ...), custom_call_target="tpu_custom_call" | custom-call | tf_op jit(solution)/shard_map/prepare/pallas_call | solution.py:334
  38.3 0.0 collective-permute-done.5.rest_1_
  38.3 0.0 collective-permute-done.6.rest_2_
  38.3 0.0 collective-permute-done.7.rest_3_
  38.3 0.0 copy-done.1
  38.4 0.6 %attend_moved.1 = bf16[2,2048]{1,0:T(2,128)(2,1)S(1)} custom-call(bf16[32,128]{1,0:T(8,128)(2,1)S(1)} %get-tuple-element.26.q_ref, f32[2,32,128]{2,1,0:T(8,128)S(1)} %get-tuple-element.27.own_ref, s32[32,128]{1,0:T(8,128)S(1)} %get-tuple-element.28.limit_ref, f32[128,128]{1,0:T(8,128)S(1)} %get-tuple-element.29.cos_ref, ...), custom_call_target="tpu_custom_call" | custom-call | tf_op jit(solution)/shard_map/attend_moved/pallas_call | solution.py:425
  39.0 0.1 collective-permute-start.8
  39.1 1.2 %collective-permute-done.8.rest_0_ = bf16[2,2048]{1,0:T(2,128)(2,1)S(1)} collective-permute-done((bf16[2,2048]{1,0:T(2,128)(2,1)S(1)}, bf16[2,2048]{1,0:T(2,128)(2,1)S(1)}, u32[]{:S(2)}, u32[]{:S(2)}) %collective-permute-start.8) | collective-permute-done | bytes 8224 | tf_op jit(solution)/shard_map/ppermute | solution.py:522
  40.3 0.5 %collective-permute-start.9 = (bf16[2,2,2048]{2,1,0:T(2,128)(2,1)S(1)}, bf16[2,2,2048]{2,1,0:T(2,128)(2,1)S(1)}, u32[]{:S(2)}, u32[]{:S(2)}) collective-permute-start(bf16[2,2,2048]{2,1,0:T(2,128)(2,1)S(1)} %pad_maximum_fusion.1), channel_id=1, source_target_pairs={{0,8},{4,12},{8,0},{12,4},{1,9},{5,13},{9,1},{13,5},{2,10},{6,14},... | collective-permute-start | bytes 49160 | tf_op jit(solution)/shard_map/ppermute | solution.py:522
  40.7 3.3 %collective-permute-done.9.rest_1_ = bf16[2,2,2048]{2,1,0:T(2,128)(2,1)S(1)} collective-permute-done((bf16[2,2,2048]{2,1,0:T(2,128)(2,1)S(1)}, bf16[2,2,2048]{2,1,0:T(2,128)(2,1)S(1)}, u32[]{:S(2)}, u32[]{:S(2)}) %collective-permute-start.9) | collective-permute-done | bytes 16416 | tf_op jit(solution)/shard_map/ppermute | solution.py:522
  44.1 0.7 %finish.1 = bf16[5,2048]{1,0:T(8,128)(2,1)} custom-call(f32[3,2048]{1,0:T(4,128)S(1)} %combine_resident.1.rest_4_.kept_ref, s32[8,128]{1,0:T(8,128)S(1)} %get-tuple-element.25.place_ref, bf16[2,2048]{1,0:T(2,128)(2,1)S(1)} %collective-permute-done.8.rest_0_, bf16[2,2,2048]{2,1,0:T(2,128)(2,1)S(1)} %collective-permute-done.9.rest_1_), custom_call_target="tpu_custom_call" | custom-call | tf_op jit(solution)/shard_map/finish/pallas_call | solution.py:511
  (1 shorter events, 0.0 us)
Async XLA Ops:
  4.1 5.9 %collective-permute-start.3 = (bf16[5,2560]{1,0:T(8,128)(2,1)}, bf16[5,2560]{1,0:T(8,128)(2,1)S(1)}, u32[]{:S(2)}, u32[]{:S(2)}) collective-permute-start(bf16[5,2560]{1,0:T(8,128)(2,1)} %get-tuple-element.20.ask_ref), channel_id=1, source_target_pairs={{0,4},{4,0},{8,12},{12,8},{1,5},{5,1},{9,13},{13,9},{2,6},{6,2},{1... | collective-permute-start | bytes 76808 | tf_op jit(solution)/shard_map/ppermute | solution.py:522
  4.6 33.7 %collective-permute-start.5 = (bf16[136,512]{1,0:T(8,128)(2,1)}, bf16[136,512]{1,0:T(8,128)(2,1)S(1)}, u32[]{:S(2)}, u32[]{:S(2)}) collective-permute-start(bf16[136,512]{1,0:T(8,128)(2,1)} %get-tuple-element.32), channel_id=1, source_target_pairs={{0,3},{1,2},{2,1},{3,0},{4,7},{5,6},{6,5},{7,4},{8,11},{9,10},{10,... | collective-permute-start | bytes 417800 | tf_op jit(solution)/shard_map/ppermute | solution.py:522
  9.3 29.1 %collective-permute-start.6 = (bf16[136,512]{1,0:T(8,128)(2,1)}, bf16[136,512]{1,0:T(8,128)(2,1)S(1)}, u32[]{:S(2)}, u32[]{:S(2)}) collective-permute-start(bf16[136,512]{1,0:T(8,128)(2,1)} %get-tuple-element.33), channel_id=1, source_target_pairs={{0,2},{1,3},{2,0},{3,1},{4,6},{5,7},{6,4},{7,5},{8,10},{9,11},{10,... | collective-permute-start | bytes 417800 | tf_op jit(solution)/shard_map/ppermute | solution.py:522
  9.3 29.1 %collective-permute-start.7 = (bf16[136,512]{1,0:T(8,128)(2,1)}, bf16[136,512]{1,0:T(8,128)(2,1)S(1)}, u32[]{:S(2)}, u32[]{:S(2)}) collective-permute-start(bf16[136,512]{1,0:T(8,128)(2,1)} %get-tuple-element.34), channel_id=1, source_target_pairs={{0,1},{1,0},{2,3},{3,2},{4,5},{5,4},{6,7},{7,6},{8,9},{9,8},{10,11... | collective-permute-start | bytes 417800 | tf_op jit(solution)/shard_map/ppermute | solution.py:522
  10.7 26.8 %collective-permute-start.4 = (bf16[2,5,2560]{2,1,0:T(8,128)(2,1)S(1)}, bf16[2,5,2560]{2,1,0:T(8,128)(2,1)S(1)}, u32[]{:S(2)}, u32[]{:S(2)}) collective-permute-start(bf16[2,5,2560]{2,1,0:T(8,128)(2,1)S(1)} %pad_maximum_fusion), channel_id=1, source_target_pairs={{0,8},{4,12},{8,0},{12,4},{1,9},{5,13},{9,1},{13,5},{2,10},{6,14},... | collective-permute-start | bytes 153608 | tf_op jit(solution)/shard_map/ppermute | solution.py:522
  12.4 24.2 %copy-start = (bf16[5,2560]{1,0:T(8,128)(2,1)S(1)}, bf16[5,2560]{1,0:T(8,128)(2,1)}, u32[]{:S(2)}) copy-start(bf16[5,2560]{1,0:T(8,128)(2,1)} %get-tuple-element.20.ask_ref) | copy-start | bytes 76804
  12.4 25.1 %copy-start.2 = (f32[128,128]{1,0:T(8,128)S(1)}, f32[128,128]{1,0:T(8,128)}, u32[]{:S(2)}) copy-start(f32[128,128]{1,0:T(8,128)} %constant.5.clone.sin_ref) | copy-start | bytes 196612
  12.4 25.1 %copy-start.3 = (f32[128,128]{1,0:T(8,128)S(1)}, f32[128,128]{1,0:T(8,128)}, u32[]{:S(2)}) copy-start(f32[128,128]{1,0:T(8,128)} %constant.4.clone.cos_ref) | copy-start | bytes 196612
  12.4 25.1 %copy-start.5 = (s32[4,2]{0,1:T(2,128)S(1)}, s32[4,2]{0,1:T(2,128)}, u32[]{:S(2)}) copy-start(s32[4,2]{0,1:T(2,128)} %param.14) | copy-start | bytes 100
  12.4 25.1 %copy-start.6 = (s32[4,2]{0,1:T(2,128)S(1)}, s32[4,2]{0,1:T(2,128)}, u32[]{:S(2)}) copy-start(s32[4,2]{0,1:T(2,128)} %param.15) | copy-start | bytes 100
  12.4 25.1 %copy-start.7 = (bf16[128]{0:T(256)(128)(2,1)S(1)}, bf16[128]{0:T(256)(128)(2,1)}, u32[]{:S(2)}) copy-start(bf16[128]{0:T(256)(128)(2,1)} %param.18) | copy-start | bytes 772
  12.4 25.9 %copy-start.1 = (bf16[136,512]{1,0:T(8,128)(2,1)S(1)}, bf16[136,512]{1,0:T(8,128)(2,1)}, u32[]{:S(2)}) copy-start(bf16[136,512]{1,0:T(8,128)(2,1)} %get-tuple-element.31.rest_0_) | copy-start | bytes 417796
  22.0 4.0 %collective-permute-start = (bf16[64,128]{1,0:T(8,128)(2,1)}, bf16[64,128]{1,0:T(8,128)(2,1)S(1)}, u32[]{:S(2)}, u32[]{:S(2)}) collective-permute-start(bf16[64,128]{1,0:T(8,128)(2,1)} %get-tuple-element.22), channel_id=1, source_target_pairs={{0,1},{1,0},{2,3},{3,2},{4,5},{5,4},{6,7},{7,6},{8,9},{9,8},{10,11... | collective-permute-start | bytes 49160 | tf_op jit(solution)/shard_map/ppermute | solution.py:522
  26.0 4.8 %collective-permute-start.1 = (bf16[64,128]{1,0:T(8,128)(2,1)}, bf16[64,128]{1,0:T(8,128)(2,1)S(1)}, u32[]{:S(2)}, u32[]{:S(2)}) collective-permute-start(bf16[64,128]{1,0:T(8,128)(2,1)} %get-tuple-element.23), channel_id=1, source_target_pairs={{0,2},{1,3},{2,0},{3,1},{4,6},{5,7},{6,4},{7,5},{8,10},{9,11},{10,... | collective-permute-start | bytes 49160 | tf_op jit(solution)/shard_map/ppermute | solution.py:522
  30.8 5.7 %collective-permute-start.2 = (bf16[64,128]{1,0:T(8,128)(2,1)}, bf16[64,128]{1,0:T(8,128)(2,1)S(1)}, u32[]{:S(2)}, u32[]{:S(2)}) collective-permute-start(bf16[64,128]{1,0:T(8,128)(2,1)} %get-tuple-element.24), channel_id=1, source_target_pairs={{0,3},{1,2},{2,1},{3,0},{4,7},{5,6},{6,5},{7,4},{8,11},{9,10},{10,... | collective-permute-start | bytes 49160 | tf_op jit(solution)/shard_map/ppermute | solution.py:522
  36.6 0.7 %copy-start.4 = (bf16[64,128]{1,0:T(8,128)(2,1)S(1)}, bf16[64,128]{1,0:T(8,128)(2,1)}, u32[]{:S(2)}) copy-start(bf16[64,128]{1,0:T(8,128)(2,1)} %get-tuple-element.21.rest_0_) | copy-start | bytes 49156
  39.0 1.2 %collective-permute-start.8 = (bf16[2,2048]{1,0:T(2,128)(2,1)S(1)}, bf16[2,2048]{1,0:T(2,128)(2,1)S(1)}, u32[]{:S(2)}, u32[]{:S(2)}) collective-permute-start(bf16[2,2048]{1,0:T(2,128)(2,1)S(1)} %attend_moved.1), channel_id=1, source_target_pairs={{0,4},{4,0},{8,12},{12,8},{1,5},{5,1},{9,13},{13,9},{2,6},{6,2},{1... | collective-permute-start | bytes 24584 | tf_op jit(solution)/shard_map/ppermute | solution.py:522
  40.3 3.8 %collective-permute-start.9 = (bf16[2,2,2048]{2,1,0:T(2,128)(2,1)S(1)}, bf16[2,2,2048]{2,1,0:T(2,128)(2,1)S(1)}, u32[]{:S(2)}, u32[]{:S(2)}) collective-permute-start(bf16[2,2,2048]{2,1,0:T(2,128)(2,1)S(1)} %pad_maximum_fusion.1), channel_id=1, source_target_pairs={{0,8},{4,12},{8,0},{12,4},{1,9},{5,13},{9,1},{13,5},{2,10},{6,14},... | collective-permute-start | bytes 49160 | tf_op jit(solution)/shard_map/ppermute | solution.py:522

commit v5 on v4

--- a/solution.py
+++ b/solution.py
@@ -163,18 +163,16 @@
     q_copy = pltpu.make_async_copy(q_hbm, q_ref, in_sems.at[1])
     q_copy.start()
     residents, positions, width = k_buf.shape
-    half = width // 2
     copies = []
     for r in range(residents):
-        trio = [pltpu.make_async_copy(k_hbm.at[r], k_buf.at[r], sems.at[0, r])]
-        for i in range(2):
-            at = slice(i * half, (i + 1) * half)
-            trio.append(
-                pltpu.make_async_copy(v_hbm.at[r, :, at], v_buf.at[r, :, at], sems.at[1 + i, r])
+        copies.append(
+            (
+                pltpu.make_async_copy(k_hbm.at[r], k_buf.at[r], sems.at[0, r]),
+                pltpu.make_async_copy(v_hbm.at[r], v_buf.at[r], sems.at[1, r]),
             )
-        copies.append(trio)
-    for trio in copies:
-        for copy in trio:
+        )
+    for pair in copies:
+        for copy in pair:
             copy.start()
     kv_heads = width // 128
     group = heads // kv_heads
@@ -215,9 +213,8 @@
         s_all[r, 0] = column_to_row(jnp.concatenate(peaks, axis=0), heads_mine)
         s_all[r, 1] = column_to_row(high.astype(F32), heads_mine)
         s_all[r, 2] = column_to_row(low.astype(F32), heads_mine)
+        copies[r][1].wait()
         for p in range(kv_heads // 2):
-            if p * 4 % kv_heads == 0:
-                copies[r][1 + p * 4 // kv_heads].wait()
             both = jnp.dot(
                 weights[p], v_buf[r, :, p * 256 : (p + 1) * 256], preferred_element_type=F32
             )
@@ -254,7 +251,7 @@
             pltpu.VMEM((residents, heads, 128), F32),
             pltpu.VMEM((residents, 3, ranks, 128), F32),
             pltpu.SemaphoreType.DMA((2,)),
-            pltpu.SemaphoreType.DMA((3, residents)),
+            pltpu.SemaphoreType.DMA((2, residents)),
         ],
         compiler_params=pltpu.CompilerParams(vmem_limit_bytes=60 * MIB),
         cost_estimate=pl.CostEstimate(
@@ -486,30 +483,29 @@
     )(asks, *payloads)
 
 
-def finish_kernel(insts, steps, kept_ref, place_ref, *rest):
-    moved = rest[:steps]
-    out_ref = rest[steps]
+def finish_kernel(kept_ref, place_ref, *rest):
+    moved, out_ref = rest[:-1], rest[-1]
     residents = kept_ref.shape[0]
     decoded, width = out_ref.shape
     requests = decoded - residents
     row = iota((decoded, 128), 0)
-    arrived = [block_of(moved, b)[...].astype(F32) for b in range(1, insts)]
+    arrived = [ref[...].astype(F32) for ref in moved]
     for c in range(0, width, 128):
         kept = kept_ref[:, c : c + 128]
         line = jnp.concatenate([kept, jnp.zeros((requests, 128), F32)], axis=0)
-        for b in range(1, insts):
+        for b in range(len(moved)):
             for i in range(requests):
-                at = b * requests + i
+                at = (b + 1) * requests + i
                 line = jnp.where(
-                    place_ref[at : at + 1, :] == row, arrived[b - 1][i : i + 1, c : c + 128], line
+                    place_ref[at : at + 1, :] == row, arrived[b][i : i + 1, c : c + 128], line
                 )
         out_ref[:, c : c + 128] = line.astype(BF16)
 
 
-def finish(kept, places, moved, insts, requests):
+def finish(kept, places, moved, requests):
     residents, width = kept.shape
     return pl.pallas_call(
-        functools.partial(finish_kernel, insts, len(moved)),
+        finish_kernel,
         in_specs=[VMEM] * (2 + len(moved)),
         out_specs=VMEM,
         out_shape=jax.ShapeDtypeStruct((residents + requests, width), BF16),
@@ -587,8 +583,9 @@
         heads_mine,
         kv_mine,
     )
-    moved = attend_moved(prepared, pieces, kept, requests, feats * ranks)
-    return finish(kept, places, gather(moved, "inst", insts), insts, requests)[None]
+    moved = attend_moved(prepared, pieces, payloads[1], requests, feats * ranks)
+    moved = [swapped(moved, "inst", b, insts) for b in range(1, insts)]
+    return finish(kept, places, moved, requests)[None]
 
 
 def solution(mesh):

time: 45 us -> 35.7 us (0.79)
  waiting for transfers between devices: 12.1 us -> 3.96 us
  Pallas kernels: 15.8 us -> 15.1 us
  starting transfers between devices: 15.1 us -> 14.6 us
    ppermute x10 -> x11, waiting for transfers between devices: 12.1 us -> 3.96 us  [swapped(): return lax.ppermute(x, axis, [(i, i ^ j) for i in range(n)])]
    pallas_call x1, Pallas kernels: 9.5 us -> 8.82 us  [attend_resident(): pl.pallas_call(functools.partial(resident_kernel, ranks, heads), in_specs...]
    ppermute x10 -> x11, starting transfers between devices: 15.1 us -> 14.6 us  [swapped(): return lax.ppermute(x, axis, [(i, i ^ j) for i in range(n)])]
  transfers between devices with their start and end apart: 10 -> 11, of which waited for: 5 -> 3; matrix products, arithmetic and copies ran while one was open for 2% -> 2% of each run, Pallas kernels for 23% -> 29%
where the time goes in v5:
time: 35.7 us; the launch traced here: 35.4 us
  Pallas kernels  15.1 us (42%)
  starting transfers between devices  14.6 us (41%)
  waiting for transfers between devices  3.96 us (11%)
  other arithmetic  0.8 us (2%)
  local copies, waits for them, and re-layouts  0.75 us (2%)
    ppermute x11, starting transfers between devices, swapped(): return lax.ppermute(x, axis, [(i, i ^ j) for i in range(n)])  14.6 us
    pallas_call x1, Pallas kernels, attend_resident(): pl.pallas_call(functools.partial(resident_kernel, ranks, heads), in_specs...  8.82 us
    pallas_call x1, Pallas kernels, project(): pl.pallas_call(functools.partial(project_kernel, ranks, group), in_specs=...  4.06 us
    ppermute x11, waiting for transfers between devices, swapped(): return lax.ppermute(x, axis, [(i, i ^ j) for i in range(n)])  3.96 us
    another operation x1, other arithmetic, gather(): held = jnp.stack([held, one]) if step == 0 else jnp.concatenate([held, one])  0.8 us
    pallas_call x1, Pallas kernels, prepare(): pl.pallas_call(functools.partial(prepare_kernel, insts, len(asks), reside...  0.79 us
    unnamed x16, local copies, waits for them, and re-layouts  0.75 us
  transfers between devices with their start and end apart: 11, of which 3 were waited for; matrix products, arithmetic and copies ran while one was open for 2% of the time, Pallas kernels for 29%

profile of v5, /device:TPU:0, one launch (start us, length us, event | category | flops | bytes accessed | tf_op | source)
XLA Modules:
  0.0 35.4 jit_solution(14569964533916041292)
XLA Ops:
  0.0 4.1 %project.1 = (bf16[136,512]{1,0:T(8,128)(2,1)}, bf16[136,512]{1,0:T(8,128)(2,1)}, bf16[136,512]{1,0:T(8,128)(2,1)}, bf16[136,512]{1,0:T(8,128)(2,1)}, bf16[5,2560]{1,0:T(8,128)(2,1)}) custom-call(bf16[1280]{0:T(1024)(128)(2,1)} %gain_hbm.1, bf16[64,2,1280]{2,1,0:T(2,128)(2,1)} %bitcast.20, bf16[1280,2048]{1,0:T(8,128)(2,1)} %w_hbm.1, ...), custom_call_target="tpu_custom_call" | custom-call | flops 671088640 | bytes 5242880 | tf_op jit(solution)/shard_map/project/pallas_call | solution.py:133
  4.1 0.5 %collective-permute-start.3 = (bf16[5,2560]{1,0:T(8,128)(2,1)}, bf16[5,2560]{1,0:T(8,128)(2,1)S(1)}, u32[]{:S(2)}, u32[]{:S(2)}) collective-permute-start(bf16[5,2560]{1,0:T(8,128)(2,1)} %get-tuple-element.20.ask_ref), channel_id=1, source_target_pairs={{0,4},{4,0},{8,12},{12,8},{1,5},{5,1},{9,13},{13,9},{2,6},{6,2},{1... | collective-permute-start | bytes 76808 | tf_op jit(solution)/shard_map/ppermute | solution.py:518
  4.6 4.7 %collective-permute-start.5 = (bf16[136,512]{1,0:T(8,128)(2,1)}, bf16[136,512]{1,0:T(8,128)(2,1)S(1)}, u32[]{:S(2)}, u32[]{:S(2)}) collective-permute-start(bf16[136,512]{1,0:T(8,128)(2,1)} %get-tuple-element.32), channel_id=1, source_target_pairs={{0,3},{1,2},{2,1},{3,0},{4,7},{5,6},{6,5},{7,4},{8,11},{9,10},{10,... | collective-permute-start | bytes 417800 | tf_op jit(solution)/shard_map/ppermute | solution.py:518
  9.3 0.0 collective-permute-start.6
  9.3 0.7 %collective-permute-start.7 = (bf16[136,512]{1,0:T(8,128)(2,1)}, bf16[136,512]{1,0:T(8,128)(2,1)S(1)}, u32[]{:S(2)}, u32[]{:S(2)}) collective-permute-start(bf16[136,512]{1,0:T(8,128)(2,1)} %get-tuple-element.34), channel_id=1, source_target_pairs={{0,1},{1,0},{2,3},{3,2},{4,5},{5,4},{6,7},{7,6},{8,9},{9,8},{10,11... | collective-permute-start | bytes 417800 | tf_op jit(solution)/shard_map/ppermute | solution.py:518
  9.9 0.0 collective-permute-done.3.rest_0_
  9.9 0.8 %pad_maximum_fusion = bf16[2,5,2560]{2,1,0:T(8,128)(2,1)S(1)} fusion(bf16[1,5,2560]{2,1,0:T(8,128)(2,1)S(1)} %bitcast.11, bf16[1,5,2560]{2,1,0:T(8,128)(2,1)} %bitcast.12), kind=kLoop, calls=%fused_computation | loop fusion | flops 25600 | bytes 102400 | tf_op jit(solution)/shard_map/stack | solution.py:527
  10.7 1.7 %collective-permute-start.4 = (bf16[2,5,2560]{2,1,0:T(8,128)(2,1)S(1)}, bf16[2,5,2560]{2,1,0:T(8,128)(2,1)S(1)}, u32[]{:S(2)}, u32[]{:S(2)}) collective-permute-start(bf16[2,5,2560]{2,1,0:T(8,128)(2,1)S(1)} %pad_maximum_fusion), channel_id=1, source_target_pairs={{0,8},{4,12},{8,0},{12,4},{1,9},{5,13},{9,1},{13,5},{2,10},{6,14},... | collective-permute-start | bytes 153608 | tf_op jit(solution)/shard_map/ppermute | solution.py:518
  12.4 0.0 copy-start.2
  12.4 0.0 copy-start.3
  12.4 0.0 copy-start.5
  12.4 0.0 copy-start.6
  12.4 0.0 copy-start.7
  12.4 0.0 copy-start.1
  12.4 0.0 copy-start
  12.5 8.8 %attend_resident.1 = (bf16[64,128]{1,0:T(8,128)(2,1)}, bf16[64,128]{1,0:T(8,128)(2,1)}, bf16[64,128]{1,0:T(8,128)(2,1)}, bf16[64,128]{1,0:T(8,128)(2,1)}) custom-call(s32[1,3]{1,0:T(1,128)} %len_hbm.1, bf16[5,8192]{1,0:T(8,128)(2,1)} %bitcast.19, bf16[3,1024,1024]{2,1,0:T(8,128)(2,1)} %bitcast.16, bf16[3,1024,1024]{2,1,0:T(8,128)(2,1)} %bitcast.17), custom_call_target="tpu_custom_call" | custom-call | flops 100663296 | bytes 12582912 | tf_op jit(solution)/shard_map/attend_resident/pallas_call | solution.py:240
  21.3 1.3 %collective-permute-start = (bf16[64,128]{1,0:T(8,128)(2,1)}, bf16[64,128]{1,0:T(8,128)(2,1)S(1)}, u32[]{:S(2)}, u32[]{:S(2)}) collective-permute-start(bf16[64,128]{1,0:T(8,128)(2,1)} %get-tuple-element.22), channel_id=1, source_target_pairs={{0,1},{1,0},{2,3},{3,2},{4,5},{5,4},{6,7},{7,6},{8,9},{9,8},{10,11... | collective-permute-start | bytes 49160 | tf_op jit(solution)/shard_map/ppermute | solution.py:518
  22.6 2.7 %collective-permute-done.rest_1_.rest_4_ = bf16[64,128]{1,0:T(8,128)(2,1)S(1)} collective-permute-done((bf16[64,128]{1,0:T(8,128)(2,1)}, bf16[64,128]{1,0:T(8,128)(2,1)S(1)}, u32[]{:S(2)}, u32[]{:S(2)}) %collective-permute-start) | collective-permute-done | bytes 16416 | tf_op jit(solution)/shard_map/ppermute | solution.py:518
  25.3 2.1 %collective-permute-start.1 = (bf16[64,128]{1,0:T(8,128)(2,1)}, bf16[64,128]{1,0:T(8,128)(2,1)S(1)}, u32[]{:S(2)}, u32[]{:S(2)}) collective-permute-start(bf16[64,128]{1,0:T(8,128)(2,1)} %get-tuple-element.23), channel_id=1, source_target_pairs={{0,2},{1,3},{2,0},{3,1},{4,6},{5,7},{6,4},{7,5},{8,10},{9,11},{10,... | collective-permute-start | bytes 49160 | tf_op jit(solution)/shard_map/ppermute | solution.py:518
  27.4 0.0 collective-permute-done.4.rest_1_
  27.4 1.5 %collective-permute-start.2 = (bf16[64,128]{1,0:T(8,128)(2,1)}, bf16[64,128]{1,0:T(8,128)(2,1)S(1)}, u32[]{:S(2)}, u32[]{:S(2)}) collective-permute-start(bf16[64,128]{1,0:T(8,128)(2,1)} %get-tuple-element.24), channel_id=1, source_target_pairs={{0,3},{1,2},{2,1},{3,0},{4,7},{5,6},{6,5},{7,4},{8,11},{9,10},{10,... | collective-permute-start | bytes 49160 | tf_op jit(solution)/shard_map/ppermute | solution.py:518
  28.9 0.0 copy-done.2
  28.9 0.0 copy-done.3
  28.9 0.0 copy-done.5
  28.9 0.0 copy-done.6
  28.9 0.0 copy-done.7
  28.9 0.8 %prepare.1 = (bf16[32,128]{1,0:T(8,128)(2,1)S(1)}, f32[2,32,128]{2,1,0:T(8,128)S(1)}, s32[32,128]{1,0:T(8,128)S(1)}, f32[128,128]{1,0:T(8,128)S(1)}, f32[128,128]{1,0:T(8,128)S(1)}, /*index=5*/s32[8,128]{1,0:T(8,128)S(1)}) custom-call(s32[2,4]{1,0:T(2,128)S(1)} %bitcast.13, s32[2,4]{1,0:T(2,128)S(1)} %bitcast.14, bf16[1,128]{1,0:T(2,128)(2,1)S(1)} %bitcast.15, ...), custom_call_target="tpu_custom_call" | custom-call | tf_op jit(solution)/shard_map/prepare/pallas_call | solution.py:331
  29.7 0.0 collective-permute-done.5.rest_1_
  29.7 0.0 collective-permute-done.6.rest_2_
  29.7 0.0 collective-permute-done.7.rest_3_
  29.7 0.0 copy-done.1
  29.8 0.6 %attend_moved.1 = bf16[2,2048]{1,0:T(2,128)(2,1)S(1)} custom-call(bf16[32,128]{1,0:T(8,128)(2,1)S(1)} %get-tuple-element.26.q_ref, f32[2,32,128]{2,1,0:T(8,128)S(1)} %get-tuple-element.27.own_ref, s32[32,128]{1,0:T(8,128)S(1)} %get-tuple-element.28.limit_ref, f32[128,128]{1,0:T(8,128)S(1)} %get-tuple-element.29.cos_ref, ...), custom_call_target="tpu_custom_call" | custom-call | tf_op jit(solution)/shard_map/attend_moved/pallas_call | solution.py:422
  30.4 0.1 collective-permute-start.10
  30.5 0.6 %collective-permute-start.8 = (bf16[2,2048]{1,0:T(2,128)(2,1)S(1)}, bf16[2,2048]{1,0:T(2,128)(2,1)S(1)}, u32[]{:S(2)}, u32[]{:S(2)}) collective-permute-start(bf16[2,2048]{1,0:T(2,128)(2,1)S(1)} %attend_moved.1), channel_id=1, source_target_pairs={{0,4},{4,0},{8,12},{12,8},{1,5},{5,1},{9,13},{13,9},{2,6},{6,2},{1... | collective-permute-start | bytes 24584 | tf_op jit(solution)/shard_map/ppermute | solution.py:518
  31.1 1.5 %collective-permute-start.9 = (bf16[2,2048]{1,0:T(2,128)(2,1)S(1)}, bf16[2,2048]{1,0:T(2,128)(2,1)S(1)}, u32[]{:S(2)}, u32[]{:S(2)}) collective-permute-start(bf16[2,2048]{1,0:T(2,128)(2,1)S(1)} %attend_moved.1), channel_id=1, source_target_pairs={{0,8},{4,12},{8,0},{12,4},{1,9},{5,13},{9,1},{13,5},{2,10},{6,14},... | collective-permute-start | bytes 24584 | tf_op jit(solution)/shard_map/ppermute | solution.py:518
  32.6 0.0 collective-permute-done.1.rest_2_
  32.6 0.6 %collective-permute-done.2.rest_3_ = bf16[64,128]{1,0:T(8,128)(2,1)S(1)} collective-permute-done((bf16[64,128]{1,0:T(8,128)(2,1)}, bf16[64,128]{1,0:T(8,128)(2,1)S(1)}, u32[]{:S(2)}, u32[]{:S(2)}) %collective-permute-start.2) | collective-permute-done | bytes 16416 | tf_op jit(solution)/shard_map/ppermute | solution.py:518
  33.2 0.0 copy-done
  33.2 0.0 copy-start.4
  33.2 0.7 %copy-done.4 = bf16[64,128]{1,0:T(8,128)(2,1)S(1)} copy-done((bf16[64,128]{1,0:T(8,128)(2,1)S(1)}, bf16[64,128]{1,0:T(8,128)(2,1)}, u32[]{:S(2)}) %copy-start.4) | copy-done | bytes 16408
  33.9 0.2 combine_resident.1.kept_ref
  34.1 0.0 collective-permute-done.10.rest_2_
  34.1 0.0 collective-permute-done.8.rest_0_
  34.1 0.6 %collective-permute-done.9.rest_1_ = bf16[2,2048]{1,0:T(2,128)(2,1)S(1)} collective-permute-done((bf16[2,2048]{1,0:T(2,128)(2,1)S(1)}, bf16[2,2048]{1,0:T(2,128)(2,1)S(1)}, u32[]{:S(2)}, u32[]{:S(2)}) %collective-permute-start.9) | collective-permute-done | bytes 8224 | tf_op jit(solution)/shard_map/ppermute | solution.py:518
  34.8 0.7 %finish.1 = bf16[5,2048]{1,0:T(8,128)(2,1)} custom-call(f32[3,2048]{1,0:T(4,128)S(1)} %combine_resident.1.kept_ref, s32[8,128]{1,0:T(8,128)S(1)} %get-tuple-element.25.place_ref, bf16[2,2048]{1,0:T(2,128)(2,1)S(1)} %collective-permute-done.8.rest_0_, bf16[2,2048]{1,0:T(2,128)(2,1)S(1)} %collective-permute-done.9.rest_1_, ...), custom_call_target="tpu_custom_call" | custom-call | tf_op jit(solution)/shard_map/finish/pallas_call | solution.py:507
Async XLA Ops:
  4.1 5.9 %collective-permute-start.3 = (bf16[5,2560]{1,0:T(8,128)(2,1)}, bf16[5,2560]{1,0:T(8,128)(2,1)S(1)}, u32[]{:S(2)}, u32[]{:S(2)}) collective-permute-start(bf16[5,2560]{1,0:T(8,128)(2,1)} %get-tuple-element.20.ask_ref), channel_id=1, source_target_pairs={{0,4},{4,0},{8,12},{12,8},{1,5},{5,1},{9,13},{13,9},{2,6},{6,2},{1... | collective-permute-start | bytes 76808 | tf_op jit(solution)/shard_map/ppermute | solution.py:518
  4.6 25.1 %collective-permute-start.5 = (bf16[136,512]{1,0:T(8,128)(2,1)}, bf16[136,512]{1,0:T(8,128)(2,1)S(1)}, u32[]{:S(2)}, u32[]{:S(2)}) collective-permute-start(bf16[136,512]{1,0:T(8,128)(2,1)} %get-tuple-element.32), channel_id=1, source_target_pairs={{0,3},{1,2},{2,1},{3,0},{4,7},{5,6},{6,5},{7,4},{8,11},{9,10},{10,... | collective-permute-start | bytes 417800 | tf_op jit(solution)/shard_map/ppermute | solution.py:518
  9.3 20.5 %collective-permute-start.6 = (bf16[136,512]{1,0:T(8,128)(2,1)}, bf16[136,512]{1,0:T(8,128)(2,1)S(1)}, u32[]{:S(2)}, u32[]{:S(2)}) collective-permute-start(bf16[136,512]{1,0:T(8,128)(2,1)} %get-tuple-element.33), channel_id=1, source_target_pairs={{0,2},{1,3},{2,0},{3,1},{4,6},{5,7},{6,4},{7,5},{8,10},{9,11},{10,... | collective-permute-start | bytes 417800 | tf_op jit(solution)/shard_map/ppermute | solution.py:518
  9.3 20.5 %collective-permute-start.7 = (bf16[136,512]{1,0:T(8,128)(2,1)}, bf16[136,512]{1,0:T(8,128)(2,1)S(1)}, u32[]{:S(2)}, u32[]{:S(2)}) collective-permute-start(bf16[136,512]{1,0:T(8,128)(2,1)} %get-tuple-element.34), channel_id=1, source_target_pairs={{0,1},{1,0},{2,3},{3,2},{4,5},{5,4},{6,7},{7,6},{8,9},{9,8},{10,11... | collective-permute-start | bytes 417800 | tf_op jit(solution)/shard_map/ppermute | solution.py:518
  10.7 16.7 %collective-permute-start.4 = (bf16[2,5,2560]{2,1,0:T(8,128)(2,1)S(1)}, bf16[2,5,2560]{2,1,0:T(8,128)(2,1)S(1)}, u32[]{:S(2)}, u32[]{:S(2)}) collective-permute-start(bf16[2,5,2560]{2,1,0:T(8,128)(2,1)S(1)} %pad_maximum_fusion), channel_id=1, source_target_pairs={{0,8},{4,12},{8,0},{12,4},{1,9},{5,13},{9,1},{13,5},{2,10},{6,14},... | collective-permute-start | bytes 153608 | tf_op jit(solution)/shard_map/ppermute | solution.py:518
  12.4 16.5 %copy-start.2 = (f32[128,128]{1,0:T(8,128)S(1)}, f32[128,128]{1,0:T(8,128)}, u32[]{:S(2)}) copy-start(f32[128,128]{1,0:T(8,128)} %constant.4.clone.cos_ref) | copy-start | bytes 196612
  12.4 16.5 %copy-start.3 = (f32[128,128]{1,0:T(8,128)S(1)}, f32[128,128]{1,0:T(8,128)}, u32[]{:S(2)}) copy-start(f32[128,128]{1,0:T(8,128)} %constant.5.clone.sin_ref) | copy-start | bytes 196612
  12.4 16.5 %copy-start.5 = (s32[4,2]{0,1:T(2,128)S(1)}, s32[4,2]{0,1:T(2,128)}, u32[]{:S(2)}) copy-start(s32[4,2]{0,1:T(2,128)} %param.14) | copy-start | bytes 100
  12.4 16.5 %copy-start.6 = (s32[4,2]{0,1:T(2,128)S(1)}, s32[4,2]{0,1:T(2,128)}, u32[]{:S(2)}) copy-start(s32[4,2]{0,1:T(2,128)} %param.15) | copy-start | bytes 100
  12.4 16.5 %copy-start.7 = (bf16[128]{0:T(256)(128)(2,1)S(1)}, bf16[128]{0:T(256)(128)(2,1)}, u32[]{:S(2)}) copy-start(bf16[128]{0:T(256)(128)(2,1)} %param.18) | copy-start | bytes 772
  12.4 17.3 %copy-start.1 = (bf16[136,512]{1,0:T(8,128)(2,1)S(1)}, bf16[136,512]{1,0:T(8,128)(2,1)}, u32[]{:S(2)}) copy-start(bf16[136,512]{1,0:T(8,128)(2,1)} %get-tuple-element.31.rest_0_) | copy-start | bytes 417796
  12.4 20.7 %copy-start = (bf16[5,2560]{1,0:T(8,128)(2,1)S(1)}, bf16[5,2560]{1,0:T(8,128)(2,1)}, u32[]{:S(2)}) copy-start(bf16[5,2560]{1,0:T(8,128)(2,1)} %get-tuple-element.20.ask_ref) | copy-start | bytes 76804
  21.3 4.0 %collective-permute-start = (bf16[64,128]{1,0:T(8,128)(2,1)}, bf16[64,128]{1,0:T(8,128)(2,1)S(1)}, u32[]{:S(2)}, u32[]{:S(2)}) collective-permute-start(bf16[64,128]{1,0:T(8,128)(2,1)} %get-tuple-element.22), channel_id=1, source_target_pairs={{0,1},{1,0},{2,3},{3,2},{4,5},{5,4},{6,7},{7,6},{8,9},{9,8},{10,11... | collective-permute-start | bytes 49160 | tf_op jit(solution)/shard_map/ppermute | solution.py:518
  25.3 7.3 %collective-permute-start.1 = (bf16[64,128]{1,0:T(8,128)(2,1)}, bf16[64,128]{1,0:T(8,128)(2,1)S(1)}, u32[]{:S(2)}, u32[]{:S(2)}) collective-permute-start(bf16[64,128]{1,0:T(8,128)(2,1)} %get-tuple-element.23), channel_id=1, source_target_pairs={{0,2},{1,3},{2,0},{3,1},{4,6},{5,7},{6,4},{7,5},{8,10},{9,11},{10,... | collective-permute-start | bytes 49160 | tf_op jit(solution)/shard_map/ppermute | solution.py:518
  27.4 5.7 %collective-permute-start.2 = (bf16[64,128]{1,0:T(8,128)(2,1)}, bf16[64,128]{1,0:T(8,128)(2,1)S(1)}, u32[]{:S(2)}, u32[]{:S(2)}) collective-permute-start(bf16[64,128]{1,0:T(8,128)(2,1)} %get-tuple-element.24), channel_id=1, source_target_pairs={{0,3},{1,2},{2,1},{3,0},{4,7},{5,6},{6,5},{7,4},{8,11},{9,10},{10,... | collective-permute-start | bytes 49160 | tf_op jit(solution)/shard_map/ppermute | solution.py:518
  30.4 3.7 %collective-permute-start.10 = (bf16[2,2048]{1,0:T(2,128)(2,1)S(1)}, bf16[2,2048]{1,0:T(2,128)(2,1)S(1)}, u32[]{:S(2)}, u32[]{:S(2)}) collective-permute-start(bf16[2,2048]{1,0:T(2,128)(2,1)S(1)} %attend_moved.1), channel_id=1, source_target_pairs={{0,12},{4,8},{8,4},{12,0},{1,13},{5,9},{9,5},{13,1},{2,14},{6,10},... | collective-permute-start | bytes 24584 | tf_op jit(solution)/shard_map/ppermute | solution.py:518
  30.5 3.6 %collective-permute-start.8 = (bf16[2,2048]{1,0:T(2,128)(2,1)S(1)}, bf16[2,2048]{1,0:T(2,128)(2,1)S(1)}, u32[]{:S(2)}, u32[]{:S(2)}) collective-permute-start(bf16[2,2048]{1,0:T(2,128)(2,1)S(1)} %attend_moved.1), channel_id=1, source_target_pairs={{0,4},{4,0},{8,12},{12,8},{1,5},{5,1},{9,13},{13,9},{2,6},{6,2},{1... | collective-permute-start | bytes 24584 | tf_op jit(solution)/shard_map/ppermute | solution.py:518
  31.1 3.7 %collective-permute-start.9 = (bf16[2,2048]{1,0:T(2,128)(2,1)S(1)}, bf16[2,2048]{1,0:T(2,128)(2,1)S(1)}, u32[]{:S(2)}, u32[]{:S(2)}) collective-permute-start(bf16[2,2048]{1,0:T(2,128)(2,1)S(1)} %attend_moved.1), channel_id=1, source_target_pairs={{0,8},{4,12},{8,0},{12,4},{1,9},{5,13},{9,1},{13,5},{2,10},{6,14},... | collective-permute-start | bytes 24584 | tf_op jit(solution)/shard_map/ppermute | solution.py:518
  33.2 0.7 %copy-start.4 = (bf16[64,128]{1,0:T(8,128)(2,1)S(1)}, bf16[64,128]{1,0:T(8,128)(2,1)}, u32[]{:S(2)}) copy-start(bf16[64,128]{1,0:T(8,128)(2,1)} %get-tuple-element.21.rest_0_) | copy-start | bytes 49156

commit v6 on v5

--- a/solution.py
+++ b/solution.py
@@ -14,7 +14,7 @@
 F32 = jnp.float32
 BF16 = jnp.bfloat16
 MIB = 1024 * 1024
-CHUNK = 256
+CHUNK = 512
 
 VMEM = pl.BlockSpec(memory_space=pltpu.VMEM)
 SMEM = pl.BlockSpec(memory_space=pltpu.SMEM)
@@ -155,72 +155,91 @@
     return outs[:ranks], outs[ranks]
 
 
-def resident_kernel(ranks, heads, len_hbm, q_hbm, k_hbm, v_hbm, *rest):
+def resident_kernel(ranks, len_hbm, q_hbm, k_hbm, v_hbm, *rest):
     outs = rest[:ranks]
-    len_ref, q_ref, q_all, k_buf, v_buf, o_all, s_all, in_sems, sems = rest[ranks:]
+    len_ref, q_ref, k_buf, v_buf, o_all, s_all, in_sems, sems = rest[ranks:]
+    residents, positions, width = k_buf.shape
     len_copy = pltpu.make_async_copy(len_hbm, len_ref, in_sems.at[0])
+    q_copy = pltpu.make_async_copy(q_hbm, q_ref, in_sems.at[1])
+    k_copies = [
+        pltpu.make_async_copy(k_hbm.at[r], k_buf.at[r], sems.at[0, r]) for r in range(residents)
+    ]
+    v_copies = [
+        pltpu.make_async_copy(v_hbm.at[r], v_buf.at[r], sems.at[1, r]) for r in range(residents)
+    ]
     len_copy.start()
-    q_copy = pltpu.make_async_copy(q_hbm, q_ref, in_sems.at[1])
     q_copy.start()
-    residents, positions, width = k_buf.shape
-    copies = []
-    for r in range(residents):
-        copies.append(
-            (
-                pltpu.make_async_copy(k_hbm.at[r], k_buf.at[r], sems.at[0, r]),
-                pltpu.make_async_copy(v_hbm.at[r], v_buf.at[r], sems.at[1, r]),
-            )
-        )
-    for pair in copies:
-        for copy in pair:
-            copy.start()
+    for r in range(residents + 1):
+        if r < residents:
+            k_copies[r].start()
+        if r > 0:
+            v_copies[r - 1].start()
+    heads = q_ref.shape[1]
     kv_heads = width // 128
     group = heads // kv_heads
     pair_rows = 2 * group
     heads_mine = heads // ranks
     rank = lax.axis_index("tp")
     top_half = iota((pair_rows, 128), 0) < group
+    pairs = [slice(p * pair_rows, (p + 1) * pair_rows) for p in range(kv_heads // 2)]
+    position = rank * positions + iota((heads, positions), 1)
     scale = F32(1.0) / jnp.sqrt(F32(128.0))
-    q_copy.wait()
-    q_lines = q_ref[...].astype(F32)
-    for r in range(residents):
-        for h in range(heads):
-            q_all[r, h : h + 1, :] = q_lines[r : r + 1, h * 128 : (h + 1) * 128]
-    len_copy.wait()
-    for r in range(residents):
-        valid = rank * positions + iota((pair_rows, positions), 1) < len_ref[0, r]
-        copies[r][0].wait()
-        weights, peaks, totals = [], [], []
-        for p in range(kv_heads // 2):
-            q = q_all[r, p * pair_rows : (p + 1) * pair_rows, :]
+    diagonal = iota((heads, 128), 0) % heads_mine == iota((heads, 128), 1)
+
+    def scores_of(r):
+        parts = []
+        for p, rows in enumerate(pairs):
+            q = q_ref[r, rows, :]
             zero = jnp.zeros_like(q)
             lhs = jnp.concatenate(
                 [jnp.where(top_half, q, zero), jnp.where(top_half, zero, q)], axis=1
-            ).astype(BF16)
-            scores = lax.dot_general(
-                lhs,
-                k_buf[r, :, p * 256 : (p + 1) * 256],
-                (((1,), (1,)), ((), ())),
-                preferred_element_type=F32,
             )
-            scores = jnp.where(valid, scores * scale, ABSENT)
-            peak = jnp.max(scores, axis=1, keepdims=True).astype(BF16).astype(F32)
-            weight = jnp.where(valid, jnp.exp(scores - peak), 0.0)
-            peaks.append(peak)
-            totals.append(jnp.sum(weight, axis=1, keepdims=True))
-            weights.append(weight.astype(BF16))
-        high, low = split_bf16(jnp.concatenate(totals, axis=0))
-        s_all[r, 0] = column_to_row(jnp.concatenate(peaks, axis=0), heads_mine)
-        s_all[r, 1] = column_to_row(high.astype(F32), heads_mine)
-        s_all[r, 2] = column_to_row(low.astype(F32), heads_mine)
-        copies[r][1].wait()
-        for p in range(kv_heads // 2):
+            parts.append(
+                lax.dot_general(
+                    lhs,
+                    k_buf[r, :, p * 256 : (p + 1) * 256],
+                    (((1,), (1,)), ((), ())),
+                    preferred_element_type=F32,
+                )
+            )
+        return jnp.concatenate(parts, axis=0)
+
+    def to_rows(column):
+        spread = jnp.where(diagonal, column, 0.0)
+        return jnp.sum(spread.reshape(ranks, heads_mine, 128), axis=1)
+
+    def weights_of(r, scores):
+        valid = position < len_ref[0, r]
+        scores = jnp.where(valid, scores * scale, ABSENT)
+        peak = jnp.max(scores, axis=1, keepdims=True).astype(BF16).astype(F32)
+        weights = jnp.where(valid, jnp.exp(scores - peak), 0.0)
+        total = to_rows(jnp.sum(weights, axis=1, keepdims=True))
+        high, low = split_bf16(total)
+        s_all[r, 0] = to_rows(peak)
+        s_all[r, 1] = high.astype(F32)
+        s_all[r, 2] = low.astype(F32)
+        return weights.astype(BF16)
+
+    def add_values(r, weights):
+        for p, rows in enumerate(pairs):
             both = jnp.dot(
-                weights[p], v_buf[r, :, p * 256 : (p + 1) * 256], preferred_element_type=F32
+                weights[rows], v_buf[r, :, p * 256 : (p + 1) * 256], preferred_element_type=F32
             )
-            o_all[r, p * pair_rows : (p + 1) * pair_rows, :] = jnp.where(
-                top_half, both[:, :128], both[:, 128:]
-            )
+            o_all[r, rows, :] = jnp.where(top_half, both[:, :128], both[:, 128:])
+
+    len_copy.wait()
+    q_copy.wait()
+    k_copies[0].wait()
+    scores = scores_of(0)
+    for r in range(residents):
+        following = None
+        if r + 1 < residents:
+            k_copies[r + 1].wait()
+            following = scores_of(r + 1)
+        weights = weights_of(r, scores)
+        v_copies[r].wait()
+        add_values(r, weights)
+        scores = following
     filled = residents * (heads_mine + 3)
     for j in range(ranks):
         target = rank ^ j
@@ -232,20 +251,19 @@
         outs[j][...] = jnp.concatenate(parts, axis=0).astype(BF16)
 
 
-def attend_resident(lengths, query, k_cache, v_cache, ranks):
+def attend_resident(lengths, queries, k_cache, v_cache, ranks):
     residents, positions, width = k_cache.shape
-    heads = query.shape[1] // 128
+    heads = queries.shape[1]
     heads_mine = heads // ranks
     rows = -(-(residents * (heads_mine + 3)) // 16) * 16
     return pl.pallas_call(
-        functools.partial(resident_kernel, ranks, heads),
+        functools.partial(resident_kernel, ranks),
         in_specs=[HBM] * 4,
         out_specs=[VMEM] * ranks,
         out_shape=[jax.ShapeDtypeStruct((rows, 128), BF16)] * ranks,
         scratch_shapes=[
             pltpu.SMEM(lengths.shape, jnp.int32),
-            pltpu.VMEM(query.shape, BF16),
-            pltpu.VMEM((residents, heads, 128), F32),
+            pltpu.VMEM(queries.shape, BF16),
             pltpu.VMEM((residents, positions, width), BF16),
             pltpu.VMEM((residents, positions, width), BF16),
             pltpu.VMEM((residents, heads, 128), F32),
@@ -260,7 +278,7 @@
             transcendentals=residents * heads * positions,
         ),
         name="attend_resident",
-    )(lengths, query, k_cache, v_cache)
+    )(lengths, queries, k_cache, v_cache)
 
 
 def block_of(blocks, b):
@@ -352,7 +370,7 @@
 
 def moved_kernel(ranks, features, q_ref, own_ref, limit_ref, cos_ref, sin_ref, *rest):
     pieces = rest[:ranks]
-    _, out_ref, line_ref = rest[ranks:]
+    out_ref, line_ref = rest[ranks:]
     requests = out_ref.shape[0]
     tokens = cos_ref.shape[0]
     piece = pieces[0].shape[1] // 2
@@ -416,18 +434,18 @@
     out_ref[...] = line_ref[...].astype(BF16)
 
 
-def attend_moved(prepared, pieces, after, requests, features):
+def attend_moved(prepared, pieces, requests, features):
     rows = prepared[0].shape[0]
     width = rows // requests * 128
     return pl.pallas_call(
         functools.partial(moved_kernel, len(pieces), features),
-        in_specs=[VMEM] * (len(prepared) + len(pieces) + 1),
+        in_specs=[VMEM] * (len(prepared) + len(pieces)),
         out_specs=VMEM,
         out_shape=jax.ShapeDtypeStruct((requests, width), BF16),
         scratch_shapes=[pltpu.VMEM((requests, width), F32)],
         compiler_params=pltpu.CompilerParams(vmem_limit_bytes=16 * MIB),
         name="attend_moved",
-    )(*prepared, *pieces, after)
+    )(*prepared, *pieces)
 
 
 def combine_kernel(ranks, residents, kv_mine, ask_ref, *rest):
@@ -568,9 +586,9 @@
     )
     pieces = [pieces[0]] + [swapped(pieces[j], "tp", j, ranks) for j in reversed(range(1, ranks))]
     asks = gather(ask, "inst", insts)
-    payloads = attend_resident(lengths, query[0], k_cache[0], v_cache[0], ranks)
+    queries = query[0].reshape(query.shape[1], heads, head_size)
+    payloads = attend_resident(lengths, queries, k_cache[0], v_cache[0], ranks)
     payloads = [payloads[0]] + [swapped(payloads[j], "tp", j, ranks) for j in range(1, ranks)]
-    kept = combine_resident(ask, payloads, residents, heads_mine, kv_mine)
     cos, sin = rotation(slots, requests, head_size)
     *prepared, places = prepare(
         mig_dest.T,
@@ -583,7 +601,9 @@
         heads_mine,
         kv_mine,
     )
-    moved = attend_moved(prepared, pieces, payloads[1], requests, feats * ranks)
+    prepared[0], payloads[0] = lax.optimization_barrier((prepared[0], payloads[0]))
+    moved = attend_moved(prepared, pieces, requests, feats * ranks)
+    kept = combine_resident(ask, payloads, residents, heads_mine, kv_mine)
     moved = [swapped(moved, "inst", b, insts) for b in range(1, insts)]
     return finish(kept, places, moved, requests)[None]
 

time: 35.7 us -> 33.9 us (0.950)
  waiting for transfers between devices: 3.96 us -> 2.12 us
  local copies, waits for them, and re-layouts: 0.75 us -> 2.3 us
  Pallas kernels: 15.1 us -> 14.3 us
  starting transfers between devices: 14.6 us -> 13.9 us
    ppermute x11, waiting for transfers between devices: 3.96 us -> 2.12 us  [swapped(): return lax.ppermute(x, axis, [(i, i ^ j) for i in range(n)])]
    unnamed x16 -> x17, local copies, waits for them, and re-layouts: 0.75 us -> 2.3 us
    pallas_call x1, Pallas kernels: 8.82 us -> 7.94 us  [attend_resident(): pl.pallas_call(functools.partial(resident_kernel, ranks), in_specs=[HBM]...]
    ppermute x11, starting transfers between devices: 14.6 us -> 13.9 us  [swapped(): return lax.ppermute(x, axis, [(i, i ^ j) for i in range(n)])]
  transfers between devices with their start and end apart: 11 -> 11, of which waited for: 3 -> 1; matrix products, arithmetic and copies ran while one was open for 2% -> 7% of each run, Pallas kernels for 29% -> 28%
where the time goes in v6:
time: 33.9 us; the launch traced here: 33.6 us
  Pallas kernels  14.3 us (42%)
  starting transfers between devices  13.9 us (41%)
  local copies, waits for them, and re-layouts  2.3 us (7%)
  waiting for transfers between devices  2.12 us (6%)
  other arithmetic  0.8 us (2%)
    ppermute x11, starting transfers between devices, swapped(): return lax.ppermute(x, axis, [(i, i ^ j) for i in range(n)])  13.9 us
    pallas_call x1, Pallas kernels, attend_resident(): pl.pallas_call(functools.partial(resident_kernel, ranks), in_specs=[HBM]...  7.94 us
    pallas_call x1, Pallas kernels, project(): pl.pallas_call(functools.partial(project_kernel, ranks, group), in_specs=...  4.11 us
    unnamed x17, local copies, waits for them, and re-layouts  2.3 us
    ppermute x11, waiting for transfers between devices, swapped(): return lax.ppermute(x, axis, [(i, i ^ j) for i in range(n)])  2.12 us
    another operation x1, other arithmetic, gather(): held = jnp.stack([held, one]) if step == 0 else jnp.concatenate([held, one])  0.8 us
    pallas_call x1, Pallas kernels, prepare(): pl.pallas_call(functools.partial(prepare_kernel, insts, len(asks), reside...  0.79 us
  transfers between devices with their start and end apart: 11, of which 1 were waited for; matrix products, arithmetic and copies ran while one was open for 7% of the time, Pallas kernels for 28%

profile of v6, /device:TPU:0, one launch (start us, length us, event | category | flops | bytes accessed | tf_op | source)
XLA Modules:
  0.0 33.6 jit_solution(7486219934871278638)
XLA Ops:
  0.0 4.1 %project.1 = (bf16[136,512]{1,0:T(8,128)(2,1)}, bf16[136,512]{1,0:T(8,128)(2,1)}, bf16[136,512]{1,0:T(8,128)(2,1)}, bf16[136,512]{1,0:T(8,128)(2,1)}, bf16[5,2560]{1,0:T(8,128)(2,1)}) custom-call(bf16[1280]{0:T(1024)(128)(2,1)} %gain_hbm.1, bf16[64,2,1280]{2,1,0:T(2,128)(2,1)} %bitcast.26, bf16[1280,2048]{1,0:T(8,128)(2,1)} %w_hbm.1, ...), custom_call_target="tpu_custom_call" | custom-call | flops 671088640 | bytes 5242880 | tf_op jit(solution)/shard_map/project/pallas_call | solution.py:133
  4.1 0.5 %collective-permute-start = (bf16[5,2560]{1,0:T(8,128)(2,1)}, bf16[5,2560]{1,0:T(8,128)(2,1)S(1)}, u32[]{:S(2)}, u32[]{:S(2)}) collective-permute-start(bf16[5,2560]{1,0:T(8,128)(2,1)} %get-tuple-element.22.ask_ref), channel_id=1, source_target_pairs={{0,4},{4,0},{8,12},{12,8},{1,5},{5,1},{9,13},{13,9},{2,6},{6,2},{1... | collective-permute-start | bytes 76808 | tf_op jit(solution)/shard_map/ppermute | solution.py:536
  4.6 4.7 %collective-permute-start.5 = (bf16[136,512]{1,0:T(8,128)(2,1)}, bf16[136,512]{1,0:T(8,128)(2,1)S(1)}, u32[]{:S(2)}, u32[]{:S(2)}) collective-permute-start(bf16[136,512]{1,0:T(8,128)(2,1)} %get-tuple-element.36), channel_id=1, source_target_pairs={{0,3},{1,2},{2,1},{3,0},{4,7},{5,6},{6,5},{7,4},{8,11},{9,10},{10,... | collective-permute-start | bytes 417800 | tf_op jit(solution)/shard_map/ppermute | solution.py:536
  9.3 0.0 collective-permute-start.6
  9.3 0.7 %collective-permute-start.7 = (bf16[136,512]{1,0:T(8,128)(2,1)}, bf16[136,512]{1,0:T(8,128)(2,1)S(1)}, u32[]{:S(2)}, u32[]{:S(2)}) collective-permute-start(bf16[136,512]{1,0:T(8,128)(2,1)} %get-tuple-element.38), channel_id=1, source_target_pairs={{0,1},{1,0},{2,3},{3,2},{4,5},{5,4},{6,7},{7,6},{8,9},{9,8},{10,11... | collective-permute-start | bytes 417800 | tf_op jit(solution)/shard_map/ppermute | solution.py:536
  10.0 0.0 collective-permute-done.rest_0_
  10.0 0.8 %pad_maximum_fusion = bf16[2,5,2560]{2,1,0:T(8,128)(2,1)S(1)} fusion(bf16[1,5,2560]{2,1,0:T(8,128)(2,1)S(1)} %bitcast.16, bf16[1,5,2560]{2,1,0:T(8,128)(2,1)} %bitcast.17), kind=kLoop, calls=%fused_computation.1 | loop fusion | flops 25600 | bytes 102400 | tf_op jit(solution)/shard_map/stack | solution.py:545
  10.8 1.7 %collective-permute-start.1 = (bf16[2,5,2560]{2,1,0:T(8,128)(2,1)S(1)}, bf16[2,5,2560]{2,1,0:T(8,128)(2,1)S(1)}, u32[]{:S(2)}, u32[]{:S(2)}) collective-permute-start(bf16[2,5,2560]{2,1,0:T(8,128)(2,1)S(1)} %pad_maximum_fusion), channel_id=1, source_target_pairs={{0,8},{4,12},{8,0},{12,4},{1,9},{5,13},{9,1},{13,5},{2,10},{6,14},... | collective-permute-start | bytes 153608 | tf_op jit(solution)/shard_map/ppermute | solution.py:536
  12.5 1.6 %copy.16 = bf16[1,5,64,128]{3,2,1,0:T(8,128)(2,1)} copy(bf16[1,5,64,128]{3,1,2,0:T(8,128)(2,1)} %bitcast.24) | data formatting | bytes 163840
  14.0 0.0 copy-start.2
  14.0 0.0 copy-start.3
  14.0 0.0 copy-start.5
  14.0 0.0 copy-start.6
  14.0 0.0 copy-start.7
  14.0 0.0 copy-start.1
  14.0 0.0 copy-start
  14.1 7.9 %attend_resident.1 = (bf16[64,128]{1,0:T(8,128)(2,1)}, bf16[64,128]{1,0:T(8,128)(2,1)}, bf16[64,128]{1,0:T(8,128)(2,1)}, bf16[64,128]{1,0:T(8,128)(2,1)}) custom-call(s32[1,3]{1,0:T(1,128)} %len_hbm.1, bf16[5,64,128]{2,1,0:T(8,128)(2,1)} %bitcast.25, bf16[3,1024,1024]{2,1,0:T(8,128)(2,1)} %bitcast.21, bf16[3,1024,1024]{2,1,0:T(8,128)(2,1)} %bitcast.22), custom_call_target="tpu_custom_call" | custom-call | flops 100663296 | bytes 12582912 | tf_op jit(solution)/shard_map/attend_resident/pallas_call | solution.py:259
  22.0 1.3 %collective-permute-start.2 = (bf16[64,128]{1,0:T(8,128)(2,1)}, bf16[64,128]{1,0:T(8,128)(2,1)S(1)}, u32[]{:S(2)}, u32[]{:S(2)}) collective-permute-start(bf16[64,128]{1,0:T(8,128)(2,1)} %get-tuple-element.26), channel_id=1, source_target_pairs={{0,1},{1,0},{2,3},{3,2},{4,5},{5,4},{6,7},{7,6},{8,9},{9,8},{10,11... | collective-permute-start | bytes 49160 | tf_op jit(solution)/shard_map/ppermute | solution.py:536
  23.3 0.0 collective-permute-done.1.rest_1_
  23.3 2.9 %collective-permute-start.3 = (bf16[64,128]{1,0:T(8,128)(2,1)}, bf16[64,128]{1,0:T(8,128)(2,1)S(1)}, u32[]{:S(2)}, u32[]{:S(2)}) collective-permute-start(bf16[64,128]{1,0:T(8,128)(2,1)} %get-tuple-element.27), channel_id=1, source_target_pairs={{0,2},{1,3},{2,0},{3,1},{4,6},{5,7},{6,4},{7,5},{8,10},{9,11},{10,... | collective-permute-start | bytes 49160 | tf_op jit(solution)/shard_map/ppermute | solution.py:536
  26.2 0.0 collective-permute-done.5.rest_1_
  26.2 0.2 collective-permute-start.4
  26.5 0.0 copy-done.2
  26.5 0.0 copy-done.3
  26.5 0.0 copy-done.5
  26.5 0.0 copy-done.6
  26.5 0.0 copy-done.7
  26.5 0.8 %prepare.1 = (bf16[32,128]{1,0:T(8,128)(2,1)S(1)}, f32[2,32,128]{2,1,0:T(8,128)S(1)}, s32[32,128]{1,0:T(8,128)S(1)}, f32[128,128]{1,0:T(8,128)S(1)}, f32[128,128]{1,0:T(8,128)S(1)}, /*index=5*/s32[8,128]{1,0:T(8,128)S(1)}) custom-call(s32[2,4]{1,0:T(2,128)S(1)} %bitcast.18, s32[2,4]{1,0:T(2,128)S(1)} %bitcast.19, bf16[1,128]{1,0:T(2,128)(2,1)S(1)} %bitcast.20, ...), custom_call_target="tpu_custom_call" | custom-call | tf_op jit(solution)/shard_map/prepare/pallas_call | solution.py:349
  27.3 0.0 collective-permute-done.6.rest_2_
  27.3 0.0 collective-permute-done.7.rest_3_
  27.3 0.0 copy-done.1
  27.3 0.6 %attend_moved.1 = bf16[2,2048]{1,0:T(2,128)(2,1)S(1)} custom-call(bf16[32,128]{1,0:T(8,128)(2,1)S(1)} %get-tuple-element.30.q_ref, f32[2,32,128]{2,1,0:T(8,128)S(1)} %get-tuple-element.31.own_ref, s32[32,128]{1,0:T(8,128)S(1)} %get-tuple-element.32.limit_ref, f32[128,128]{1,0:T(8,128)S(1)} %get-tuple-element.33.cos_ref, ...), custom_call_target="tpu_custom_call" | custom-call | tf_op jit(solution)/shard_map/attend_moved/pallas_call | solution.py:440
  27.9 0.1 collective-permute-start.8
  28.0 0.5 %collective-permute-start.9 = (bf16[2,2048]{1,0:T(2,128)(2,1)S(1)}, bf16[2,2048]{1,0:T(2,128)(2,1)S(1)}, u32[]{:S(2)}, u32[]{:S(2)}) collective-permute-start(bf16[2,2048]{1,0:T(2,128)(2,1)S(1)} %attend_moved.1), channel_id=1, source_target_pairs={{0,8},{4,12},{8,0},{12,4},{1,9},{5,13},{9,1},{13,5},{2,10},{6,14},... | collective-permute-start | bytes 24584 | tf_op jit(solution)/shard_map/ppermute | solution.py:536
  28.5 0.0 collective-permute-done.2.rest_1_
  28.5 1.4 %collective-permute-start.10 = (bf16[2,2048]{1,0:T(2,128)(2,1)S(1)}, bf16[2,2048]{1,0:T(2,128)(2,1)S(1)}, u32[]{:S(2)}, u32[]{:S(2)}) collective-permute-start(bf16[2,2048]{1,0:T(2,128)(2,1)S(1)} %attend_moved.1), channel_id=1, source_target_pairs={{0,12},{4,8},{8,4},{12,0},{1,13},{5,9},{9,5},{13,1},{2,14},{6,10},... | collective-permute-start | bytes 24584 | tf_op jit(solution)/shard_map/ppermute | solution.py:536
  29.9 0.0 collective-permute-done.3.rest_2_
  29.9 2.1 %collective-permute-done.4.rest_3_ = bf16[64,128]{1,0:T(8,128)(2,1)S(1)} collective-permute-done((bf16[64,128]{1,0:T(8,128)(2,1)}, bf16[64,128]{1,0:T(8,128)(2,1)S(1)}, u32[]{:S(2)}, u32[]{:S(2)}) %collective-permute-start.4) | collective-permute-done | bytes 16416 | tf_op jit(solution)/shard_map/ppermute | solution.py:536
  32.0 0.0 copy-done
  32.0 0.0 copy-start.4
  32.0 0.7 %copy-done.4 = bf16[64,128]{1,0:T(8,128)(2,1)S(1)} copy-done((bf16[64,128]{1,0:T(8,128)(2,1)S(1)}, bf16[64,128]{1,0:T(8,128)(2,1)}, u32[]{:S(2)}) %copy-start.4) | copy-done | bytes 16408
  32.7 0.2 combine_resident.1.kept_ref
  32.9 0.0 collective-permute-done.8.rest_0_
  32.9 0.0 collective-permute-done.9.rest_1_
  32.9 0.0 collective-permute-done.10.rest_2_
  32.9 0.7 %finish.1 = bf16[5,2048]{1,0:T(8,128)(2,1)} custom-call(f32[3,2048]{1,0:T(4,128)S(1)} %combine_resident.1.kept_ref, s32[8,128]{1,0:T(8,128)S(1)} %get-tuple-element.29.place_ref, bf16[2,2048]{1,0:T(2,128)(2,1)S(1)} %collective-permute-done.8.rest_0_, bf16[2,2048]{1,0:T(2,128)(2,1)S(1)} %collective-permute-done.9.rest_1_, ...), custom_call_target="tpu_custom_call" | custom-call | tf_op jit(solution)/shard_map/finish/pallas_call | solution.py:525
Async XLA Ops:
  4.1 5.8 %collective-permute-start = (bf16[5,2560]{1,0:T(8,128)(2,1)}, bf16[5,2560]{1,0:T(8,128)(2,1)S(1)}, u32[]{:S(2)}, u32[]{:S(2)}) collective-permute-start(bf16[5,2560]{1,0:T(8,128)(2,1)} %get-tuple-element.22.ask_ref), channel_id=1, source_target_pairs={{0,4},{4,0},{8,12},{12,8},{1,5},{5,1},{9,13},{13,9},{2,6},{6,2},{1... | collective-permute-start | bytes 76808 | tf_op jit(solution)/shard_map/ppermute | solution.py:536
  4.6 21.6 %collective-permute-start.5 = (bf16[136,512]{1,0:T(8,128)(2,1)}, bf16[136,512]{1,0:T(8,128)(2,1)S(1)}, u32[]{:S(2)}, u32[]{:S(2)}) collective-permute-start(bf16[136,512]{1,0:T(8,128)(2,1)} %get-tuple-element.36), channel_id=1, source_target_pairs={{0,3},{1,2},{2,1},{3,0},{4,7},{5,6},{6,5},{7,4},{8,11},{9,10},{10,... | collective-permute-start | bytes 417800 | tf_op jit(solution)/shard_map/ppermute | solution.py:536
  9.3 18.0 %collective-permute-start.6 = (bf16[136,512]{1,0:T(8,128)(2,1)}, bf16[136,512]{1,0:T(8,128)(2,1)S(1)}, u32[]{:S(2)}, u32[]{:S(2)}) collective-permute-start(bf16[136,512]{1,0:T(8,128)(2,1)} %get-tuple-element.37), channel_id=1, source_target_pairs={{0,2},{1,3},{2,0},{3,1},{4,6},{5,7},{6,4},{7,5},{8,10},{9,11},{10,... | collective-permute-start | bytes 417800 | tf_op jit(solution)/shard_map/ppermute | solution.py:536
  9.3 18.0 %collective-permute-start.7 = (bf16[136,512]{1,0:T(8,128)(2,1)}, bf16[136,512]{1,0:T(8,128)(2,1)S(1)}, u32[]{:S(2)}, u32[]{:S(2)}) collective-permute-start(bf16[136,512]{1,0:T(8,128)(2,1)} %get-tuple-element.38), channel_id=1, source_target_pairs={{0,1},{1,0},{2,3},{3,2},{4,5},{5,4},{6,7},{7,6},{8,9},{9,8},{10,11... | collective-permute-start | bytes 417800 | tf_op jit(solution)/shard_map/ppermute | solution.py:536
  10.8 12.5 %collective-permute-start.1 = (bf16[2,5,2560]{2,1,0:T(8,128)(2,1)S(1)}, bf16[2,5,2560]{2,1,0:T(8,128)(2,1)S(1)}, u32[]{:S(2)}, u32[]{:S(2)}) collective-permute-start(bf16[2,5,2560]{2,1,0:T(8,128)(2,1)S(1)} %pad_maximum_fusion), channel_id=1, source_target_pairs={{0,8},{4,12},{8,0},{12,4},{1,9},{5,13},{9,1},{13,5},{2,10},{6,14},... | collective-permute-start | bytes 153608 | tf_op jit(solution)/shard_map/ppermute | solution.py:536
  14.0 12.5 %copy-start.2 = (f32[128,128]{1,0:T(8,128)S(1)}, f32[128,128]{1,0:T(8,128)}, u32[]{:S(2)}) copy-start(f32[128,128]{1,0:T(8,128)} %constant.4.clone.cos_ref) | copy-start | bytes 196612
  14.0 12.5 %copy-start.3 = (f32[128,128]{1,0:T(8,128)S(1)}, f32[128,128]{1,0:T(8,128)}, u32[]{:S(2)}) copy-start(f32[128,128]{1,0:T(8,128)} %constant.5.clone.sin_ref) | copy-start | bytes 196612
  14.0 12.5 %copy-start.5 = (s32[4,2]{0,1:T(2,128)S(1)}, s32[4,2]{0,1:T(2,128)}, u32[]{:S(2)}) copy-start(s32[4,2]{0,1:T(2,128)} %param.14) | copy-start | bytes 100
  14.0 12.5 %copy-start.6 = (s32[4,2]{0,1:T(2,128)S(1)}, s32[4,2]{0,1:T(2,128)}, u32[]{:S(2)}) copy-start(s32[4,2]{0,1:T(2,128)} %param.15) | copy-start | bytes 100
  14.0 12.5 %copy-start.7 = (bf16[128]{0:T(256)(128)(2,1)S(1)}, bf16[128]{0:T(256)(128)(2,1)}, u32[]{:S(2)}) copy-start(bf16[128]{0:T(256)(128)(2,1)} %param.18) | copy-start | bytes 772
  14.0 13.3 %copy-start.1 = (bf16[136,512]{1,0:T(8,128)(2,1)S(1)}, bf16[136,512]{1,0:T(8,128)(2,1)}, u32[]{:S(2)}) copy-start(bf16[136,512]{1,0:T(8,128)(2,1)} %get-tuple-element.35.rest_0_) | copy-start | bytes 417796
  14.0 17.9 %copy-start = (bf16[5,2560]{1,0:T(8,128)(2,1)S(1)}, bf16[5,2560]{1,0:T(8,128)(2,1)}, u32[]{:S(2)}) copy-start(bf16[5,2560]{1,0:T(8,128)(2,1)} %get-tuple-element.22.ask_ref) | copy-start | bytes 76804
  22.0 6.5 %collective-permute-start.2 = (bf16[64,128]{1,0:T(8,128)(2,1)}, bf16[64,128]{1,0:T(8,128)(2,1)S(1)}, u32[]{:S(2)}, u32[]{:S(2)}) collective-permute-start(bf16[64,128]{1,0:T(8,128)(2,1)} %get-tuple-element.26), channel_id=1, source_target_pairs={{0,1},{1,0},{2,3},{3,2},{4,5},{5,4},{6,7},{7,6},{8,9},{9,8},{10,11... | collective-permute-start | bytes 49160 | tf_op jit(solution)/shard_map/ppermute | solution.py:536
  23.3 6.6 %collective-permute-start.3 = (bf16[64,128]{1,0:T(8,128)(2,1)}, bf16[64,128]{1,0:T(8,128)(2,1)S(1)}, u32[]{:S(2)}, u32[]{:S(2)}) collective-permute-start(bf16[64,128]{1,0:T(8,128)(2,1)} %get-tuple-element.27), channel_id=1, source_target_pairs={{0,2},{1,3},{2,0},{3,1},{4,6},{5,7},{6,4},{7,5},{8,10},{9,11},{10,... | collective-permute-start | bytes 49160 | tf_op jit(solution)/shard_map/ppermute | solution.py:536
  26.2 5.7 %collective-permute-start.4 = (bf16[64,128]{1,0:T(8,128)(2,1)}, bf16[64,128]{1,0:T(8,128)(2,1)S(1)}, u32[]{:S(2)}, u32[]{:S(2)}) collective-permute-start(bf16[64,128]{1,0:T(8,128)(2,1)} %get-tuple-element.28), channel_id=1, source_target_pairs={{0,3},{1,2},{2,1},{3,0},{4,7},{5,6},{6,5},{7,4},{8,11},{9,10},{10,... | collective-permute-start | bytes 49160 | tf_op jit(solution)/shard_map/ppermute | solution.py:536
  27.9 5.0 %collective-permute-start.8 = (bf16[2,2048]{1,0:T(2,128)(2,1)S(1)}, bf16[2,2048]{1,0:T(2,128)(2,1)S(1)}, u32[]{:S(2)}, u32[]{:S(2)}) collective-permute-start(bf16[2,2048]{1,0:T(2,128)(2,1)S(1)} %attend_moved.1), channel_id=1, source_target_pairs={{0,4},{4,0},{8,12},{12,8},{1,5},{5,1},{9,13},{13,9},{2,6},{6,2},{1... | collective-permute-start | bytes 24584 | tf_op jit(solution)/shard_map/ppermute | solution.py:536
  28.0 4.9 %collective-permute-start.9 = (bf16[2,2048]{1,0:T(2,128)(2,1)S(1)}, bf16[2,2048]{1,0:T(2,128)(2,1)S(1)}, u32[]{:S(2)}, u32[]{:S(2)}) collective-permute-start(bf16[2,2048]{1,0:T(2,128)(2,1)S(1)} %attend_moved.1), channel_id=1, source_target_pairs={{0,8},{4,12},{8,0},{12,4},{1,9},{5,13},{9,1},{13,5},{2,10},{6,14},... | collective-permute-start | bytes 24584 | tf_op jit(solution)/shard_map/ppermute | solution.py:536
  28.5 4.4 %collective-permute-start.10 = (bf16[2,2048]{1,0:T(2,128)(2,1)S(1)}, bf16[2,2048]{1,0:T(2,128)(2,1)S(1)}, u32[]{:S(2)}, u32[]{:S(2)}) collective-permute-start(bf16[2,2048]{1,0:T(2,128)(2,1)S(1)} %attend_moved.1), channel_id=1, source_target_pairs={{0,12},{4,8},{8,4},{12,0},{1,13},{5,9},{9,5},{13,1},{2,14},{6,10},... | collective-permute-start | bytes 24584 | tf_op jit(solution)/shard_map/ppermute | solution.py:536
  32.0 0.7 %copy-start.4 = (bf16[64,128]{1,0:T(8,128)(2,1)S(1)}, bf16[64,128]{1,0:T(8,128)(2,1)}, u32[]{:S(2)}) copy-start(bf16[64,128]{1,0:T(8,128)(2,1)} %get-tuple-element.25.rest_0_) | copy-start | bytes 49156

commit v7 on v5

--- a/solution.py
+++ b/solution.py
@@ -14,7 +14,7 @@
 F32 = jnp.float32
 BF16 = jnp.bfloat16
 MIB = 1024 * 1024
-CHUNK = 256
+CHUNK = 512
 
 VMEM = pl.BlockSpec(memory_space=pltpu.VMEM)
 SMEM = pl.BlockSpec(memory_space=pltpu.SMEM)
@@ -144,7 +144,7 @@
             pltpu.SemaphoreType.DMA((5,)),
             pltpu.SemaphoreType.DMA((-(-feats // CHUNK),)),
         ],
-        compiler_params=pltpu.CompilerParams(vmem_limit_bytes=60 * MIB),
+        compiler_params=pltpu.CompilerParams(vmem_limit_bytes=56 * MIB),
         cost_estimate=pl.CostEstimate(
             flops=2 * rows * feats * weight.shape[1],
             bytes_accessed=2 * feats * weight.shape[1],
@@ -155,14 +155,14 @@
     return outs[:ranks], outs[ranks]
 
 
-def resident_kernel(ranks, heads, len_hbm, q_hbm, k_hbm, v_hbm, *rest):
+def resident_kernel(ranks, len_hbm, q_hbm, k_hbm, v_hbm, *rest):
     outs = rest[:ranks]
     len_ref, q_ref, q_all, k_buf, v_buf, o_all, s_all, in_sems, sems = rest[ranks:]
+    residents, positions, width = k_buf.shape
     len_copy = pltpu.make_async_copy(len_hbm, len_ref, in_sems.at[0])
+    q_copy = pltpu.make_async_copy(q_hbm, q_ref, in_sems.at[1])
     len_copy.start()
-    q_copy = pltpu.make_async_copy(q_hbm, q_ref, in_sems.at[1])
     q_copy.start()
-    residents, positions, width = k_buf.shape
     copies = []
     for r in range(residents):
         copies.append(
@@ -174,29 +174,39 @@
     for pair in copies:
         for copy in pair:
             copy.start()
+    heads = q_ref.shape[1] // 128
     kv_heads = width // 128
     group = heads // kv_heads
     pair_rows = 2 * group
     heads_mine = heads // ranks
     rank = lax.axis_index("tp")
     top_half = iota((pair_rows, 128), 0) < group
+    position = iota((pair_rows, positions), 1)
     scale = F32(1.0) / jnp.sqrt(F32(128.0))
+    diagonal = iota((heads, 128), 0) % heads_mine == iota((heads, 128), 1)
+
+    def to_rows(columns):
+        spread = jnp.where(diagonal, jnp.concatenate(columns, axis=0), 0.0)
+        return jnp.sum(spread.reshape(ranks, heads_mine, 128), axis=1)
+
+    len_copy.wait()
     q_copy.wait()
-    q_lines = q_ref[...].astype(F32)
+    for h in range(heads):
+        q_all[h * 8 : h * 8 + residents, :] = q_ref[:residents, h * 128 : (h + 1) * 128].astype(F32)
+    peaks, totals = [], []
     for r in range(residents):
-        for h in range(heads):
-            q_all[r, h : h + 1, :] = q_lines[r : r + 1, h * 128 : (h + 1) * 128]
-    len_copy.wait()
-    for r in range(residents):
-        valid = rank * positions + iota((pair_rows, positions), 1) < len_ref[0, r]
+        q_mine = q_all[pl.ds(r, heads, stride=8), :]
+        peaks.append([])
+        totals.append([])
+        valid = position < len_ref[0, r] - rank * positions
         copies[r][0].wait()
-        weights, peaks, totals = [], [], []
+        weights = []
         for p in range(kv_heads // 2):
-            q = q_all[r, p * pair_rows : (p + 1) * pair_rows, :]
+            q = q_mine[p * pair_rows : (p + 1) * pair_rows].astype(BF16)
             zero = jnp.zeros_like(q)
             lhs = jnp.concatenate(
                 [jnp.where(top_half, q, zero), jnp.where(top_half, zero, q)], axis=1
-            ).astype(BF16)
+            )
             scores = lax.dot_general(
                 lhs,
                 k_buf[r, :, p * 256 : (p + 1) * 256],
@@ -206,13 +216,9 @@
             scores = jnp.where(valid, scores * scale, ABSENT)
             peak = jnp.max(scores, axis=1, keepdims=True).astype(BF16).astype(F32)
             weight = jnp.where(valid, jnp.exp(scores - peak), 0.0)
-            peaks.append(peak)
-            totals.append(jnp.sum(weight, axis=1, keepdims=True))
+            peaks[r].append(peak)
+            totals[r].append(jnp.sum(weight, axis=1, keepdims=True))
             weights.append(weight.astype(BF16))
-        high, low = split_bf16(jnp.concatenate(totals, axis=0))
-        s_all[r, 0] = column_to_row(jnp.concatenate(peaks, axis=0), heads_mine)
-        s_all[r, 1] = column_to_row(high.astype(F32), heads_mine)
-        s_all[r, 2] = column_to_row(low.astype(F32), heads_mine)
         copies[r][1].wait()
         for p in range(kv_heads // 2):
             both = jnp.dot(
@@ -221,6 +227,11 @@
             o_all[r, p * pair_rows : (p + 1) * pair_rows, :] = jnp.where(
                 top_half, both[:, :128], both[:, 128:]
             )
+    for r in range(residents):
+        s_all[r, 0] = to_rows(peaks[r])
+        high, low = split_bf16(to_rows(totals[r]))
+        s_all[r, 1] = high.astype(F32)
+        s_all[r, 2] = low.astype(F32)
     filled = residents * (heads_mine + 3)
     for j in range(ranks):
         target = rank ^ j
@@ -238,14 +249,14 @@
     heads_mine = heads // ranks
     rows = -(-(residents * (heads_mine + 3)) // 16) * 16
     return pl.pallas_call(
-        functools.partial(resident_kernel, ranks, heads),
+        functools.partial(resident_kernel, ranks),
         in_specs=[HBM] * 4,
         out_specs=[VMEM] * ranks,
         out_shape=[jax.ShapeDtypeStruct((rows, 128), BF16)] * ranks,
         scratch_shapes=[
             pltpu.SMEM(lengths.shape, jnp.int32),
             pltpu.VMEM(query.shape, BF16),
-            pltpu.VMEM((residents, heads, 128), F32),
+            pltpu.VMEM((heads * 8, 128), F32),
             pltpu.VMEM((residents, positions, width), BF16),
             pltpu.VMEM((residents, positions, width), BF16),
             pltpu.VMEM((residents, heads, 128), F32),
@@ -253,7 +264,7 @@
             pltpu.SemaphoreType.DMA((2,)),
             pltpu.SemaphoreType.DMA((2, residents)),
         ],
-        compiler_params=pltpu.CompilerParams(vmem_limit_bytes=60 * MIB),
+        compiler_params=pltpu.CompilerParams(vmem_limit_bytes=56 * MIB),
         cost_estimate=pl.CostEstimate(
             flops=4 * residents * heads * positions * 128,
             bytes_accessed=4 * residents * positions * width,
@@ -263,22 +274,35 @@
     )(lengths, query, k_cache, v_cache)
 
 
-def block_of(blocks, b):
-    step = b.bit_length() - 1
-    array = blocks[step]
-    return array if step == 0 else array.at[b - (1 << step)]
-
-
-def prepare_kernel(insts, steps, residents, kv_mine, dest_ref, count_ref, gain_ref, cos_ref, sin_ref, *rest):
-    asks, rest = rest[:steps], rest[steps:]
+def expand(own, rows):
+    which = iota((rows, 128), 0) // (rows // own.shape[0])
+    out = jnp.broadcast_to(own[0:1], (rows, 128))
+    for h in range(1, own.shape[0]):
+        out = jnp.where(which == h, own[h : h + 1], out)
+    return out
+
+
+def heads_of(line, heads_mine, kv_mine):
+    per = heads_mine // kv_mine
+    blocks = [line[:, c : c + 128] for c in range(0, line.shape[1], 128)]
+    q = jnp.concatenate(blocks[:heads_mine], axis=0)
+    k = blocks[heads_mine : heads_mine + kv_mine]
+    v = blocks[heads_mine + kv_mine :]
+    return (
+        q,
+        expand(jnp.concatenate(k, axis=0), heads_mine),
+        expand(jnp.concatenate(v, axis=0), heads_mine),
+    )
+
+
+def prepare_kernel(insts, residents, kv_mine, dest_ref, count_ref, gain_ref, cos_ref, sin_ref, *rest):
+    asks, rest = rest[: insts - 1], rest[insts - 1 :]
     q_out, own_out, limit_out, cos_out, sin_out, place_out, line_ref, q_ref, k_ref = rest
     requests = dest_ref.shape[0]
     rows = q_out.shape[0]
     heads_mine = rows // requests
-    per = heads_mine // kv_mine
-    decoded = asks[0].shape[0]
     here = lax.axis_index("inst")
-    ask_row = iota((decoded, line_ref.shape[1]), 0)
+    ask_row = iota(asks[0].shape, 0)
     limit = jnp.zeros((rows, 128), jnp.int32)
     for r in range(requests):
         dest = dest_ref[r, here]
@@ -291,19 +315,15 @@
 
             @pl.when(here ^ b == dest)
             def _():
-                ask = block_of(asks, b)[...].astype(F32)
+                ask = asks[b - 1][...].astype(F32)
                 line_ref[r : r + 1, :] = jnp.sum(
                     jnp.where(ask_row == place, ask, 0.0), axis=0, keepdims=True
                 )
 
-        line = line_ref[r : r + 1, :]
-        for h in range(heads_mine):
-            at = r * heads_mine + h
-            k_at = (heads_mine + h // per) * 128
-            v_at = k_at + kv_mine * 128
-            q_ref[at : at + 1, :] = line[:, h * 128 : (h + 1) * 128]
-            k_ref[at : at + 1, :] = line[:, k_at : k_at + 128]
-            own_out[0, at : at + 1, :] = line[:, v_at : v_at + 128]
+        at = slice(r * heads_mine, (r + 1) * heads_mine)
+        q_ref[at, :], k_ref[at, :], own_out[0, at, :] = heads_of(
+            line_ref[r : r + 1, :], heads_mine, kv_mine
+        )
     scale = F32(1.0) / jnp.sqrt(F32(128.0))
     q = q_ref[...]
     q_out[...] = q.astype(BF16)
@@ -329,7 +349,7 @@
     requests, insts = dest.shape
     rows = requests * heads_mine
     return pl.pallas_call(
-        functools.partial(prepare_kernel, insts, len(asks), residents, kv_mine),
+        functools.partial(prepare_kernel, insts, residents, kv_mine),
         in_specs=[SMEM] * 2 + [VMEM] * (3 + len(asks)),
         out_specs=[VMEM] * 6,
         out_shape=[
@@ -352,7 +372,7 @@
 
 def moved_kernel(ranks, features, q_ref, own_ref, limit_ref, cos_ref, sin_ref, *rest):
     pieces = rest[:ranks]
-    _, out_ref, line_ref = rest[ranks:]
+    out_ref, line_ref = rest[ranks:]
     requests = out_ref.shape[0]
     tokens = cos_ref.shape[0]
     piece = pieces[0].shape[1] // 2
@@ -416,36 +436,33 @@
     out_ref[...] = line_ref[...].astype(BF16)
 
 
-def attend_moved(prepared, pieces, after, requests, features):
+def attend_moved(prepared, pieces, requests, features):
     rows = prepared[0].shape[0]
     width = rows // requests * 128
     return pl.pallas_call(
         functools.partial(moved_kernel, len(pieces), features),
-        in_specs=[VMEM] * (len(prepared) + len(pieces) + 1),
+        in_specs=[VMEM] * (len(prepared) + len(pieces)),
         out_specs=VMEM,
         out_shape=jax.ShapeDtypeStruct((requests, width), BF16),
         scratch_shapes=[pltpu.VMEM((requests, width), F32)],
         compiler_params=pltpu.CompilerParams(vmem_limit_bytes=16 * MIB),
+        cost_estimate=pl.CostEstimate(
+            flops=4 * rows * rows * 128 * 64, bytes_accessed=4 * 1024 * 1024, transcendentals=rows * 128
+        ),
         name="attend_moved",
-    )(*prepared, *pieces, after)
+    )(*prepared, *pieces)
 
 
 def combine_kernel(ranks, residents, kv_mine, ask_ref, *rest):
     payloads = rest[:ranks]
-    out_ref, q_ref, own_ref = rest[ranks:]
-    heads_mine = q_ref.shape[0]
-    per = heads_mine // kv_mine
+    out_ref = rest[ranks]
+    heads_mine = out_ref.shape[1] // 128
     scale = F32(1.0) / jnp.sqrt(F32(128.0))
     at = residents * heads_mine
     ask = ask_ref[...].astype(F32)
     for r in range(residents):
-        for h in range(heads_mine):
-            k_at = (heads_mine + h // per) * 128
-            v_at = k_at + kv_mine * 128
-            q_ref[h : h + 1, :] = ask[r : r + 1, h * 128 : (h + 1) * 128]
-            own_ref[0, h : h + 1, :] = ask[r : r + 1, k_at : k_at + 128]
-            own_ref[1, h : h + 1, :] = ask[r : r + 1, v_at : v_at + 128]
-        own_score = jnp.sum(q_ref[...] * own_ref[0], axis=1, keepdims=True) * scale
+        q, own_k, own_v = heads_of(ask[r : r + 1], heads_mine, kv_mine)
+        own_score = jnp.sum(q * own_k, axis=1, keepdims=True) * scale
         peaks, totals = [], []
         for t in range(ranks):
             stat = payloads[t][at : at + 3 * residents, :].astype(F32)
@@ -458,7 +475,7 @@
             top = jnp.maximum(top, peaks[t])
         own_weight = jnp.exp(own_score - top)
         denom = own_weight
-        numer = own_weight.astype(BF16).astype(F32) * own_ref[1]
+        numer = own_weight.astype(BF16).astype(F32) * own_v
         for t in range(ranks):
             keep = jnp.exp(peaks[t] - top)
             denom = denom + keep * totals[t]
@@ -474,10 +491,6 @@
         in_specs=[VMEM] * (1 + len(payloads)),
         out_specs=VMEM,
         out_shape=jax.ShapeDtypeStruct((residents, heads_mine * 128), F32),
-        scratch_shapes=[
-            pltpu.VMEM((heads_mine, 128), F32),
-            pltpu.VMEM((2, heads_mine, 128), F32),
-        ],
         compiler_params=pltpu.CompilerParams(vmem_limit_bytes=8 * MIB),
         name="combine_resident",
     )(asks, *payloads)
@@ -516,16 +529,6 @@
 
 def swapped(x, axis, j, n):
     return lax.ppermute(x, axis, [(i, i ^ j) for i in range(n)])
-
-
-def gather(x, axis, n):
-    held, blocks = x, []
-    for step in range(n.bit_length() - 1):
-        blocks.append(swapped(held, axis, 1 << step, n))
-        if 2 << step < n:
-            one = blocks[-1]
-            held = jnp.stack([held, one]) if step == 0 else jnp.concatenate([held, one])
-    return blocks
 
 
 def rotation(slots, requests, head_size):
@@ -566,11 +569,15 @@
     pieces, ask = project(
         mig_hidden[0], attn_gain, kv_weight, query[0], new_kv[0], ranks, group, kv_mine
     )
-    pieces = [pieces[0]] + [swapped(pieces[j], "tp", j, ranks) for j in reversed(range(1, ranks))]
-    asks = gather(ask, "inst", insts)
+    last = ranks - 1
+    far = swapped(pieces[last], "tp", last, ranks)
+    asks = [swapped(ask, "inst", b, insts) for b in range(1, insts)]
+    asks[0], *near = lax.optimization_barrier((asks[0], *pieces[1:last]))
+    near = [swapped(near[j - 1], "tp", j, ranks) for j in reversed(range(1, last))]
+    pieces = [pieces[0], far] + near
     payloads = attend_resident(lengths, query[0], k_cache[0], v_cache[0], ranks)
-    payloads = [payloads[0]] + [swapped(payloads[j], "tp", j, ranks) for j in range(1, ranks)]
-    kept = combine_resident(ask, payloads, residents, heads_mine, kv_mine)
+    own_payload = payloads[0]
+    payloads = [swapped(payloads[j], "tp", j, ranks) for j in reversed(range(1, ranks))]
     cos, sin = rotation(slots, requests, head_size)
     *prepared, places = prepare(
         mig_dest.T,
@@ -583,8 +590,10 @@
         heads_mine,
         kv_mine,
     )
-    moved = attend_moved(prepared, pieces, payloads[1], requests, feats * ranks)
-    moved = [swapped(moved, "inst", b, insts) for b in range(1, insts)]
+    prepared[0], own_payload = lax.optimization_barrier((prepared[0], own_payload))
+    moved = attend_moved(prepared, pieces, requests, feats * ranks)
+    kept = combine_resident(ask, [own_payload] + payloads, residents, heads_mine, kv_mine)
+    moved = [swapped(moved, "inst", b, insts) for b in reversed(range(1, insts))][::-1]
     return finish(kept, places, moved, requests)[None]
 
 

time: 35.7 us -> 32.6 us (0.913)
  waiting for transfers between devices: 3.96 us -> 1.61 us
  other arithmetic: 0.8 us -> 0 us
  starting transfers between devices: 14.6 us -> 15 us
    ppermute x11 -> x12, waiting for transfers between devices: 3.96 us -> 1.61 us  [swapped(): return lax.ppermute(x, axis, [(i, i ^ j) for i in range(n)])]
    another operation x1 -> x0, other arithmetic: 0.8 us -> none  [gather(): held = jnp.stack([held, one]) if step == 0 else jnp.concatenate([held, one])]
    ppermute x11 -> x12, starting transfers between devices: 14.6 us -> 15 us  [swapped(): return lax.ppermute(x, axis, [(i, i ^ j) for i in range(n)])]
  transfers between devices with their start and end apart: 11 -> 12, of which waited for: 3 -> 2; matrix products, arithmetic and copies ran while one was open for 2% -> 0% of each run, Pallas kernels for 29% -> 31%
where the time goes in v7:
time: 32.6 us; the launch traced here: 32.4 us
  starting transfers between devices  15 us (46%)
  Pallas kernels  14.9 us (46%)
  waiting for transfers between devices  1.61 us (5%)
  local copies, waits for them, and re-layouts  0.74 us (2%)
    ppermute x12, starting transfers between devices, swapped(): return lax.ppermute(x, axis, [(i, i ^ j) for i in range(n)])  15 us
    pallas_call x1, Pallas kernels, attend_resident(): pl.pallas_call(functools.partial(resident_kernel, ranks), in_specs=[HBM]...  8.5 us
    pallas_call x1, Pallas kernels, project(): pl.pallas_call(functools.partial(project_kernel, ranks, group), in_specs=...  4.12 us
    ppermute x12, waiting for transfers between devices, swapped(): return lax.ppermute(x, axis, [(i, i ^ j) for i in range(n)])  1.61 us
    pallas_call x1, Pallas kernels, prepare(): pl.pallas_call(functools.partial(prepare_kernel, insts, residents, kv_min...  0.78 us
    unnamed x16, local copies, waits for them, and re-layouts  0.74 us
    pallas_call x1, Pallas kernels, finish(): pl.pallas_call(finish_kernel, in_specs=[VMEM] * (2 + len(moved)), out_spe...  0.67 us
  transfers between devices with their start and end apart: 12, of which 2 were waited for; matrix products, arithmetic and copies ran while one was open for 0% of the time, Pallas kernels for 31%

profile of v7, /device:TPU:0, one launch (start us, length us, event | category | flops | bytes accessed | tf_op | source)
XLA Modules:
  0.0 32.4 jit_solution(7280745887088325765)
XLA Ops:
  0.0 4.1 %project.1 = (bf16[136,512]{1,0:T(8,128)(2,1)}, bf16[136,512]{1,0:T(8,128)(2,1)}, bf16[136,512]{1,0:T(8,128)(2,1)}, bf16[136,512]{1,0:T(8,128)(2,1)}, bf16[5,2560]{1,0:T(8,128)(2,1)}) custom-call(bf16[1280]{0:T(1024)(128)(2,1)} %gain_hbm.1, bf16[64,2,1280]{2,1,0:T(2,128)(2,1)} %bitcast.16, bf16[1280,2048]{1,0:T(8,128)(2,1)} %w_hbm.1, ...), custom_call_target="tpu_custom_call" | custom-call | flops 671088640 | bytes 5242880 | tf_op jit(solution)/shard_map/project/pallas_call | solution.py:133
  4.1 0.5 %collective-permute-start = (bf16[5,2560]{1,0:T(8,128)(2,1)}, bf16[5,2560]{1,0:T(8,128)(2,1)S(1)}, u32[]{:S(2)}, u32[]{:S(2)}) collective-permute-start(bf16[5,2560]{1,0:T(8,128)(2,1)} %get-tuple-element.25.ask_ref), channel_id=1, source_target_pairs={{0,4},{4,0},{8,12},{12,8},{1,5},{5,1},{9,13},{13,9},{2,6},{6,2},{1... | collective-permute-start | bytes 76808 | tf_op jit(solution)/shard_map/ppermute | solution.py:531
  4.6 4.7 %collective-permute-start.6 = (bf16[136,512]{1,0:T(8,128)(2,1)}, bf16[136,512]{1,0:T(8,128)(2,1)S(1)}, u32[]{:S(2)}, u32[]{:S(2)}) collective-permute-start(bf16[136,512]{1,0:T(8,128)(2,1)} %get-tuple-element.42), channel_id=1, source_target_pairs={{0,3},{1,2},{2,1},{3,0},{4,7},{5,6},{6,5},{7,4},{8,11},{9,10},{10,... | collective-permute-start | bytes 417800 | tf_op jit(solution)/shard_map/ppermute | solution.py:531
  9.3 0.0 collective-permute-done.rest_0_
  9.3 0.3 %collective-permute-start.7 = (bf16[136,512]{1,0:T(8,128)(2,1)}, bf16[136,512]{1,0:T(8,128)(2,1)S(1)}, u32[]{:S(2)}, u32[]{:S(2)}) collective-permute-start(bf16[136,512]{1,0:T(8,128)(2,1)} %get-tuple-element.43), channel_id=1, source_target_pairs={{0,2},{1,3},{2,0},{3,1},{4,6},{5,7},{6,4},{7,5},{8,10},{9,11},{10,... | collective-permute-start | bytes 417800 | tf_op jit(solution)/shard_map/ppermute | solution.py:531
  9.7 1.6 %collective-permute-start.8 = (bf16[136,512]{1,0:T(8,128)(2,1)}, bf16[136,512]{1,0:T(8,128)(2,1)S(1)}, u32[]{:S(2)}, u32[]{:S(2)}) collective-permute-start(bf16[136,512]{1,0:T(8,128)(2,1)} %get-tuple-element.44), channel_id=1, source_target_pairs={{0,1},{1,0},{2,3},{3,2},{4,5},{5,4},{6,7},{7,6},{8,9},{9,8},{10,11... | collective-permute-start | bytes 417800 | tf_op jit(solution)/shard_map/ppermute | solution.py:531
  11.2 1.5 %collective-permute-start.1 = (bf16[5,2560]{1,0:T(8,128)(2,1)}, bf16[5,2560]{1,0:T(8,128)(2,1)S(1)}, u32[]{:S(2)}, u32[]{:S(2)}) collective-permute-start(bf16[5,2560]{1,0:T(8,128)(2,1)} %get-tuple-element.25.ask_ref), channel_id=1, source_target_pairs={{0,8},{4,12},{8,0},{12,4},{1,9},{5,13},{9,1},{13,5},{2,10},{6,14},... | collective-permute-start | bytes 76808 | tf_op jit(solution)/shard_map/ppermute | solution.py:531
  12.7 0.0 collective-permute-start.2
  12.7 0.0 copy-start.1
  12.7 0.0 copy-start.2
  12.7 0.0 copy-start.5
  12.7 0.0 copy-start.6
  12.8 0.0 copy-start.7
  12.8 0.0 copy-start
  12.8 0.0 copy-start.3
  12.8 8.5 %attend_resident.1 = (bf16[64,128]{1,0:T(8,128)(2,1)}, bf16[64,128]{1,0:T(8,128)(2,1)}, bf16[64,128]{1,0:T(8,128)(2,1)}, bf16[64,128]{1,0:T(8,128)(2,1)}) custom-call(s32[1,3]{1,0:T(1,128)} %len_hbm.1, bf16[5,8192]{1,0:T(8,128)(2,1)} %bitcast.15, bf16[3,1024,1024]{2,1,0:T(8,128)(2,1)} %bitcast.12, bf16[3,1024,1024]{2,1,0:T(8,128)(2,1)} %bitcast.13), custom_call_target="tpu_custom_call" | custom-call | flops 100663296 | bytes 12582912 | tf_op jit(solution)/shard_map/attend_resident/pallas_call | solution.py:251
  21.3 0.0 collective-permute-done.1.rest_1_
  21.3 2.5 %collective-permute-start.3 = (bf16[64,128]{1,0:T(8,128)(2,1)}, bf16[64,128]{1,0:T(8,128)(2,1)S(1)}, u32[]{:S(2)}, u32[]{:S(2)}) collective-permute-start(bf16[64,128]{1,0:T(8,128)(2,1)} %get-tuple-element.32), channel_id=1, source_target_pairs={{0,3},{1,2},{2,1},{3,0},{4,7},{5,6},{6,5},{7,4},{8,11},{9,10},{10,... | collective-permute-start | bytes 49160 | tf_op jit(solution)/shard_map/ppermute | solution.py:531
  23.8 0.0 collective-permute-done.2.rest_2_
  23.8 0.0 collective-permute-start.4
  23.9 0.0 collective-permute-done.6.rest_1_
  23.9 1.9 %collective-permute-start.5 = (bf16[64,128]{1,0:T(8,128)(2,1)}, bf16[64,128]{1,0:T(8,128)(2,1)S(1)}, u32[]{:S(2)}, u32[]{:S(2)}) collective-permute-start(bf16[64,128]{1,0:T(8,128)(2,1)} %get-tuple-element.34), channel_id=1, source_target_pairs={{0,1},{1,0},{2,3},{3,2},{4,5},{5,4},{6,7},{7,6},{8,9},{9,8},{10,11... | collective-permute-start | bytes 49160 | tf_op jit(solution)/shard_map/ppermute | solution.py:531
  25.8 0.0 copy-done.1
  25.8 0.0 copy-done.2
  25.8 0.0 copy-done.5
  25.8 0.0 copy-done.6
  25.8 0.0 copy-done.7
  25.8 0.8 %prepare.1 = (bf16[32,128]{1,0:T(8,128)(2,1)S(1)}, f32[2,32,128]{2,1,0:T(8,128)S(1)}, s32[32,128]{1,0:T(8,128)S(1)}, f32[128,128]{1,0:T(8,128)S(1)}, f32[128,128]{1,0:T(8,128)S(1)}, /*index=5*/s32[8,128]{1,0:T(8,128)S(1)}) custom-call(s32[2,4]{1,0:T(2,128)S(1)} %bitcast.9, s32[2,4]{1,0:T(2,128)S(1)} %bitcast.10, bf16[1,128]{1,0:T(2,128)(2,1)S(1)} %bitcast.11, ...), custom_call_target="tpu_custom_call" | custom-call | tf_op jit(solution)/shard_map/prepare/pallas_call | solution.py:351
  26.6 0.0 collective-permute-done.7.rest_2_
  26.6 0.0 collective-permute-done.8.rest_3_
  26.6 0.0 copy-done
  26.6 0.6 %attend_moved.1 = bf16[2,2048]{1,0:T(2,128)(2,1)S(1)} custom-call(bf16[32,128]{1,0:T(8,128)(2,1)S(1)} %get-tuple-element.36.q_ref, f32[2,32,128]{2,1,0:T(8,128)S(1)} %get-tuple-element.37.own_ref, s32[32,128]{1,0:T(8,128)S(1)} %get-tuple-element.38.limit_ref, f32[128,128]{1,0:T(8,128)S(1)} %get-tuple-element.39.cos_ref, ...), custom_call_target="tpu_custom_call" | custom-call | flops 33554432 | bytes 4194304 | tf_op jit(solution)/shard_map/attend_moved/pallas_call | solution.py:442
  27.3 0.1 collective-permute-start.9
  27.3 1.3 %collective-permute-start.10 = (bf16[2,2048]{1,0:T(2,128)(2,1)S(1)}, bf16[2,2048]{1,0:T(2,128)(2,1)S(1)}, u32[]{:S(2)}, u32[]{:S(2)}) collective-permute-start(bf16[2,2048]{1,0:T(2,128)(2,1)S(1)} %attend_moved.1), channel_id=1, source_target_pairs={{0,8},{4,12},{8,0},{12,4},{1,9},{5,13},{9,1},{13,5},{2,10},{6,14},... | collective-permute-start | bytes 24584 | tf_op jit(solution)/shard_map/ppermute | solution.py:531
  28.6 0.0 collective-permute-done.3.rest_1_
  28.6 0.6 %collective-permute-start.11 = (bf16[2,2048]{1,0:T(2,128)(2,1)S(1)}, bf16[2,2048]{1,0:T(2,128)(2,1)S(1)}, u32[]{:S(2)}, u32[]{:S(2)}) collective-permute-start(bf16[2,2048]{1,0:T(2,128)(2,1)S(1)} %attend_moved.1), channel_id=1, source_target_pairs={{0,12},{4,8},{8,4},{12,0},{1,13},{5,9},{9,5},{13,1},{2,14},{6,10},... | collective-permute-start | bytes 24584 | tf_op jit(solution)/shard_map/ppermute | solution.py:531
  29.2 0.0 collective-permute-done.4.rest_2_
  29.2 0.0 collective-permute-done.5.rest_3_
  29.2 0.0 copy-done.3
  29.2 0.0 copy-start.4
  29.2 0.7 %copy-done.4 = bf16[64,128]{1,0:T(8,128)(2,1)S(1)} copy-done((bf16[64,128]{1,0:T(8,128)(2,1)S(1)}, bf16[64,128]{1,0:T(8,128)(2,1)}, u32[]{:S(2)}) %copy-start.4) | copy-done | bytes 16408
  29.9 0.2 combine_resident.1.kept_ref
  30.1 0.0 collective-permute-done.9.rest_0_
  30.1 0.9 %collective-permute-done.10.rest_1_ = bf16[2,2048]{1,0:T(2,128)(2,1)S(1)} collective-permute-done((bf16[2,2048]{1,0:T(2,128)(2,1)S(1)}, bf16[2,2048]{1,0:T(2,128)(2,1)S(1)}, u32[]{:S(2)}, u32[]{:S(2)}) %collective-permute-start.10) | collective-permute-done | bytes 8224 | tf_op jit(solution)/shard_map/ppermute | solution.py:531
  31.1 0.6 %collective-permute-done.11.rest_2_ = bf16[2,2048]{1,0:T(2,128)(2,1)S(1)} collective-permute-done((bf16[2,2048]{1,0:T(2,128)(2,1)S(1)}, bf16[2,2048]{1,0:T(2,128)(2,1)S(1)}, u32[]{:S(2)}, u32[]{:S(2)}) %collective-permute-start.11) | collective-permute-done | bytes 8224 | tf_op jit(solution)/shard_map/ppermute | solution.py:531
  31.7 0.7 %finish.1 = bf16[5,2048]{1,0:T(8,128)(2,1)} custom-call(f32[3,2048]{1,0:T(4,128)S(1)} %combine_resident.1.kept_ref, s32[8,128]{1,0:T(8,128)S(1)} %get-tuple-element.35.place_ref, bf16[2,2048]{1,0:T(2,128)(2,1)S(1)} %collective-permute-done.9.rest_0_, bf16[2,2048]{1,0:T(2,128)(2,1)S(1)} %collective-permute-done.10.rest_1_, ...), custom_call_target="tpu_custom_call" | custom-call | tf_op jit(solution)/shard_map/finish/pallas_call | solution.py:520
Async XLA Ops:
  4.1 5.2 %collective-permute-start = (bf16[5,2560]{1,0:T(8,128)(2,1)}, bf16[5,2560]{1,0:T(8,128)(2,1)S(1)}, u32[]{:S(2)}, u32[]{:S(2)}) collective-permute-start(bf16[5,2560]{1,0:T(8,128)(2,1)} %get-tuple-element.25.ask_ref), channel_id=1, source_target_pairs={{0,4},{4,0},{8,12},{12,8},{1,5},{5,1},{9,13},{13,9},{2,6},{6,2},{1... | collective-permute-start | bytes 76808 | tf_op jit(solution)/shard_map/ppermute | solution.py:531
  4.6 19.2 %collective-permute-start.6 = (bf16[136,512]{1,0:T(8,128)(2,1)}, bf16[136,512]{1,0:T(8,128)(2,1)S(1)}, u32[]{:S(2)}, u32[]{:S(2)}) collective-permute-start(bf16[136,512]{1,0:T(8,128)(2,1)} %get-tuple-element.42), channel_id=1, source_target_pairs={{0,3},{1,2},{2,1},{3,0},{4,7},{5,6},{6,5},{7,4},{8,11},{9,10},{10,... | collective-permute-start | bytes 417800 | tf_op jit(solution)/shard_map/ppermute | solution.py:531
  9.3 17.3 %collective-permute-start.7 = (bf16[136,512]{1,0:T(8,128)(2,1)}, bf16[136,512]{1,0:T(8,128)(2,1)S(1)}, u32[]{:S(2)}, u32[]{:S(2)}) collective-permute-start(bf16[136,512]{1,0:T(8,128)(2,1)} %get-tuple-element.43), channel_id=1, source_target_pairs={{0,2},{1,3},{2,0},{3,1},{4,6},{5,7},{6,4},{7,5},{8,10},{9,11},{10,... | collective-permute-start | bytes 417800 | tf_op jit(solution)/shard_map/ppermute | solution.py:531
  9.7 16.9 %collective-permute-start.8 = (bf16[136,512]{1,0:T(8,128)(2,1)}, bf16[136,512]{1,0:T(8,128)(2,1)S(1)}, u32[]{:S(2)}, u32[]{:S(2)}) collective-permute-start(bf16[136,512]{1,0:T(8,128)(2,1)} %get-tuple-element.44), channel_id=1, source_target_pairs={{0,1},{1,0},{2,3},{3,2},{4,5},{5,4},{6,7},{7,6},{8,9},{9,8},{10,11... | collective-permute-start | bytes 417800 | tf_op jit(solution)/shard_map/ppermute | solution.py:531
  11.2 10.1 %collective-permute-start.1 = (bf16[5,2560]{1,0:T(8,128)(2,1)}, bf16[5,2560]{1,0:T(8,128)(2,1)S(1)}, u32[]{:S(2)}, u32[]{:S(2)}) collective-permute-start(bf16[5,2560]{1,0:T(8,128)(2,1)} %get-tuple-element.25.ask_ref), channel_id=1, source_target_pairs={{0,8},{4,12},{8,0},{12,4},{1,9},{5,13},{9,1},{13,5},{2,10},{6,14},... | collective-permute-start | bytes 76808 | tf_op jit(solution)/shard_map/ppermute | solution.py:531
  12.7 11.1 %collective-permute-start.2 = (bf16[5,2560]{1,0:T(8,128)(2,1)}, bf16[5,2560]{1,0:T(8,128)(2,1)S(1)}, u32[]{:S(2)}, u32[]{:S(2)}) collective-permute-start(bf16[5,2560]{1,0:T(8,128)(2,1)} %get-tuple-element.25.ask_ref), channel_id=1, source_target_pairs={{0,12},{4,8},{8,4},{12,0},{1,13},{5,9},{9,5},{13,1},{2,14},{6,10},... | collective-permute-start | bytes 76808 | tf_op jit(solution)/shard_map/ppermute | solution.py:531
  12.7 13.1 %copy-start.1 = (f32[128,128]{1,0:T(8,128)S(1)}, f32[128,128]{1,0:T(8,128)}, u32[]{:S(2)}) copy-start(f32[128,128]{1,0:T(8,128)} %constant.4.clone.cos_ref) | copy-start | bytes 196612
  12.7 13.1 %copy-start.2 = (f32[128,128]{1,0:T(8,128)S(1)}, f32[128,128]{1,0:T(8,128)}, u32[]{:S(2)}) copy-start(f32[128,128]{1,0:T(8,128)} %constant.5.clone.sin_ref) | copy-start | bytes 196612
  12.7 13.1 %copy-start.5 = (s32[4,2]{0,1:T(2,128)S(1)}, s32[4,2]{0,1:T(2,128)}, u32[]{:S(2)}) copy-start(s32[4,2]{0,1:T(2,128)} %param.14) | copy-start | bytes 100
  12.7 13.0 %copy-start.6 = (s32[4,2]{0,1:T(2,128)S(1)}, s32[4,2]{0,1:T(2,128)}, u32[]{:S(2)}) copy-start(s32[4,2]{0,1:T(2,128)} %param.15) | copy-start | bytes 100
  12.8 13.0 %copy-start.7 = (bf16[128]{0:T(256)(128)(2,1)S(1)}, bf16[128]{0:T(256)(128)(2,1)}, u32[]{:S(2)}) copy-start(bf16[128]{0:T(256)(128)(2,1)} %param.18) | copy-start | bytes 772
  12.8 13.8 %copy-start = (bf16[136,512]{1,0:T(8,128)(2,1)S(1)}, bf16[136,512]{1,0:T(8,128)(2,1)}, u32[]{:S(2)}) copy-start(bf16[136,512]{1,0:T(8,128)(2,1)} %get-tuple-element.41.rest_0_) | copy-start | bytes 417796
  12.8 16.4 %copy-start.3 = (bf16[5,2560]{1,0:T(8,128)(2,1)S(1)}, bf16[5,2560]{1,0:T(8,128)(2,1)}, u32[]{:S(2)}) copy-start(bf16[5,2560]{1,0:T(8,128)(2,1)} %get-tuple-element.25.ask_ref) | copy-start | bytes 76804
  21.3 7.3 %collective-permute-start.3 = (bf16[64,128]{1,0:T(8,128)(2,1)}, bf16[64,128]{1,0:T(8,128)(2,1)S(1)}, u32[]{:S(2)}, u32[]{:S(2)}) collective-permute-start(bf16[64,128]{1,0:T(8,128)(2,1)} %get-tuple-element.32), channel_id=1, source_target_pairs={{0,3},{1,2},{2,1},{3,0},{4,7},{5,6},{6,5},{7,4},{8,11},{9,10},{10,... | collective-permute-start | bytes 49160 | tf_op jit(solution)/shard_map/ppermute | solution.py:531
  23.8 5.4 %collective-permute-start.4 = (bf16[64,128]{1,0:T(8,128)(2,1)}, bf16[64,128]{1,0:T(8,128)(2,1)S(1)}, u32[]{:S(2)}, u32[]{:S(2)}) collective-permute-start(bf16[64,128]{1,0:T(8,128)(2,1)} %get-tuple-element.33), channel_id=1, source_target_pairs={{0,2},{1,3},{2,0},{3,1},{4,6},{5,7},{6,4},{7,5},{8,10},{9,11},{10,... | collective-permute-start | bytes 49160 | tf_op jit(solution)/shard_map/ppermute | solution.py:531
  23.9 5.3 %collective-permute-start.5 = (bf16[64,128]{1,0:T(8,128)(2,1)}, bf16[64,128]{1,0:T(8,128)(2,1)S(1)}, u32[]{:S(2)}, u32[]{:S(2)}) collective-permute-start(bf16[64,128]{1,0:T(8,128)(2,1)} %get-tuple-element.34), channel_id=1, source_target_pairs={{0,1},{1,0},{2,3},{3,2},{4,5},{5,4},{6,7},{7,6},{8,9},{9,8},{10,11... | collective-permute-start | bytes 49160 | tf_op jit(solution)/shard_map/ppermute | solution.py:531
  27.3 2.8 %collective-permute-start.9 = (bf16[2,2048]{1,0:T(2,128)(2,1)S(1)}, bf16[2,2048]{1,0:T(2,128)(2,1)S(1)}, u32[]{:S(2)}, u32[]{:S(2)}) collective-permute-start(bf16[2,2048]{1,0:T(2,128)(2,1)S(1)} %attend_moved.1), channel_id=1, source_target_pairs={{0,4},{4,0},{8,12},{12,8},{1,5},{5,1},{9,13},{13,9},{2,6},{6,2},{1... | collective-permute-start | bytes 24584 | tf_op jit(solution)/shard_map/ppermute | solution.py:531
  27.3 3.7 %collective-permute-start.10 = (bf16[2,2048]{1,0:T(2,128)(2,1)S(1)}, bf16[2,2048]{1,0:T(2,128)(2,1)S(1)}, u32[]{:S(2)}, u32[]{:S(2)}) collective-permute-start(bf16[2,2048]{1,0:T(2,128)(2,1)S(1)} %attend_moved.1), channel_id=1, source_target_pairs={{0,8},{4,12},{8,0},{12,4},{1,9},{5,13},{9,1},{13,5},{2,10},{6,14},... | collective-permute-start | bytes 24584 | tf_op jit(solution)/shard_map/ppermute | solution.py:531
  28.6 3.1 %collective-permute-start.11 = (bf16[2,2048]{1,0:T(2,128)(2,1)S(1)}, bf16[2,2048]{1,0:T(2,128)(2,1)S(1)}, u32[]{:S(2)}, u32[]{:S(2)}) collective-permute-start(bf16[2,2048]{1,0:T(2,128)(2,1)S(1)} %attend_moved.1), channel_id=1, source_target_pairs={{0,12},{4,8},{8,4},{12,0},{1,13},{5,9},{9,5},{13,1},{2,14},{6,10},... | collective-permute-start | bytes 24584 | tf_op jit(solution)/shard_map/ppermute | solution.py:531
  29.2 0.7 %copy-start.4 = (bf16[64,128]{1,0:T(8,128)(2,1)S(1)}, bf16[64,128]{1,0:T(8,128)(2,1)}, u32[]{:S(2)}) copy-start(bf16[64,128]{1,0:T(8,128)(2,1)} %get-tuple-element.31.rest_0_) | copy-start | bytes 49156

commit v8 on v7

--- a/solution.py
+++ b/solution.py
@@ -15,6 +15,7 @@
 BF16 = jnp.bfloat16
 MIB = 1024 * 1024
 CHUNK = 512
+AHEAD = 3
 
 VMEM = pl.BlockSpec(memory_space=pltpu.VMEM)
 SMEM = pl.BlockSpec(memory_space=pltpu.SMEM)
@@ -64,11 +65,9 @@
     copies = []
     for i, (low, high) in enumerate(chunks):
         copies.append(
-            pltpu.make_async_copy(
-                w_hbm.at[low:high, :], w_ref.at[low:high, :], w_sems.at[i]
-            )
+            pltpu.make_async_copy(w_hbm.at[low:high, :], w_ref.at[low:high, :], w_sems.at[i])
         )
-        copies[-1].start()
+    copies[0].start()
     mine = heads_mine * 128
     q_first = pl.multiple_of(rank * mine, 128)
     asking = [
@@ -88,6 +87,8 @@
         copy.start()
     gain_copy.wait()
     x_copy.wait()
+    if len(copies) > 1:
+        copies[1].start()
     squares = jnp.zeros((rows, 128), F32)
     for i, (low, high) in enumerate(chunks):
         parts = []
@@ -102,6 +103,8 @@
             squares = squares + x
         xg = parts[0] if len(parts) == 1 else jnp.concatenate(parts, axis=1)
         copies[i].wait()
+        if i + 2 < len(copies):
+            copies[i + 2].start()
         for n in range(0, 2 * kv_width, 512):
             part = jnp.dot(xg, w_ref[low:high, n : n + 512], preferred_element_type=F32)
             if i == 0:
@@ -111,8 +114,8 @@
     sq = column_to_row(jnp.sum(squares, axis=1, keepdims=True), 128)
     high, low = split_bf16(sq)
     tail = jnp.concatenate([high.astype(F32), low.astype(F32)], axis=0)
-    if outs[0].shape[0] - rows > tail.shape[0]:
-        fill = outs[0].shape[0] - rows - tail.shape[0]
+    fill = outs[1].shape[0] - rows - tail.shape[0]
+    if fill:
         tail = jnp.concatenate([tail, jnp.zeros((fill, 128), F32)], axis=0)
     extra = jnp.concatenate([tail.astype(BF16)] * (2 * piece // 128), axis=1)
     for j in range(ranks):
@@ -157,23 +160,31 @@
 
 def resident_kernel(ranks, len_hbm, q_hbm, k_hbm, v_hbm, *rest):
     outs = rest[:ranks]
-    len_ref, q_ref, q_all, k_buf, v_buf, o_all, s_all, in_sems, sems = rest[ranks:]
+    len_ref, q_ref, q_all, k_buf, v_buf, s_buf, o_all, s_all, in_sems, sems = rest[ranks:]
     residents, positions, width = k_buf.shape
-    len_copy = pltpu.make_async_copy(len_hbm, len_ref, in_sems.at[0])
-    q_copy = pltpu.make_async_copy(q_hbm, q_ref, in_sems.at[1])
+    half = positions // 2
+    chunks = []
+    for r in range(residents):
+        for hbm, buf in ((k_hbm, k_buf), (v_hbm, v_buf)):
+            for i in range(2):
+                at = slice(i * half, (i + 1) * half)
+                chunks.append(
+                    pltpu.make_async_copy(
+                        hbm.at[r, at, :], buf.at[r, at, :], sems.at[len(chunks)]
+                    )
+                )
+    for chunk in chunks[:AHEAD]:
+        chunk.start()
+    q_copy = pltpu.make_async_copy(q_hbm, q_ref, in_sems.at[0])
+    len_copy = pltpu.make_async_copy(len_hbm, len_ref, in_sems.at[1])
+    q_copy.start()
     len_copy.start()
-    q_copy.start()
-    copies = []
-    for r in range(residents):
-        copies.append(
-            (
-                pltpu.make_async_copy(k_hbm.at[r], k_buf.at[r], sems.at[0, r]),
-                pltpu.make_async_copy(v_hbm.at[r], v_buf.at[r], sems.at[1, r]),
-            )
-        )
-    for pair in copies:
-        for copy in pair:
-            copy.start()
+
+    def arrived(i):
+        chunks[i].wait()
+        if i + AHEAD < len(chunks):
+            chunks[i + AHEAD].start()
+
     heads = q_ref.shape[1] // 128
     kv_heads = width // 128
     group = heads // kv_heads
@@ -181,16 +192,17 @@
     heads_mine = heads // ranks
     rank = lax.axis_index("tp")
     top_half = iota((pair_rows, 128), 0) < group
-    position = iota((pair_rows, positions), 1)
+    position = rank * positions + iota((pair_rows, positions), 1)
     scale = F32(1.0) / jnp.sqrt(F32(128.0))
     diagonal = iota((heads, 128), 0) % heads_mine == iota((heads, 128), 1)
+    pairs = [slice(p * pair_rows, (p + 1) * pair_rows) for p in range(kv_heads // 2)]
 
     def to_rows(columns):
         spread = jnp.where(diagonal, jnp.concatenate(columns, axis=0), 0.0)
         return jnp.sum(spread.reshape(ranks, heads_mine, 128), axis=1)
 
+    q_copy.wait()
     len_copy.wait()
-    q_copy.wait()
     for h in range(heads):
         q_all[h * 8 : h * 8 + residents, :] = q_ref[:residents, h * 128 : (h + 1) * 128].astype(F32)
     peaks, totals = [], []
@@ -198,35 +210,48 @@
         q_mine = q_all[pl.ds(r, heads, stride=8), :]
         peaks.append([])
         totals.append([])
-        valid = position < len_ref[0, r] - rank * positions
-        copies[r][0].wait()
+        valid = position < len_ref[0:1, r : r + 1]
+        both_of = []
+        for rows in pairs:
+            q = q_mine[rows].astype(BF16)
+            zero = jnp.zeros_like(q)
+            both_of.append(
+                jnp.concatenate(
+                    [jnp.where(top_half, q, zero), jnp.where(top_half, zero, q)], axis=1
+                )
+            )
+        for i in range(2):
+            arrived(4 * r + i)
+            at = slice(i * half, (i + 1) * half)
+            for p, rows in enumerate(pairs):
+                s_buf[rows, at] = lax.dot_general(
+                    both_of[p],
+                    k_buf[r, at, p * 256 : (p + 1) * 256],
+                    (((1,), (1,)), ((), ())),
+                    preferred_element_type=F32,
+                )
         weights = []
-        for p in range(kv_heads // 2):
-            q = q_mine[p * pair_rows : (p + 1) * pair_rows].astype(BF16)
-            zero = jnp.zeros_like(q)
-            lhs = jnp.concatenate(
-                [jnp.where(top_half, q, zero), jnp.where(top_half, zero, q)], axis=1
-            )
-            scores = lax.dot_general(
-                lhs,
-                k_buf[r, :, p * 256 : (p + 1) * 256],
-                (((1,), (1,)), ((), ())),
-                preferred_element_type=F32,
-            )
-            scores = jnp.where(valid, scores * scale, ABSENT)
+        for rows in pairs:
+            scores = jnp.where(valid, s_buf[rows, :] * scale, ABSENT)
             peak = jnp.max(scores, axis=1, keepdims=True).astype(BF16).astype(F32)
             weight = jnp.where(valid, jnp.exp(scores - peak), 0.0)
             peaks[r].append(peak)
             totals[r].append(jnp.sum(weight, axis=1, keepdims=True))
             weights.append(weight.astype(BF16))
-        copies[r][1].wait()
-        for p in range(kv_heads // 2):
-            both = jnp.dot(
-                weights[p], v_buf[r, :, p * 256 : (p + 1) * 256], preferred_element_type=F32
-            )
-            o_all[r, p * pair_rows : (p + 1) * pair_rows, :] = jnp.where(
-                top_half, both[:, :128], both[:, 128:]
-            )
+        for i in range(2):
+            arrived(4 * r + 2 + i)
+            at = slice(i * half, (i + 1) * half)
+            for p, rows in enumerate(pairs):
+                both = jnp.dot(
+                    weights[p][:, at],
+                    v_buf[r, at, p * 256 : (p + 1) * 256],
+                    preferred_element_type=F32,
+                )
+                part = jnp.where(top_half, both[:, :128], both[:, 128:])
+                if i == 0:
+                    o_all[r, rows, :] = part
+                else:
+                    o_all[r, rows, :] += part
     for r in range(residents):
         s_all[r, 0] = to_rows(peaks[r])
         high, low = split_bf16(to_rows(totals[r]))
@@ -254,15 +279,16 @@
         out_specs=[VMEM] * ranks,
         out_shape=[jax.ShapeDtypeStruct((rows, 128), BF16)] * ranks,
         scratch_shapes=[
-            pltpu.SMEM(lengths.shape, jnp.int32),
+            pltpu.VMEM(lengths.shape, jnp.int32),
             pltpu.VMEM(query.shape, BF16),
             pltpu.VMEM((heads * 8, 128), F32),
             pltpu.VMEM((residents, positions, width), BF16),
             pltpu.VMEM((residents, positions, width), BF16),
+            pltpu.VMEM((heads, positions), F32),
             pltpu.VMEM((residents, heads, 128), F32),
             pltpu.VMEM((residents, 3, ranks, 128), F32),
             pltpu.SemaphoreType.DMA((2,)),
-            pltpu.SemaphoreType.DMA((2, residents)),
+            pltpu.SemaphoreType.DMA((4 * residents,)),
         ],
         compiler_params=pltpu.CompilerParams(vmem_limit_bytes=56 * MIB),
         cost_estimate=pl.CostEstimate(
@@ -381,11 +407,12 @@
     heads_mine = rows // requests
     scale = F32(1.0) / jnp.sqrt(F32(128.0))
 
-    tail = pieces[0][tokens:, :].astype(F32)
+    blocks = tokens // 128
+    last = tokens + 2 * blocks
+    tail = pieces[0][tokens:last, :128].astype(F32)
     for t in range(1, ranks):
-        tail = tail + pieces[t][tokens:, :].astype(F32)
-    blocks = tokens // 128
-    squares = tail[:blocks, :128] + tail[blocks : 2 * blocks, :128]
+        tail = tail + pieces[t][tokens:last, :128].astype(F32)
+    squares = tail[:blocks] + tail[blocks:]
     squares = jnp.concatenate(
         [row_to_column(squares[b : b + 1], 128) for b in range(blocks)], axis=0
     )
@@ -454,38 +481,38 @@
 
 
 def combine_kernel(ranks, residents, kv_mine, ask_ref, *rest):
-    payloads = rest[:ranks]
-    out_ref = rest[ranks]
+    refs, out_ref = rest[:ranks], rest[ranks]
     heads_mine = out_ref.shape[1] // 128
     scale = F32(1.0) / jnp.sqrt(F32(128.0))
+    payloads = [ref[...].astype(F32) for ref in refs]
     at = residents * heads_mine
     ask = ask_ref[...].astype(F32)
     for r in range(residents):
         q, own_k, own_v = heads_of(ask[r : r + 1], heads_mine, kv_mine)
         own_score = jnp.sum(q * own_k, axis=1, keepdims=True) * scale
         peaks, totals = [], []
-        for t in range(ranks):
-            stat = payloads[t][at : at + 3 * residents, :].astype(F32)
+        for payload in payloads:
+            stat = payload[at : at + 3 * residents]
             peaks.append(row_to_column(stat[r : r + 1], heads_mine))
             total = stat[residents + r : residents + r + 1]
             total = total + stat[2 * residents + r : 2 * residents + r + 1]
             totals.append(row_to_column(total, heads_mine))
         top = own_score
-        for t in range(ranks):
-            top = jnp.maximum(top, peaks[t])
+        for peak in peaks:
+            top = jnp.maximum(top, peak)
         own_weight = jnp.exp(own_score - top)
         denom = own_weight
         numer = own_weight.astype(BF16).astype(F32) * own_v
-        for t in range(ranks):
-            keep = jnp.exp(peaks[t] - top)
-            denom = denom + keep * totals[t]
-            numer = numer + keep * payloads[t][r * heads_mine : (r + 1) * heads_mine, :].astype(F32)
+        for peak, total, payload in zip(peaks, totals, payloads):
+            keep = jnp.exp(peak - top)
+            denom = denom + keep * total
+            numer = numer + keep * payload[r * heads_mine : (r + 1) * heads_mine]
         result = numer / denom
         for h in range(heads_mine):
             out_ref[r : r + 1, h * 128 : (h + 1) * 128] = result[h : h + 1, :]
 
 
-def combine_resident(asks, payloads, residents, heads_mine, kv_mine):
+def combine_resident(ask, payloads, residents, heads_mine, kv_mine):
     return pl.pallas_call(
         functools.partial(combine_kernel, len(payloads), residents, kv_mine),
         in_specs=[VMEM] * (1 + len(payloads)),
@@ -493,7 +520,7 @@
         out_shape=jax.ShapeDtypeStruct((residents, heads_mine * 128), F32),
         compiler_params=pltpu.CompilerParams(vmem_limit_bytes=8 * MIB),
         name="combine_resident",
-    )(asks, *payloads)
+    )(ask, *payloads)
 
 
 def finish_kernel(kept_ref, place_ref, *rest):
@@ -572,9 +599,9 @@
     last = ranks - 1
     far = swapped(pieces[last], "tp", last, ranks)
     asks = [swapped(ask, "inst", b, insts) for b in range(1, insts)]
-    asks[0], *near = lax.optimization_barrier((asks[0], *pieces[1:last]))
-    near = [swapped(near[j - 1], "tp", j, ranks) for j in reversed(range(1, last))]
-    pieces = [pieces[0], far] + near
+    asks[0], *others = lax.optimization_barrier((asks[0], *pieces[1:last]))
+    others = [swapped(others[j - 1], "tp", j, ranks) for j in reversed(range(1, last))]
+    pieces = [pieces[0], far] + others
     payloads = attend_resident(lengths, query[0], k_cache[0], v_cache[0], ranks)
     own_payload = payloads[0]
     payloads = [swapped(payloads[j], "tp", j, ranks) for j in reversed(range(1, ranks))]

time: 32.6 us -> 32.5 us (level)
    pallas_call x1, Pallas kernels: 8.5 us -> 7.93 us  [attend_resident(): pl.pallas_call(functools.partial(resident_kernel, ranks), in_specs=[HBM]...]
    pallas_call x1, Pallas kernels: 4.12 us -> 4.51 us  [project(): pl.pallas_call(functools.partial(project_kernel, ranks, group), in_specs=...]
  transfers between devices with their start and end apart: 12 -> 12, of which waited for: 2 -> 2; matrix products, arithmetic and copies ran while one was open for 0% -> 0% of each run, Pallas kernels for 31% -> 30%
where the time goes in v8:
time: 32.5 us; the launch traced here: 32.2 us
  starting transfers between devices  15 us (46%)
  Pallas kernels  14.7 us (45%)
  waiting for transfers between devices  1.62 us (5%)
  local copies, waits for them, and re-layouts  0.74 us (2%)
    ppermute x12, starting transfers between devices, swapped(): return lax.ppermute(x, axis, [(i, i ^ j) for i in range(n)])  15 us
    pallas_call x1, Pallas kernels, attend_resident(): pl.pallas_call(functools.partial(resident_kernel, ranks), in_specs=[HBM]...  7.93 us
    pallas_call x1, Pallas kernels, project(): pl.pallas_call(functools.partial(project_kernel, ranks, group), in_specs=...  4.51 us
    ppermute x12, waiting for transfers between devices, swapped(): return lax.ppermute(x, axis, [(i, i ^ j) for i in range(n)])  1.62 us
    pallas_call x1, Pallas kernels, prepare(): pl.pallas_call(functools.partial(prepare_kernel, insts, residents, kv_min...  0.78 us
    unnamed x16, local copies, waits for them, and re-layouts  0.74 us
    pallas_call x1, Pallas kernels, finish(): pl.pallas_call(finish_kernel, in_specs=[VMEM] * (2 + len(moved)), out_spe...  0.67 us
  transfers between devices with their start and end apart: 12, of which 2 were waited for; matrix products, arithmetic and copies ran while one was open for 0% of the time, Pallas kernels for 30%

profile of v8, /device:TPU:0, one launch (start us, length us, event | category | flops | bytes accessed | tf_op | source)
XLA Modules:
  0.0 32.2 jit_solution(2364220156799681564)
XLA Ops:
  0.0 4.5 %project.1 = (bf16[136,512]{1,0:T(8,128)(2,1)}, bf16[136,512]{1,0:T(8,128)(2,1)}, bf16[136,512]{1,0:T(8,128)(2,1)}, bf16[136,512]{1,0:T(8,128)(2,1)}, bf16[5,2560]{1,0:T(8,128)(2,1)}) custom-call(bf16[1280]{0:T(1024)(128)(2,1)} %gain_hbm.1, bf16[64,2,1280]{2,1,0:T(2,128)(2,1)} %bitcast.16, bf16[1280,2048]{1,0:T(8,128)(2,1)} %w_hbm.1, ...), custom_call_target="tpu_custom_call" | custom-call | flops 671088640 | bytes 5242880 | tf_op jit(solution)/shard_map/project/pallas_call | solution.py:136
  4.5 0.5 %collective-permute-start = (bf16[5,2560]{1,0:T(8,128)(2,1)}, bf16[5,2560]{1,0:T(8,128)(2,1)S(1)}, u32[]{:S(2)}, u32[]{:S(2)}) collective-permute-start(bf16[5,2560]{1,0:T(8,128)(2,1)} %get-tuple-element.25.ask_ref), channel_id=1, source_target_pairs={{0,4},{4,0},{8,12},{12,8},{1,5},{5,1},{9,13},{13,9},{2,6},{6,2},{1... | collective-permute-start | bytes 76808 | tf_op jit(solution)/shard_map/ppermute | solution.py:558
  5.0 4.7 %collective-permute-start.6 = (bf16[136,512]{1,0:T(8,128)(2,1)}, bf16[136,512]{1,0:T(8,128)(2,1)S(1)}, u32[]{:S(2)}, u32[]{:S(2)}) collective-permute-start(bf16[136,512]{1,0:T(8,128)(2,1)} %get-tuple-element.42), channel_id=1, source_target_pairs={{0,3},{1,2},{2,1},{3,0},{4,7},{5,6},{6,5},{7,4},{8,11},{9,10},{10,... | collective-permute-start | bytes 417800 | tf_op jit(solution)/shard_map/ppermute | solution.py:558
  9.7 0.0 collective-permute-done.rest_0_
  9.7 0.3 %collective-permute-start.7 = (bf16[136,512]{1,0:T(8,128)(2,1)}, bf16[136,512]{1,0:T(8,128)(2,1)S(1)}, u32[]{:S(2)}, u32[]{:S(2)}) collective-permute-start(bf16[136,512]{1,0:T(8,128)(2,1)} %get-tuple-element.43), channel_id=1, source_target_pairs={{0,2},{1,3},{2,0},{3,1},{4,6},{5,7},{6,4},{7,5},{8,10},{9,11},{10,... | collective-permute-start | bytes 417800 | tf_op jit(solution)/shard_map/ppermute | solution.py:558
  10.1 1.6 %collective-permute-start.8 = (bf16[136,512]{1,0:T(8,128)(2,1)}, bf16[136,512]{1,0:T(8,128)(2,1)S(1)}, u32[]{:S(2)}, u32[]{:S(2)}) collective-permute-start(bf16[136,512]{1,0:T(8,128)(2,1)} %get-tuple-element.44), channel_id=1, source_target_pairs={{0,1},{1,0},{2,3},{3,2},{4,5},{5,4},{6,7},{7,6},{8,9},{9,8},{10,11... | collective-permute-start | bytes 417800 | tf_op jit(solution)/shard_map/ppermute | solution.py:558
  11.6 1.5 %collective-permute-start.1 = (bf16[5,2560]{1,0:T(8,128)(2,1)}, bf16[5,2560]{1,0:T(8,128)(2,1)S(1)}, u32[]{:S(2)}, u32[]{:S(2)}) collective-permute-start(bf16[5,2560]{1,0:T(8,128)(2,1)} %get-tuple-element.25.ask_ref), channel_id=1, source_target_pairs={{0,8},{4,12},{8,0},{12,4},{1,9},{5,13},{9,1},{13,5},{2,10},{6,14},... | collective-permute-start | bytes 76808 | tf_op jit(solution)/shard_map/ppermute | solution.py:558
  13.1 0.0 collective-permute-start.2
  13.1 0.0 copy-start.1
  13.1 0.0 copy-start.2
  13.1 0.0 copy-start.5
  13.1 0.0 copy-start.6
  13.1 0.0 copy-start.7
  13.2 0.0 copy-start
  13.2 0.0 copy-start.3
  13.2 7.9 %attend_resident.1 = (bf16[64,128]{1,0:T(8,128)(2,1)}, bf16[64,128]{1,0:T(8,128)(2,1)}, bf16[64,128]{1,0:T(8,128)(2,1)}, bf16[64,128]{1,0:T(8,128)(2,1)}) custom-call(s32[1,3]{1,0:T(1,128)} %len_hbm.1, bf16[5,8192]{1,0:T(8,128)(2,1)} %bitcast.15, bf16[3,1024,1024]{2,1,0:T(8,128)(2,1)} %bitcast.12, bf16[3,1024,1024]{2,1,0:T(8,128)(2,1)} %bitcast.13), custom_call_target="tpu_custom_call" | custom-call | flops 100663296 | bytes 12582912 | tf_op jit(solution)/shard_map/attend_resident/pallas_call | solution.py:276
  21.1 0.0 collective-permute-done.1.rest_1_
  21.1 2.5 %collective-permute-start.3 = (bf16[64,128]{1,0:T(8,128)(2,1)}, bf16[64,128]{1,0:T(8,128)(2,1)S(1)}, u32[]{:S(2)}, u32[]{:S(2)}) collective-permute-start(bf16[64,128]{1,0:T(8,128)(2,1)} %get-tuple-element.32), channel_id=1, source_target_pairs={{0,3},{1,2},{2,1},{3,0},{4,7},{5,6},{6,5},{7,4},{8,11},{9,10},{10,... | collective-permute-start | bytes 49160 | tf_op jit(solution)/shard_map/ppermute | solution.py:558
  23.7 0.0 collective-permute-done.2.rest_2_
  23.7 0.0 collective-permute-start.4
  23.7 0.0 collective-permute-done.6.rest_1_
  23.7 1.9 %collective-permute-start.5 = (bf16[64,128]{1,0:T(8,128)(2,1)}, bf16[64,128]{1,0:T(8,128)(2,1)S(1)}, u32[]{:S(2)}, u32[]{:S(2)}) collective-permute-start(bf16[64,128]{1,0:T(8,128)(2,1)} %get-tuple-element.34), channel_id=1, source_target_pairs={{0,1},{1,0},{2,3},{3,2},{4,5},{5,4},{6,7},{7,6},{8,9},{9,8},{10,11... | collective-permute-start | bytes 49160 | tf_op jit(solution)/shard_map/ppermute | solution.py:558
  25.6 0.0 copy-done.1
  25.6 0.0 copy-done.2
  25.6 0.0 copy-done.5
  25.6 0.0 copy-done.6
  25.6 0.0 copy-done.7
  25.6 0.8 %prepare.1 = (bf16[32,128]{1,0:T(8,128)(2,1)S(1)}, f32[2,32,128]{2,1,0:T(8,128)S(1)}, s32[32,128]{1,0:T(8,128)S(1)}, f32[128,128]{1,0:T(8,128)S(1)}, f32[128,128]{1,0:T(8,128)S(1)}, /*index=5*/s32[8,128]{1,0:T(8,128)S(1)}) custom-call(s32[2,4]{1,0:T(2,128)S(1)} %bitcast.9, s32[2,4]{1,0:T(2,128)S(1)} %bitcast.10, bf16[1,128]{1,0:T(2,128)(2,1)S(1)} %bitcast.11, ...), custom_call_target="tpu_custom_call" | custom-call | tf_op jit(solution)/shard_map/prepare/pallas_call | solution.py:377
  26.4 0.0 collective-permute-done.7.rest_2_
  26.4 0.0 collective-permute-done.8.rest_3_
  26.4 0.0 copy-done
  26.4 0.6 %attend_moved.1 = bf16[2,2048]{1,0:T(2,128)(2,1)S(1)} custom-call(bf16[32,128]{1,0:T(8,128)(2,1)S(1)} %get-tuple-element.36.q_ref, f32[2,32,128]{2,1,0:T(8,128)S(1)} %get-tuple-element.37.own_ref, s32[32,128]{1,0:T(8,128)S(1)} %get-tuple-element.38.limit_ref, f32[128,128]{1,0:T(8,128)S(1)} %get-tuple-element.39.cos_ref, ...), custom_call_target="tpu_custom_call" | custom-call | flops 33554432 | bytes 4194304 | tf_op jit(solution)/shard_map/attend_moved/pallas_call | solution.py:469
  27.1 0.1 collective-permute-start.9
  27.2 1.3 %collective-permute-start.10 = (bf16[2,2048]{1,0:T(2,128)(2,1)S(1)}, bf16[2,2048]{1,0:T(2,128)(2,1)S(1)}, u32[]{:S(2)}, u32[]{:S(2)}) collective-permute-start(bf16[2,2048]{1,0:T(2,128)(2,1)S(1)} %attend_moved.1), channel_id=1, source_target_pairs={{0,8},{4,12},{8,0},{12,4},{1,9},{5,13},{9,1},{13,5},{2,10},{6,14},... | collective-permute-start | bytes 24584 | tf_op jit(solution)/shard_map/ppermute | solution.py:558
  28.4 0.0 collective-permute-done.3.rest_1_
  28.4 0.6 %collective-permute-start.11 = (bf16[2,2048]{1,0:T(2,128)(2,1)S(1)}, bf16[2,2048]{1,0:T(2,128)(2,1)S(1)}, u32[]{:S(2)}, u32[]{:S(2)}) collective-permute-start(bf16[2,2048]{1,0:T(2,128)(2,1)S(1)} %attend_moved.1), channel_id=1, source_target_pairs={{0,12},{4,8},{8,4},{12,0},{1,13},{5,9},{9,5},{13,1},{2,14},{6,10},... | collective-permute-start | bytes 24584 | tf_op jit(solution)/shard_map/ppermute | solution.py:558
  29.0 0.0 collective-permute-done.4.rest_2_
  29.0 0.0 collective-permute-done.5.rest_3_
  29.0 0.0 copy-done.3
  29.0 0.0 copy-start.4
  29.0 0.7 %copy-done.4 = bf16[64,128]{1,0:T(8,128)(2,1)S(1)} copy-done((bf16[64,128]{1,0:T(8,128)(2,1)S(1)}, bf16[64,128]{1,0:T(8,128)(2,1)}, u32[]{:S(2)}) %copy-start.4) | copy-done | bytes 16408
  29.8 0.2 combine_resident.1.kept_ref
  29.9 0.0 collective-permute-done.9.rest_0_
  29.9 0.9 %collective-permute-done.10.rest_1_ = bf16[2,2048]{1,0:T(2,128)(2,1)S(1)} collective-permute-done((bf16[2,2048]{1,0:T(2,128)(2,1)S(1)}, bf16[2,2048]{1,0:T(2,128)(2,1)S(1)}, u32[]{:S(2)}, u32[]{:S(2)}) %collective-permute-start.10) | collective-permute-done | bytes 8224 | tf_op jit(solution)/shard_map/ppermute | solution.py:558
  30.9 0.7 %collective-permute-done.11.rest_2_ = bf16[2,2048]{1,0:T(2,128)(2,1)S(1)} collective-permute-done((bf16[2,2048]{1,0:T(2,128)(2,1)S(1)}, bf16[2,2048]{1,0:T(2,128)(2,1)S(1)}, u32[]{:S(2)}, u32[]{:S(2)}) %collective-permute-start.11) | collective-permute-done | bytes 8224 | tf_op jit(solution)/shard_map/ppermute | solution.py:558
  31.5 0.7 %finish.1 = bf16[5,2048]{1,0:T(8,128)(2,1)} custom-call(f32[3,2048]{1,0:T(4,128)S(1)} %combine_resident.1.kept_ref, s32[8,128]{1,0:T(8,128)S(1)} %get-tuple-element.35.place_ref, bf16[2,2048]{1,0:T(2,128)(2,1)S(1)} %collective-permute-done.9.rest_0_, bf16[2,2048]{1,0:T(2,128)(2,1)S(1)} %collective-permute-done.10.rest_1_, ...), custom_call_target="tpu_custom_call" | custom-call | tf_op jit(solution)/shard_map/finish/pallas_call | solution.py:547
Async XLA Ops:
  4.5 5.2 %collective-permute-start = (bf16[5,2560]{1,0:T(8,128)(2,1)}, bf16[5,2560]{1,0:T(8,128)(2,1)S(1)}, u32[]{:S(2)}, u32[]{:S(2)}) collective-permute-start(bf16[5,2560]{1,0:T(8,128)(2,1)} %get-tuple-element.25.ask_ref), channel_id=1, source_target_pairs={{0,4},{4,0},{8,12},{12,8},{1,5},{5,1},{9,13},{13,9},{2,6},{6,2},{1... | collective-permute-start | bytes 76808 | tf_op jit(solution)/shard_map/ppermute | solution.py:558
  5.0 18.6 %collective-permute-start.6 = (bf16[136,512]{1,0:T(8,128)(2,1)}, bf16[136,512]{1,0:T(8,128)(2,1)S(1)}, u32[]{:S(2)}, u32[]{:S(2)}) collective-permute-start(bf16[136,512]{1,0:T(8,128)(2,1)} %get-tuple-element.42), channel_id=1, source_target_pairs={{0,3},{1,2},{2,1},{3,0},{4,7},{5,6},{6,5},{7,4},{8,11},{9,10},{10,... | collective-permute-start | bytes 417800 | tf_op jit(solution)/shard_map/ppermute | solution.py:558
  9.7 16.7 %collective-permute-start.7 = (bf16[136,512]{1,0:T(8,128)(2,1)}, bf16[136,512]{1,0:T(8,128)(2,1)S(1)}, u32[]{:S(2)}, u32[]{:S(2)}) collective-permute-start(bf16[136,512]{1,0:T(8,128)(2,1)} %get-tuple-element.43), channel_id=1, source_target_pairs={{0,2},{1,3},{2,0},{3,1},{4,6},{5,7},{6,4},{7,5},{8,10},{9,11},{10,... | collective-permute-start | bytes 417800 | tf_op jit(solution)/shard_map/ppermute | solution.py:558
  10.1 16.4 %collective-permute-start.8 = (bf16[136,512]{1,0:T(8,128)(2,1)}, bf16[136,512]{1,0:T(8,128)(2,1)S(1)}, u32[]{:S(2)}, u32[]{:S(2)}) collective-permute-start(bf16[136,512]{1,0:T(8,128)(2,1)} %get-tuple-element.44), channel_id=1, source_target_pairs={{0,1},{1,0},{2,3},{3,2},{4,5},{5,4},{6,7},{7,6},{8,9},{9,8},{10,11... | collective-permute-start | bytes 417800 | tf_op jit(solution)/shard_map/ppermute | solution.py:558
  11.6 9.5 %collective-permute-start.1 = (bf16[5,2560]{1,0:T(8,128)(2,1)}, bf16[5,2560]{1,0:T(8,128)(2,1)S(1)}, u32[]{:S(2)}, u32[]{:S(2)}) collective-permute-start(bf16[5,2560]{1,0:T(8,128)(2,1)} %get-tuple-element.25.ask_ref), channel_id=1, source_target_pairs={{0,8},{4,12},{8,0},{12,4},{1,9},{5,13},{9,1},{13,5},{2,10},{6,14},... | collective-permute-start | bytes 76808 | tf_op jit(solution)/shard_map/ppermute | solution.py:558
  13.1 10.6 %collective-permute-start.2 = (bf16[5,2560]{1,0:T(8,128)(2,1)}, bf16[5,2560]{1,0:T(8,128)(2,1)S(1)}, u32[]{:S(2)}, u32[]{:S(2)}) collective-permute-start(bf16[5,2560]{1,0:T(8,128)(2,1)} %get-tuple-element.25.ask_ref), channel_id=1, source_target_pairs={{0,12},{4,8},{8,4},{12,0},{1,13},{5,9},{9,5},{13,1},{2,14},{6,10},... | collective-permute-start | bytes 76808 | tf_op jit(solution)/shard_map/ppermute | solution.py:558
  13.1 12.5 %copy-start.1 = (f32[128,128]{1,0:T(8,128)S(1)}, f32[128,128]{1,0:T(8,128)}, u32[]{:S(2)}) copy-start(f32[128,128]{1,0:T(8,128)} %constant.4.clone.cos_ref) | copy-start | bytes 196612
  13.1 12.5 %copy-start.2 = (f32[128,128]{1,0:T(8,128)S(1)}, f32[128,128]{1,0:T(8,128)}, u32[]{:S(2)}) copy-start(f32[128,128]{1,0:T(8,128)} %constant.5.clone.sin_ref) | copy-start | bytes 196612
  13.1 12.5 %copy-start.5 = (s32[4,2]{0,1:T(2,128)S(1)}, s32[4,2]{0,1:T(2,128)}, u32[]{:S(2)}) copy-start(s32[4,2]{0,1:T(2,128)} %param.14) | copy-start | bytes 100
  13.1 12.5 %copy-start.6 = (s32[4,2]{0,1:T(2,128)S(1)}, s32[4,2]{0,1:T(2,128)}, u32[]{:S(2)}) copy-start(s32[4,2]{0,1:T(2,128)} %param.15) | copy-start | bytes 100
  13.1 12.5 %copy-start.7 = (bf16[128]{0:T(256)(128)(2,1)S(1)}, bf16[128]{0:T(256)(128)(2,1)}, u32[]{:S(2)}) copy-start(bf16[128]{0:T(256)(128)(2,1)} %param.18) | copy-start | bytes 772
  13.2 13.3 %copy-start = (bf16[136,512]{1,0:T(8,128)(2,1)S(1)}, bf16[136,512]{1,0:T(8,128)(2,1)}, u32[]{:S(2)}) copy-start(bf16[136,512]{1,0:T(8,128)(2,1)} %get-tuple-element.41.rest_0_) | copy-start | bytes 417796
  13.2 15.9 %copy-start.3 = (bf16[5,2560]{1,0:T(8,128)(2,1)S(1)}, bf16[5,2560]{1,0:T(8,128)(2,1)}, u32[]{:S(2)}) copy-start(bf16[5,2560]{1,0:T(8,128)(2,1)} %get-tuple-element.25.ask_ref) | copy-start | bytes 76804
  21.1 7.3 %collective-permute-start.3 = (bf16[64,128]{1,0:T(8,128)(2,1)}, bf16[64,128]{1,0:T(8,128)(2,1)S(1)}, u32[]{:S(2)}, u32[]{:S(2)}) collective-permute-start(bf16[64,128]{1,0:T(8,128)(2,1)} %get-tuple-element.32), channel_id=1, source_target_pairs={{0,3},{1,2},{2,1},{3,0},{4,7},{5,6},{6,5},{7,4},{8,11},{9,10},{10,... | collective-permute-start | bytes 49160 | tf_op jit(solution)/shard_map/ppermute | solution.py:558
  23.7 5.4 %collective-permute-start.4 = (bf16[64,128]{1,0:T(8,128)(2,1)}, bf16[64,128]{1,0:T(8,128)(2,1)S(1)}, u32[]{:S(2)}, u32[]{:S(2)}) collective-permute-start(bf16[64,128]{1,0:T(8,128)(2,1)} %get-tuple-element.33), channel_id=1, source_target_pairs={{0,2},{1,3},{2,0},{3,1},{4,6},{5,7},{6,4},{7,5},{8,10},{9,11},{10,... | collective-permute-start | bytes 49160 | tf_op jit(solution)/shard_map/ppermute | solution.py:558
  23.7 5.3 %collective-permute-start.5 = (bf16[64,128]{1,0:T(8,128)(2,1)}, bf16[64,128]{1,0:T(8,128)(2,1)S(1)}, u32[]{:S(2)}, u32[]{:S(2)}) collective-permute-start(bf16[64,128]{1,0:T(8,128)(2,1)} %get-tuple-element.34), channel_id=1, source_target_pairs={{0,1},{1,0},{2,3},{3,2},{4,5},{5,4},{6,7},{7,6},{8,9},{9,8},{10,11... | collective-permute-start | bytes 49160 | tf_op jit(solution)/shard_map/ppermute | solution.py:558
  27.1 2.8 %collective-permute-start.9 = (bf16[2,2048]{1,0:T(2,128)(2,1)S(1)}, bf16[2,2048]{1,0:T(2,128)(2,1)S(1)}, u32[]{:S(2)}, u32[]{:S(2)}) collective-permute-start(bf16[2,2048]{1,0:T(2,128)(2,1)S(1)} %attend_moved.1), channel_id=1, source_target_pairs={{0,4},{4,0},{8,12},{12,8},{1,5},{5,1},{9,13},{13,9},{2,6},{6,2},{1... | collective-permute-start | bytes 24584 | tf_op jit(solution)/shard_map/ppermute | solution.py:558
  27.2 3.7 %collective-permute-start.10 = (bf16[2,2048]{1,0:T(2,128)(2,1)S(1)}, bf16[2,2048]{1,0:T(2,128)(2,1)S(1)}, u32[]{:S(2)}, u32[]{:S(2)}) collective-permute-start(bf16[2,2048]{1,0:T(2,128)(2,1)S(1)} %attend_moved.1), channel_id=1, source_target_pairs={{0,8},{4,12},{8,0},{12,4},{1,9},{5,13},{9,1},{13,5},{2,10},{6,14},... | collective-permute-start | bytes 24584 | tf_op jit(solution)/shard_map/ppermute | solution.py:558
  28.4 3.1 %collective-permute-start.11 = (bf16[2,2048]{1,0:T(2,128)(2,1)S(1)}, bf16[2,2048]{1,0:T(2,128)(2,1)S(1)}, u32[]{:S(2)}, u32[]{:S(2)}) collective-permute-start(bf16[2,2048]{1,0:T(2,128)(2,1)S(1)} %attend_moved.1), channel_id=1, source_target_pairs={{0,12},{4,8},{8,4},{12,0},{1,13},{5,9},{9,5},{13,1},{2,14},{6,10},... | collective-permute-start | bytes 24584 | tf_op jit(solution)/shard_map/ppermute | solution.py:558
  29.0 0.7 %copy-start.4 = (bf16[64,128]{1,0:T(8,128)(2,1)S(1)}, bf16[64,128]{1,0:T(8,128)(2,1)}, u32[]{:S(2)}) copy-start(bf16[64,128]{1,0:T(8,128)(2,1)} %get-tuple-element.31.rest_0_) | copy-start | bytes 49156

commit v9 on v8

--- a/solution.py
+++ b/solution.py
@@ -15,7 +15,7 @@
 BF16 = jnp.bfloat16
 MIB = 1024 * 1024
 CHUNK = 512
-AHEAD = 3
+AHEAD = 4
 
 VMEM = pl.BlockSpec(memory_space=pltpu.VMEM)
 SMEM = pl.BlockSpec(memory_space=pltpu.SMEM)
@@ -67,7 +67,7 @@
         copies.append(
             pltpu.make_async_copy(w_hbm.at[low:high, :], w_ref.at[low:high, :], w_sems.at[i])
         )
-    copies[0].start()
+        copies[-1].start()
     mine = heads_mine * 128
     q_first = pl.multiple_of(rank * mine, 128)
     asking = [
@@ -87,8 +87,6 @@
         copy.start()
     gain_copy.wait()
     x_copy.wait()
-    if len(copies) > 1:
-        copies[1].start()
     squares = jnp.zeros((rows, 128), F32)
     for i, (low, high) in enumerate(chunks):
         parts = []
@@ -103,8 +101,6 @@
             squares = squares + x
         xg = parts[0] if len(parts) == 1 else jnp.concatenate(parts, axis=1)
         copies[i].wait()
-        if i + 2 < len(copies):
-            copies[i + 2].start()
         for n in range(0, 2 * kv_width, 512):
             part = jnp.dot(xg, w_ref[low:high, n : n + 512], preferred_element_type=F32)
             if i == 0:
@@ -160,7 +156,9 @@
 
 def resident_kernel(ranks, len_hbm, q_hbm, k_hbm, v_hbm, *rest):
     outs = rest[:ranks]
-    len_ref, q_ref, q_all, k_buf, v_buf, s_buf, o_all, s_all, in_sems, sems = rest[ranks:]
+    len_ref, q_ref, q_all, k_buf, v_buf, wide_ref, s_buf, w_buf, o_all, s_all, in_sems, sems = rest[
+        ranks:
+    ]
     residents, positions, width = k_buf.shape
     half = positions // 2
     chunks = []
@@ -188,14 +186,12 @@
     heads = q_ref.shape[1] // 128
     kv_heads = width // 128
     group = heads // kv_heads
-    pair_rows = 2 * group
     heads_mine = heads // ranks
     rank = lax.axis_index("tp")
-    top_half = iota((pair_rows, 128), 0) < group
-    position = rank * positions + iota((pair_rows, positions), 1)
+    position = rank * positions + iota((16, positions), 1)
     scale = F32(1.0) / jnp.sqrt(F32(128.0))
     diagonal = iota((heads, 128), 0) % heads_mine == iota((heads, 128), 1)
-    pairs = [slice(p * pair_rows, (p + 1) * pair_rows) for p in range(kv_heads // 2)]
+    own_block = iota((heads, width), 0) // group == iota((heads, width), 1) // 128
 
     def to_rows(columns):
         spread = jnp.where(diagonal, jnp.concatenate(columns, axis=0), 0.0)
@@ -207,51 +203,40 @@
         q_all[h * 8 : h * 8 + residents, :] = q_ref[:residents, h * 128 : (h + 1) * 128].astype(F32)
     peaks, totals = [], []
     for r in range(residents):
-        q_mine = q_all[pl.ds(r, heads, stride=8), :]
+        q = q_all[pl.ds(r, heads, stride=8), :].astype(BF16)
+        wide = jnp.concatenate([q] * kv_heads, axis=1)
+        wide_ref[...] = jnp.where(own_block, wide, jnp.zeros_like(wide))
         peaks.append([])
         totals.append([])
         valid = position < len_ref[0:1, r : r + 1]
-        both_of = []
-        for rows in pairs:
-            q = q_mine[rows].astype(BF16)
-            zero = jnp.zeros_like(q)
-            both_of.append(
-                jnp.concatenate(
-                    [jnp.where(top_half, q, zero), jnp.where(top_half, zero, q)], axis=1
-                )
-            )
         for i in range(2):
             arrived(4 * r + i)
             at = slice(i * half, (i + 1) * half)
-            for p, rows in enumerate(pairs):
-                s_buf[rows, at] = lax.dot_general(
-                    both_of[p],
-                    k_buf[r, at, p * 256 : (p + 1) * 256],
-                    (((1,), (1,)), ((), ())),
-                    preferred_element_type=F32,
-                )
-        weights = []
-        for rows in pairs:
+            s_buf[:, at] = lax.dot_general(
+                wide_ref[...],
+                k_buf[r, at, :],
+                (((1,), (1,)), ((), ())),
+                preferred_element_type=F32,
+            )
+        for c in range(0, heads, 16):
+            rows = slice(c, c + 16)
             scores = jnp.where(valid, s_buf[rows, :] * scale, ABSENT)
             peak = jnp.max(scores, axis=1, keepdims=True).astype(BF16).astype(F32)
             weight = jnp.where(valid, jnp.exp(scores - peak), 0.0)
             peaks[r].append(peak)
             totals[r].append(jnp.sum(weight, axis=1, keepdims=True))
-            weights.append(weight.astype(BF16))
+            w_buf[rows, :] = weight.astype(BF16)
         for i in range(2):
             arrived(4 * r + 2 + i)
             at = slice(i * half, (i + 1) * half)
-            for p, rows in enumerate(pairs):
-                both = jnp.dot(
-                    weights[p][:, at],
-                    v_buf[r, at, p * 256 : (p + 1) * 256],
-                    preferred_element_type=F32,
-                )
-                part = jnp.where(top_half, both[:, :128], both[:, 128:])
+            part = jnp.dot(w_buf[:, at], v_buf[r, at, :], preferred_element_type=F32)
+            for g in range(kv_heads):
+                rows = slice(g * group, (g + 1) * group)
+                block = part[rows, g * 128 : (g + 1) * 128]
                 if i == 0:
-                    o_all[r, rows, :] = part
+                    o_all[r, rows, :] = block
                 else:
-                    o_all[r, rows, :] += part
+                    o_all[r, rows, :] += block
     for r in range(residents):
         s_all[r, 0] = to_rows(peaks[r])
         high, low = split_bf16(to_rows(totals[r]))
@@ -284,7 +269,9 @@
             pltpu.VMEM((heads * 8, 128), F32),
             pltpu.VMEM((residents, positions, width), BF16),
             pltpu.VMEM((residents, positions, width), BF16),
+            pltpu.VMEM((heads, width), BF16),
             pltpu.VMEM((heads, positions), F32),
+            pltpu.VMEM((heads, positions), BF16),
             pltpu.VMEM((residents, heads, 128), F32),
             pltpu.VMEM((residents, 3, ranks, 128), F32),
             pltpu.SemaphoreType.DMA((2,)),

time: 32.5 us -> 32.1 us (0.988)
  Pallas kernels: 14.7 us -> 14.3 us
    pallas_call x1, Pallas kernels: 4.51 us -> 4.12 us  [project(): pl.pallas_call(functools.partial(project_kernel, ranks, group), in_specs=...]
where the time goes in v9:
time: 32.1 us; the launch traced here: 31.8 us
  starting transfers between devices  15 us (47%)
  Pallas kernels  14.3 us (45%)
  waiting for transfers between devices  1.62 us (5%)
  local copies, waits for them, and re-layouts  0.74 us (2%)
    ppermute x12, starting transfers between devices, swapped(): return lax.ppermute(x, axis, [(i, i ^ j) for i in range(n)])  15 us
    pallas_call x1, Pallas kernels, attend_resident(): pl.pallas_call(functools.partial(resident_kernel, ranks), in_specs=[HBM]...  7.95 us
    pallas_call x1, Pallas kernels, project(): pl.pallas_call(functools.partial(project_kernel, ranks, group), in_specs=...  4.12 us
    ppermute x12, waiting for transfers between devices, swapped(): return lax.ppermute(x, axis, [(i, i ^ j) for i in range(n)])  1.62 us
    pallas_call x1, Pallas kernels, prepare(): pl.pallas_call(functools.partial(prepare_kernel, insts, residents, kv_min...  0.78 us
    unnamed x16, local copies, waits for them, and re-layouts  0.74 us
    pallas_call x1, Pallas kernels, finish(): pl.pallas_call(finish_kernel, in_specs=[VMEM] * (2 + len(moved)), out_spe...  0.67 us
  transfers between devices with their start and end apart: 12, of which 2 were waited for; matrix products, arithmetic and copies ran while one was open for 0% of the time, Pallas kernels for 30%

profile of v9, /device:TPU:0, one launch (start us, length us, event | category | flops | bytes accessed | tf_op | source)
XLA Modules:
  0.0 31.8 jit_solution(12854587190269887735)
XLA Ops:
  0.0 4.1 %project.1 = (bf16[136,512]{1,0:T(8,128)(2,1)}, bf16[136,512]{1,0:T(8,128)(2,1)}, bf16[136,512]{1,0:T(8,128)(2,1)}, bf16[136,512]{1,0:T(8,128)(2,1)}, bf16[5,2560]{1,0:T(8,128)(2,1)}) custom-call(bf16[1280]{0:T(1024)(128)(2,1)} %gain_hbm.1, bf16[64,2,1280]{2,1,0:T(2,128)(2,1)} %bitcast.16, bf16[1280,2048]{1,0:T(8,128)(2,1)} %w_hbm.1, ...), custom_call_target="tpu_custom_call" | custom-call | flops 671088640 | bytes 5242880 | tf_op jit(solution)/shard_map/project/pallas_call | solution.py:132
  4.1 0.5 %collective-permute-start = (bf16[5,2560]{1,0:T(8,128)(2,1)}, bf16[5,2560]{1,0:T(8,128)(2,1)S(1)}, u32[]{:S(2)}, u32[]{:S(2)}) collective-permute-start(bf16[5,2560]{1,0:T(8,128)(2,1)} %get-tuple-element.25.ask_ref), channel_id=1, source_target_pairs={{0,4},{4,0},{8,12},{12,8},{1,5},{5,1},{9,13},{13,9},{2,6},{6,2},{1... | collective-permute-start | bytes 76808 | tf_op jit(solution)/shard_map/ppermute | solution.py:545
  4.6 4.7 %collective-permute-start.6 = (bf16[136,512]{1,0:T(8,128)(2,1)}, bf16[136,512]{1,0:T(8,128)(2,1)S(1)}, u32[]{:S(2)}, u32[]{:S(2)}) collective-permute-start(bf16[136,512]{1,0:T(8,128)(2,1)} %get-tuple-element.42), channel_id=1, source_target_pairs={{0,3},{1,2},{2,1},{3,0},{4,7},{5,6},{6,5},{7,4},{8,11},{9,10},{10,... | collective-permute-start | bytes 417800 | tf_op jit(solution)/shard_map/ppermute | solution.py:545
  9.3 0.0 collective-permute-done.rest_0_
  9.3 0.3 %collective-permute-start.7 = (bf16[136,512]{1,0:T(8,128)(2,1)}, bf16[136,512]{1,0:T(8,128)(2,1)S(1)}, u32[]{:S(2)}, u32[]{:S(2)}) collective-permute-start(bf16[136,512]{1,0:T(8,128)(2,1)} %get-tuple-element.43), channel_id=1, source_target_pairs={{0,2},{1,3},{2,0},{3,1},{4,6},{5,7},{6,4},{7,5},{8,10},{9,11},{10,... | collective-permute-start | bytes 417800 | tf_op jit(solution)/shard_map/ppermute | solution.py:545
  9.7 1.6 %collective-permute-start.8 = (bf16[136,512]{1,0:T(8,128)(2,1)}, bf16[136,512]{1,0:T(8,128)(2,1)S(1)}, u32[]{:S(2)}, u32[]{:S(2)}) collective-permute-start(bf16[136,512]{1,0:T(8,128)(2,1)} %get-tuple-element.44), channel_id=1, source_target_pairs={{0,1},{1,0},{2,3},{3,2},{4,5},{5,4},{6,7},{7,6},{8,9},{9,8},{10,11... | collective-permute-start | bytes 417800 | tf_op jit(solution)/shard_map/ppermute | solution.py:545
  11.2 1.5 %collective-permute-start.1 = (bf16[5,2560]{1,0:T(8,128)(2,1)}, bf16[5,2560]{1,0:T(8,128)(2,1)S(1)}, u32[]{:S(2)}, u32[]{:S(2)}) collective-permute-start(bf16[5,2560]{1,0:T(8,128)(2,1)} %get-tuple-element.25.ask_ref), channel_id=1, source_target_pairs={{0,8},{4,12},{8,0},{12,4},{1,9},{5,13},{9,1},{13,5},{2,10},{6,14},... | collective-permute-start | bytes 76808 | tf_op jit(solution)/shard_map/ppermute | solution.py:545
  12.7 0.0 collective-permute-start.2
  12.7 0.0 copy-start.1
  12.7 0.0 copy-start.2
  12.7 0.0 copy-start.5
  12.7 0.0 copy-start.6
  12.8 0.0 copy-start.7
  12.8 0.0 copy-start
  12.8 0.0 copy-start.3
  12.8 8.0 %attend_resident.1 = (bf16[64,128]{1,0:T(8,128)(2,1)}, bf16[64,128]{1,0:T(8,128)(2,1)}, bf16[64,128]{1,0:T(8,128)(2,1)}, bf16[64,128]{1,0:T(8,128)(2,1)}) custom-call(s32[1,3]{1,0:T(1,128)} %len_hbm.1, bf16[5,8192]{1,0:T(8,128)(2,1)} %bitcast.15, bf16[3,1024,1024]{2,1,0:T(8,128)(2,1)} %bitcast.12, bf16[3,1024,1024]{2,1,0:T(8,128)(2,1)} %bitcast.13), custom_call_target="tpu_custom_call" | custom-call | flops 100663296 | bytes 12582912 | tf_op jit(solution)/shard_map/attend_resident/pallas_call | solution.py:261
  20.7 0.0 collective-permute-done.1.rest_1_
  20.8 2.5 %collective-permute-start.3 = (bf16[64,128]{1,0:T(8,128)(2,1)}, bf16[64,128]{1,0:T(8,128)(2,1)S(1)}, u32[]{:S(2)}, u32[]{:S(2)}) collective-permute-start(bf16[64,128]{1,0:T(8,128)(2,1)} %get-tuple-element.32), channel_id=1, source_target_pairs={{0,3},{1,2},{2,1},{3,0},{4,7},{5,6},{6,5},{7,4},{8,11},{9,10},{10,... | collective-permute-start | bytes 49160 | tf_op jit(solution)/shard_map/ppermute | solution.py:545
  23.3 0.0 collective-permute-done.2.rest_2_
  23.3 0.0 collective-permute-start.4
  23.3 0.0 collective-permute-done.6.rest_1_
  23.3 1.9 %collective-permute-start.5 = (bf16[64,128]{1,0:T(8,128)(2,1)}, bf16[64,128]{1,0:T(8,128)(2,1)S(1)}, u32[]{:S(2)}, u32[]{:S(2)}) collective-permute-start(bf16[64,128]{1,0:T(8,128)(2,1)} %get-tuple-element.34), channel_id=1, source_target_pairs={{0,1},{1,0},{2,3},{3,2},{4,5},{5,4},{6,7},{7,6},{8,9},{9,8},{10,11... | collective-permute-start | bytes 49160 | tf_op jit(solution)/shard_map/ppermute | solution.py:545
  25.2 0.0 copy-done.1
  25.2 0.0 copy-done.2
  25.2 0.0 copy-done.5
  25.2 0.0 copy-done.6
  25.2 0.0 copy-done.7
  25.3 0.8 %prepare.1 = (bf16[32,128]{1,0:T(8,128)(2,1)S(1)}, f32[2,32,128]{2,1,0:T(8,128)S(1)}, s32[32,128]{1,0:T(8,128)S(1)}, f32[128,128]{1,0:T(8,128)S(1)}, f32[128,128]{1,0:T(8,128)S(1)}, /*index=5*/s32[8,128]{1,0:T(8,128)S(1)}) custom-call(s32[2,4]{1,0:T(2,128)S(1)} %bitcast.9, s32[2,4]{1,0:T(2,128)S(1)} %bitcast.10, bf16[1,128]{1,0:T(2,128)(2,1)S(1)} %bitcast.11, ...), custom_call_target="tpu_custom_call" | custom-call | tf_op jit(solution)/shard_map/prepare/pallas_call | solution.py:364
  26.0 0.0 collective-permute-done.7.rest_2_
  26.0 0.0 collective-permute-done.8.rest_3_
  26.1 0.0 copy-done
  26.1 0.6 %attend_moved.1 = bf16[2,2048]{1,0:T(2,128)(2,1)S(1)} custom-call(bf16[32,128]{1,0:T(8,128)(2,1)S(1)} %get-tuple-element.36.q_ref, f32[2,32,128]{2,1,0:T(8,128)S(1)} %get-tuple-element.37.own_ref, s32[32,128]{1,0:T(8,128)S(1)} %get-tuple-element.38.limit_ref, f32[128,128]{1,0:T(8,128)S(1)} %get-tuple-element.39.cos_ref, ...), custom_call_target="tpu_custom_call" | custom-call | flops 33554432 | bytes 4194304 | tf_op jit(solution)/shard_map/attend_moved/pallas_call | solution.py:456
  26.7 0.1 collective-permute-start.9
  26.8 1.3 %collective-permute-start.10 = (bf16[2,2048]{1,0:T(2,128)(2,1)S(1)}, bf16[2,2048]{1,0:T(2,128)(2,1)S(1)}, u32[]{:S(2)}, u32[]{:S(2)}) collective-permute-start(bf16[2,2048]{1,0:T(2,128)(2,1)S(1)} %attend_moved.1), channel_id=1, source_target_pairs={{0,8},{4,12},{8,0},{12,4},{1,9},{5,13},{9,1},{13,5},{2,10},{6,14},... | collective-permute-start | bytes 24584 | tf_op jit(solution)/shard_map/ppermute | solution.py:545
  28.1 0.0 collective-permute-done.3.rest_1_
  28.1 0.6 %collective-permute-start.11 = (bf16[2,2048]{1,0:T(2,128)(2,1)S(1)}, bf16[2,2048]{1,0:T(2,128)(2,1)S(1)}, u32[]{:S(2)}, u32[]{:S(2)}) collective-permute-start(bf16[2,2048]{1,0:T(2,128)(2,1)S(1)} %attend_moved.1), channel_id=1, source_target_pairs={{0,12},{4,8},{8,4},{12,0},{1,13},{5,9},{9,5},{13,1},{2,14},{6,10},... | collective-permute-start | bytes 24584 | tf_op jit(solution)/shard_map/ppermute | solution.py:545
  28.7 0.0 collective-permute-done.4.rest_2_
  28.7 0.0 collective-permute-done.5.rest_3_
  28.7 0.0 copy-done.3
  28.7 0.0 copy-start.4
  28.7 0.7 %copy-done.4 = bf16[64,128]{1,0:T(8,128)(2,1)S(1)} copy-done((bf16[64,128]{1,0:T(8,128)(2,1)S(1)}, bf16[64,128]{1,0:T(8,128)(2,1)}, u32[]{:S(2)}) %copy-start.4) | copy-done | bytes 16408
  29.4 0.2 combine_resident.1.kept_ref
  29.6 0.0 collective-permute-done.9.rest_0_
  29.6 0.9 %collective-permute-done.10.rest_1_ = bf16[2,2048]{1,0:T(2,128)(2,1)S(1)} collective-permute-done((bf16[2,2048]{1,0:T(2,128)(2,1)S(1)}, bf16[2,2048]{1,0:T(2,128)(2,1)S(1)}, u32[]{:S(2)}, u32[]{:S(2)}) %collective-permute-start.10) | collective-permute-done | bytes 8224 | tf_op jit(solution)/shard_map/ppermute | solution.py:545
  30.5 0.7 %collective-permute-done.11.rest_2_ = bf16[2,2048]{1,0:T(2,128)(2,1)S(1)} collective-permute-done((bf16[2,2048]{1,0:T(2,128)(2,1)S(1)}, bf16[2,2048]{1,0:T(2,128)(2,1)S(1)}, u32[]{:S(2)}, u32[]{:S(2)}) %collective-permute-start.11) | collective-permute-done | bytes 8224 | tf_op jit(solution)/shard_map/ppermute | solution.py:545
  31.2 0.7 %finish.1 = bf16[5,2048]{1,0:T(8,128)(2,1)} custom-call(f32[3,2048]{1,0:T(4,128)S(1)} %combine_resident.1.kept_ref, s32[8,128]{1,0:T(8,128)S(1)} %get-tuple-element.35.place_ref, bf16[2,2048]{1,0:T(2,128)(2,1)S(1)} %collective-permute-done.9.rest_0_, bf16[2,2048]{1,0:T(2,128)(2,1)S(1)} %collective-permute-done.10.rest_1_, ...), custom_call_target="tpu_custom_call" | custom-call | tf_op jit(solution)/shard_map/finish/pallas_call | solution.py:534
Async XLA Ops:
  4.1 5.2 %collective-permute-start = (bf16[5,2560]{1,0:T(8,128)(2,1)}, bf16[5,2560]{1,0:T(8,128)(2,1)S(1)}, u32[]{:S(2)}, u32[]{:S(2)}) collective-permute-start(bf16[5,2560]{1,0:T(8,128)(2,1)} %get-tuple-element.25.ask_ref), channel_id=1, source_target_pairs={{0,4},{4,0},{8,12},{12,8},{1,5},{5,1},{9,13},{13,9},{2,6},{6,2},{1... | collective-permute-start | bytes 76808 | tf_op jit(solution)/shard_map/ppermute | solution.py:545
  4.6 18.7 %collective-permute-start.6 = (bf16[136,512]{1,0:T(8,128)(2,1)}, bf16[136,512]{1,0:T(8,128)(2,1)S(1)}, u32[]{:S(2)}, u32[]{:S(2)}) collective-permute-start(bf16[136,512]{1,0:T(8,128)(2,1)} %get-tuple-element.42), channel_id=1, source_target_pairs={{0,3},{1,2},{2,1},{3,0},{4,7},{5,6},{6,5},{7,4},{8,11},{9,10},{10,... | collective-permute-start | bytes 417800 | tf_op jit(solution)/shard_map/ppermute | solution.py:545
  9.3 16.7 %collective-permute-start.7 = (bf16[136,512]{1,0:T(8,128)(2,1)}, bf16[136,512]{1,0:T(8,128)(2,1)S(1)}, u32[]{:S(2)}, u32[]{:S(2)}) collective-permute-start(bf16[136,512]{1,0:T(8,128)(2,1)} %get-tuple-element.43), channel_id=1, source_target_pairs={{0,2},{1,3},{2,0},{3,1},{4,6},{5,7},{6,4},{7,5},{8,10},{9,11},{10,... | collective-permute-start | bytes 417800 | tf_op jit(solution)/shard_map/ppermute | solution.py:545
  9.7 16.4 %collective-permute-start.8 = (bf16[136,512]{1,0:T(8,128)(2,1)}, bf16[136,512]{1,0:T(8,128)(2,1)S(1)}, u32[]{:S(2)}, u32[]{:S(2)}) collective-permute-start(bf16[136,512]{1,0:T(8,128)(2,1)} %get-tuple-element.44), channel_id=1, source_target_pairs={{0,1},{1,0},{2,3},{3,2},{4,5},{5,4},{6,7},{7,6},{8,9},{9,8},{10,11... | collective-permute-start | bytes 417800 | tf_op jit(solution)/shard_map/ppermute | solution.py:545
  11.2 9.5 %collective-permute-start.1 = (bf16[5,2560]{1,0:T(8,128)(2,1)}, bf16[5,2560]{1,0:T(8,128)(2,1)S(1)}, u32[]{:S(2)}, u32[]{:S(2)}) collective-permute-start(bf16[5,2560]{1,0:T(8,128)(2,1)} %get-tuple-element.25.ask_ref), channel_id=1, source_target_pairs={{0,8},{4,12},{8,0},{12,4},{1,9},{5,13},{9,1},{13,5},{2,10},{6,14},... | collective-permute-start | bytes 76808 | tf_op jit(solution)/shard_map/ppermute | solution.py:545
  12.7 10.6 %collective-permute-start.2 = (bf16[5,2560]{1,0:T(8,128)(2,1)}, bf16[5,2560]{1,0:T(8,128)(2,1)S(1)}, u32[]{:S(2)}, u32[]{:S(2)}) collective-permute-start(bf16[5,2560]{1,0:T(8,128)(2,1)} %get-tuple-element.25.ask_ref), channel_id=1, source_target_pairs={{0,12},{4,8},{8,4},{12,0},{1,13},{5,9},{9,5},{13,1},{2,14},{6,10},... | collective-permute-start | bytes 76808 | tf_op jit(solution)/shard_map/ppermute | solution.py:545
  12.7 12.5 %copy-start.1 = (f32[128,128]{1,0:T(8,128)S(1)}, f32[128,128]{1,0:T(8,128)}, u32[]{:S(2)}) copy-start(f32[128,128]{1,0:T(8,128)} %constant.4.clone.cos_ref) | copy-start | bytes 196612
  12.7 12.5 %copy-start.2 = (f32[128,128]{1,0:T(8,128)S(1)}, f32[128,128]{1,0:T(8,128)}, u32[]{:S(2)}) copy-start(f32[128,128]{1,0:T(8,128)} %constant.5.clone.sin_ref) | copy-start | bytes 196612
  12.7 12.5 %copy-start.5 = (s32[4,2]{0,1:T(2,128)S(1)}, s32[4,2]{0,1:T(2,128)}, u32[]{:S(2)}) copy-start(s32[4,2]{0,1:T(2,128)} %param.14) | copy-start | bytes 100
  12.7 12.5 %copy-start.6 = (s32[4,2]{0,1:T(2,128)S(1)}, s32[4,2]{0,1:T(2,128)}, u32[]{:S(2)}) copy-start(s32[4,2]{0,1:T(2,128)} %param.15) | copy-start | bytes 100
  12.8 12.5 %copy-start.7 = (bf16[128]{0:T(256)(128)(2,1)S(1)}, bf16[128]{0:T(256)(128)(2,1)}, u32[]{:S(2)}) copy-start(bf16[128]{0:T(256)(128)(2,1)} %param.18) | copy-start | bytes 772
  12.8 13.3 %copy-start = (bf16[136,512]{1,0:T(8,128)(2,1)S(1)}, bf16[136,512]{1,0:T(8,128)(2,1)}, u32[]{:S(2)}) copy-start(bf16[136,512]{1,0:T(8,128)(2,1)} %get-tuple-element.41.rest_0_) | copy-start | bytes 417796
  12.8 15.9 %copy-start.3 = (bf16[5,2560]{1,0:T(8,128)(2,1)S(1)}, bf16[5,2560]{1,0:T(8,128)(2,1)}, u32[]{:S(2)}) copy-start(bf16[5,2560]{1,0:T(8,128)(2,1)} %get-tuple-element.25.ask_ref) | copy-start | bytes 76804
  20.8 7.3 %collective-permute-start.3 = (bf16[64,128]{1,0:T(8,128)(2,1)}, bf16[64,128]{1,0:T(8,128)(2,1)S(1)}, u32[]{:S(2)}, u32[]{:S(2)}) collective-permute-start(bf16[64,128]{1,0:T(8,128)(2,1)} %get-tuple-element.32), channel_id=1, source_target_pairs={{0,3},{1,2},{2,1},{3,0},{4,7},{5,6},{6,5},{7,4},{8,11},{9,10},{10,... | collective-permute-start | bytes 49160 | tf_op jit(solution)/shard_map/ppermute | solution.py:545
  23.3 5.4 %collective-permute-start.4 = (bf16[64,128]{1,0:T(8,128)(2,1)}, bf16[64,128]{1,0:T(8,128)(2,1)S(1)}, u32[]{:S(2)}, u32[]{:S(2)}) collective-permute-start(bf16[64,128]{1,0:T(8,128)(2,1)} %get-tuple-element.33), channel_id=1, source_target_pairs={{0,2},{1,3},{2,0},{3,1},{4,6},{5,7},{6,4},{7,5},{8,10},{9,11},{10,... | collective-permute-start | bytes 49160 | tf_op jit(solution)/shard_map/ppermute | solution.py:545
  23.3 5.3 %collective-permute-start.5 = (bf16[64,128]{1,0:T(8,128)(2,1)}, bf16[64,128]{1,0:T(8,128)(2,1)S(1)}, u32[]{:S(2)}, u32[]{:S(2)}) collective-permute-start(bf16[64,128]{1,0:T(8,128)(2,1)} %get-tuple-element.34), channel_id=1, source_target_pairs={{0,1},{1,0},{2,3},{3,2},{4,5},{5,4},{6,7},{7,6},{8,9},{9,8},{10,11... | collective-permute-start | bytes 49160 | tf_op jit(solution)/shard_map/ppermute | solution.py:545
  26.7 2.8 %collective-permute-start.9 = (bf16[2,2048]{1,0:T(2,128)(2,1)S(1)}, bf16[2,2048]{1,0:T(2,128)(2,1)S(1)}, u32[]{:S(2)}, u32[]{:S(2)}) collective-permute-start(bf16[2,2048]{1,0:T(2,128)(2,1)S(1)} %attend_moved.1), channel_id=1, source_target_pairs={{0,4},{4,0},{8,12},{12,8},{1,5},{5,1},{9,13},{13,9},{2,6},{6,2},{1... | collective-permute-start | bytes 24584 | tf_op jit(solution)/shard_map/ppermute | solution.py:545
  26.8 3.7 %collective-permute-start.10 = (bf16[2,2048]{1,0:T(2,128)(2,1)S(1)}, bf16[2,2048]{1,0:T(2,128)(2,1)S(1)}, u32[]{:S(2)}, u32[]{:S(2)}) collective-permute-start(bf16[2,2048]{1,0:T(2,128)(2,1)S(1)} %attend_moved.1), channel_id=1, source_target_pairs={{0,8},{4,12},{8,0},{12,4},{1,9},{5,13},{9,1},{13,5},{2,10},{6,14},... | collective-permute-start | bytes 24584 | tf_op jit(solution)/shard_map/ppermute | solution.py:545
  28.1 3.1 %collective-permute-start.11 = (bf16[2,2048]{1,0:T(2,128)(2,1)S(1)}, bf16[2,2048]{1,0:T(2,128)(2,1)S(1)}, u32[]{:S(2)}, u32[]{:S(2)}) collective-permute-start(bf16[2,2048]{1,0:T(2,128)(2,1)S(1)} %attend_moved.1), channel_id=1, source_target_pairs={{0,12},{4,8},{8,4},{12,0},{1,13},{5,9},{9,5},{13,1},{2,14},{6,10},... | collective-permute-start | bytes 24584 | tf_op jit(solution)/shard_map/ppermute | solution.py:545
  28.7 0.7 %copy-start.4 = (bf16[64,128]{1,0:T(8,128)(2,1)S(1)}, bf16[64,128]{1,0:T(8,128)(2,1)}, u32[]{:S(2)}) copy-start(bf16[64,128]{1,0:T(8,128)(2,1)} %get-tuple-element.31.rest_0_) | copy-start | bytes 49156

commit v10 on v9

--- a/solution.py
+++ b/solution.py
@@ -198,7 +198,6 @@
         return jnp.sum(spread.reshape(ranks, heads_mine, 128), axis=1)
 
     q_copy.wait()
-    len_copy.wait()
     for h in range(heads):
         q_all[h * 8 : h * 8 + residents, :] = q_ref[:residents, h * 128 : (h + 1) * 128].astype(F32)
     peaks, totals = [], []
@@ -208,7 +207,6 @@
         wide_ref[...] = jnp.where(own_block, wide, jnp.zeros_like(wide))
         peaks.append([])
         totals.append([])
-        valid = position < len_ref[0:1, r : r + 1]
         for i in range(2):
             arrived(4 * r + i)
             at = slice(i * half, (i + 1) * half)
@@ -218,6 +216,9 @@
                 (((1,), (1,)), ((), ())),
                 preferred_element_type=F32,
             )
+        if r == 0:
+            len_copy.wait()
+        valid = position < len_ref[0:1, r : r + 1]
         for c in range(0, heads, 16):
             rows = slice(c, c + 16)
             scores = jnp.where(valid, s_buf[rows, :] * scale, ABSENT)
@@ -590,7 +591,7 @@
     others = [swapped(others[j - 1], "tp", j, ranks) for j in reversed(range(1, last))]
     pieces = [pieces[0], far] + others
     payloads = attend_resident(lengths, query[0], k_cache[0], v_cache[0], ranks)
-    own_payload = payloads[0]
+    own_payload = swapped(payloads[0], "tp", 0, ranks)
     payloads = [swapped(payloads[j], "tp", j, ranks) for j in reversed(range(1, ranks))]
     cos, sin = rotation(slots, requests, head_size)
     *prepared, places = prepare(

time: 32.1 us -> 35.8 us (1.12)
  waiting for transfers between devices: 1.62 us -> 5.35 us
  starting transfers between devices: 15 us -> 15.8 us
  local copies, waits for them, and re-layouts: 0.74 us -> 0.03 us
    ppermute x12 -> x13, waiting for transfers between devices: 1.62 us -> 5.35 us  [swapped(): return lax.ppermute(x, axis, [(i, i ^ j) for i in range(n)])]
    ppermute x12 -> x13, starting transfers between devices: 15 us -> 15.8 us  [swapped(): return lax.ppermute(x, axis, [(i, i ^ j) for i in range(n)])]
    unnamed x16 -> x14, local copies, waits for them, and re-layouts: 0.74 us -> 0.03 us
  transfers between devices with their start and end apart: 12 -> 13, of which waited for: 2 -> 3; matrix products, arithmetic and copies ran while one was open for 0% -> 0% of each run, Pallas kernels for 30% -> 27%
where the time goes in v10:
time: 35.8 us; the launch traced here: 35.6 us
  starting transfers between devices  15.8 us (44%)
  Pallas kernels  14.3 us (40%)
  waiting for transfers between devices  5.35 us (15%)
    ppermute x13, starting transfers between devices, swapped(): return lax.ppermute(x, axis, [(i, i ^ j) for i in range(n)])  15.8 us
    pallas_call x1, Pallas kernels, attend_resident(): pl.pallas_call(functools.partial(resident_kernel, ranks), in_specs=[HBM]...  7.9 us
    ppermute x13, waiting for transfers between devices, swapped(): return lax.ppermute(x, axis, [(i, i ^ j) for i in range(n)])  5.35 us
    pallas_call x1, Pallas kernels, project(): pl.pallas_call(functools.partial(project_kernel, ranks, group), in_specs=...  4.12 us
    pallas_call x1, Pallas kernels, prepare(): pl.pallas_call(functools.partial(prepare_kernel, insts, residents, kv_min...  0.78 us
  transfers between devices with their start and end apart: 13, of which 3 were waited for; matrix products, arithmetic and copies ran while one was open for 0% of the time, Pallas kernels for 27%

profile of v10, /device:TPU:0, one launch (start us, length us, event | category | flops | bytes accessed | tf_op | source)
XLA Modules:
  0.0 35.6 jit_solution(9181327771525186503)
XLA Ops:
  0.0 4.1 %project.1 = (bf16[136,512]{1,0:T(8,128)(2,1)}, bf16[136,512]{1,0:T(8,128)(2,1)}, bf16[136,512]{1,0:T(8,128)(2,1)}, bf16[136,512]{1,0:T(8,128)(2,1)}, bf16[5,2560]{1,0:T(8,128)(2,1)}) custom-call(bf16[1280]{0:T(1024)(128)(2,1)} %gain_hbm.1, bf16[64,2,1280]{2,1,0:T(2,128)(2,1)} %bitcast.16, bf16[1280,2048]{1,0:T(8,128)(2,1)} %w_hbm.1, ...), custom_call_target="tpu_custom_call" | custom-call | flops 671088640 | bytes 5242880 | tf_op jit(solution)/shard_map/project/pallas_call | solution.py:132
  4.1 0.5 %collective-permute-start = (bf16[5,2560]{1,0:T(8,128)(2,1)}, bf16[5,2560]{1,0:T(8,128)(2,1)S(1)}, u32[]{:S(2)}, u32[]{:S(2)}) collective-permute-start(bf16[5,2560]{1,0:T(8,128)(2,1)} %get-tuple-element.25.ask_ref), channel_id=1, source_target_pairs={{0,4},{4,0},{8,12},{12,8},{1,5},{5,1},{9,13},{13,9},{2,6},{6,2},{1... | collective-permute-start | bytes 76808 | tf_op jit(solution)/shard_map/ppermute | solution.py:546
  4.6 4.7 %collective-permute-start.7 = (bf16[136,512]{1,0:T(8,128)(2,1)}, bf16[136,512]{1,0:T(8,128)(2,1)S(1)}, u32[]{:S(2)}, u32[]{:S(2)}) collective-permute-start(bf16[136,512]{1,0:T(8,128)(2,1)} %get-tuple-element.42), channel_id=1, source_target_pairs={{0,3},{1,2},{2,1},{3,0},{4,7},{5,6},{6,5},{7,4},{8,11},{9,10},{10,... | collective-permute-start | bytes 417800 | tf_op jit(solution)/shard_map/ppermute | solution.py:546
  9.3 0.0 collective-permute-done.rest_0_
  9.3 0.3 collective-permute-start.8
  9.7 1.6 %collective-permute-start.9 = (bf16[136,512]{1,0:T(8,128)(2,1)}, bf16[136,512]{1,0:T(8,128)(2,1)S(1)}, u32[]{:S(2)}, u32[]{:S(2)}) collective-permute-start(bf16[136,512]{1,0:T(8,128)(2,1)} %get-tuple-element.44), channel_id=1, source_target_pairs={{0,1},{1,0},{2,3},{3,2},{4,5},{5,4},{6,7},{7,6},{8,9},{9,8},{10,11... | collective-permute-start | bytes 417800 | tf_op jit(solution)/shard_map/ppermute | solution.py:546
  11.2 0.0 copy-start.3
  11.2 0.0 copy-start.1
  11.2 0.0 copy-start.2
  11.2 0.0 copy-start.4
  11.2 0.0 copy-start.5
  11.3 0.0 copy-start.6
  11.3 0.0 copy-start
  11.3 7.9 %attend_resident.1 = (bf16[64,128]{1,0:T(8,128)(2,1)}, bf16[64,128]{1,0:T(8,128)(2,1)}, bf16[64,128]{1,0:T(8,128)(2,1)}, bf16[64,128]{1,0:T(8,128)(2,1)}) custom-call(s32[1,3]{1,0:T(1,128)} %len_hbm.1, bf16[5,8192]{1,0:T(8,128)(2,1)} %bitcast.15, bf16[3,1024,1024]{2,1,0:T(8,128)(2,1)} %bitcast.12, bf16[3,1024,1024]{2,1,0:T(8,128)(2,1)} %bitcast.13), custom_call_target="tpu_custom_call" | custom-call | flops 100663296 | bytes 12582912 | tf_op jit(solution)/shard_map/attend_resident/pallas_call | solution.py:262
  19.2 0.7 %collective-permute-start.3 = (bf16[64,128]{1,0:T(8,128)(2,1)}, bf16[64,128]{1,0:T(8,128)(2,1)S(1)}, u32[]{:S(2)}, u32[]{:S(2)}) collective-permute-start(bf16[64,128]{1,0:T(8,128)(2,1)} %get-tuple-element.30), channel_id=1, source_target_pairs={{0,0},{1,1},{2,2},{3,3},{4,4},{5,5},{6,6},{7,7},{8,8},{9,9},{10,10... | collective-permute-start | bytes 49160 | tf_op jit(solution)/shard_map/ppermute | solution.py:546
  19.9 0.0 copy-done.3
  19.9 1.5 %collective-permute-start.1 = (bf16[5,2560]{1,0:T(8,128)(2,1)S(1)}, bf16[5,2560]{1,0:T(8,128)(2,1)S(1)}, u32[]{:S(2)}, u32[]{:S(2)}) collective-permute-start(bf16[5,2560]{1,0:T(8,128)(2,1)S(1)} %copy-done.3), channel_id=1, source_target_pairs={{0,8},{4,12},{8,0},{12,4},{1,9},{5,13},{9,1},{13,5},{2,10},{6,14},... | collective-permute-start | bytes 76808 | tf_op jit(solution)/shard_map/ppermute | solution.py:546
  21.4 0.0 collective-permute-done.3.rest_0_
  21.4 0.0 collective-permute-start.2
  21.4 2.5 %collective-permute-done.1.rest_1_ = bf16[5,2560]{1,0:T(8,128)(2,1)S(1)} collective-permute-done((bf16[5,2560]{1,0:T(8,128)(2,1)S(1)}, bf16[5,2560]{1,0:T(8,128)(2,1)S(1)}, u32[]{:S(2)}, u32[]{:S(2)}) %collective-permute-start.1) | collective-permute-done | bytes 25632 | tf_op jit(solution)/shard_map/ppermute | solution.py:546
  23.9 2.5 %collective-permute-start.4 = (bf16[64,128]{1,0:T(8,128)(2,1)}, bf16[64,128]{1,0:T(8,128)(2,1)S(1)}, u32[]{:S(2)}, u32[]{:S(2)}) collective-permute-start(bf16[64,128]{1,0:T(8,128)(2,1)} %get-tuple-element.32), channel_id=1, source_target_pairs={{0,3},{1,2},{2,1},{3,0},{4,7},{5,6},{6,5},{7,4},{8,11},{9,10},{10,... | collective-permute-start | bytes 49160 | tf_op jit(solution)/shard_map/ppermute | solution.py:546
  26.4 0.0 collective-permute-done.2.rest_2_
  26.4 0.0 collective-permute-start.5
  26.4 0.0 collective-permute-done.7.rest_1_
  26.4 1.9 %collective-permute-start.6 = (bf16[64,128]{1,0:T(8,128)(2,1)}, bf16[64,128]{1,0:T(8,128)(2,1)S(1)}, u32[]{:S(2)}, u32[]{:S(2)}) collective-permute-start(bf16[64,128]{1,0:T(8,128)(2,1)} %get-tuple-element.34), channel_id=1, source_target_pairs={{0,1},{1,0},{2,3},{3,2},{4,5},{5,4},{6,7},{7,6},{8,9},{9,8},{10,11... | collective-permute-start | bytes 49160 | tf_op jit(solution)/shard_map/ppermute | solution.py:546
  28.3 0.0 copy-done.1
  28.3 0.0 copy-done.2
  28.3 0.0 copy-done.4
  28.3 0.0 copy-done.5
  28.3 0.0 copy-done.6
  28.3 0.8 %prepare.1 = (bf16[32,128]{1,0:T(8,128)(2,1)S(1)}, f32[2,32,128]{2,1,0:T(8,128)S(1)}, s32[32,128]{1,0:T(8,128)S(1)}, f32[128,128]{1,0:T(8,128)S(1)}, f32[128,128]{1,0:T(8,128)S(1)}, /*index=5*/s32[8,128]{1,0:T(8,128)S(1)}) custom-call(s32[2,4]{1,0:T(2,128)S(1)} %bitcast.9, s32[2,4]{1,0:T(2,128)S(1)} %bitcast.10, bf16[1,128]{1,0:T(2,128)(2,1)S(1)} %bitcast.11, ...), custom_call_target="tpu_custom_call" | custom-call | tf_op jit(solution)/shard_map/prepare/pallas_call | solution.py:365
  29.1 0.0 collective-permute-done.8.rest_2_
  29.1 0.0 collective-permute-done.9.rest_3_
  29.1 0.0 copy-done
  29.1 0.6 %attend_moved.1 = bf16[2,2048]{1,0:T(2,128)(2,1)S(1)} custom-call(bf16[32,128]{1,0:T(8,128)(2,1)S(1)} %get-tuple-element.36.q_ref, f32[2,32,128]{2,1,0:T(8,128)S(1)} %get-tuple-element.37.own_ref, s32[32,128]{1,0:T(8,128)S(1)} %get-tuple-element.38.limit_ref, f32[128,128]{1,0:T(8,128)S(1)} %get-tuple-element.39.cos_ref, ...), custom_call_target="tpu_custom_call" | custom-call | flops 33554432 | bytes 4194304 | tf_op jit(solution)/shard_map/attend_moved/pallas_call | solution.py:457
  29.8 0.1 collective-permute-start.10
  29.9 2.0 %collective-permute-start.11 = (bf16[2,2048]{1,0:T(2,128)(2,1)S(1)}, bf16[2,2048]{1,0:T(2,128)(2,1)S(1)}, u32[]{:S(2)}, u32[]{:S(2)}) collective-permute-start(bf16[2,2048]{1,0:T(2,128)(2,1)S(1)} %attend_moved.1), channel_id=1, source_target_pairs={{0,8},{4,12},{8,0},{12,4},{1,9},{5,13},{9,1},{13,5},{2,10},{6,14},... | collective-permute-start | bytes 24584 | tf_op jit(solution)/shard_map/ppermute | solution.py:546
  31.8 0.0 collective-permute-done.4.rest_1_
  31.8 0.1 collective-permute-start.12
  31.9 0.0 collective-permute-done.5.rest_2_
  31.9 0.0 collective-permute-done.6.rest_3_
  31.9 0.2 combine_resident.1.kept_ref
  32.1 0.0 collective-permute-done.10.rest_0_
  32.1 1.5 %collective-permute-done.11.rest_1_ = bf16[2,2048]{1,0:T(2,128)(2,1)S(1)} collective-permute-done((bf16[2,2048]{1,0:T(2,128)(2,1)S(1)}, bf16[2,2048]{1,0:T(2,128)(2,1)S(1)}, u32[]{:S(2)}, u32[]{:S(2)}) %collective-permute-start.11) | collective-permute-done | bytes 8224 | tf_op jit(solution)/shard_map/ppermute | solution.py:546
  33.6 1.3 %collective-permute-done.12.rest_2_ = bf16[2,2048]{1,0:T(2,128)(2,1)S(1)} collective-permute-done((bf16[2,2048]{1,0:T(2,128)(2,1)S(1)}, bf16[2,2048]{1,0:T(2,128)(2,1)S(1)}, u32[]{:S(2)}, u32[]{:S(2)}) %collective-permute-start.12) | collective-permute-done | bytes 8224 | tf_op jit(solution)/shard_map/ppermute | solution.py:546
  34.9 0.7 %finish.1 = bf16[5,2048]{1,0:T(8,128)(2,1)} custom-call(f32[3,2048]{1,0:T(4,128)S(1)} %combine_resident.1.kept_ref, s32[8,128]{1,0:T(8,128)S(1)} %get-tuple-element.35.place_ref, bf16[2,2048]{1,0:T(2,128)(2,1)S(1)} %collective-permute-done.10.rest_0_, bf16[2,2048]{1,0:T(2,128)(2,1)S(1)} %collective-permute-done.11.rest_1_, ...), custom_call_target="tpu_custom_call" | custom-call | tf_op jit(solution)/shard_map/finish/pallas_call | solution.py:535
Async XLA Ops:
  4.1 5.2 %collective-permute-start = (bf16[5,2560]{1,0:T(8,128)(2,1)}, bf16[5,2560]{1,0:T(8,128)(2,1)S(1)}, u32[]{:S(2)}, u32[]{:S(2)}) collective-permute-start(bf16[5,2560]{1,0:T(8,128)(2,1)} %get-tuple-element.25.ask_ref), channel_id=1, source_target_pairs={{0,4},{4,0},{8,12},{12,8},{1,5},{5,1},{9,13},{13,9},{2,6},{6,2},{1... | collective-permute-start | bytes 76808 | tf_op jit(solution)/shard_map/ppermute | solution.py:546
  4.6 21.8 %collective-permute-start.7 = (bf16[136,512]{1,0:T(8,128)(2,1)}, bf16[136,512]{1,0:T(8,128)(2,1)S(1)}, u32[]{:S(2)}, u32[]{:S(2)}) collective-permute-start(bf16[136,512]{1,0:T(8,128)(2,1)} %get-tuple-element.42), channel_id=1, source_target_pairs={{0,3},{1,2},{2,1},{3,0},{4,7},{5,6},{6,5},{7,4},{8,11},{9,10},{10,... | collective-permute-start | bytes 417800 | tf_op jit(solution)/shard_map/ppermute | solution.py:546
  9.3 19.8 %collective-permute-start.8 = (bf16[136,512]{1,0:T(8,128)(2,1)}, bf16[136,512]{1,0:T(8,128)(2,1)S(1)}, u32[]{:S(2)}, u32[]{:S(2)}) collective-permute-start(bf16[136,512]{1,0:T(8,128)(2,1)} %get-tuple-element.43), channel_id=1, source_target_pairs={{0,2},{1,3},{2,0},{3,1},{4,6},{5,7},{6,4},{7,5},{8,10},{9,11},{10,... | collective-permute-start | bytes 417800 | tf_op jit(solution)/shard_map/ppermute | solution.py:546
  9.7 19.5 %collective-permute-start.9 = (bf16[136,512]{1,0:T(8,128)(2,1)}, bf16[136,512]{1,0:T(8,128)(2,1)S(1)}, u32[]{:S(2)}, u32[]{:S(2)}) collective-permute-start(bf16[136,512]{1,0:T(8,128)(2,1)} %get-tuple-element.44), channel_id=1, source_target_pairs={{0,1},{1,0},{2,3},{3,2},{4,5},{5,4},{6,7},{7,6},{8,9},{9,8},{10,11... | collective-permute-start | bytes 417800 | tf_op jit(solution)/shard_map/ppermute | solution.py:546
  11.2 8.7 %copy-start.3 = (bf16[5,2560]{1,0:T(8,128)(2,1)S(1)}, bf16[5,2560]{1,0:T(8,128)(2,1)}, u32[]{:S(2)}) copy-start(bf16[5,2560]{1,0:T(8,128)(2,1)} %get-tuple-element.25.ask_ref) | copy-start | bytes 76804
  11.2 17.1 %copy-start.1 = (f32[128,128]{1,0:T(8,128)S(1)}, f32[128,128]{1,0:T(8,128)}, u32[]{:S(2)}) copy-start(f32[128,128]{1,0:T(8,128)} %constant.4.clone.cos_ref) | copy-start | bytes 196612
  11.2 17.1 %copy-start.2 = (f32[128,128]{1,0:T(8,128)S(1)}, f32[128,128]{1,0:T(8,128)}, u32[]{:S(2)}) copy-start(f32[128,128]{1,0:T(8,128)} %constant.5.clone.sin_ref) | copy-start | bytes 196612
  11.2 17.1 %copy-start.4 = (s32[4,2]{0,1:T(2,128)S(1)}, s32[4,2]{0,1:T(2,128)}, u32[]{:S(2)}) copy-start(s32[4,2]{0,1:T(2,128)} %param.14) | copy-start | bytes 100
  11.2 17.1 %copy-start.5 = (s32[4,2]{0,1:T(2,128)S(1)}, s32[4,2]{0,1:T(2,128)}, u32[]{:S(2)}) copy-start(s32[4,2]{0,1:T(2,128)} %param.15) | copy-start | bytes 100
  11.3 17.1 %copy-start.6 = (bf16[128]{0:T(256)(128)(2,1)S(1)}, bf16[128]{0:T(256)(128)(2,1)}, u32[]{:S(2)}) copy-start(bf16[128]{0:T(256)(128)(2,1)} %param.18) | copy-start | bytes 772
  11.3 17.9 %copy-start = (bf16[136,512]{1,0:T(8,128)(2,1)S(1)}, bf16[136,512]{1,0:T(8,128)(2,1)}, u32[]{:S(2)}) copy-start(bf16[136,512]{1,0:T(8,128)(2,1)} %get-tuple-element.41.rest_0_) | copy-start | bytes 417796
  19.2 2.2 %collective-permute-start.3 = (bf16[64,128]{1,0:T(8,128)(2,1)}, bf16[64,128]{1,0:T(8,128)(2,1)S(1)}, u32[]{:S(2)}, u32[]{:S(2)}) collective-permute-start(bf16[64,128]{1,0:T(8,128)(2,1)} %get-tuple-element.30), channel_id=1, source_target_pairs={{0,0},{1,1},{2,2},{3,3},{4,4},{5,5},{6,6},{7,7},{8,8},{9,9},{10,10... | collective-permute-start | bytes 49160 | tf_op jit(solution)/shard_map/ppermute | solution.py:546
  19.9 4.0 %collective-permute-start.1 = (bf16[5,2560]{1,0:T(8,128)(2,1)S(1)}, bf16[5,2560]{1,0:T(8,128)(2,1)S(1)}, u32[]{:S(2)}, u32[]{:S(2)}) collective-permute-start(bf16[5,2560]{1,0:T(8,128)(2,1)S(1)} %copy-done.3), channel_id=1, source_target_pairs={{0,8},{4,12},{8,0},{12,4},{1,9},{5,13},{9,1},{13,5},{2,10},{6,14},... | collective-permute-start | bytes 76808 | tf_op jit(solution)/shard_map/ppermute | solution.py:546
  21.4 5.0 %collective-permute-start.2 = (bf16[5,2560]{1,0:T(8,128)(2,1)S(1)}, bf16[5,2560]{1,0:T(8,128)(2,1)S(1)}, u32[]{:S(2)}, u32[]{:S(2)}) collective-permute-start(bf16[5,2560]{1,0:T(8,128)(2,1)S(1)} %copy-done.3), channel_id=1, source_target_pairs={{0,12},{4,8},{8,4},{12,0},{1,13},{5,9},{9,5},{13,1},{2,14},{6,10},... | collective-permute-start | bytes 76808 | tf_op jit(solution)/shard_map/ppermute | solution.py:546
  23.9 7.9 %collective-permute-start.4 = (bf16[64,128]{1,0:T(8,128)(2,1)}, bf16[64,128]{1,0:T(8,128)(2,1)S(1)}, u32[]{:S(2)}, u32[]{:S(2)}) collective-permute-start(bf16[64,128]{1,0:T(8,128)(2,1)} %get-tuple-element.32), channel_id=1, source_target_pairs={{0,3},{1,2},{2,1},{3,0},{4,7},{5,6},{6,5},{7,4},{8,11},{9,10},{10,... | collective-permute-start | bytes 49160 | tf_op jit(solution)/shard_map/ppermute | solution.py:546
  26.4 5.5 %collective-permute-start.5 = (bf16[64,128]{1,0:T(8,128)(2,1)}, bf16[64,128]{1,0:T(8,128)(2,1)S(1)}, u32[]{:S(2)}, u32[]{:S(2)}) collective-permute-start(bf16[64,128]{1,0:T(8,128)(2,1)} %get-tuple-element.33), channel_id=1, source_target_pairs={{0,2},{1,3},{2,0},{3,1},{4,6},{5,7},{6,4},{7,5},{8,10},{9,11},{10,... | collective-permute-start | bytes 49160 | tf_op jit(solution)/shard_map/ppermute | solution.py:546
  26.4 5.5 %collective-permute-start.6 = (bf16[64,128]{1,0:T(8,128)(2,1)}, bf16[64,128]{1,0:T(8,128)(2,1)S(1)}, u32[]{:S(2)}, u32[]{:S(2)}) collective-permute-start(bf16[64,128]{1,0:T(8,128)(2,1)} %get-tuple-element.34), channel_id=1, source_target_pairs={{0,1},{1,0},{2,3},{3,2},{4,5},{5,4},{6,7},{7,6},{8,9},{9,8},{10,11... | collective-permute-start | bytes 49160 | tf_op jit(solution)/shard_map/ppermute | solution.py:546
  29.8 2.3 %collective-permute-start.10 = (bf16[2,2048]{1,0:T(2,128)(2,1)S(1)}, bf16[2,2048]{1,0:T(2,128)(2,1)S(1)}, u32[]{:S(2)}, u32[]{:S(2)}) collective-permute-start(bf16[2,2048]{1,0:T(2,128)(2,1)S(1)} %attend_moved.1), channel_id=1, source_target_pairs={{0,4},{4,0},{8,12},{12,8},{1,5},{5,1},{9,13},{13,9},{2,6},{6,2},{1... | collective-permute-start | bytes 24584 | tf_op jit(solution)/shard_map/ppermute | solution.py:546
  29.9 3.7 %collective-permute-start.11 = (bf16[2,2048]{1,0:T(2,128)(2,1)S(1)}, bf16[2,2048]{1,0:T(2,128)(2,1)S(1)}, u32[]{:S(2)}, u32[]{:S(2)}) collective-permute-start(bf16[2,2048]{1,0:T(2,128)(2,1)S(1)} %attend_moved.1), channel_id=1, source_target_pairs={{0,8},{4,12},{8,0},{12,4},{1,9},{5,13},{9,1},{13,5},{2,10},{6,14},... | collective-permute-start | bytes 24584 | tf_op jit(solution)/shard_map/ppermute | solution.py:546
  31.8 3.1 %collective-permute-start.12 = (bf16[2,2048]{1,0:T(2,128)(2,1)S(1)}, bf16[2,2048]{1,0:T(2,128)(2,1)S(1)}, u32[]{:S(2)}, u32[]{:S(2)}) collective-permute-start(bf16[2,2048]{1,0:T(2,128)(2,1)S(1)} %attend_moved.1), channel_id=1, source_target_pairs={{0,12},{4,8},{8,4},{12,0},{1,13},{5,9},{9,5},{13,1},{2,14},{6,10},... | collective-permute-start | bytes 24584 | tf_op jit(solution)/shard_map/ppermute | solution.py:546

commit v11 on v9

--- a/solution.py
+++ b/solution.py
@@ -15,7 +15,6 @@
 BF16 = jnp.bfloat16
 MIB = 1024 * 1024
 CHUNK = 512
-AHEAD = 4
 
 VMEM = pl.BlockSpec(memory_space=pltpu.VMEM)
 SMEM = pl.BlockSpec(memory_space=pltpu.SMEM)
@@ -161,34 +160,29 @@
     ]
     residents, positions, width = k_buf.shape
     half = positions // 2
-    chunks = []
-    for r in range(residents):
-        for hbm, buf in ((k_hbm, k_buf), (v_hbm, v_buf)):
-            for i in range(2):
-                at = slice(i * half, (i + 1) * half)
-                chunks.append(
-                    pltpu.make_async_copy(
-                        hbm.at[r, at, :], buf.at[r, at, :], sems.at[len(chunks)]
-                    )
-                )
-    for chunk in chunks[:AHEAD]:
-        chunk.start()
-    q_copy = pltpu.make_async_copy(q_hbm, q_ref, in_sems.at[0])
-    len_copy = pltpu.make_async_copy(len_hbm, len_ref, in_sems.at[1])
+    halves = [slice(i * half, (i + 1) * half) for i in range(2)]
+
+    def copies(which, hbm, buf):
+        return [
+            [
+                pltpu.make_async_copy(hbm.at[r, at, :], buf.at[r, at, :], sems.at[which, r, i])
+                for i, at in enumerate(halves)
+            ]
+            for r in range(residents)
+        ]
+
+    k_copies, v_copies = copies(0, k_hbm, k_buf), copies(1, v_hbm, v_buf)
+    len_copy = pltpu.make_async_copy(len_hbm, len_ref, in_sems.at[0])
+    q_copy = pltpu.make_async_copy(q_hbm, q_ref, in_sems.at[1])
+    len_copy.start()
+    k_copies[0][0].start()
     q_copy.start()
-    len_copy.start()
-
-    def arrived(i):
-        chunks[i].wait()
-        if i + AHEAD < len(chunks):
-            chunks[i + AHEAD].start()
-
     heads = q_ref.shape[1] // 128
     kv_heads = width // 128
     group = heads // kv_heads
     heads_mine = heads // ranks
     rank = lax.axis_index("tp")
-    position = rank * positions + iota((16, positions), 1)
+    position = iota((16, positions), 1)
     scale = F32(1.0) / jnp.sqrt(F32(128.0))
     diagonal = iota((heads, 128), 0) % heads_mine == iota((heads, 128), 1)
     own_block = iota((heads, width), 0) // group == iota((heads, width), 1) // 128
@@ -197,51 +191,77 @@
         spread = jnp.where(diagonal, jnp.concatenate(columns, axis=0), 0.0)
         return jnp.sum(spread.reshape(ranks, heads_mine, 128), axis=1)
 
+    len_copy.wait()
+    counts = [len_ref[0, r] - rank * positions for r in range(residents)]
+    for r in range(residents):
+        for of in (k_copies, v_copies):
+            for i in range(2):
+                if r > 0 or i > 0 or of is v_copies:
+                    pl.when(counts[r] > i * half)(of[r][i].start)
     q_copy.wait()
-    len_copy.wait()
     for h in range(heads):
         q_all[h * 8 : h * 8 + residents, :] = q_ref[:residents, h * 128 : (h + 1) * 128].astype(F32)
-    peaks, totals = [], []
+    k_copies[0][0].wait()
     for r in range(residents):
-        q = q_all[pl.ds(r, heads, stride=8), :].astype(BF16)
-        wide = jnp.concatenate([q] * kv_heads, axis=1)
-        wide_ref[...] = jnp.where(own_block, wide, jnp.zeros_like(wide))
-        peaks.append([])
-        totals.append([])
-        valid = position < len_ref[0:1, r : r + 1]
-        for i in range(2):
-            arrived(4 * r + i)
-            at = slice(i * half, (i + 1) * half)
-            s_buf[:, at] = lax.dot_general(
-                wide_ref[...],
-                k_buf[r, at, :],
-                (((1,), (1,)), ((), ())),
-                preferred_element_type=F32,
-            )
-        for c in range(0, heads, 16):
-            rows = slice(c, c + 16)
-            scores = jnp.where(valid, s_buf[rows, :] * scale, ABSENT)
-            peak = jnp.max(scores, axis=1, keepdims=True).astype(BF16).astype(F32)
-            weight = jnp.where(valid, jnp.exp(scores - peak), 0.0)
-            peaks[r].append(peak)
-            totals[r].append(jnp.sum(weight, axis=1, keepdims=True))
-            w_buf[rows, :] = weight.astype(BF16)
-        for i in range(2):
-            arrived(4 * r + 2 + i)
-            at = slice(i * half, (i + 1) * half)
-            part = jnp.dot(w_buf[:, at], v_buf[r, at, :], preferred_element_type=F32)
-            for g in range(kv_heads):
-                rows = slice(g * group, (g + 1) * group)
-                block = part[rows, g * 128 : (g + 1) * 128]
-                if i == 0:
-                    o_all[r, rows, :] = block
-                else:
-                    o_all[r, rows, :] += block
-    for r in range(residents):
-        s_all[r, 0] = to_rows(peaks[r])
-        high, low = split_bf16(to_rows(totals[r]))
-        s_all[r, 1] = high.astype(F32)
-        s_all[r, 2] = low.astype(F32)
+        some = counts[r] > 0
+
+        @pl.when(some)
+        def _():
+            q = q_all[pl.ds(r, heads, stride=8), :].astype(BF16)
+            wide = jnp.concatenate([q] * kv_heads, axis=1)
+            wide_ref[...] = jnp.where(own_block, wide, jnp.zeros_like(wide))
+
+        for i, at in enumerate(halves):
+
+            @pl.when(counts[r] > i * half)
+            def _():
+                if r > 0 or i > 0:
+                    k_copies[r][i].wait()
+                s_buf[:, at] = lax.dot_general(
+                    wide_ref[...],
+                    k_buf[r, at, :],
+                    (((1,), (1,)), ((), ())),
+                    preferred_element_type=F32,
+                )
+
+        @pl.when(some)
+        def _():
+            valid = position < counts[r]
+            peaks, totals = [], []
+            for c in range(0, heads, 16):
+                rows = slice(c, c + 16)
+                scores = jnp.where(valid, s_buf[rows, :] * scale, ABSENT)
+                peak = jnp.max(scores, axis=1, keepdims=True).astype(BF16).astype(F32)
+                weight = jnp.where(valid, jnp.exp(scores - peak), 0.0)
+                peaks.append(peak)
+                totals.append(jnp.sum(weight, axis=1, keepdims=True))
+                w_buf[rows, :] = weight.astype(BF16)
+            s_all[r, 0] = to_rows(peaks)
+            high, low = split_bf16(to_rows(totals))
+            s_all[r, 1] = high.astype(F32)
+            s_all[r, 2] = low.astype(F32)
+
+        @pl.when(jnp.logical_not(some))
+        def _():
+            s_all[r, 0] = jnp.full((ranks, 128), ABSENT, F32)
+            s_all[r, 1] = jnp.zeros((ranks, 128), F32)
+            s_all[r, 2] = jnp.zeros((ranks, 128), F32)
+            o_all[r] = jnp.zeros((heads, 128), F32)
+
+        for i, at in enumerate(halves):
+
+            @pl.when(counts[r] > i * half)
+            def _():
+                v_copies[r][i].wait()
+                part = jnp.dot(w_buf[:, at], v_buf[r, at, :], preferred_element_type=F32)
+                for g in range(kv_heads):
+                    rows = slice(g * group, (g + 1) * group)
+                    block = part[rows, g * 128 : (g + 1) * 128]
+                    if i == 0:
+                        o_all[r, rows, :] = block
+                    else:
+                        o_all[r, rows, :] += block
+
     filled = residents * (heads_mine + 3)
     for j in range(ranks):
         target = rank ^ j
@@ -264,7 +284,7 @@
         out_specs=[VMEM] * ranks,
         out_shape=[jax.ShapeDtypeStruct((rows, 128), BF16)] * ranks,
         scratch_shapes=[
-            pltpu.VMEM(lengths.shape, jnp.int32),
+            pltpu.SMEM(lengths.shape, jnp.int32),
             pltpu.VMEM(query.shape, BF16),
             pltpu.VMEM((heads * 8, 128), F32),
             pltpu.VMEM((residents, positions, width), BF16),
@@ -275,7 +295,7 @@
             pltpu.VMEM((residents, heads, 128), F32),
             pltpu.VMEM((residents, 3, ranks, 128), F32),
             pltpu.SemaphoreType.DMA((2,)),
-            pltpu.SemaphoreType.DMA((4 * residents,)),
+            pltpu.SemaphoreType.DMA((2, residents, 2)),
         ],
         compiler_params=pltpu.CompilerParams(vmem_limit_bytes=56 * MIB),
         cost_estimate=pl.CostEstimate(

time: 32.1 us -> 31.9 us (level)
  no operation moved by 1% of the time
where the time goes in v11:
time: 31.9 us; the launch traced here: 31.5 us
  starting transfers between devices  15 us (47%)
  Pallas kernels  14.3 us (45%)
  waiting for transfers between devices  1.34 us (4%)
  local copies, waits for them, and re-layouts  0.74 us (2%)
    ppermute x12, starting transfers between devices, swapped(): return lax.ppermute(x, axis, [(i, i ^ j) for i in range(n)])  15 us
    pallas_call x1, Pallas kernels, attend_resident(): pl.pallas_call(functools.partial(resident_kernel, ranks), in_specs=[HBM]...  7.94 us
    pallas_call x1, Pallas kernels, project(): pl.pallas_call(functools.partial(project_kernel, ranks, group), in_specs=...  4.12 us
    ppermute x12, waiting for transfers between devices, swapped(): return lax.ppermute(x, axis, [(i, i ^ j) for i in range(n)])  1.34 us
    pallas_call x1, Pallas kernels, prepare(): pl.pallas_call(functools.partial(prepare_kernel, insts, residents, kv_min...  0.78 us
    unnamed x16, local copies, waits for them, and re-layouts  0.74 us
    pallas_call x1, Pallas kernels, finish(): pl.pallas_call(finish_kernel, in_specs=[VMEM] * (2 + len(moved)), out_spe...  0.67 us
  transfers between devices with their start and end apart: 12, of which 2 were waited for; matrix products, arithmetic and copies ran while one was open for 0% of the time, Pallas kernels for 30%

profile of v11, /device:TPU:0, one launch (start us, length us, event | category | flops | bytes accessed | tf_op | source)
XLA Modules:
  0.0 31.5 jit_solution(9005461124196435349)
XLA Ops:
  0.0 4.1 %project.1 = (bf16[136,512]{1,0:T(8,128)(2,1)}, bf16[136,512]{1,0:T(8,128)(2,1)}, bf16[136,512]{1,0:T(8,128)(2,1)}, bf16[136,512]{1,0:T(8,128)(2,1)}, bf16[5,2560]{1,0:T(8,128)(2,1)}) custom-call(bf16[1280]{0:T(1024)(128)(2,1)} %gain_hbm.1, bf16[64,2,1280]{2,1,0:T(2,128)(2,1)} %bitcast.16, bf16[1280,2048]{1,0:T(8,128)(2,1)} %w_hbm.1, ...), custom_call_target="tpu_custom_call" | custom-call | flops 671088640 | bytes 5242880 | tf_op jit(solution)/shard_map/project/pallas_call | solution.py:131
  4.1 0.5 %collective-permute-start = (bf16[5,2560]{1,0:T(8,128)(2,1)}, bf16[5,2560]{1,0:T(8,128)(2,1)S(1)}, u32[]{:S(2)}, u32[]{:S(2)}) collective-permute-start(bf16[5,2560]{1,0:T(8,128)(2,1)} %get-tuple-element.25.ask_ref), channel_id=1, source_target_pairs={{0,4},{4,0},{8,12},{12,8},{1,5},{5,1},{9,13},{13,9},{2,6},{6,2},{1... | collective-permute-start | bytes 76808 | tf_op jit(solution)/shard_map/ppermute | solution.py:565
  4.6 4.7 %collective-permute-start.6 = (bf16[136,512]{1,0:T(8,128)(2,1)}, bf16[136,512]{1,0:T(8,128)(2,1)S(1)}, u32[]{:S(2)}, u32[]{:S(2)}) collective-permute-start(bf16[136,512]{1,0:T(8,128)(2,1)} %get-tuple-element.42), channel_id=1, source_target_pairs={{0,3},{1,2},{2,1},{3,0},{4,7},{5,6},{6,5},{7,4},{8,11},{9,10},{10,... | collective-permute-start | bytes 417800 | tf_op jit(solution)/shard_map/ppermute | solution.py:565
  9.3 0.0 collective-permute-done.rest_0_
  9.3 0.3 %collective-permute-start.7 = (bf16[136,512]{1,0:T(8,128)(2,1)}, bf16[136,512]{1,0:T(8,128)(2,1)S(1)}, u32[]{:S(2)}, u32[]{:S(2)}) collective-permute-start(bf16[136,512]{1,0:T(8,128)(2,1)} %get-tuple-element.43), channel_id=1, source_target_pairs={{0,2},{1,3},{2,0},{3,1},{4,6},{5,7},{6,4},{7,5},{8,10},{9,11},{10,... | collective-permute-start | bytes 417800 | tf_op jit(solution)/shard_map/ppermute | solution.py:565
  9.7 1.6 %collective-permute-start.8 = (bf16[136,512]{1,0:T(8,128)(2,1)}, bf16[136,512]{1,0:T(8,128)(2,1)S(1)}, u32[]{:S(2)}, u32[]{:S(2)}) collective-permute-start(bf16[136,512]{1,0:T(8,128)(2,1)} %get-tuple-element.44), channel_id=1, source_target_pairs={{0,1},{1,0},{2,3},{3,2},{4,5},{5,4},{6,7},{7,6},{8,9},{9,8},{10,11... | collective-permute-start | bytes 417800 | tf_op jit(solution)/shard_map/ppermute | solution.py:565
  11.2 1.5 %collective-permute-start.1 = (bf16[5,2560]{1,0:T(8,128)(2,1)}, bf16[5,2560]{1,0:T(8,128)(2,1)S(1)}, u32[]{:S(2)}, u32[]{:S(2)}) collective-permute-start(bf16[5,2560]{1,0:T(8,128)(2,1)} %get-tuple-element.25.ask_ref), channel_id=1, source_target_pairs={{0,8},{4,12},{8,0},{12,4},{1,9},{5,13},{9,1},{13,5},{2,10},{6,14},... | collective-permute-start | bytes 76808 | tf_op jit(solution)/shard_map/ppermute | solution.py:565
  12.7 0.0 collective-permute-start.2
  12.7 0.0 copy-start.1
  12.7 0.0 copy-start.2
  12.7 0.0 copy-start.5
  12.7 0.0 copy-start.6
  12.8 0.0 copy-start.7
  12.8 0.0 copy-start
  12.8 0.0 copy-start.3
  12.8 7.9 %attend_resident.1 = (bf16[64,128]{1,0:T(8,128)(2,1)}, bf16[64,128]{1,0:T(8,128)(2,1)}, bf16[64,128]{1,0:T(8,128)(2,1)}, bf16[64,128]{1,0:T(8,128)(2,1)}) custom-call(s32[1,3]{1,0:T(1,128)} %len_hbm.1, bf16[5,8192]{1,0:T(8,128)(2,1)} %bitcast.15, bf16[3,1024,1024]{2,1,0:T(8,128)(2,1)} %bitcast.12, bf16[3,1024,1024]{2,1,0:T(8,128)(2,1)} %bitcast.13), custom_call_target="tpu_custom_call" | custom-call | flops 100663296 | bytes 12582912 | tf_op jit(solution)/shard_map/attend_resident/pallas_call | solution.py:281
  20.7 0.0 collective-permute-done.1.rest_1_
  20.7 0.1 collective-permute-start.3
  20.8 0.0 collective-permute-done.2.rest_2_
  20.8 0.1 collective-permute-start.4
  20.9 0.0 collective-permute-done.6.rest_1_
  20.9 4.3 %collective-permute-start.5 = (bf16[64,128]{1,0:T(8,128)(2,1)}, bf16[64,128]{1,0:T(8,128)(2,1)S(1)}, u32[]{:S(2)}, u32[]{:S(2)}) collective-permute-start(bf16[64,128]{1,0:T(8,128)(2,1)} %get-tuple-element.34), channel_id=1, source_target_pairs={{0,1},{1,0},{2,3},{3,2},{4,5},{5,4},{6,7},{7,6},{8,9},{9,8},{10,11... | collective-permute-start | bytes 49160 | tf_op jit(solution)/shard_map/ppermute | solution.py:565
  25.2 0.0 copy-done.1
  25.2 0.0 copy-done.2
  25.2 0.0 copy-done.5
  25.2 0.0 copy-done.6
  25.2 0.0 copy-done.7
  25.2 0.8 %prepare.1 = (bf16[32,128]{1,0:T(8,128)(2,1)S(1)}, f32[2,32,128]{2,1,0:T(8,128)S(1)}, s32[32,128]{1,0:T(8,128)S(1)}, f32[128,128]{1,0:T(8,128)S(1)}, f32[128,128]{1,0:T(8,128)S(1)}, /*index=5*/s32[8,128]{1,0:T(8,128)S(1)}) custom-call(s32[2,4]{1,0:T(2,128)S(1)} %bitcast.9, s32[2,4]{1,0:T(2,128)S(1)} %bitcast.10, bf16[1,128]{1,0:T(2,128)(2,1)S(1)} %bitcast.11, ...), custom_call_target="tpu_custom_call" | custom-call | tf_op jit(solution)/shard_map/prepare/pallas_call | solution.py:384
  26.0 0.0 collective-permute-done.7.rest_2_
  26.0 0.0 collective-permute-done.8.rest_3_
  26.0 0.0 copy-done
  26.0 0.6 %attend_moved.1 = bf16[2,2048]{1,0:T(2,128)(2,1)S(1)} custom-call(bf16[32,128]{1,0:T(8,128)(2,1)S(1)} %get-tuple-element.36.q_ref, f32[2,32,128]{2,1,0:T(8,128)S(1)} %get-tuple-element.37.own_ref, s32[32,128]{1,0:T(8,128)S(1)} %get-tuple-element.38.limit_ref, f32[128,128]{1,0:T(8,128)S(1)} %get-tuple-element.39.cos_ref, ...), custom_call_target="tpu_custom_call" | custom-call | flops 33554432 | bytes 4194304 | tf_op jit(solution)/shard_map/attend_moved/pallas_call | solution.py:476
  26.7 0.1 collective-permute-start.9
  26.8 1.0 %collective-permute-start.10 = (bf16[2,2048]{1,0:T(2,128)(2,1)S(1)}, bf16[2,2048]{1,0:T(2,128)(2,1)S(1)}, u32[]{:S(2)}, u32[]{:S(2)}) collective-permute-start(bf16[2,2048]{1,0:T(2,128)(2,1)S(1)} %attend_moved.1), channel_id=1, source_target_pairs={{0,8},{4,12},{8,0},{12,4},{1,9},{5,13},{9,1},{13,5},{2,10},{6,14},... | collective-permute-start | bytes 24584 | tf_op jit(solution)/shard_map/ppermute | solution.py:565
  27.8 0.0 collective-permute-done.3.rest_1_
  27.8 0.9 %collective-permute-start.11 = (bf16[2,2048]{1,0:T(2,128)(2,1)S(1)}, bf16[2,2048]{1,0:T(2,128)(2,1)S(1)}, u32[]{:S(2)}, u32[]{:S(2)}) collective-permute-start(bf16[2,2048]{1,0:T(2,128)(2,1)S(1)} %attend_moved.1), channel_id=1, source_target_pairs={{0,12},{4,8},{8,4},{12,0},{1,13},{5,9},{9,5},{13,1},{2,14},{6,10},... | collective-permute-start | bytes 24584 | tf_op jit(solution)/shard_map/ppermute | solution.py:565
  28.6 0.0 collective-permute-done.4.rest_2_
  28.6 0.0 collective-permute-done.5.rest_3_
  28.6 0.0 copy-done.3
  28.6 0.0 copy-start.4
  28.6 0.7 %copy-done.4 = bf16[64,128]{1,0:T(8,128)(2,1)S(1)} copy-done((bf16[64,128]{1,0:T(8,128)(2,1)S(1)}, bf16[64,128]{1,0:T(8,128)(2,1)}, u32[]{:S(2)}) %copy-start.4) | copy-done | bytes 16408
  29.4 0.2 combine_resident.1.kept_ref
  29.5 0.0 collective-permute-done.9.rest_0_
  29.5 0.9 %collective-permute-done.10.rest_1_ = bf16[2,2048]{1,0:T(2,128)(2,1)S(1)} collective-permute-done((bf16[2,2048]{1,0:T(2,128)(2,1)S(1)}, bf16[2,2048]{1,0:T(2,128)(2,1)S(1)}, u32[]{:S(2)}, u32[]{:S(2)}) %collective-permute-start.10) | collective-permute-done | bytes 8224 | tf_op jit(solution)/shard_map/ppermute | solution.py:565
  30.5 0.4 %collective-permute-done.11.rest_2_ = bf16[2,2048]{1,0:T(2,128)(2,1)S(1)} collective-permute-done((bf16[2,2048]{1,0:T(2,128)(2,1)S(1)}, bf16[2,2048]{1,0:T(2,128)(2,1)S(1)}, u32[]{:S(2)}, u32[]{:S(2)}) %collective-permute-start.11) | collective-permute-done | bytes 8224 | tf_op jit(solution)/shard_map/ppermute | solution.py:565
  30.8 0.7 %finish.1 = bf16[5,2048]{1,0:T(8,128)(2,1)} custom-call(f32[3,2048]{1,0:T(4,128)S(1)} %combine_resident.1.kept_ref, s32[8,128]{1,0:T(8,128)S(1)} %get-tuple-element.35.place_ref, bf16[2,2048]{1,0:T(2,128)(2,1)S(1)} %collective-permute-done.9.rest_0_, bf16[2,2048]{1,0:T(2,128)(2,1)S(1)} %collective-permute-done.10.rest_1_, ...), custom_call_target="tpu_custom_call" | custom-call | tf_op jit(solution)/shard_map/finish/pallas_call | solution.py:554
Async XLA Ops:
  4.1 5.2 %collective-permute-start = (bf16[5,2560]{1,0:T(8,128)(2,1)}, bf16[5,2560]{1,0:T(8,128)(2,1)S(1)}, u32[]{:S(2)}, u32[]{:S(2)}) collective-permute-start(bf16[5,2560]{1,0:T(8,128)(2,1)} %get-tuple-element.25.ask_ref), channel_id=1, source_target_pairs={{0,4},{4,0},{8,12},{12,8},{1,5},{5,1},{9,13},{13,9},{2,6},{6,2},{1... | collective-permute-start | bytes 76808 | tf_op jit(solution)/shard_map/ppermute | solution.py:565
  4.6 16.3 %collective-permute-start.6 = (bf16[136,512]{1,0:T(8,128)(2,1)}, bf16[136,512]{1,0:T(8,128)(2,1)S(1)}, u32[]{:S(2)}, u32[]{:S(2)}) collective-permute-start(bf16[136,512]{1,0:T(8,128)(2,1)} %get-tuple-element.42), channel_id=1, source_target_pairs={{0,3},{1,2},{2,1},{3,0},{4,7},{5,6},{6,5},{7,4},{8,11},{9,10},{10,... | collective-permute-start | bytes 417800 | tf_op jit(solution)/shard_map/ppermute | solution.py:565
  9.3 16.7 %collective-permute-start.7 = (bf16[136,512]{1,0:T(8,128)(2,1)}, bf16[136,512]{1,0:T(8,128)(2,1)S(1)}, u32[]{:S(2)}, u32[]{:S(2)}) collective-permute-start(bf16[136,512]{1,0:T(8,128)(2,1)} %get-tuple-element.43), channel_id=1, source_target_pairs={{0,2},{1,3},{2,0},{3,1},{4,6},{5,7},{6,4},{7,5},{8,10},{9,11},{10,... | collective-permute-start | bytes 417800 | tf_op jit(solution)/shard_map/ppermute | solution.py:565
  9.7 16.4 %collective-permute-start.8 = (bf16[136,512]{1,0:T(8,128)(2,1)}, bf16[136,512]{1,0:T(8,128)(2,1)S(1)}, u32[]{:S(2)}, u32[]{:S(2)}) collective-permute-start(bf16[136,512]{1,0:T(8,128)(2,1)} %get-tuple-element.44), channel_id=1, source_target_pairs={{0,1},{1,0},{2,3},{3,2},{4,5},{5,4},{6,7},{7,6},{8,9},{9,8},{10,11... | collective-permute-start | bytes 417800 | tf_op jit(solution)/shard_map/ppermute | solution.py:565
  11.2 9.5 %collective-permute-start.1 = (bf16[5,2560]{1,0:T(8,128)(2,1)}, bf16[5,2560]{1,0:T(8,128)(2,1)S(1)}, u32[]{:S(2)}, u32[]{:S(2)}) collective-permute-start(bf16[5,2560]{1,0:T(8,128)(2,1)} %get-tuple-element.25.ask_ref), channel_id=1, source_target_pairs={{0,8},{4,12},{8,0},{12,4},{1,9},{5,13},{9,1},{13,5},{2,10},{6,14},... | collective-permute-start | bytes 76808 | tf_op jit(solution)/shard_map/ppermute | solution.py:565
  12.7 8.1 %collective-permute-start.2 = (bf16[5,2560]{1,0:T(8,128)(2,1)}, bf16[5,2560]{1,0:T(8,128)(2,1)S(1)}, u32[]{:S(2)}, u32[]{:S(2)}) collective-permute-start(bf16[5,2560]{1,0:T(8,128)(2,1)} %get-tuple-element.25.ask_ref), channel_id=1, source_target_pairs={{0,12},{4,8},{8,4},{12,0},{1,13},{5,9},{9,5},{13,1},{2,14},{6,10},... | collective-permute-start | bytes 76808 | tf_op jit(solution)/shard_map/ppermute | solution.py:565
  12.7 12.5 %copy-start.1 = (f32[128,128]{1,0:T(8,128)S(1)}, f32[128,128]{1,0:T(8,128)}, u32[]{:S(2)}) copy-start(f32[128,128]{1,0:T(8,128)} %constant.4.clone.cos_ref) | copy-start | bytes 196612
  12.7 12.5 %copy-start.2 = (f32[128,128]{1,0:T(8,128)S(1)}, f32[128,128]{1,0:T(8,128)}, u32[]{:S(2)}) copy-start(f32[128,128]{1,0:T(8,128)} %constant.5.clone.sin_ref) | copy-start | bytes 196612
  12.7 12.5 %copy-start.5 = (s32[4,2]{0,1:T(2,128)S(1)}, s32[4,2]{0,1:T(2,128)}, u32[]{:S(2)}) copy-start(s32[4,2]{0,1:T(2,128)} %param.14) | copy-start | bytes 100
  12.7 12.5 %copy-start.6 = (s32[4,2]{0,1:T(2,128)S(1)}, s32[4,2]{0,1:T(2,128)}, u32[]{:S(2)}) copy-start(s32[4,2]{0,1:T(2,128)} %param.15) | copy-start | bytes 100
  12.8 12.5 %copy-start.7 = (bf16[128]{0:T(256)(128)(2,1)S(1)}, bf16[128]{0:T(256)(128)(2,1)}, u32[]{:S(2)}) copy-start(bf16[128]{0:T(256)(128)(2,1)} %param.18) | copy-start | bytes 772
  12.8 13.3 %copy-start = (bf16[136,512]{1,0:T(8,128)(2,1)S(1)}, bf16[136,512]{1,0:T(8,128)(2,1)}, u32[]{:S(2)}) copy-start(bf16[136,512]{1,0:T(8,128)(2,1)} %get-tuple-element.41.rest_0_) | copy-start | bytes 417796
  12.8 15.9 %copy-start.3 = (bf16[5,2560]{1,0:T(8,128)(2,1)S(1)}, bf16[5,2560]{1,0:T(8,128)(2,1)}, u32[]{:S(2)}) copy-start(bf16[5,2560]{1,0:T(8,128)(2,1)} %get-tuple-element.25.ask_ref) | copy-start | bytes 76804
  20.7 7.0 %collective-permute-start.3 = (bf16[64,128]{1,0:T(8,128)(2,1)}, bf16[64,128]{1,0:T(8,128)(2,1)S(1)}, u32[]{:S(2)}, u32[]{:S(2)}) collective-permute-start(bf16[64,128]{1,0:T(8,128)(2,1)} %get-tuple-element.32), channel_id=1, source_target_pairs={{0,3},{1,2},{2,1},{3,0},{4,7},{5,6},{6,5},{7,4},{8,11},{9,10},{10,... | collective-permute-start | bytes 49160 | tf_op jit(solution)/shard_map/ppermute | solution.py:565
  20.8 7.8 %collective-permute-start.4 = (bf16[64,128]{1,0:T(8,128)(2,1)}, bf16[64,128]{1,0:T(8,128)(2,1)S(1)}, u32[]{:S(2)}, u32[]{:S(2)}) collective-permute-start(bf16[64,128]{1,0:T(8,128)(2,1)} %get-tuple-element.33), channel_id=1, source_target_pairs={{0,2},{1,3},{2,0},{3,1},{4,6},{5,7},{6,4},{7,5},{8,10},{9,11},{10,... | collective-permute-start | bytes 49160 | tf_op jit(solution)/shard_map/ppermute | solution.py:565
  20.9 7.7 %collective-permute-start.5 = (bf16[64,128]{1,0:T(8,128)(2,1)}, bf16[64,128]{1,0:T(8,128)(2,1)S(1)}, u32[]{:S(2)}, u32[]{:S(2)}) collective-permute-start(bf16[64,128]{1,0:T(8,128)(2,1)} %get-tuple-element.34), channel_id=1, source_target_pairs={{0,1},{1,0},{2,3},{3,2},{4,5},{5,4},{6,7},{7,6},{8,9},{9,8},{10,11... | collective-permute-start | bytes 49160 | tf_op jit(solution)/shard_map/ppermute | solution.py:565
  26.7 2.8 %collective-permute-start.9 = (bf16[2,2048]{1,0:T(2,128)(2,1)S(1)}, bf16[2,2048]{1,0:T(2,128)(2,1)S(1)}, u32[]{:S(2)}, u32[]{:S(2)}) collective-permute-start(bf16[2,2048]{1,0:T(2,128)(2,1)S(1)} %attend_moved.1), channel_id=1, source_target_pairs={{0,4},{4,0},{8,12},{12,8},{1,5},{5,1},{9,13},{13,9},{2,6},{6,2},{1... | collective-permute-start | bytes 24584 | tf_op jit(solution)/shard_map/ppermute | solution.py:565
  26.8 3.7 %collective-permute-start.10 = (bf16[2,2048]{1,0:T(2,128)(2,1)S(1)}, bf16[2,2048]{1,0:T(2,128)(2,1)S(1)}, u32[]{:S(2)}, u32[]{:S(2)}) collective-permute-start(bf16[2,2048]{1,0:T(2,128)(2,1)S(1)} %attend_moved.1), channel_id=1, source_target_pairs={{0,8},{4,12},{8,0},{12,4},{1,9},{5,13},{9,1},{13,5},{2,10},{6,14},... | collective-permute-start | bytes 24584 | tf_op jit(solution)/shard_map/ppermute | solution.py:565
  27.8 3.1 %collective-permute-start.11 = (bf16[2,2048]{1,0:T(2,128)(2,1)S(1)}, bf16[2,2048]{1,0:T(2,128)(2,1)S(1)}, u32[]{:S(2)}, u32[]{:S(2)}) collective-permute-start(bf16[2,2048]{1,0:T(2,128)(2,1)S(1)} %attend_moved.1), channel_id=1, source_target_pairs={{0,12},{4,8},{8,4},{12,0},{1,13},{5,9},{9,5},{13,1},{2,14},{6,10},... | collective-permute-start | bytes 24584 | tf_op jit(solution)/shard_map/ppermute | solution.py:565
  28.6 0.7 %copy-start.4 = (bf16[64,128]{1,0:T(8,128)(2,1)S(1)}, bf16[64,128]{1,0:T(8,128)(2,1)}, u32[]{:S(2)}) copy-start(bf16[64,128]{1,0:T(8,128)(2,1)} %get-tuple-element.31.rest_0_) | copy-start | bytes 49156

commit v12 on v11

--- a/solution.py
+++ b/solution.py
@@ -154,10 +154,9 @@
 
 
 def resident_kernel(ranks, len_hbm, q_hbm, k_hbm, v_hbm, *rest):
-    outs = rest[:ranks]
-    len_ref, q_ref, q_all, k_buf, v_buf, wide_ref, s_buf, w_buf, o_all, s_all, in_sems, sems = rest[
-        ranks:
-    ]
+    out, len_ref, q_ref, q_all, k_buf, v_buf, wide_ref, s_buf, w_buf, o_all, s_all, in_sems, sems = (
+        rest
+    )
     residents, positions, width = k_buf.shape
     half = positions // 2
     halves = [slice(i * half, (i + 1) * half) for i in range(2)]
@@ -175,13 +174,20 @@
     len_copy = pltpu.make_async_copy(len_hbm, len_ref, in_sems.at[0])
     q_copy = pltpu.make_async_copy(q_hbm, q_ref, in_sems.at[1])
     len_copy.start()
-    k_copies[0][0].start()
     q_copy.start()
+    rank = lax.axis_index("tp")
+
+    @pl.when(rank == 0)
+    def _():
+        for r in range(residents):
+            for of in (k_copies, v_copies):
+                for copy in of[r]:
+                    copy.start()
+
     heads = q_ref.shape[1] // 128
     kv_heads = width // 128
     group = heads // kv_heads
     heads_mine = heads // ranks
-    rank = lax.axis_index("tp")
     position = iota((16, positions), 1)
     scale = F32(1.0) / jnp.sqrt(F32(128.0))
     diagonal = iota((heads, 128), 0) % heads_mine == iota((heads, 128), 1)
@@ -196,14 +202,12 @@
     for r in range(residents):
         for of in (k_copies, v_copies):
             for i in range(2):
-                if r > 0 or i > 0 or of is v_copies:
-                    pl.when(counts[r] > i * half)(of[r][i].start)
+                pl.when((rank > 0) & (counts[r] > i * half))(of[r][i].start)
     q_copy.wait()
     for h in range(heads):
         q_all[h * 8 : h * 8 + residents, :] = q_ref[:residents, h * 128 : (h + 1) * 128].astype(F32)
-    k_copies[0][0].wait()
     for r in range(residents):
-        some = counts[r] > 0
+        some = (rank == 0) | (counts[r] > 0)
 
         @pl.when(some)
         def _():
@@ -213,10 +217,9 @@
 
         for i, at in enumerate(halves):
 
-            @pl.when(counts[r] > i * half)
+            @pl.when((rank == 0) | (counts[r] > i * half))
             def _():
-                if r > 0 or i > 0:
-                    k_copies[r][i].wait()
+                k_copies[r][i].wait()
                 s_buf[:, at] = lax.dot_general(
                     wide_ref[...],
                     k_buf[r, at, :],
@@ -250,7 +253,7 @@
 
         for i, at in enumerate(halves):
 
-            @pl.when(counts[r] > i * half)
+            @pl.when((rank == 0) | (counts[r] > i * half))
             def _():
                 v_copies[r][i].wait()
                 part = jnp.dot(w_buf[:, at], v_buf[r, at, :], preferred_element_type=F32)
@@ -263,14 +266,12 @@
                         o_all[r, rows, :] += block
 
     filled = residents * (heads_mine + 3)
-    for j in range(ranks):
-        target = rank ^ j
-        first = pl.multiple_of(target * heads_mine, heads_mine)
-        parts = [o_all[r, pl.ds(first, heads_mine), :] for r in range(residents)]
-        parts += [s_all[r, i, pl.ds(target, 1), :] for i in range(3) for r in range(residents)]
-        if outs[j].shape[0] > filled:
-            parts.append(jnp.zeros((outs[j].shape[0] - filled, 128), F32))
-        outs[j][...] = jnp.concatenate(parts, axis=0).astype(BF16)
+    for t in range(ranks):
+        parts = [o_all[r, t * heads_mine : (t + 1) * heads_mine, :] for r in range(residents)]
+        parts += [s_all[r, i, t : t + 1, :] for i in range(3) for r in range(residents)]
+        if out.shape[1] > filled:
+            parts.append(jnp.zeros((out.shape[1] - filled, 128), F32))
+        out[t] = jnp.concatenate(parts, axis=0).astype(BF16)
 
 
 def attend_resident(lengths, query, k_cache, v_cache, ranks):
@@ -281,8 +282,8 @@
     return pl.pallas_call(
         functools.partial(resident_kernel, ranks),
         in_specs=[HBM] * 4,
-        out_specs=[VMEM] * ranks,
-        out_shape=[jax.ShapeDtypeStruct((rows, 128), BF16)] * ranks,
+        out_specs=VMEM,
+        out_shape=jax.ShapeDtypeStruct((ranks, rows, 128), BF16),
         scratch_shapes=[
             pltpu.SMEM(lengths.shape, jnp.int32),
             pltpu.VMEM(query.shape, BF16),
@@ -328,18 +329,27 @@
     )
 
 
-def prepare_kernel(insts, residents, kv_mine, dest_ref, count_ref, gain_ref, cos_ref, sin_ref, *rest):
+def moved_kernel(
+    insts, ranks, residents, features, dest_ref, count_ref, gain_ref, cos_ref, sin_ref, *rest
+):
     asks, rest = rest[: insts - 1], rest[insts - 1 :]
-    q_out, own_out, limit_out, cos_out, sin_out, place_out, line_ref, q_ref, k_ref = rest
-    requests = dest_ref.shape[0]
-    rows = q_out.shape[0]
+    pieces, rest = rest[:ranks], rest[ranks:]
+    out_ref, place_out, ask_ref, q_ref, own_ref, line_ref = rest
+    requests = out_ref.shape[0]
+    tokens = cos_ref.shape[0]
+    piece = pieces[0].shape[1] // 2
+    kv_mine = piece // 128
+    rows = q_ref.shape[0]
     heads_mine = rows // requests
+    scale = F32(1.0) / jnp.sqrt(F32(128.0))
     here = lax.axis_index("inst")
+
     ask_row = iota(asks[0].shape, 0)
-    limit = jnp.zeros((rows, 128), jnp.int32)
+    row_request = iota((rows, tokens), 0) // heads_mine
+    limit = jnp.zeros((rows, tokens), jnp.int32)
     for r in range(requests):
         dest = dest_ref[r, here]
-        limit = jnp.where(iota((rows, 128), 0) // heads_mine == r, count_ref[r, here], limit)
+        limit = jnp.where(row_request == r, count_ref[r, here], limit)
         place = jnp.int32(residents)
         for s in range(insts):
             for c in range(requests):
@@ -349,24 +359,14 @@
             @pl.when(here ^ b == dest)
             def _():
                 ask = asks[b - 1][...].astype(F32)
-                line_ref[r : r + 1, :] = jnp.sum(
+                ask_ref[r : r + 1, :] = jnp.sum(
                     jnp.where(ask_row == place, ask, 0.0), axis=0, keepdims=True
                 )
 
         at = slice(r * heads_mine, (r + 1) * heads_mine)
-        q_ref[at, :], k_ref[at, :], own_out[0, at, :] = heads_of(
-            line_ref[r : r + 1, :], heads_mine, kv_mine
+        q_ref[at, :], own_ref[0, at, :], own_ref[1, at, :] = heads_of(
+            ask_ref[r : r + 1, :], heads_mine, kv_mine
         )
-    scale = F32(1.0) / jnp.sqrt(F32(128.0))
-    q = q_ref[...]
-    q_out[...] = q.astype(BF16)
-    own_out[1] = jnp.broadcast_to(
-        jnp.sum(q * k_ref[...], axis=1, keepdims=True) * scale, (rows, 128)
-    )
-    limit_out[...] = limit
-    gain = gain_ref[...].astype(F32)
-    cos_out[...] = cos_ref[...] * gain
-    sin_out[...] = sin_ref[...] * pltpu.roll(jnp.broadcast_to(gain, (8, 128)), 64, 1)[:1]
     places = jnp.full(place_out.shape, -1, jnp.int32)
     row = iota(place_out.shape, 0)
     place = jnp.int32(residents)
@@ -377,43 +377,6 @@
             place += jnp.where(mine, 1, 0).astype(jnp.int32)
     place_out[...] = places
 
-
-def prepare(dest, count, k_gain, cos, sin, asks, residents, heads_mine, kv_mine):
-    requests, insts = dest.shape
-    rows = requests * heads_mine
-    return pl.pallas_call(
-        functools.partial(prepare_kernel, insts, residents, kv_mine),
-        in_specs=[SMEM] * 2 + [VMEM] * (3 + len(asks)),
-        out_specs=[VMEM] * 6,
-        out_shape=[
-            jax.ShapeDtypeStruct((rows, 128), BF16),
-            jax.ShapeDtypeStruct((2, rows, 128), F32),
-            jax.ShapeDtypeStruct((rows, 128), jnp.int32),
-            jax.ShapeDtypeStruct(cos.shape, F32),
-            jax.ShapeDtypeStruct(sin.shape, F32),
-            jax.ShapeDtypeStruct((insts * requests, 128), jnp.int32),
-        ],
-        scratch_shapes=[
-            pltpu.VMEM((requests, asks[0].shape[1]), F32),
-            pltpu.VMEM((rows, 128), F32),
-            pltpu.VMEM((rows, 128), F32),
-        ],
-        compiler_params=pltpu.CompilerParams(vmem_limit_bytes=16 * MIB),
-        name="prepare",
-    )(dest, count, k_gain, cos, sin, *asks)
-
-
-def moved_kernel(ranks, features, q_ref, own_ref, limit_ref, cos_ref, sin_ref, *rest):
-    pieces = rest[:ranks]
-    out_ref, line_ref = rest[ranks:]
-    requests = out_ref.shape[0]
-    tokens = cos_ref.shape[0]
-    piece = pieces[0].shape[1] // 2
-    kv_mine = piece // 128
-    rows = q_ref.shape[0]
-    heads_mine = rows // requests
-    scale = F32(1.0) / jnp.sqrt(F32(128.0))
-
     blocks = tokens // 128
     last = tokens + 2 * blocks
     tail = pieces[0][tokens:last, :128].astype(F32)
@@ -431,28 +394,25 @@
             total = total + pieces[t][:tokens, c : c + 128].astype(F32)
         return total * token_scale
 
+    gain = gain_ref[...].astype(F32)
     q = q_ref[...]
+    q16 = q.astype(BF16)
     which = iota((rows, tokens), 0) % heads_mine // (heads_mine // kv_mine)
     scores = None
     for h in range(kv_mine):
         key = column_block(h * 128)
-        key = key * lax.rsqrt(jnp.mean(key * key, axis=1, keepdims=True) + EPS)
+        key = key * lax.rsqrt(jnp.mean(key * key, axis=1, keepdims=True) + EPS) * gain
         key = key * cos_ref[...] + pltpu.roll(key, 64, 1) * sin_ref[...]
         part = lax.dot_general(
-            q, key.astype(BF16), (((1,), (1,)), ((), ())), preferred_element_type=F32
+            q16, key.astype(BF16), (((1,), (1,)), ((), ())), preferred_element_type=F32
         )
         scores = part if scores is None else jnp.where(which == h, part, scores)
     token = iota((rows, tokens), 1)
-    limit = jnp.concatenate([limit_ref[...]] * (tokens // 128), axis=1)
-    valid = (token % requests == iota((rows, tokens), 0) // heads_mine) & (
-        token // requests < limit
-    )
+    valid = (token % requests == row_request) & (token // requests < limit)
     scores = jnp.where(valid, scores * scale, ABSENT)
-    own_score = own_ref[1]
+    own_score = jnp.sum(q * own_ref[0], axis=1, keepdims=True) * scale
     top = jnp.maximum(jnp.max(scores, axis=1, keepdims=True), own_score)
-    weights = jnp.where(
-        valid, jnp.exp(scores - jnp.concatenate([top] * (tokens // 128), axis=1)), 0.0
-    )
+    weights = jnp.where(valid, jnp.exp(scores - top), 0.0)
     own_weight = jnp.exp(own_score - top)
     total = jnp.sum(weights, axis=1, keepdims=True) + own_weight
     weights = weights.astype(BF16)
@@ -461,7 +421,7 @@
         value = column_block(piece + h * 128).astype(BF16)
         part = jnp.dot(weights, value, preferred_element_type=F32)
         summed = part if summed is None else jnp.where(which[:, :128] == h, part, summed)
-    summed = summed + own_weight.astype(BF16).astype(F32) * own_ref[0]
+    summed = summed + own_weight.astype(BF16).astype(F32) * own_ref[1]
     result = summed / total
     for r in range(requests):
         for h in range(heads_mine):
@@ -470,28 +430,32 @@
     out_ref[...] = line_ref[...].astype(BF16)
 
 
-def attend_moved(prepared, pieces, requests, features):
-    rows = prepared[0].shape[0]
-    width = rows // requests * 128
+def attend_moved(dest, count, k_gain, cos, sin, asks, pieces, residents, heads_mine, features):
+    requests, insts = dest.shape
+    rows = requests * heads_mine
     return pl.pallas_call(
-        functools.partial(moved_kernel, len(pieces), features),
-        in_specs=[VMEM] * (len(prepared) + len(pieces)),
-        out_specs=VMEM,
-        out_shape=jax.ShapeDtypeStruct((requests, width), BF16),
-        scratch_shapes=[pltpu.VMEM((requests, width), F32)],
+        functools.partial(moved_kernel, insts, len(pieces), residents, features),
+        in_specs=[SMEM] * 2 + [VMEM] * (3 + len(asks) + len(pieces)),
+        out_specs=[VMEM] * 2,
+        out_shape=[
+            jax.ShapeDtypeStruct((requests, heads_mine * 128), BF16),
+            jax.ShapeDtypeStruct((insts * requests, 128), jnp.int32),
+        ],
+        scratch_shapes=[
+            pltpu.VMEM((requests, asks[0].shape[1]), F32),
+            pltpu.VMEM((rows, 128), F32),
+            pltpu.VMEM((2, rows, 128), F32),
+            pltpu.VMEM((requests, heads_mine * 128), F32),
+        ],
         compiler_params=pltpu.CompilerParams(vmem_limit_bytes=16 * MIB),
-        cost_estimate=pl.CostEstimate(
-            flops=4 * rows * rows * 128 * 64, bytes_accessed=4 * 1024 * 1024, transcendentals=rows * 128
-        ),
         name="attend_moved",
-    )(*prepared, *pieces)
-
-
-def combine_kernel(ranks, residents, kv_mine, ask_ref, *rest):
-    refs, out_ref = rest[:ranks], rest[ranks]
+    )(dest, count, k_gain, cos, sin, *asks, *pieces)
+
+
+def combine_kernel(residents, kv_mine, ask_ref, payload_ref, out_ref):
     heads_mine = out_ref.shape[1] // 128
     scale = F32(1.0) / jnp.sqrt(F32(128.0))
-    payloads = [ref[...].astype(F32) for ref in refs]
+    payloads = [payload_ref[t].astype(F32) for t in range(payload_ref.shape[0])]
     at = residents * heads_mine
     ask = ask_ref[...].astype(F32)
     for r in range(residents):
@@ -521,13 +485,13 @@
 
 def combine_resident(ask, payloads, residents, heads_mine, kv_mine):
     return pl.pallas_call(
-        functools.partial(combine_kernel, len(payloads), residents, kv_mine),
-        in_specs=[VMEM] * (1 + len(payloads)),
+        functools.partial(combine_kernel, residents, kv_mine),
+        in_specs=[VMEM] * 2,
         out_specs=VMEM,
         out_shape=jax.ShapeDtypeStruct((residents, heads_mine * 128), F32),
         compiler_params=pltpu.CompilerParams(vmem_limit_bytes=8 * MIB),
         name="combine_resident",
-    )(ask, *payloads)
+    )(ask, payloads)
 
 
 def finish_kernel(kept_ref, place_ref, *rest):
@@ -610,23 +574,22 @@
     others = [swapped(others[j - 1], "tp", j, ranks) for j in reversed(range(1, last))]
     pieces = [pieces[0], far] + others
     payloads = attend_resident(lengths, query[0], k_cache[0], v_cache[0], ranks)
-    own_payload = payloads[0]
-    payloads = [swapped(payloads[j], "tp", j, ranks) for j in reversed(range(1, ranks))]
+    asks, payloads = lax.optimization_barrier((asks, payloads))
+    received = lax.all_to_all(payloads, "tp", 0, 0, tiled=True)
     cos, sin = rotation(slots, requests, head_size)
-    *prepared, places = prepare(
+    moved, places = attend_moved(
         mig_dest.T,
         mig_count.T,
         k_gain.reshape(1, head_size),
         cos,
         sin,
         asks,
+        pieces,
         residents,
         heads_mine,
-        kv_mine,
-    )
-    prepared[0], own_payload = lax.optimization_barrier((prepared[0], own_payload))
-    moved = attend_moved(prepared, pieces, requests, feats * ranks)
-    kept = combine_resident(ask, [own_payload] + payloads, residents, heads_mine, kv_mine)
+        feats * ranks,
+    )
+    kept = combine_resident(ask, received, residents, heads_mine, kv_mine)
     moved = [swapped(moved, "inst", b, insts) for b in reversed(range(1, insts))][::-1]
     return finish(kept, places, moved, requests)[None]
 

time: 31.9 us -> 34.4 us (1.078)
  Pallas kernels: 14.3 us -> 17 us
  waiting for transfers between devices: 1.34 us -> 2.95 us
  starting transfers between devices: 15 us -> 14 us
  local copies, waits for them, and re-layouts: 0.74 us -> 0.03 us
    ppermute x12 -> x9, starting transfers between devices: 15 us -> 10.7 us  [swapped(): return lax.ppermute(x, axis, [(i, i ^ j) for i in range(n)])]
    all_to_all x0 -> x1, starting transfers between devices: none -> 3.29 us  [per_device(): received = lax.all_to_all(payloads, 'tp', 0, 0, tiled=True)]
    pallas_call x1, Pallas kernels: 7.94 us -> 10.7 us  [attend_resident(): pl.pallas_call(functools.partial(resident_kernel, ranks), in_specs=[HBM]...]
    all_to_all x0 -> x1, waiting for transfers between devices: none -> 2.25 us  [per_device(): received = lax.all_to_all(payloads, 'tp', 0, 0, tiled=True)]
    unnamed x16 -> x14, local copies, waits for them, and re-layouts: 0.74 us -> 0.03 us
    ppermute x12 -> x9, waiting for transfers between devices: 1.34 us -> 0.7 us  [swapped(): return lax.ppermute(x, axis, [(i, i ^ j) for i in range(n)])]
    pallas_call x3 -> x2, Pallas kernels: 1.57 us -> 1.48 us  [the longest x1 1.32 us: attend_moved(): pl.pallas_call(functools.partial(moved_kernel, insts, len(pieces), reside...]
  transfers between devices with their start and end apart: 12 -> 10, of which waited for: 2 -> 2; matrix products, arithmetic and copies ran while one was open for 0% -> 0% of each run, Pallas kernels for 30% -> 36%
where the time goes in v12:
time: 34.4 us; the launch traced here: 34.1 us
  Pallas kernels  17 us (49%)
  starting transfers between devices  14 us (41%)
  waiting for transfers between devices  2.95 us (9%)
    pallas_call x1, Pallas kernels, attend_resident(): pl.pallas_call(functools.partial(resident_kernel, ranks), in_specs=[HBM]...  10.7 us
    ppermute x9, starting transfers between devices, swapped(): return lax.ppermute(x, axis, [(i, i ^ j) for i in range(n)])  10.7 us
    pallas_call x1, Pallas kernels, project(): pl.pallas_call(functools.partial(project_kernel, ranks, group), in_specs=...  4.13 us
    all_to_all x1, starting transfers between devices, per_device(): received = lax.all_to_all(payloads, 'tp', 0, 0, tiled=True)  3.29 us
    all_to_all x1, waiting for transfers between devices, per_device(): received = lax.all_to_all(payloads, 'tp', 0, 0, tiled=True)  2.25 us
    pallas_call x1, Pallas kernels, attend_moved(): pl.pallas_call(functools.partial(moved_kernel, insts, len(pieces), reside...  1.32 us
    ppermute x9, waiting for transfers between devices, swapped(): return lax.ppermute(x, axis, [(i, i ^ j) for i in range(n)])  0.7 us
  transfers between devices with their start and end apart: 10, of which 2 were waited for; matrix products, arithmetic and copies ran while one was open for 0% of the time, Pallas kernels for 36%

profile of v12, /device:TPU:0, one launch (start us, length us, event | category | flops | bytes accessed | tf_op | source)
XLA Modules:
  0.0 34.1 jit_solution(8888754089876137615)
XLA Ops:
  0.0 4.1 %project.1 = (bf16[136,512]{1,0:T(8,128)(2,1)}, bf16[136,512]{1,0:T(8,128)(2,1)}, bf16[136,512]{1,0:T(8,128)(2,1)}, bf16[136,512]{1,0:T(8,128)(2,1)}, bf16[5,2560]{1,0:T(8,128)(2,1)}) custom-call(bf16[1280]{0:T(1024)(128)(2,1)} %gain_hbm.1, bf16[64,2,1280]{2,1,0:T(2,128)(2,1)} %bitcast.16, bf16[1280,2048]{1,0:T(8,128)(2,1)} %w_hbm.1, ...), custom_call_target="tpu_custom_call" | custom-call | flops 671088640 | bytes 5242880 | tf_op jit(solution)/shard_map/project/pallas_call | solution.py:131
  4.1 0.5 %collective-permute-start = (bf16[5,2560]{1,0:T(8,128)(2,1)}, bf16[5,2560]{1,0:T(8,128)(2,1)S(1)}, u32[]{:S(2)}, u32[]{:S(2)}) collective-permute-start(bf16[5,2560]{1,0:T(8,128)(2,1)} %get-tuple-element.19.ask_ref), channel_id=1, source_target_pairs={{0,4},{4,0},{8,12},{12,8},{1,5},{5,1},{9,13},{13,9},{2,6},{6,2},{1... | collective-permute-start | bytes 76808 | tf_op jit(solution)/shard_map/ppermute | solution.py:529
  4.7 4.7 %collective-permute-start.3 = (bf16[136,512]{1,0:T(8,128)(2,1)}, bf16[136,512]{1,0:T(8,128)(2,1)S(1)}, u32[]{:S(2)}, u32[]{:S(2)}) collective-permute-start(bf16[136,512]{1,0:T(8,128)(2,1)} %get-tuple-element.28), channel_id=1, source_target_pairs={{0,3},{1,2},{2,1},{3,0},{4,7},{5,6},{6,5},{7,4},{8,11},{9,10},{10,... | collective-permute-start | bytes 417800 | tf_op jit(solution)/shard_map/ppermute | solution.py:529
  9.3 0.0 collective-permute-done.rest_0_
  9.3 0.3 collective-permute-start.4
  9.7 1.6 %collective-permute-start.5 = (bf16[136,512]{1,0:T(8,128)(2,1)}, bf16[136,512]{1,0:T(8,128)(2,1)S(1)}, u32[]{:S(2)}, u32[]{:S(2)}) collective-permute-start(bf16[136,512]{1,0:T(8,128)(2,1)} %get-tuple-element.30), channel_id=1, source_target_pairs={{0,1},{1,0},{2,3},{3,2},{4,5},{5,4},{6,7},{7,6},{8,9},{9,8},{10,11... | collective-permute-start | bytes 417800 | tf_op jit(solution)/shard_map/ppermute | solution.py:529
  11.2 0.7 %collective-permute-start.2 = (bf16[5,2560]{1,0:T(8,128)(2,1)}, bf16[5,2560]{1,0:T(8,128)(2,1)S(1)}, u32[]{:S(2)}, u32[]{:S(2)}) collective-permute-start(bf16[5,2560]{1,0:T(8,128)(2,1)} %get-tuple-element.19.ask_ref), channel_id=1, source_target_pairs={{0,12},{4,8},{8,4},{12,0},{1,13},{5,9},{9,5},{13,1},{2,14},{6,10},... | collective-permute-start | bytes 76808 | tf_op jit(solution)/shard_map/ppermute | solution.py:529
  11.9 0.8 %collective-permute-start.1 = (bf16[5,2560]{1,0:T(8,128)(2,1)}, bf16[5,2560]{1,0:T(8,128)(2,1)S(1)}, u32[]{:S(2)}, u32[]{:S(2)}) collective-permute-start(bf16[5,2560]{1,0:T(8,128)(2,1)} %get-tuple-element.19.ask_ref), channel_id=1, source_target_pairs={{0,8},{4,12},{8,0},{12,4},{1,9},{5,13},{9,1},{13,5},{2,10},{6,14},... | collective-permute-start | bytes 76808 | tf_op jit(solution)/shard_map/ppermute | solution.py:529
  12.8 0.0 copy-start
  12.8 0.0 copy-start.1
  12.8 0.0 copy-start.2
  12.8 0.0 copy-start.4
  12.8 0.0 copy-start.5
  12.8 0.0 copy-start.6
  12.8 0.0 copy-start.3
  12.8 10.7 %attend_resident.1 = bf16[4,64,128]{2,1,0:T(8,128)(2,1)} custom-call(s32[1,3]{1,0:T(1,128)} %len_hbm.1, bf16[5,8192]{1,0:T(8,128)(2,1)} %bitcast.15, bf16[3,1024,1024]{2,1,0:T(8,128)(2,1)} %bitcast.12, bf16[3,1024,1024]{2,1,0:T(8,128)(2,1)} %bitcast.13), custom_call_target="tpu_custom_call" | custom-call | flops 100663296 | bytes 12582912 | tf_op jit(solution)/shard_map/attend_resident/pallas_call | solution.py:282
  23.5 0.0 collective-permute-done.2.rest_2_
  23.5 0.0 collective-permute-done.1.rest_1_
  23.6 3.3 %all-to-all-start = ((bf16[4,64,128]{2,1,0:T(8,128)(2,1)}), bf16[4,64,128]{2,1,0:T(8,128)(2,1)S(1)}, u32[]{:S(2)}, u32[]{:S(2)}) async-start(bf16[4,64,128]{2,1,0:T(8,128)(2,1)} %attend_resident.1), calls=%async_computation | async-start | bytes 131072 | tf_op jit(solution)/shard_map/all_to_all | solution.py:578
  26.9 0.0 collective-permute-done.3.rest_4_
  26.9 0.0 collective-permute-done.4.rest_5_
  26.9 0.0 collective-permute-done.5.rest_6_
  26.9 0.0 copy-done
  26.9 0.0 copy-done.1
  26.9 0.0 copy-done.2
  26.9 0.0 copy-done.4
  26.9 0.0 copy-done.5
  26.9 0.0 copy-done.6
  26.9 1.3 %attend_moved.1 = (bf16[2,2048]{1,0:T(2,128)(2,1)S(1)}, s32[8,128]{1,0:T(8,128)S(1)}) custom-call(s32[2,4]{1,0:T(2,128)S(1)} %bitcast.9, s32[2,4]{1,0:T(2,128)S(1)} %bitcast.10, bf16[1,128]{1,0:T(2,128)(2,1)S(1)} %bitcast.11, f32[128,128]{1,0:T(8,128)S(1)} %copy-done.2, f32[128,128]{1,0:T(8,128)S(1)} %copy-done.1, ...), custom_call_target="tpu_custom_call" | custom-call | tf_op jit(solution)/shard_map/attend_moved/pallas_call | solution.py:436
  28.3 1.5 %collective-permute-start.8 = (bf16[2,2048]{1,0:T(2,128)(2,1)S(1)}, bf16[2,2048]{1,0:T(2,128)(2,1)S(1)}, u32[]{:S(2)}, u32[]{:S(2)}) collective-permute-start(bf16[2,2048]{1,0:T(2,128)(2,1)S(1)} %get-tuple-element.32), channel_id=1, source_target_pairs={{0,12},{4,8},{8,4},{12,0},{1,13},{5,9},{9,5},{13,1},{2,14},{6,10},... | collective-permute-start | bytes 24584 | tf_op jit(solution)/shard_map/ppermute | solution.py:529
  29.8 0.5 %collective-permute-start.7 = (bf16[2,2048]{1,0:T(2,128)(2,1)S(1)}, bf16[2,2048]{1,0:T(2,128)(2,1)S(1)}, u32[]{:S(2)}, u32[]{:S(2)}) collective-permute-start(bf16[2,2048]{1,0:T(2,128)(2,1)S(1)} %get-tuple-element.32), channel_id=1, source_target_pairs={{0,8},{4,12},{8,0},{12,4},{1,9},{5,13},{9,1},{13,5},{2,10},{6,14},... | collective-permute-start | bytes 24584 | tf_op jit(solution)/shard_map/ppermute | solution.py:529
  30.3 0.0 collective-permute-start.6
  30.3 2.2 %all-to-all-done.payload_ref = bf16[4,64,128]{2,1,0:T(8,128)(2,1)S(1)} async-done(((bf16[4,64,128]{2,1,0:T(8,128)(2,1)}), bf16[4,64,128]{2,1,0:T(8,128)(2,1)S(1)}, u32[]{:S(2)}, u32[]{:S(2)}) %all-to-all-start) | async-done | bytes 65568 | tf_op jit(solution)/shard_map/all_to_all | solution.py:578
  32.6 0.0 copy-done.3
  32.6 0.2 combine_resident.1.kept_ref
  32.7 0.0 collective-permute-done.8.rest_2_
  32.7 0.7 %collective-permute-done.7.rest_1_ = bf16[2,2048]{1,0:T(2,128)(2,1)S(1)} collective-permute-done((bf16[2,2048]{1,0:T(2,128)(2,1)S(1)}, bf16[2,2048]{1,0:T(2,128)(2,1)S(1)}, u32[]{:S(2)}, u32[]{:S(2)}) %collective-permute-start.7) | collective-permute-done | bytes 8224 | tf_op jit(solution)/shard_map/ppermute | solution.py:529
  33.4 0.0 collective-permute-done.6.rest_0_
  33.4 0.7 %finish.1 = bf16[5,2048]{1,0:T(8,128)(2,1)} custom-call(f32[3,2048]{1,0:T(4,128)S(1)} %combine_resident.1.kept_ref, s32[8,128]{1,0:T(8,128)S(1)} %get-tuple-element.31.place_ref, bf16[2,2048]{1,0:T(2,128)(2,1)S(1)} %collective-permute-done.6.rest_0_, bf16[2,2048]{1,0:T(2,128)(2,1)S(1)} %collective-permute-done.7.rest_1_, ...), custom_call_target="tpu_custom_call" | custom-call | tf_op jit(solution)/shard_map/finish/pallas_call | solution.py:518
Async XLA Ops:
  4.1 5.2 %collective-permute-start = (bf16[5,2560]{1,0:T(8,128)(2,1)}, bf16[5,2560]{1,0:T(8,128)(2,1)S(1)}, u32[]{:S(2)}, u32[]{:S(2)}) collective-permute-start(bf16[5,2560]{1,0:T(8,128)(2,1)} %get-tuple-element.19.ask_ref), channel_id=1, source_target_pairs={{0,4},{4,0},{8,12},{12,8},{1,5},{5,1},{9,13},{13,9},{2,6},{6,2},{1... | collective-permute-start | bytes 76808 | tf_op jit(solution)/shard_map/ppermute | solution.py:529
  4.7 22.2 %collective-permute-start.3 = (bf16[136,512]{1,0:T(8,128)(2,1)}, bf16[136,512]{1,0:T(8,128)(2,1)S(1)}, u32[]{:S(2)}, u32[]{:S(2)}) collective-permute-start(bf16[136,512]{1,0:T(8,128)(2,1)} %get-tuple-element.28), channel_id=1, source_target_pairs={{0,3},{1,2},{2,1},{3,0},{4,7},{5,6},{6,5},{7,4},{8,11},{9,10},{10,... | collective-permute-start | bytes 417800 | tf_op jit(solution)/shard_map/ppermute | solution.py:529
  9.3 17.5 %collective-permute-start.4 = (bf16[136,512]{1,0:T(8,128)(2,1)}, bf16[136,512]{1,0:T(8,128)(2,1)S(1)}, u32[]{:S(2)}, u32[]{:S(2)}) collective-permute-start(bf16[136,512]{1,0:T(8,128)(2,1)} %get-tuple-element.29), channel_id=1, source_target_pairs={{0,2},{1,3},{2,0},{3,1},{4,6},{5,7},{6,4},{7,5},{8,10},{9,11},{10,... | collective-permute-start | bytes 417800 | tf_op jit(solution)/shard_map/ppermute | solution.py:529
  9.7 17.2 %collective-permute-start.5 = (bf16[136,512]{1,0:T(8,128)(2,1)}, bf16[136,512]{1,0:T(8,128)(2,1)S(1)}, u32[]{:S(2)}, u32[]{:S(2)}) collective-permute-start(bf16[136,512]{1,0:T(8,128)(2,1)} %get-tuple-element.30), channel_id=1, source_target_pairs={{0,1},{1,0},{2,3},{3,2},{4,5},{5,4},{6,7},{7,6},{8,9},{9,8},{10,11... | collective-permute-start | bytes 417800 | tf_op jit(solution)/shard_map/ppermute | solution.py:529
  11.2 12.3 %collective-permute-start.2 = (bf16[5,2560]{1,0:T(8,128)(2,1)}, bf16[5,2560]{1,0:T(8,128)(2,1)S(1)}, u32[]{:S(2)}, u32[]{:S(2)}) collective-permute-start(bf16[5,2560]{1,0:T(8,128)(2,1)} %get-tuple-element.19.ask_ref), channel_id=1, source_target_pairs={{0,12},{4,8},{8,4},{12,0},{1,13},{5,9},{9,5},{13,1},{2,14},{6,10},... | collective-permute-start | bytes 76808 | tf_op jit(solution)/shard_map/ppermute | solution.py:529
  11.9 11.6 %collective-permute-start.1 = (bf16[5,2560]{1,0:T(8,128)(2,1)}, bf16[5,2560]{1,0:T(8,128)(2,1)S(1)}, u32[]{:S(2)}, u32[]{:S(2)}) collective-permute-start(bf16[5,2560]{1,0:T(8,128)(2,1)} %get-tuple-element.19.ask_ref), channel_id=1, source_target_pairs={{0,8},{4,12},{8,0},{12,4},{1,9},{5,13},{9,1},{13,5},{2,10},{6,14},... | collective-permute-start | bytes 76808 | tf_op jit(solution)/shard_map/ppermute | solution.py:529
  12.8 14.1 %copy-start = (bf16[136,512]{1,0:T(8,128)(2,1)S(1)}, bf16[136,512]{1,0:T(8,128)(2,1)}, u32[]{:S(2)}) copy-start(bf16[136,512]{1,0:T(8,128)(2,1)} %get-tuple-element.27.rest_3_) | copy-start | bytes 417796
  12.8 14.1 %copy-start.1 = (f32[128,128]{1,0:T(8,128)S(1)}, f32[128,128]{1,0:T(8,128)}, u32[]{:S(2)}) copy-start(f32[128,128]{1,0:T(8,128)} %constant.5.clone.sin_ref) | copy-start | bytes 196612
  12.8 14.1 %copy-start.2 = (f32[128,128]{1,0:T(8,128)S(1)}, f32[128,128]{1,0:T(8,128)}, u32[]{:S(2)}) copy-start(f32[128,128]{1,0:T(8,128)} %constant.4.clone.cos_ref) | copy-start | bytes 196612
  12.8 14.1 %copy-start.4 = (s32[4,2]{0,1:T(2,128)S(1)}, s32[4,2]{0,1:T(2,128)}, u32[]{:S(2)}) copy-start(s32[4,2]{0,1:T(2,128)} %param.14) | copy-start | bytes 100
  12.8 14.2 %copy-start.5 = (s32[4,2]{0,1:T(2,128)S(1)}, s32[4,2]{0,1:T(2,128)}, u32[]{:S(2)}) copy-start(s32[4,2]{0,1:T(2,128)} %param.15) | copy-start | bytes 100
  12.8 14.1 %copy-start.6 = (bf16[128]{0:T(256)(128)(2,1)S(1)}, bf16[128]{0:T(256)(128)(2,1)}, u32[]{:S(2)}) copy-start(bf16[128]{0:T(256)(128)(2,1)} %param.18) | copy-start | bytes 772
  12.8 19.8 %copy-start.3 = (bf16[5,2560]{1,0:T(8,128)(2,1)S(1)}, bf16[5,2560]{1,0:T(8,128)(2,1)}, u32[]{:S(2)}) copy-start(bf16[5,2560]{1,0:T(8,128)(2,1)} %get-tuple-element.19.ask_ref) | copy-start | bytes 76804
  23.6 9.0 %all-to-all-start = ((bf16[4,64,128]{2,1,0:T(8,128)(2,1)}), bf16[4,64,128]{2,1,0:T(8,128)(2,1)S(1)}, u32[]{:S(2)}, u32[]{:S(2)}) async-start(bf16[4,64,128]{2,1,0:T(8,128)(2,1)} %attend_resident.1), calls=%async_computation | async-start | bytes 131072 | tf_op jit(solution)/shard_map/all_to_all | solution.py:578
  28.3 4.5 %collective-permute-start.8 = (bf16[2,2048]{1,0:T(2,128)(2,1)S(1)}, bf16[2,2048]{1,0:T(2,128)(2,1)S(1)}, u32[]{:S(2)}, u32[]{:S(2)}) collective-permute-start(bf16[2,2048]{1,0:T(2,128)(2,1)S(1)} %get-tuple-element.32), channel_id=1, source_target_pairs={{0,12},{4,8},{8,4},{12,0},{1,13},{5,9},{9,5},{13,1},{2,14},{6,10},... | collective-permute-start | bytes 24584 | tf_op jit(solution)/shard_map/ppermute | solution.py:529
  29.8 3.7 %collective-permute-start.7 = (bf16[2,2048]{1,0:T(2,128)(2,1)S(1)}, bf16[2,2048]{1,0:T(2,128)(2,1)S(1)}, u32[]{:S(2)}, u32[]{:S(2)}) collective-permute-start(bf16[2,2048]{1,0:T(2,128)(2,1)S(1)} %get-tuple-element.32), channel_id=1, source_target_pairs={{0,8},{4,12},{8,0},{12,4},{1,9},{5,13},{9,1},{13,5},{2,10},{6,14},... | collective-permute-start | bytes 24584 | tf_op jit(solution)/shard_map/ppermute | solution.py:529
  30.3 3.1 %collective-permute-start.6 = (bf16[2,2048]{1,0:T(2,128)(2,1)S(1)}, bf16[2,2048]{1,0:T(2,128)(2,1)S(1)}, u32[]{:S(2)}, u32[]{:S(2)}) collective-permute-start(bf16[2,2048]{1,0:T(2,128)(2,1)S(1)} %get-tuple-element.32), channel_id=1, source_target_pairs={{0,4},{4,0},{8,12},{12,8},{1,5},{5,1},{9,13},{13,9},{2,6},{6,2},{1... | collective-permute-start | bytes 24584 | tf_op jit(solution)/shard_map/ppermute | solution.py:529

commit v13 on v12

--- a/solution.py
+++ b/solution.py
@@ -153,118 +153,74 @@
     return outs[:ranks], outs[ranks]
 
 
-def resident_kernel(ranks, len_hbm, q_hbm, k_hbm, v_hbm, *rest):
-    out, len_ref, q_ref, q_all, k_buf, v_buf, wide_ref, s_buf, w_buf, o_all, s_all, in_sems, sems = (
-        rest
-    )
+def resident_kernel(ranks, len_ref, q_hbm, k_hbm, v_hbm, out, *rest):
+    q_ref, q_wide, k_buf, v_buf, o_all, s_all, q_sem, sems = rest
     residents, positions, width = k_buf.shape
-    half = positions // 2
-    halves = [slice(i * half, (i + 1) * half) for i in range(2)]
-
-    def copies(which, hbm, buf):
-        return [
-            [
-                pltpu.make_async_copy(hbm.at[r, at, :], buf.at[r, at, :], sems.at[which, r, i])
-                for i, at in enumerate(halves)
-            ]
-            for r in range(residents)
-        ]
-
-    k_copies, v_copies = copies(0, k_hbm, k_buf), copies(1, v_hbm, v_buf)
-    len_copy = pltpu.make_async_copy(len_hbm, len_ref, in_sems.at[0])
-    q_copy = pltpu.make_async_copy(q_hbm, q_ref, in_sems.at[1])
-    len_copy.start()
+    q_copy = pltpu.make_async_copy(q_hbm, q_ref, q_sem)
+    copies = []
+    for r in range(residents):
+        copies.append(
+            (
+                pltpu.make_async_copy(k_hbm.at[r], k_buf.at[r], sems.at[0, r]),
+                pltpu.make_async_copy(v_hbm.at[r], v_buf.at[r], sems.at[1, r]),
+            )
+        )
     q_copy.start()
-    rank = lax.axis_index("tp")
-
-    @pl.when(rank == 0)
-    def _():
-        for r in range(residents):
-            for of in (k_copies, v_copies):
-                for copy in of[r]:
-                    copy.start()
-
-    heads = q_ref.shape[1] // 128
+    for pair in copies:
+        for copy in pair:
+            copy.start()
+    heads = q_ref.shape[0]
     kv_heads = width // 128
     group = heads // kv_heads
+    pair_rows = 2 * group
     heads_mine = heads // ranks
-    position = iota((16, positions), 1)
+    rank = lax.axis_index("tp")
+    top_half = iota((pair_rows, 128), 0) < group
+    position = rank * positions + iota((pair_rows, positions), 1)
     scale = F32(1.0) / jnp.sqrt(F32(128.0))
     diagonal = iota((heads, 128), 0) % heads_mine == iota((heads, 128), 1)
-    own_block = iota((heads, width), 0) // group == iota((heads, width), 1) // 128
 
     def to_rows(columns):
         spread = jnp.where(diagonal, jnp.concatenate(columns, axis=0), 0.0)
         return jnp.sum(spread.reshape(ranks, heads_mine, 128), axis=1)
 
-    len_copy.wait()
-    counts = [len_ref[0, r] - rank * positions for r in range(residents)]
+    q_copy.wait()
+    q_wide[...] = q_ref[...].astype(F32)
+    queries = [q_wide[:, r, :].astype(BF16) for r in range(residents)]
     for r in range(residents):
-        for of in (k_copies, v_copies):
-            for i in range(2):
-                pl.when((rank > 0) & (counts[r] > i * half))(of[r][i].start)
-    q_copy.wait()
-    for h in range(heads):
-        q_all[h * 8 : h * 8 + residents, :] = q_ref[:residents, h * 128 : (h + 1) * 128].astype(F32)
-    for r in range(residents):
-        some = (rank == 0) | (counts[r] > 0)
-
-        @pl.when(some)
-        def _():
-            q = q_all[pl.ds(r, heads, stride=8), :].astype(BF16)
-            wide = jnp.concatenate([q] * kv_heads, axis=1)
-            wide_ref[...] = jnp.where(own_block, wide, jnp.zeros_like(wide))
-
-        for i, at in enumerate(halves):
-
-            @pl.when((rank == 0) | (counts[r] > i * half))
-            def _():
-                k_copies[r][i].wait()
-                s_buf[:, at] = lax.dot_general(
-                    wide_ref[...],
-                    k_buf[r, at, :],
-                    (((1,), (1,)), ((), ())),
-                    preferred_element_type=F32,
-                )
-
-        @pl.when(some)
-        def _():
-            valid = position < counts[r]
-            peaks, totals = [], []
-            for c in range(0, heads, 16):
-                rows = slice(c, c + 16)
-                scores = jnp.where(valid, s_buf[rows, :] * scale, ABSENT)
-                peak = jnp.max(scores, axis=1, keepdims=True).astype(BF16).astype(F32)
-                weight = jnp.where(valid, jnp.exp(scores - peak), 0.0)
-                peaks.append(peak)
-                totals.append(jnp.sum(weight, axis=1, keepdims=True))
-                w_buf[rows, :] = weight.astype(BF16)
-            s_all[r, 0] = to_rows(peaks)
-            high, low = split_bf16(to_rows(totals))
-            s_all[r, 1] = high.astype(F32)
-            s_all[r, 2] = low.astype(F32)
-
-        @pl.when(jnp.logical_not(some))
-        def _():
-            s_all[r, 0] = jnp.full((ranks, 128), ABSENT, F32)
-            s_all[r, 1] = jnp.zeros((ranks, 128), F32)
-            s_all[r, 2] = jnp.zeros((ranks, 128), F32)
-            o_all[r] = jnp.zeros((heads, 128), F32)
-
-        for i, at in enumerate(halves):
-
-            @pl.when((rank == 0) | (counts[r] > i * half))
-            def _():
-                v_copies[r][i].wait()
-                part = jnp.dot(w_buf[:, at], v_buf[r, at, :], preferred_element_type=F32)
-                for g in range(kv_heads):
-                    rows = slice(g * group, (g + 1) * group)
-                    block = part[rows, g * 128 : (g + 1) * 128]
-                    if i == 0:
-                        o_all[r, rows, :] = block
-                    else:
-                        o_all[r, rows, :] += block
-
+        valid = position < len_ref[0, r]
+        copies[r][0].wait()
+        weights, peaks, totals = [], [], []
+        for p in range(kv_heads // 2):
+            q = queries[r][p * pair_rows : (p + 1) * pair_rows]
+            zero = jnp.zeros_like(q)
+            lhs = jnp.concatenate(
+                [jnp.where(top_half, q, zero), jnp.where(top_half, zero, q)], axis=1
+            )
+            scores = lax.dot_general(
+                lhs,
+                k_buf[r, :, p * 256 : (p + 1) * 256],
+                (((1,), (1,)), ((), ())),
+                preferred_element_type=F32,
+            )
+            scores = jnp.where(valid, scores * scale, ABSENT)
+            peak = jnp.max(scores, axis=1, keepdims=True).astype(BF16).astype(F32)
+            weight = jnp.where(valid, jnp.exp(scores - peak), 0.0)
+            peaks.append(peak)
+            totals.append(jnp.sum(weight, axis=1, keepdims=True))
+            weights.append(weight.astype(BF16))
+        s_all[r, 0] = to_rows(peaks)
+        high, low = split_bf16(to_rows(totals))
+        s_all[r, 1] = high.astype(F32)
+        s_all[r, 2] = low.astype(F32)
+        copies[r][1].wait()
+        for p in range(kv_heads // 2):
+            both = jnp.dot(
+                weights[p], v_buf[r, :, p * 256 : (p + 1) * 256], preferred_element_type=F32
+            )
+            o_all[r, p * pair_rows : (p + 1) * pair_rows, :] = jnp.where(
+                top_half, both[:, :128], both[:, 128:]
+            )
     filled = residents * (heads_mine + 3)
     for t in range(ranks):
         parts = [o_all[r, t * heads_mine : (t + 1) * heads_mine, :] for r in range(residents)]
@@ -274,29 +230,25 @@
         out[t] = jnp.concatenate(parts, axis=0).astype(BF16)
 
 
-def attend_resident(lengths, query, k_cache, v_cache, ranks):
+def attend_resident(lengths, queries, k_cache, v_cache, ranks):
     residents, positions, width = k_cache.shape
-    heads = query.shape[1] // 128
+    heads = queries.shape[0]
     heads_mine = heads // ranks
     rows = -(-(residents * (heads_mine + 3)) // 16) * 16
     return pl.pallas_call(
         functools.partial(resident_kernel, ranks),
-        in_specs=[HBM] * 4,
+        in_specs=[SMEM, HBM, HBM, HBM],
         out_specs=VMEM,
         out_shape=jax.ShapeDtypeStruct((ranks, rows, 128), BF16),
         scratch_shapes=[
-            pltpu.SMEM(lengths.shape, jnp.int32),
-            pltpu.VMEM(query.shape, BF16),
-            pltpu.VMEM((heads * 8, 128), F32),
+            pltpu.VMEM(queries.shape, BF16),
+            pltpu.VMEM(queries.shape, F32),
             pltpu.VMEM((residents, positions, width), BF16),
             pltpu.VMEM((residents, positions, width), BF16),
-            pltpu.VMEM((heads, width), BF16),
-            pltpu.VMEM((heads, positions), F32),
-            pltpu.VMEM((heads, positions), BF16),
             pltpu.VMEM((residents, heads, 128), F32),
             pltpu.VMEM((residents, 3, ranks, 128), F32),
-            pltpu.SemaphoreType.DMA((2,)),
-            pltpu.SemaphoreType.DMA((2, residents, 2)),
+            pltpu.SemaphoreType.DMA,
+            pltpu.SemaphoreType.DMA((2, residents)),
         ],
         compiler_params=pltpu.CompilerParams(vmem_limit_bytes=56 * MIB),
         cost_estimate=pl.CostEstimate(
@@ -305,7 +257,7 @@
             transcendentals=residents * heads * positions,
         ),
         name="attend_resident",
-    )(lengths, query, k_cache, v_cache)
+    )(lengths, queries, k_cache, v_cache)
 
 
 def expand(own, rows):
@@ -573,7 +525,8 @@
     asks[0], *others = lax.optimization_barrier((asks[0], *pieces[1:last]))
     others = [swapped(others[j - 1], "tp", j, ranks) for j in reversed(range(1, last))]
     pieces = [pieces[0], far] + others
-    payloads = attend_resident(lengths, query[0], k_cache[0], v_cache[0], ranks)
+    queries = jnp.transpose(query[0].reshape(query.shape[1], heads, head_size), (1, 0, 2))
+    payloads = attend_resident(lengths, queries, k_cache[0], v_cache[0], ranks)
     asks, payloads = lax.optimization_barrier((asks, payloads))
     received = lax.all_to_all(payloads, "tp", 0, 0, tiled=True)
     cos, sin = rotation(slots, requests, head_size)

time: 34.4 us -> 33.3 us (0.968)
  Pallas kernels: 17 us -> 15.7 us
    pallas_call x1, Pallas kernels: 10.7 us -> 9.46 us  [attend_resident(): pl.pallas_call(functools.partial(resident_kernel, ranks), in_specs=[SMEM,...]
    all_to_all x1, starting transfers between devices: 3.29 us -> 3.76 us  [per_device(): received = lax.all_to_all(payloads, 'tp', 0, 0, tiled=True)]
  transfers between devices with their start and end apart: 10 -> 10, of which waited for: 2 -> 2; matrix products, arithmetic and copies ran while one was open for 0% -> 0% of each run, Pallas kernels for 36% -> 33%
where the time goes in v13:
time: 33.3 us; the launch traced here: 33 us
  Pallas kernels  15.7 us (47%)
  starting transfers between devices  14.3 us (43%)
  waiting for transfers between devices  2.78 us (8%)
    ppermute x9, starting transfers between devices, swapped(): return lax.ppermute(x, axis, [(i, i ^ j) for i in range(n)])  10.5 us
    pallas_call x1, Pallas kernels, attend_resident(): pl.pallas_call(functools.partial(resident_kernel, ranks), in_specs=[SMEM,...  9.46 us
    pallas_call x1, Pallas kernels, project(): pl.pallas_call(functools.partial(project_kernel, ranks, group), in_specs=...  4.13 us
    all_to_all x1, starting transfers between devices, per_device(): received = lax.all_to_all(payloads, 'tp', 0, 0, tiled=True)  3.76 us
    all_to_all x1, waiting for transfers between devices, per_device(): received = lax.all_to_all(payloads, 'tp', 0, 0, tiled=True)  2.41 us
    pallas_call x1, Pallas kernels, attend_moved(): pl.pallas_call(functools.partial(moved_kernel, insts, len(pieces), reside...  1.32 us
  transfers between devices with their start and end apart: 10, of which 2 were waited for; matrix products, arithmetic and copies ran while one was open for 0% of the time, Pallas kernels for 33%

profile of v13, /device:TPU:0, one launch (start us, length us, event | category | flops | bytes accessed | tf_op | source)
XLA Modules:
  0.0 33.0 jit_solution(7021061057150076892)
XLA Ops:
  0.0 4.1 %project.1 = (bf16[136,512]{1,0:T(8,128)(2,1)}, bf16[136,512]{1,0:T(8,128)(2,1)}, bf16[136,512]{1,0:T(8,128)(2,1)}, bf16[136,512]{1,0:T(8,128)(2,1)}, bf16[5,2560]{1,0:T(8,128)(2,1)}) custom-call(bf16[1280]{0:T(1024)(128)(2,1)} %gain_hbm.1, bf16[64,2,1280]{2,1,0:T(2,128)(2,1)} %bitcast.19, bf16[1280,2048]{1,0:T(8,128)(2,1)} %w_hbm.1, ...), custom_call_target="tpu_custom_call" | custom-call | flops 671088640 | bytes 5242880 | tf_op jit(solution)/shard_map/project/pallas_call | solution.py:131
  4.1 0.5 %collective-permute-start = (bf16[5,2560]{1,0:T(8,128)(2,1)}, bf16[5,2560]{1,0:T(8,128)(2,1)S(1)}, u32[]{:S(2)}, u32[]{:S(2)}) collective-permute-start(bf16[5,2560]{1,0:T(8,128)(2,1)} %get-tuple-element.19.ask_ref), channel_id=1, source_target_pairs={{0,4},{4,0},{8,12},{12,8},{1,5},{5,1},{9,13},{13,9},{2,6},{6,2},{1... | collective-permute-start | bytes 76808 | tf_op jit(solution)/shard_map/ppermute | solution.py:481
  4.7 4.7 %collective-permute-start.3 = (bf16[136,512]{1,0:T(8,128)(2,1)}, bf16[136,512]{1,0:T(8,128)(2,1)S(1)}, u32[]{:S(2)}, u32[]{:S(2)}) collective-permute-start(bf16[136,512]{1,0:T(8,128)(2,1)} %get-tuple-element.28), channel_id=1, source_target_pairs={{0,3},{1,2},{2,1},{3,0},{4,7},{5,6},{6,5},{7,4},{8,11},{9,10},{10,... | collective-permute-start | bytes 417800 | tf_op jit(solution)/shard_map/ppermute | solution.py:481
  9.3 0.0 collective-permute-done.rest_0_
  9.3 0.3 %collective-permute-start.4 = (bf16[136,512]{1,0:T(8,128)(2,1)}, bf16[136,512]{1,0:T(8,128)(2,1)S(1)}, u32[]{:S(2)}, u32[]{:S(2)}) collective-permute-start(bf16[136,512]{1,0:T(8,128)(2,1)} %get-tuple-element.29), channel_id=1, source_target_pairs={{0,2},{1,3},{2,0},{3,1},{4,6},{5,7},{6,4},{7,5},{8,10},{9,11},{10,... | collective-permute-start | bytes 417800 | tf_op jit(solution)/shard_map/ppermute | solution.py:481
  9.7 1.6 %collective-permute-start.5 = (bf16[136,512]{1,0:T(8,128)(2,1)}, bf16[136,512]{1,0:T(8,128)(2,1)S(1)}, u32[]{:S(2)}, u32[]{:S(2)}) collective-permute-start(bf16[136,512]{1,0:T(8,128)(2,1)} %get-tuple-element.30), channel_id=1, source_target_pairs={{0,1},{1,0},{2,3},{3,2},{4,5},{5,4},{6,7},{7,6},{8,9},{9,8},{10,11... | collective-permute-start | bytes 417800 | tf_op jit(solution)/shard_map/ppermute | solution.py:481
  11.2 0.7 %collective-permute-start.2 = (bf16[5,2560]{1,0:T(8,128)(2,1)}, bf16[5,2560]{1,0:T(8,128)(2,1)S(1)}, u32[]{:S(2)}, u32[]{:S(2)}) collective-permute-start(bf16[5,2560]{1,0:T(8,128)(2,1)} %get-tuple-element.19.ask_ref), channel_id=1, source_target_pairs={{0,12},{4,8},{8,4},{12,0},{1,13},{5,9},{9,5},{13,1},{2,14},{6,10},... | collective-permute-start | bytes 76808 | tf_op jit(solution)/shard_map/ppermute | solution.py:481
  11.9 0.8 %collective-permute-start.1 = (bf16[5,2560]{1,0:T(8,128)(2,1)}, bf16[5,2560]{1,0:T(8,128)(2,1)S(1)}, u32[]{:S(2)}, u32[]{:S(2)}) collective-permute-start(bf16[5,2560]{1,0:T(8,128)(2,1)} %get-tuple-element.19.ask_ref), channel_id=1, source_target_pairs={{0,8},{4,12},{8,0},{12,4},{1,9},{5,13},{9,1},{13,5},{2,10},{6,14},... | collective-permute-start | bytes 76808 | tf_op jit(solution)/shard_map/ppermute | solution.py:481
  12.8 0.0 copy-start
  12.8 0.0 copy-start.1
  12.8 0.0 copy-start.2
  12.8 0.0 copy-start.4
  12.8 0.0 copy-start.5
  12.8 0.0 copy-start.6
  12.8 0.0 copy-start.3
  12.8 9.5 %attend_resident.1 = bf16[4,64,128]{2,1,0:T(8,128)(2,1)} custom-call(s32[1,3]{1,0:T(1,128)} %len_ref.1, bf16[64,5,128]{2,1,0:T(8,128)(2,1)} %bitcast.18, bf16[3,1024,1024]{2,1,0:T(8,128)(2,1)} %bitcast.15, bf16[3,1024,1024]{2,1,0:T(8,128)(2,1)} %bitcast.16), custom_call_target="tpu_custom_call" | custom-call | flops 100663296 | bytes 12582912 | tf_op jit(solution)/shard_map/attend_resident/pallas_call | solution.py:238
  22.3 0.0 collective-permute-done.2.rest_2_
  22.3 0.0 collective-permute-done.1.rest_1_
  22.3 3.8 %all-to-all-start = ((bf16[4,64,128]{2,1,0:T(8,128)(2,1)}), bf16[4,64,128]{2,1,0:T(8,128)(2,1)S(1)}, u32[]{:S(2)}, u32[]{:S(2)}) async-start(bf16[4,64,128]{2,1,0:T(8,128)(2,1)} %attend_resident.1), calls=%async_computation | async-start | bytes 131072 | tf_op jit(solution)/shard_map/all_to_all | solution.py:531
  26.1 0.0 collective-permute-done.3.rest_4_
  26.1 0.0 collective-permute-done.4.rest_5_
  26.1 0.0 collective-permute-done.5.rest_6_
  26.1 0.0 copy-done
  26.1 0.0 copy-done.1
  26.1 0.0 copy-done.2
  26.1 0.0 copy-done.4
  26.1 0.0 copy-done.5
  26.1 0.0 copy-done.6
  26.1 1.3 %attend_moved.1 = (bf16[2,2048]{1,0:T(2,128)(2,1)S(1)}, s32[8,128]{1,0:T(8,128)S(1)}) custom-call(s32[2,4]{1,0:T(2,128)S(1)} %bitcast.12, s32[2,4]{1,0:T(2,128)S(1)} %bitcast.13, bf16[1,128]{1,0:T(2,128)(2,1)S(1)} %bitcast.14, f32[128,128]{1,0:T(8,128)S(1)} %copy-done.2, f32[128,128]{1,0:T(8,128)S(1)} %copy-done.1, ...), custom_call_target="tpu_custom_call" | custom-call | tf_op jit(solution)/shard_map/attend_moved/pallas_call | solution.py:388
  27.5 1.2 %collective-permute-start.8 = (bf16[2,2048]{1,0:T(2,128)(2,1)S(1)}, bf16[2,2048]{1,0:T(2,128)(2,1)S(1)}, u32[]{:S(2)}, u32[]{:S(2)}) collective-permute-start(bf16[2,2048]{1,0:T(2,128)(2,1)S(1)} %get-tuple-element.32), channel_id=1, source_target_pairs={{0,12},{4,8},{8,4},{12,0},{1,13},{5,9},{9,5},{13,1},{2,14},{6,10},... | collective-permute-start | bytes 24584 | tf_op jit(solution)/shard_map/ppermute | solution.py:481
  28.7 0.5 %collective-permute-start.7 = (bf16[2,2048]{1,0:T(2,128)(2,1)S(1)}, bf16[2,2048]{1,0:T(2,128)(2,1)S(1)}, u32[]{:S(2)}, u32[]{:S(2)}) collective-permute-start(bf16[2,2048]{1,0:T(2,128)(2,1)S(1)} %get-tuple-element.32), channel_id=1, source_target_pairs={{0,8},{4,12},{8,0},{12,4},{1,9},{5,13},{9,1},{13,5},{2,10},{6,14},... | collective-permute-start | bytes 24584 | tf_op jit(solution)/shard_map/ppermute | solution.py:481
  29.2 0.2 collective-permute-start.6
  29.4 2.4 %all-to-all-done.payload_ref = bf16[4,64,128]{2,1,0:T(8,128)(2,1)S(1)} async-done(((bf16[4,64,128]{2,1,0:T(8,128)(2,1)}), bf16[4,64,128]{2,1,0:T(8,128)(2,1)S(1)}, u32[]{:S(2)}, u32[]{:S(2)}) %all-to-all-start) | async-done | bytes 65568 | tf_op jit(solution)/shard_map/all_to_all | solution.py:531
  31.8 0.0 copy-done.3
  31.8 0.2 combine_resident.1.kept_ref
  32.0 0.0 collective-permute-done.8.rest_2_
  32.0 0.3 %collective-permute-done.7.rest_1_ = bf16[2,2048]{1,0:T(2,128)(2,1)S(1)} collective-permute-done((bf16[2,2048]{1,0:T(2,128)(2,1)S(1)}, bf16[2,2048]{1,0:T(2,128)(2,1)S(1)}, u32[]{:S(2)}, u32[]{:S(2)}) %collective-permute-start.7) | collective-permute-done | bytes 8224 | tf_op jit(solution)/shard_map/ppermute | solution.py:481
  32.3 0.0 collective-permute-done.6.rest_0_
  32.3 0.7 %finish.1 = bf16[5,2048]{1,0:T(8,128)(2,1)} custom-call(f32[3,2048]{1,0:T(4,128)S(1)} %combine_resident.1.kept_ref, s32[8,128]{1,0:T(8,128)S(1)} %get-tuple-element.31.place_ref, bf16[2,2048]{1,0:T(2,128)(2,1)S(1)} %collective-permute-done.6.rest_0_, bf16[2,2048]{1,0:T(2,128)(2,1)S(1)} %collective-permute-done.7.rest_1_, ...), custom_call_target="tpu_custom_call" | custom-call | tf_op jit(solution)/shard_map/finish/pallas_call | solution.py:470
Async XLA Ops:
  4.1 5.2 %collective-permute-start = (bf16[5,2560]{1,0:T(8,128)(2,1)}, bf16[5,2560]{1,0:T(8,128)(2,1)S(1)}, u32[]{:S(2)}, u32[]{:S(2)}) collective-permute-start(bf16[5,2560]{1,0:T(8,128)(2,1)} %get-tuple-element.19.ask_ref), channel_id=1, source_target_pairs={{0,4},{4,0},{8,12},{12,8},{1,5},{5,1},{9,13},{13,9},{2,6},{6,2},{1... | collective-permute-start | bytes 76808 | tf_op jit(solution)/shard_map/ppermute | solution.py:481
  4.7 21.4 %collective-permute-start.3 = (bf16[136,512]{1,0:T(8,128)(2,1)}, bf16[136,512]{1,0:T(8,128)(2,1)S(1)}, u32[]{:S(2)}, u32[]{:S(2)}) collective-permute-start(bf16[136,512]{1,0:T(8,128)(2,1)} %get-tuple-element.28), channel_id=1, source_target_pairs={{0,3},{1,2},{2,1},{3,0},{4,7},{5,6},{6,5},{7,4},{8,11},{9,10},{10,... | collective-permute-start | bytes 417800 | tf_op jit(solution)/shard_map/ppermute | solution.py:481
  9.3 16.7 %collective-permute-start.4 = (bf16[136,512]{1,0:T(8,128)(2,1)}, bf16[136,512]{1,0:T(8,128)(2,1)S(1)}, u32[]{:S(2)}, u32[]{:S(2)}) collective-permute-start(bf16[136,512]{1,0:T(8,128)(2,1)} %get-tuple-element.29), channel_id=1, source_target_pairs={{0,2},{1,3},{2,0},{3,1},{4,6},{5,7},{6,4},{7,5},{8,10},{9,11},{10,... | collective-permute-start | bytes 417800 | tf_op jit(solution)/shard_map/ppermute | solution.py:481
  9.7 16.4 %collective-permute-start.5 = (bf16[136,512]{1,0:T(8,128)(2,1)}, bf16[136,512]{1,0:T(8,128)(2,1)S(1)}, u32[]{:S(2)}, u32[]{:S(2)}) collective-permute-start(bf16[136,512]{1,0:T(8,128)(2,1)} %get-tuple-element.30), channel_id=1, source_target_pairs={{0,1},{1,0},{2,3},{3,2},{4,5},{5,4},{6,7},{7,6},{8,9},{9,8},{10,11... | collective-permute-start | bytes 417800 | tf_op jit(solution)/shard_map/ppermute | solution.py:481
  11.2 11.0 %collective-permute-start.2 = (bf16[5,2560]{1,0:T(8,128)(2,1)}, bf16[5,2560]{1,0:T(8,128)(2,1)S(1)}, u32[]{:S(2)}, u32[]{:S(2)}) collective-permute-start(bf16[5,2560]{1,0:T(8,128)(2,1)} %get-tuple-element.19.ask_ref), channel_id=1, source_target_pairs={{0,12},{4,8},{8,4},{12,0},{1,13},{5,9},{9,5},{13,1},{2,14},{6,10},... | collective-permute-start | bytes 76808 | tf_op jit(solution)/shard_map/ppermute | solution.py:481
  11.9 10.4 %collective-permute-start.1 = (bf16[5,2560]{1,0:T(8,128)(2,1)}, bf16[5,2560]{1,0:T(8,128)(2,1)S(1)}, u32[]{:S(2)}, u32[]{:S(2)}) collective-permute-start(bf16[5,2560]{1,0:T(8,128)(2,1)} %get-tuple-element.19.ask_ref), channel_id=1, source_target_pairs={{0,8},{4,12},{8,0},{12,4},{1,9},{5,13},{9,1},{13,5},{2,10},{6,14},... | collective-permute-start | bytes 76808 | tf_op jit(solution)/shard_map/ppermute | solution.py:481
  12.8 13.3 %copy-start = (bf16[136,512]{1,0:T(8,128)(2,1)S(1)}, bf16[136,512]{1,0:T(8,128)(2,1)}, u32[]{:S(2)}) copy-start(bf16[136,512]{1,0:T(8,128)(2,1)} %get-tuple-element.27.rest_3_) | copy-start | bytes 417796
  12.8 13.3 %copy-start.1 = (f32[128,128]{1,0:T(8,128)S(1)}, f32[128,128]{1,0:T(8,128)}, u32[]{:S(2)}) copy-start(f32[128,128]{1,0:T(8,128)} %constant.5.clone.sin_ref) | copy-start | bytes 196612
  12.8 13.3 %copy-start.2 = (f32[128,128]{1,0:T(8,128)S(1)}, f32[128,128]{1,0:T(8,128)}, u32[]{:S(2)}) copy-start(f32[128,128]{1,0:T(8,128)} %constant.4.clone.cos_ref) | copy-start | bytes 196612
  12.8 13.3 %copy-start.4 = (s32[4,2]{0,1:T(2,128)S(1)}, s32[4,2]{0,1:T(2,128)}, u32[]{:S(2)}) copy-start(s32[4,2]{0,1:T(2,128)} %param.14) | copy-start | bytes 100
  12.8 13.3 %copy-start.5 = (s32[4,2]{0,1:T(2,128)S(1)}, s32[4,2]{0,1:T(2,128)}, u32[]{:S(2)}) copy-start(s32[4,2]{0,1:T(2,128)} %param.15) | copy-start | bytes 100
  12.8 13.3 %copy-start.6 = (bf16[128]{0:T(256)(128)(2,1)S(1)}, bf16[128]{0:T(256)(128)(2,1)}, u32[]{:S(2)}) copy-start(bf16[128]{0:T(256)(128)(2,1)} %param.18) | copy-start | bytes 772
  12.8 19.0 %copy-start.3 = (bf16[5,2560]{1,0:T(8,128)(2,1)S(1)}, bf16[5,2560]{1,0:T(8,128)(2,1)}, u32[]{:S(2)}) copy-start(bf16[5,2560]{1,0:T(8,128)(2,1)} %get-tuple-element.19.ask_ref) | copy-start | bytes 76804
  22.3 9.5 %all-to-all-start = ((bf16[4,64,128]{2,1,0:T(8,128)(2,1)}), bf16[4,64,128]{2,1,0:T(8,128)(2,1)S(1)}, u32[]{:S(2)}, u32[]{:S(2)}) async-start(bf16[4,64,128]{2,1,0:T(8,128)(2,1)} %attend_resident.1), calls=%async_computation | async-start | bytes 131072 | tf_op jit(solution)/shard_map/all_to_all | solution.py:531
  27.5 4.5 %collective-permute-start.8 = (bf16[2,2048]{1,0:T(2,128)(2,1)S(1)}, bf16[2,2048]{1,0:T(2,128)(2,1)S(1)}, u32[]{:S(2)}, u32[]{:S(2)}) collective-permute-start(bf16[2,2048]{1,0:T(2,128)(2,1)S(1)} %get-tuple-element.32), channel_id=1, source_target_pairs={{0,12},{4,8},{8,4},{12,0},{1,13},{5,9},{9,5},{13,1},{2,14},{6,10},... | collective-permute-start | bytes 24584 | tf_op jit(solution)/shard_map/ppermute | solution.py:481
  28.7 3.7 %collective-permute-start.7 = (bf16[2,2048]{1,0:T(2,128)(2,1)S(1)}, bf16[2,2048]{1,0:T(2,128)(2,1)S(1)}, u32[]{:S(2)}, u32[]{:S(2)}) collective-permute-start(bf16[2,2048]{1,0:T(2,128)(2,1)S(1)} %get-tuple-element.32), channel_id=1, source_target_pairs={{0,8},{4,12},{8,0},{12,4},{1,9},{5,13},{9,1},{13,5},{2,10},{6,14},... | collective-permute-start | bytes 24584 | tf_op jit(solution)/shard_map/ppermute | solution.py:481
  29.2 3.1 %collective-permute-start.6 = (bf16[2,2048]{1,0:T(2,128)(2,1)S(1)}, bf16[2,2048]{1,0:T(2,128)(2,1)S(1)}, u32[]{:S(2)}, u32[]{:S(2)}) collective-permute-start(bf16[2,2048]{1,0:T(2,128)(2,1)S(1)} %get-tuple-element.32), channel_id=1, source_target_pairs={{0,4},{4,0},{8,12},{12,8},{1,5},{5,1},{9,13},{13,9},{2,6},{6,2},{1... | collective-permute-start | bytes 24584 | tf_op jit(solution)/shard_map/ppermute | solution.py:481

commit v14 on v13

--- a/solution.py
+++ b/solution.py
@@ -153,10 +153,9 @@
     return outs[:ranks], outs[ranks]
 
 
-def resident_kernel(ranks, len_ref, q_hbm, k_hbm, v_hbm, out, *rest):
-    q_ref, q_wide, k_buf, v_buf, o_all, s_all, q_sem, sems = rest
+def resident_kernel(ranks, len_ref, q_ref, k_hbm, v_hbm, out, *rest):
+    q_wide, q_all, k_buf, v_buf, o_all, m_all, l_all, s_all, sems = rest
     residents, positions, width = k_buf.shape
-    q_copy = pltpu.make_async_copy(q_hbm, q_ref, q_sem)
     copies = []
     for r in range(residents):
         copies.append(
@@ -165,7 +164,6 @@
                 pltpu.make_async_copy(v_hbm.at[r], v_buf.at[r], sems.at[1, r]),
             )
         )
-    q_copy.start()
     for pair in copies:
         for copy in pair:
             copy.start()
@@ -180,19 +178,20 @@
     scale = F32(1.0) / jnp.sqrt(F32(128.0))
     diagonal = iota((heads, 128), 0) % heads_mine == iota((heads, 128), 1)
 
-    def to_rows(columns):
-        spread = jnp.where(diagonal, jnp.concatenate(columns, axis=0), 0.0)
+    def to_rows(column):
+        spread = jnp.where(diagonal, column, 0.0)
         return jnp.sum(spread.reshape(ranks, heads_mine, 128), axis=1)
 
-    q_copy.wait()
     q_wide[...] = q_ref[...].astype(F32)
-    queries = [q_wide[:, r, :].astype(BF16) for r in range(residents)]
+    for r in range(residents):
+        q_all[r] = q_wide[:, r, :].astype(BF16)
     for r in range(residents):
         valid = position < len_ref[0, r]
         copies[r][0].wait()
-        weights, peaks, totals = [], [], []
+        weights = []
         for p in range(kv_heads // 2):
-            q = queries[r][p * pair_rows : (p + 1) * pair_rows]
+            rows = slice(p * pair_rows, (p + 1) * pair_rows)
+            q = q_all[r, rows, :]
             zero = jnp.zeros_like(q)
             lhs = jnp.concatenate(
                 [jnp.where(top_half, q, zero), jnp.where(top_half, zero, q)], axis=1
@@ -206,13 +205,9 @@
             scores = jnp.where(valid, scores * scale, ABSENT)
             peak = jnp.max(scores, axis=1, keepdims=True).astype(BF16).astype(F32)
             weight = jnp.where(valid, jnp.exp(scores - peak), 0.0)
-            peaks.append(peak)
-            totals.append(jnp.sum(weight, axis=1, keepdims=True))
+            m_all[r, rows, :] = peak
+            l_all[r, rows, :] = jnp.sum(weight, axis=1, keepdims=True)
             weights.append(weight.astype(BF16))
-        s_all[r, 0] = to_rows(peaks)
-        high, low = split_bf16(to_rows(totals))
-        s_all[r, 1] = high.astype(F32)
-        s_all[r, 2] = low.astype(F32)
         copies[r][1].wait()
         for p in range(kv_heads // 2):
             both = jnp.dot(
@@ -221,6 +216,11 @@
             o_all[r, p * pair_rows : (p + 1) * pair_rows, :] = jnp.where(
                 top_half, both[:, :128], both[:, 128:]
             )
+    for r in range(residents):
+        s_all[r, 0] = to_rows(m_all[r])
+        high, low = split_bf16(to_rows(l_all[r]))
+        s_all[r, 1] = high.astype(F32)
+        s_all[r, 2] = low.astype(F32)
     filled = residents * (heads_mine + 3)
     for t in range(ranks):
         parts = [o_all[r, t * heads_mine : (t + 1) * heads_mine, :] for r in range(residents)]
@@ -237,17 +237,18 @@
     rows = -(-(residents * (heads_mine + 3)) // 16) * 16
     return pl.pallas_call(
         functools.partial(resident_kernel, ranks),
-        in_specs=[SMEM, HBM, HBM, HBM],
+        in_specs=[SMEM, VMEM, HBM, HBM],
         out_specs=VMEM,
         out_shape=jax.ShapeDtypeStruct((ranks, rows, 128), BF16),
         scratch_shapes=[
-            pltpu.VMEM(queries.shape, BF16),
             pltpu.VMEM(queries.shape, F32),
+            pltpu.VMEM((residents, heads, 128), BF16),
             pltpu.VMEM((residents, positions, width), BF16),
             pltpu.VMEM((residents, positions, width), BF16),
             pltpu.VMEM((residents, heads, 128), F32),
+            pltpu.VMEM((residents, heads, 1), F32),
+            pltpu.VMEM((residents, heads, 1), F32),
             pltpu.VMEM((residents, 3, ranks, 128), F32),
-            pltpu.SemaphoreType.DMA,
             pltpu.SemaphoreType.DMA((2, residents)),
         ],
         compiler_params=pltpu.CompilerParams(vmem_limit_bytes=56 * MIB),

time: 33.3 us -> 30.8 us (0.925)
  Pallas kernels: 15.7 us -> 13.3 us
    pallas_call x1, Pallas kernels: 9.46 us -> 6.99 us  [attend_resident(): pl.pallas_call(functools.partial(resident_kernel, ranks), in_specs=[SMEM,...]
  transfers between devices with their start and end apart: 10 -> 10, of which waited for: 2 -> 2; matrix products, arithmetic and copies ran while one was open for 0% -> 0% of each run, Pallas kernels for 33% -> 28%
where the time goes in v14:
time: 30.8 us; the launch traced here: 30.5 us
  starting transfers between devices  14.3 us (46%)
  Pallas kernels  13.3 us (43%)
  waiting for transfers between devices  2.78 us (9%)
    ppermute x9, starting transfers between devices, swapped(): return lax.ppermute(x, axis, [(i, i ^ j) for i in range(n)])  10.5 us
    pallas_call x1, Pallas kernels, attend_resident(): pl.pallas_call(functools.partial(resident_kernel, ranks), in_specs=[SMEM,...  6.99 us
    pallas_call x1, Pallas kernels, project(): pl.pallas_call(functools.partial(project_kernel, ranks, group), in_specs=...  4.13 us
    all_to_all x1, starting transfers between devices, per_device(): received = lax.all_to_all(payloads, 'tp', 0, 0, tiled=True)  3.76 us
    all_to_all x1, waiting for transfers between devices, per_device(): received = lax.all_to_all(payloads, 'tp', 0, 0, tiled=True)  2.41 us
    pallas_call x1, Pallas kernels, attend_moved(): pl.pallas_call(functools.partial(moved_kernel, insts, len(pieces), reside...  1.32 us
    pallas_call x1, Pallas kernels, finish(): pl.pallas_call(finish_kernel, in_specs=[VMEM] * (2 + len(moved)), out_spe...  0.67 us
  transfers between devices with their start and end apart: 10, of which 2 were waited for; matrix products, arithmetic and copies ran while one was open for 0% of the time, Pallas kernels for 28%

profile of v14, /device:TPU:0, one launch (start us, length us, event | category | flops | bytes accessed | tf_op | source)
XLA Modules:
  0.0 30.5 jit_solution(7632084322596807046)
XLA Ops:
  0.0 4.1 %project.1 = (bf16[136,512]{1,0:T(8,128)(2,1)}, bf16[136,512]{1,0:T(8,128)(2,1)}, bf16[136,512]{1,0:T(8,128)(2,1)}, bf16[136,512]{1,0:T(8,128)(2,1)}, bf16[5,2560]{1,0:T(8,128)(2,1)}) custom-call(bf16[1280]{0:T(1024)(128)(2,1)} %gain_hbm.1, bf16[64,2,1280]{2,1,0:T(2,128)(2,1)} %bitcast.19, bf16[1280,2048]{1,0:T(8,128)(2,1)} %w_hbm.1, ...), custom_call_target="tpu_custom_call" | custom-call | flops 671088640 | bytes 5242880 | tf_op jit(solution)/shard_map/project/pallas_call | solution.py:131
  4.1 0.5 %collective-permute-start = (bf16[5,2560]{1,0:T(8,128)(2,1)}, bf16[5,2560]{1,0:T(8,128)(2,1)S(1)}, u32[]{:S(2)}, u32[]{:S(2)}) collective-permute-start(bf16[5,2560]{1,0:T(8,128)(2,1)} %get-tuple-element.19.ask_ref), channel_id=1, source_target_pairs={{0,4},{4,0},{8,12},{12,8},{1,5},{5,1},{9,13},{13,9},{2,6},{6,2},{1... | collective-permute-start | bytes 76808 | tf_op jit(solution)/shard_map/ppermute | solution.py:482
  4.7 4.7 %collective-permute-start.3 = (bf16[136,512]{1,0:T(8,128)(2,1)}, bf16[136,512]{1,0:T(8,128)(2,1)S(1)}, u32[]{:S(2)}, u32[]{:S(2)}) collective-permute-start(bf16[136,512]{1,0:T(8,128)(2,1)} %get-tuple-element.28), channel_id=1, source_target_pairs={{0,3},{1,2},{2,1},{3,0},{4,7},{5,6},{6,5},{7,4},{8,11},{9,10},{10,... | collective-permute-start | bytes 417800 | tf_op jit(solution)/shard_map/ppermute | solution.py:482
  9.3 0.0 collective-permute-done.rest_0_
  9.3 0.3 %collective-permute-start.4 = (bf16[136,512]{1,0:T(8,128)(2,1)}, bf16[136,512]{1,0:T(8,128)(2,1)S(1)}, u32[]{:S(2)}, u32[]{:S(2)}) collective-permute-start(bf16[136,512]{1,0:T(8,128)(2,1)} %get-tuple-element.29), channel_id=1, source_target_pairs={{0,2},{1,3},{2,0},{3,1},{4,6},{5,7},{6,4},{7,5},{8,10},{9,11},{10,... | collective-permute-start | bytes 417800 | tf_op jit(solution)/shard_map/ppermute | solution.py:482
  9.7 1.6 %collective-permute-start.5 = (bf16[136,512]{1,0:T(8,128)(2,1)}, bf16[136,512]{1,0:T(8,128)(2,1)S(1)}, u32[]{:S(2)}, u32[]{:S(2)}) collective-permute-start(bf16[136,512]{1,0:T(8,128)(2,1)} %get-tuple-element.30), channel_id=1, source_target_pairs={{0,1},{1,0},{2,3},{3,2},{4,5},{5,4},{6,7},{7,6},{8,9},{9,8},{10,11... | collective-permute-start | bytes 417800 | tf_op jit(solution)/shard_map/ppermute | solution.py:482
  11.2 0.7 %collective-permute-start.2 = (bf16[5,2560]{1,0:T(8,128)(2,1)}, bf16[5,2560]{1,0:T(8,128)(2,1)S(1)}, u32[]{:S(2)}, u32[]{:S(2)}) collective-permute-start(bf16[5,2560]{1,0:T(8,128)(2,1)} %get-tuple-element.19.ask_ref), channel_id=1, source_target_pairs={{0,12},{4,8},{8,4},{12,0},{1,13},{5,9},{9,5},{13,1},{2,14},{6,10},... | collective-permute-start | bytes 76808 | tf_op jit(solution)/shard_map/ppermute | solution.py:482
  11.9 0.8 %collective-permute-start.1 = (bf16[5,2560]{1,0:T(8,128)(2,1)}, bf16[5,2560]{1,0:T(8,128)(2,1)S(1)}, u32[]{:S(2)}, u32[]{:S(2)}) collective-permute-start(bf16[5,2560]{1,0:T(8,128)(2,1)} %get-tuple-element.19.ask_ref), channel_id=1, source_target_pairs={{0,8},{4,12},{8,0},{12,4},{1,9},{5,13},{9,1},{13,5},{2,10},{6,14},... | collective-permute-start | bytes 76808 | tf_op jit(solution)/shard_map/ppermute | solution.py:482
  12.8 0.0 copy-start
  12.8 0.0 copy-start.1
  12.8 0.0 copy-start.2
  12.8 0.0 copy-start.4
  12.8 0.0 copy-start.5
  12.8 0.0 copy-start.6
  12.8 0.0 copy-start.3
  12.8 7.0 %attend_resident.1 = bf16[4,64,128]{2,1,0:T(8,128)(2,1)} custom-call(s32[1,3]{1,0:T(1,128)} %len_ref.1, bf16[64,5,128]{2,1,0:T(8,128)(2,1)} %bitcast.18, bf16[3,1024,1024]{2,1,0:T(8,128)(2,1)} %bitcast.15, bf16[3,1024,1024]{2,1,0:T(8,128)(2,1)} %bitcast.16), custom_call_target="tpu_custom_call" | custom-call | flops 100663296 | bytes 12582912 | tf_op jit(solution)/shard_map/attend_resident/pallas_call | solution.py:238
  19.8 0.0 collective-permute-done.2.rest_2_
  19.8 0.0 collective-permute-done.1.rest_1_
  19.8 3.8 %all-to-all-start = ((bf16[4,64,128]{2,1,0:T(8,128)(2,1)}), bf16[4,64,128]{2,1,0:T(8,128)(2,1)S(1)}, u32[]{:S(2)}, u32[]{:S(2)}) async-start(bf16[4,64,128]{2,1,0:T(8,128)(2,1)} %attend_resident.1), calls=%async_computation | async-start | bytes 131072 | tf_op jit(solution)/shard_map/all_to_all | solution.py:532
  23.6 0.0 collective-permute-done.3.rest_4_
  23.6 0.0 collective-permute-done.4.rest_5_
  23.6 0.0 collective-permute-done.5.rest_6_
  23.6 0.0 copy-done
  23.6 0.0 copy-done.1
  23.6 0.0 copy-done.2
  23.6 0.0 copy-done.4
  23.6 0.0 copy-done.5
  23.7 0.0 copy-done.6
  23.7 1.3 %attend_moved.1 = (bf16[2,2048]{1,0:T(2,128)(2,1)S(1)}, s32[8,128]{1,0:T(8,128)S(1)}) custom-call(s32[2,4]{1,0:T(2,128)S(1)} %bitcast.12, s32[2,4]{1,0:T(2,128)S(1)} %bitcast.13, bf16[1,128]{1,0:T(2,128)(2,1)S(1)} %bitcast.14, f32[128,128]{1,0:T(8,128)S(1)} %copy-done.2, f32[128,128]{1,0:T(8,128)S(1)} %copy-done.1, ...), custom_call_target="tpu_custom_call" | custom-call | tf_op jit(solution)/shard_map/attend_moved/pallas_call | solution.py:389
  25.0 1.2 %collective-permute-start.8 = (bf16[2,2048]{1,0:T(2,128)(2,1)S(1)}, bf16[2,2048]{1,0:T(2,128)(2,1)S(1)}, u32[]{:S(2)}, u32[]{:S(2)}) collective-permute-start(bf16[2,2048]{1,0:T(2,128)(2,1)S(1)} %get-tuple-element.32), channel_id=1, source_target_pairs={{0,12},{4,8},{8,4},{12,0},{1,13},{5,9},{9,5},{13,1},{2,14},{6,10},... | collective-permute-start | bytes 24584 | tf_op jit(solution)/shard_map/ppermute | solution.py:482
  26.2 0.5 %collective-permute-start.7 = (bf16[2,2048]{1,0:T(2,128)(2,1)S(1)}, bf16[2,2048]{1,0:T(2,128)(2,1)S(1)}, u32[]{:S(2)}, u32[]{:S(2)}) collective-permute-start(bf16[2,2048]{1,0:T(2,128)(2,1)S(1)} %get-tuple-element.32), channel_id=1, source_target_pairs={{0,8},{4,12},{8,0},{12,4},{1,9},{5,13},{9,1},{13,5},{2,10},{6,14},... | collective-permute-start | bytes 24584 | tf_op jit(solution)/shard_map/ppermute | solution.py:482
  26.7 0.2 collective-permute-start.6
  26.9 2.4 %all-to-all-done.payload_ref = bf16[4,64,128]{2,1,0:T(8,128)(2,1)S(1)} async-done(((bf16[4,64,128]{2,1,0:T(8,128)(2,1)}), bf16[4,64,128]{2,1,0:T(8,128)(2,1)S(1)}, u32[]{:S(2)}, u32[]{:S(2)}) %all-to-all-start) | async-done | bytes 65568 | tf_op jit(solution)/shard_map/all_to_all | solution.py:532
  29.3 0.0 copy-done.3
  29.3 0.2 combine_resident.1.kept_ref
  29.5 0.0 collective-permute-done.8.rest_2_
  29.5 0.3 %collective-permute-done.7.rest_1_ = bf16[2,2048]{1,0:T(2,128)(2,1)S(1)} collective-permute-done((bf16[2,2048]{1,0:T(2,128)(2,1)S(1)}, bf16[2,2048]{1,0:T(2,128)(2,1)S(1)}, u32[]{:S(2)}, u32[]{:S(2)}) %collective-permute-start.7) | collective-permute-done | bytes 8224 | tf_op jit(solution)/shard_map/ppermute | solution.py:482
  29.9 0.0 collective-permute-done.6.rest_0_
  29.9 0.7 %finish.1 = bf16[5,2048]{1,0:T(8,128)(2,1)} custom-call(f32[3,2048]{1,0:T(4,128)S(1)} %combine_resident.1.kept_ref, s32[8,128]{1,0:T(8,128)S(1)} %get-tuple-element.31.place_ref, bf16[2,2048]{1,0:T(2,128)(2,1)S(1)} %collective-permute-done.6.rest_0_, bf16[2,2048]{1,0:T(2,128)(2,1)S(1)} %collective-permute-done.7.rest_1_, ...), custom_call_target="tpu_custom_call" | custom-call | tf_op jit(solution)/shard_map/finish/pallas_call | solution.py:471
Async XLA Ops:
  4.1 5.2 %collective-permute-start = (bf16[5,2560]{1,0:T(8,128)(2,1)}, bf16[5,2560]{1,0:T(8,128)(2,1)S(1)}, u32[]{:S(2)}, u32[]{:S(2)}) collective-permute-start(bf16[5,2560]{1,0:T(8,128)(2,1)} %get-tuple-element.19.ask_ref), channel_id=1, source_target_pairs={{0,4},{4,0},{8,12},{12,8},{1,5},{5,1},{9,13},{13,9},{2,6},{6,2},{1... | collective-permute-start | bytes 76808 | tf_op jit(solution)/shard_map/ppermute | solution.py:482
  4.7 18.9 %collective-permute-start.3 = (bf16[136,512]{1,0:T(8,128)(2,1)}, bf16[136,512]{1,0:T(8,128)(2,1)S(1)}, u32[]{:S(2)}, u32[]{:S(2)}) collective-permute-start(bf16[136,512]{1,0:T(8,128)(2,1)} %get-tuple-element.28), channel_id=1, source_target_pairs={{0,3},{1,2},{2,1},{3,0},{4,7},{5,6},{6,5},{7,4},{8,11},{9,10},{10,... | collective-permute-start | bytes 417800 | tf_op jit(solution)/shard_map/ppermute | solution.py:482
  9.3 14.3 %collective-permute-start.4 = (bf16[136,512]{1,0:T(8,128)(2,1)}, bf16[136,512]{1,0:T(8,128)(2,1)S(1)}, u32[]{:S(2)}, u32[]{:S(2)}) collective-permute-start(bf16[136,512]{1,0:T(8,128)(2,1)} %get-tuple-element.29), channel_id=1, source_target_pairs={{0,2},{1,3},{2,0},{3,1},{4,6},{5,7},{6,4},{7,5},{8,10},{9,11},{10,... | collective-permute-start | bytes 417800 | tf_op jit(solution)/shard_map/ppermute | solution.py:482
  9.7 13.9 %collective-permute-start.5 = (bf16[136,512]{1,0:T(8,128)(2,1)}, bf16[136,512]{1,0:T(8,128)(2,1)S(1)}, u32[]{:S(2)}, u32[]{:S(2)}) collective-permute-start(bf16[136,512]{1,0:T(8,128)(2,1)} %get-tuple-element.30), channel_id=1, source_target_pairs={{0,1},{1,0},{2,3},{3,2},{4,5},{5,4},{6,7},{7,6},{8,9},{9,8},{10,11... | collective-permute-start | bytes 417800 | tf_op jit(solution)/shard_map/ppermute | solution.py:482
  11.2 8.6 %collective-permute-start.2 = (bf16[5,2560]{1,0:T(8,128)(2,1)}, bf16[5,2560]{1,0:T(8,128)(2,1)S(1)}, u32[]{:S(2)}, u32[]{:S(2)}) collective-permute-start(bf16[5,2560]{1,0:T(8,128)(2,1)} %get-tuple-element.19.ask_ref), channel_id=1, source_target_pairs={{0,12},{4,8},{8,4},{12,0},{1,13},{5,9},{9,5},{13,1},{2,14},{6,10},... | collective-permute-start | bytes 76808 | tf_op jit(solution)/shard_map/ppermute | solution.py:482
  11.9 7.9 %collective-permute-start.1 = (bf16[5,2560]{1,0:T(8,128)(2,1)}, bf16[5,2560]{1,0:T(8,128)(2,1)S(1)}, u32[]{:S(2)}, u32[]{:S(2)}) collective-permute-start(bf16[5,2560]{1,0:T(8,128)(2,1)} %get-tuple-element.19.ask_ref), channel_id=1, source_target_pairs={{0,8},{4,12},{8,0},{12,4},{1,9},{5,13},{9,1},{13,5},{2,10},{6,14},... | collective-permute-start | bytes 76808 | tf_op jit(solution)/shard_map/ppermute | solution.py:482
  12.8 10.8 %copy-start = (bf16[136,512]{1,0:T(8,128)(2,1)S(1)}, bf16[136,512]{1,0:T(8,128)(2,1)}, u32[]{:S(2)}) copy-start(bf16[136,512]{1,0:T(8,128)(2,1)} %get-tuple-element.27.rest_3_) | copy-start | bytes 417796
  12.8 10.8 %copy-start.1 = (f32[128,128]{1,0:T(8,128)S(1)}, f32[128,128]{1,0:T(8,128)}, u32[]{:S(2)}) copy-start(f32[128,128]{1,0:T(8,128)} %constant.5.clone.sin_ref) | copy-start | bytes 196612
  12.8 10.9 %copy-start.2 = (f32[128,128]{1,0:T(8,128)S(1)}, f32[128,128]{1,0:T(8,128)}, u32[]{:S(2)}) copy-start(f32[128,128]{1,0:T(8,128)} %constant.4.clone.cos_ref) | copy-start | bytes 196612
  12.8 10.9 %copy-start.4 = (s32[4,2]{0,1:T(2,128)S(1)}, s32[4,2]{0,1:T(2,128)}, u32[]{:S(2)}) copy-start(s32[4,2]{0,1:T(2,128)} %param.14) | copy-start | bytes 100
  12.8 10.9 %copy-start.5 = (s32[4,2]{0,1:T(2,128)S(1)}, s32[4,2]{0,1:T(2,128)}, u32[]{:S(2)}) copy-start(s32[4,2]{0,1:T(2,128)} %param.15) | copy-start | bytes 100
  12.8 10.9 %copy-start.6 = (bf16[128]{0:T(256)(128)(2,1)S(1)}, bf16[128]{0:T(256)(128)(2,1)}, u32[]{:S(2)}) copy-start(bf16[128]{0:T(256)(128)(2,1)} %param.18) | copy-start | bytes 772
  12.8 16.5 %copy-start.3 = (bf16[5,2560]{1,0:T(8,128)(2,1)S(1)}, bf16[5,2560]{1,0:T(8,128)(2,1)}, u32[]{:S(2)}) copy-start(bf16[5,2560]{1,0:T(8,128)(2,1)} %get-tuple-element.19.ask_ref) | copy-start | bytes 76804
  19.8 9.5 %all-to-all-start = ((bf16[4,64,128]{2,1,0:T(8,128)(2,1)}), bf16[4,64,128]{2,1,0:T(8,128)(2,1)S(1)}, u32[]{:S(2)}, u32[]{:S(2)}) async-start(bf16[4,64,128]{2,1,0:T(8,128)(2,1)} %attend_resident.1), calls=%async_computation | async-start | bytes 131072 | tf_op jit(solution)/shard_map/all_to_all | solution.py:532
  25.0 4.5 %collective-permute-start.8 = (bf16[2,2048]{1,0:T(2,128)(2,1)S(1)}, bf16[2,2048]{1,0:T(2,128)(2,1)S(1)}, u32[]{:S(2)}, u32[]{:S(2)}) collective-permute-start(bf16[2,2048]{1,0:T(2,128)(2,1)S(1)} %get-tuple-element.32), channel_id=1, source_target_pairs={{0,12},{4,8},{8,4},{12,0},{1,13},{5,9},{9,5},{13,1},{2,14},{6,10},... | collective-permute-start | bytes 24584 | tf_op jit(solution)/shard_map/ppermute | solution.py:482
  26.2 3.7 %collective-permute-start.7 = (bf16[2,2048]{1,0:T(2,128)(2,1)S(1)}, bf16[2,2048]{1,0:T(2,128)(2,1)S(1)}, u32[]{:S(2)}, u32[]{:S(2)}) collective-permute-start(bf16[2,2048]{1,0:T(2,128)(2,1)S(1)} %get-tuple-element.32), channel_id=1, source_target_pairs={{0,8},{4,12},{8,0},{12,4},{1,9},{5,13},{9,1},{13,5},{2,10},{6,14},... | collective-permute-start | bytes 24584 | tf_op jit(solution)/shard_map/ppermute | solution.py:482
  26.7 3.1 %collective-permute-start.6 = (bf16[2,2048]{1,0:T(2,128)(2,1)S(1)}, bf16[2,2048]{1,0:T(2,128)(2,1)S(1)}, u32[]{:S(2)}, u32[]{:S(2)}) collective-permute-start(bf16[2,2048]{1,0:T(2,128)(2,1)S(1)} %get-tuple-element.32), channel_id=1, source_target_pairs={{0,4},{4,0},{8,12},{12,8},{1,5},{5,1},{9,13},{13,9},{2,6},{6,2},{1... | collective-permute-start | bytes 24584 | tf_op jit(solution)/shard_map/ppermute | solution.py:482

commit v15 on v14

--- a/solution.py
+++ b/solution.py
@@ -520,12 +520,10 @@
     pieces, ask = project(
         mig_hidden[0], attn_gain, kv_weight, query[0], new_kv[0], ranks, group, kv_mine
     )
-    last = ranks - 1
-    far = swapped(pieces[last], "tp", last, ranks)
+    order = sorted(range(1, ranks), key=lambda j: (j == 1, abs(j - ranks // 2), j))
+    sent = {j: swapped(pieces[j], "tp", j, ranks) for j in order}
+    pieces = [pieces[0]] + [sent[j] for j in order]
     asks = [swapped(ask, "inst", b, insts) for b in range(1, insts)]
-    asks[0], *others = lax.optimization_barrier((asks[0], *pieces[1:last]))
-    others = [swapped(others[j - 1], "tp", j, ranks) for j in reversed(range(1, last))]
-    pieces = [pieces[0], far] + others
     queries = jnp.transpose(query[0].reshape(query.shape[1], heads, head_size), (1, 0, 2))
     payloads = attend_resident(lengths, queries, k_cache[0], v_cache[0], ranks)
     asks, payloads = lax.optimization_barrier((asks, payloads))

time: 30.8 us -> 30 us (0.974)
  starting transfers between devices: 14.3 us -> 13.4 us
    ppermute x9, starting transfers between devices: 10.5 us -> 9.17 us  [swapped(): return lax.ppermute(x, axis, [(i, i ^ j) for i in range(n)])]
    all_to_all x1, starting transfers between devices: 3.76 us -> 4.2 us  [per_device(): received = lax.all_to_all(payloads, 'tp', 0, 0, tiled=True)]
  transfers between devices with their start and end apart: 10 -> 10, of which waited for: 2 -> 2; matrix products, arithmetic and copies ran while one was open for 0% -> 0% of each run, Pallas kernels for 28% -> 29%
where the time goes in v15:
time: 30 us; the launch traced here: 29.7 us
  starting transfers between devices  13.4 us (45%)
  Pallas kernels  13.3 us (44%)
  waiting for transfers between devices  2.82 us (9%)
    ppermute x9, starting transfers between devices, swapped(): return lax.ppermute(x, axis, [(i, i ^ j) for i in range(n)])  9.17 us
    pallas_call x1, Pallas kernels, attend_resident(): pl.pallas_call(functools.partial(resident_kernel, ranks), in_specs=[SMEM,...  7.03 us
    all_to_all x1, starting transfers between devices, per_device(): received = lax.all_to_all(payloads, 'tp', 0, 0, tiled=True)  4.2 us
    pallas_call x1, Pallas kernels, project(): pl.pallas_call(functools.partial(project_kernel, ranks, group), in_specs=...  4.13 us
    all_to_all x1, waiting for transfers between devices, per_device(): received = lax.all_to_all(payloads, 'tp', 0, 0, tiled=True)  2.41 us
    pallas_call x1, Pallas kernels, attend_moved(): pl.pallas_call(functools.partial(moved_kernel, insts, len(pieces), reside...  1.32 us
    pallas_call x1, Pallas kernels, finish(): pl.pallas_call(finish_kernel, in_specs=[VMEM] * (2 + len(moved)), out_spe...  0.67 us
  transfers between devices with their start and end apart: 10, of which 2 were waited for; matrix products, arithmetic and copies ran while one was open for 0% of the time, Pallas kernels for 29%

profile of v15, /device:TPU:0, one launch (start us, length us, event | category | flops | bytes accessed | tf_op | source)
XLA Modules:
  0.0 29.7 jit_solution(5731600781869540648)
XLA Ops:
  0.0 4.1 %project.1 = (bf16[136,512]{1,0:T(8,128)(2,1)}, bf16[136,512]{1,0:T(8,128)(2,1)}, bf16[136,512]{1,0:T(8,128)(2,1)}, bf16[136,512]{1,0:T(8,128)(2,1)}, bf16[5,2560]{1,0:T(8,128)(2,1)}) custom-call(bf16[1280]{0:T(1024)(128)(2,1)} %gain_hbm.1, bf16[64,2,1280]{2,1,0:T(2,128)(2,1)} %bitcast.19, bf16[1280,2048]{1,0:T(8,128)(2,1)} %w_hbm.1, ...), custom_call_target="tpu_custom_call" | custom-call | flops 671088640 | bytes 5242880 | tf_op jit(solution)/shard_map/project/pallas_call | solution.py:131
  4.1 2.4 %collective-permute-start.2 = (bf16[5,2560]{1,0:T(8,128)(2,1)}, bf16[5,2560]{1,0:T(8,128)(2,1)S(1)}, u32[]{:S(2)}, u32[]{:S(2)}) collective-permute-start(bf16[5,2560]{1,0:T(8,128)(2,1)} %get-tuple-element.16.ask_ref), channel_id=1, source_target_pairs={{0,12},{4,8},{8,4},{12,0},{1,13},{5,9},{9,5},{13,1},{2,14},{6,10},... | collective-permute-start | bytes 76808 | tf_op jit(solution)/shard_map/ppermute | solution.py:482
  6.6 2.6 %collective-permute-start.3 = (bf16[136,512]{1,0:T(8,128)(2,1)}, bf16[136,512]{1,0:T(8,128)(2,1)S(1)}, u32[]{:S(2)}, u32[]{:S(2)}) collective-permute-start(bf16[136,512]{1,0:T(8,128)(2,1)} %get-tuple-element.22), channel_id=1, source_target_pairs={{0,2},{1,3},{2,0},{3,1},{4,6},{5,7},{6,4},{7,5},{8,10},{9,11},{10,... | collective-permute-start | bytes 417800 | tf_op jit(solution)/shard_map/ppermute | solution.py:482
  9.2 1.4 %collective-permute-start.4 = (bf16[136,512]{1,0:T(8,128)(2,1)}, bf16[136,512]{1,0:T(8,128)(2,1)S(1)}, u32[]{:S(2)}, u32[]{:S(2)}) collective-permute-start(bf16[136,512]{1,0:T(8,128)(2,1)} %get-tuple-element.23), channel_id=1, source_target_pairs={{0,3},{1,2},{2,1},{3,0},{4,7},{5,6},{6,5},{7,4},{8,11},{9,10},{10,... | collective-permute-start | bytes 417800 | tf_op jit(solution)/shard_map/ppermute | solution.py:482
  10.5 0.3 collective-permute-start.5
  10.8 0.6 %collective-permute-start.1 = (bf16[5,2560]{1,0:T(8,128)(2,1)}, bf16[5,2560]{1,0:T(8,128)(2,1)S(1)}, u32[]{:S(2)}, u32[]{:S(2)}) collective-permute-start(bf16[5,2560]{1,0:T(8,128)(2,1)} %get-tuple-element.16.ask_ref), channel_id=1, source_target_pairs={{0,8},{4,12},{8,0},{12,4},{1,9},{5,13},{9,1},{13,5},{2,10},{6,14},... | collective-permute-start | bytes 76808 | tf_op jit(solution)/shard_map/ppermute | solution.py:482
  11.4 0.0 collective-permute-done.2.rest_2_
  11.4 0.0 collective-permute-start
  11.4 0.0 copy-start
  11.4 0.0 copy-start.1
  11.4 0.0 copy-start.2
  11.4 0.0 copy-start.4
  11.4 0.0 copy-start.5
  11.4 0.0 copy-start.6
  11.5 0.0 copy-start.3
  11.5 7.0 %attend_resident.1 = bf16[4,64,128]{2,1,0:T(8,128)(2,1)} custom-call(s32[1,3]{1,0:T(1,128)} %len_ref.1, bf16[64,5,128]{2,1,0:T(8,128)(2,1)} %bitcast.18, bf16[3,1024,1024]{2,1,0:T(8,128)(2,1)} %bitcast.15, bf16[3,1024,1024]{2,1,0:T(8,128)(2,1)} %bitcast.16), custom_call_target="tpu_custom_call" | custom-call | flops 100663296 | bytes 12582912 | tf_op jit(solution)/shard_map/attend_resident/pallas_call | solution.py:238
  18.5 0.0 collective-permute-done.1.rest_1_
  18.5 0.0 collective-permute-done.rest_0_
  18.5 4.2 %all-to-all-start = ((bf16[4,64,128]{2,1,0:T(8,128)(2,1)}), bf16[4,64,128]{2,1,0:T(8,128)(2,1)S(1)}, u32[]{:S(2)}, u32[]{:S(2)}) async-start(bf16[4,64,128]{2,1,0:T(8,128)(2,1)} %attend_resident.1), calls=%async_computation | async-start | bytes 131072 | tf_op jit(solution)/shard_map/all_to_all | solution.py:530
  22.7 0.0 collective-permute-done.3.rest_4_
  22.7 0.0 collective-permute-done.4.rest_5_
  22.7 0.0 collective-permute-done.5.rest_6_
  22.8 0.0 copy-done
  22.8 0.0 copy-done.1
  22.8 0.0 copy-done.2
  22.8 0.0 copy-done.4
  22.8 0.0 copy-done.5
  22.8 0.0 copy-done.6
  22.8 1.3 %attend_moved.1 = (bf16[2,2048]{1,0:T(2,128)(2,1)S(1)}, s32[8,128]{1,0:T(8,128)S(1)}) custom-call(s32[2,4]{1,0:T(2,128)S(1)} %bitcast.12, s32[2,4]{1,0:T(2,128)S(1)} %bitcast.13, bf16[1,128]{1,0:T(2,128)(2,1)S(1)} %bitcast.14, f32[128,128]{1,0:T(8,128)S(1)} %copy-done.2, f32[128,128]{1,0:T(8,128)S(1)} %copy-done.1, ...), custom_call_target="tpu_custom_call" | custom-call | tf_op jit(solution)/shard_map/attend_moved/pallas_call | solution.py:389
  24.1 1.3 %collective-permute-start.8 = (bf16[2,2048]{1,0:T(2,128)(2,1)S(1)}, bf16[2,2048]{1,0:T(2,128)(2,1)S(1)}, u32[]{:S(2)}, u32[]{:S(2)}) collective-permute-start(bf16[2,2048]{1,0:T(2,128)(2,1)S(1)} %get-tuple-element.26), channel_id=1, source_target_pairs={{0,12},{4,8},{8,4},{12,0},{1,13},{5,9},{9,5},{13,1},{2,14},{6,10},... | collective-permute-start | bytes 24584 | tf_op jit(solution)/shard_map/ppermute | solution.py:482
  25.4 0.6 %collective-permute-start.7 = (bf16[2,2048]{1,0:T(2,128)(2,1)S(1)}, bf16[2,2048]{1,0:T(2,128)(2,1)S(1)}, u32[]{:S(2)}, u32[]{:S(2)}) collective-permute-start(bf16[2,2048]{1,0:T(2,128)(2,1)S(1)} %get-tuple-element.26), channel_id=1, source_target_pairs={{0,8},{4,12},{8,0},{12,4},{1,9},{5,13},{9,1},{13,5},{2,10},{6,14},... | collective-permute-start | bytes 24584 | tf_op jit(solution)/shard_map/ppermute | solution.py:482
  26.0 0.1 collective-permute-start.6
  26.1 2.4 %all-to-all-done.payload_ref = bf16[4,64,128]{2,1,0:T(8,128)(2,1)S(1)} async-done(((bf16[4,64,128]{2,1,0:T(8,128)(2,1)}), bf16[4,64,128]{2,1,0:T(8,128)(2,1)S(1)}, u32[]{:S(2)}, u32[]{:S(2)}) %all-to-all-start) | async-done | bytes 65568 | tf_op jit(solution)/shard_map/all_to_all | solution.py:530
  28.5 0.0 copy-done.3
  28.5 0.2 combine_resident.1.kept_ref
  28.6 0.0 collective-permute-done.8.rest_2_
  28.7 0.4 %collective-permute-done.7.rest_1_ = bf16[2,2048]{1,0:T(2,128)(2,1)S(1)} collective-permute-done((bf16[2,2048]{1,0:T(2,128)(2,1)S(1)}, bf16[2,2048]{1,0:T(2,128)(2,1)S(1)}, u32[]{:S(2)}, u32[]{:S(2)}) %collective-permute-start.7) | collective-permute-done | bytes 8224 | tf_op jit(solution)/shard_map/ppermute | solution.py:482
  29.0 0.0 collective-permute-done.6.rest_0_
  29.1 0.7 %finish.1 = bf16[5,2048]{1,0:T(8,128)(2,1)} custom-call(f32[3,2048]{1,0:T(4,128)S(1)} %combine_resident.1.kept_ref, s32[8,128]{1,0:T(8,128)S(1)} %get-tuple-element.25.place_ref, bf16[2,2048]{1,0:T(2,128)(2,1)S(1)} %collective-permute-done.6.rest_0_, bf16[2,2048]{1,0:T(2,128)(2,1)S(1)} %collective-permute-done.7.rest_1_, ...), custom_call_target="tpu_custom_call" | custom-call | tf_op jit(solution)/shard_map/finish/pallas_call | solution.py:471
Async XLA Ops:
  4.1 7.2 %collective-permute-start.2 = (bf16[5,2560]{1,0:T(8,128)(2,1)}, bf16[5,2560]{1,0:T(8,128)(2,1)S(1)}, u32[]{:S(2)}, u32[]{:S(2)}) collective-permute-start(bf16[5,2560]{1,0:T(8,128)(2,1)} %get-tuple-element.16.ask_ref), channel_id=1, source_target_pairs={{0,12},{4,8},{8,4},{12,0},{1,13},{5,9},{9,5},{13,1},{2,14},{6,10},... | collective-permute-start | bytes 76808 | tf_op jit(solution)/shard_map/ppermute | solution.py:482
  6.6 16.1 %collective-permute-start.3 = (bf16[136,512]{1,0:T(8,128)(2,1)}, bf16[136,512]{1,0:T(8,128)(2,1)S(1)}, u32[]{:S(2)}, u32[]{:S(2)}) collective-permute-start(bf16[136,512]{1,0:T(8,128)(2,1)} %get-tuple-element.22), channel_id=1, source_target_pairs={{0,2},{1,3},{2,0},{3,1},{4,6},{5,7},{6,4},{7,5},{8,10},{9,11},{10,... | collective-permute-start | bytes 417800 | tf_op jit(solution)/shard_map/ppermute | solution.py:482
  9.2 13.6 %collective-permute-start.4 = (bf16[136,512]{1,0:T(8,128)(2,1)}, bf16[136,512]{1,0:T(8,128)(2,1)S(1)}, u32[]{:S(2)}, u32[]{:S(2)}) collective-permute-start(bf16[136,512]{1,0:T(8,128)(2,1)} %get-tuple-element.23), channel_id=1, source_target_pairs={{0,3},{1,2},{2,1},{3,0},{4,7},{5,6},{6,5},{7,4},{8,11},{9,10},{10,... | collective-permute-start | bytes 417800 | tf_op jit(solution)/shard_map/ppermute | solution.py:482
  10.5 12.2 %collective-permute-start.5 = (bf16[136,512]{1,0:T(8,128)(2,1)}, bf16[136,512]{1,0:T(8,128)(2,1)S(1)}, u32[]{:S(2)}, u32[]{:S(2)}) collective-permute-start(bf16[136,512]{1,0:T(8,128)(2,1)} %get-tuple-element.24), channel_id=1, source_target_pairs={{0,1},{1,0},{2,3},{3,2},{4,5},{5,4},{6,7},{7,6},{8,9},{9,8},{10,11... | collective-permute-start | bytes 417800 | tf_op jit(solution)/shard_map/ppermute | solution.py:482
  10.8 7.7 %collective-permute-start.1 = (bf16[5,2560]{1,0:T(8,128)(2,1)}, bf16[5,2560]{1,0:T(8,128)(2,1)S(1)}, u32[]{:S(2)}, u32[]{:S(2)}) collective-permute-start(bf16[5,2560]{1,0:T(8,128)(2,1)} %get-tuple-element.16.ask_ref), channel_id=1, source_target_pairs={{0,8},{4,12},{8,0},{12,4},{1,9},{5,13},{9,1},{13,5},{2,10},{6,14},... | collective-permute-start | bytes 76808 | tf_op jit(solution)/shard_map/ppermute | solution.py:482
  11.4 7.1 %collective-permute-start = (bf16[5,2560]{1,0:T(8,128)(2,1)}, bf16[5,2560]{1,0:T(8,128)(2,1)S(1)}, u32[]{:S(2)}, u32[]{:S(2)}) collective-permute-start(bf16[5,2560]{1,0:T(8,128)(2,1)} %get-tuple-element.16.ask_ref), channel_id=1, source_target_pairs={{0,4},{4,0},{8,12},{12,8},{1,5},{5,1},{9,13},{13,9},{2,6},{6,2},{1... | collective-permute-start | bytes 76808 | tf_op jit(solution)/shard_map/ppermute | solution.py:482
  11.4 11.4 %copy-start = (bf16[136,512]{1,0:T(8,128)(2,1)S(1)}, bf16[136,512]{1,0:T(8,128)(2,1)}, u32[]{:S(2)}) copy-start(bf16[136,512]{1,0:T(8,128)(2,1)} %get-tuple-element.21.rest_3_) | copy-start | bytes 417796
  11.4 11.4 %copy-start.1 = (f32[128,128]{1,0:T(8,128)S(1)}, f32[128,128]{1,0:T(8,128)}, u32[]{:S(2)}) copy-start(f32[128,128]{1,0:T(8,128)} %constant.5.clone.sin_ref) | copy-start | bytes 196612
  11.4 11.4 %copy-start.2 = (f32[128,128]{1,0:T(8,128)S(1)}, f32[128,128]{1,0:T(8,128)}, u32[]{:S(2)}) copy-start(f32[128,128]{1,0:T(8,128)} %constant.4.clone.cos_ref) | copy-start | bytes 196612
  11.4 11.4 %copy-start.4 = (s32[4,2]{0,1:T(2,128)S(1)}, s32[4,2]{0,1:T(2,128)}, u32[]{:S(2)}) copy-start(s32[4,2]{0,1:T(2,128)} %param.14) | copy-start | bytes 100
  11.4 11.4 %copy-start.5 = (s32[4,2]{0,1:T(2,128)S(1)}, s32[4,2]{0,1:T(2,128)}, u32[]{:S(2)}) copy-start(s32[4,2]{0,1:T(2,128)} %param.15) | copy-start | bytes 100
  11.4 11.4 %copy-start.6 = (bf16[128]{0:T(256)(128)(2,1)S(1)}, bf16[128]{0:T(256)(128)(2,1)}, u32[]{:S(2)}) copy-start(bf16[128]{0:T(256)(128)(2,1)} %param.18) | copy-start | bytes 772
  11.5 17.0 %copy-start.3 = (bf16[5,2560]{1,0:T(8,128)(2,1)S(1)}, bf16[5,2560]{1,0:T(8,128)(2,1)}, u32[]{:S(2)}) copy-start(bf16[5,2560]{1,0:T(8,128)(2,1)} %get-tuple-element.16.ask_ref) | copy-start | bytes 76804
  18.5 9.9 %all-to-all-start = ((bf16[4,64,128]{2,1,0:T(8,128)(2,1)}), bf16[4,64,128]{2,1,0:T(8,128)(2,1)S(1)}, u32[]{:S(2)}, u32[]{:S(2)}) async-start(bf16[4,64,128]{2,1,0:T(8,128)(2,1)} %attend_resident.1), calls=%async_computation | async-start | bytes 131072 | tf_op jit(solution)/shard_map/all_to_all | solution.py:530
  24.1 4.5 %collective-permute-start.8 = (bf16[2,2048]{1,0:T(2,128)(2,1)S(1)}, bf16[2,2048]{1,0:T(2,128)(2,1)S(1)}, u32[]{:S(2)}, u32[]{:S(2)}) collective-permute-start(bf16[2,2048]{1,0:T(2,128)(2,1)S(1)} %get-tuple-element.26), channel_id=1, source_target_pairs={{0,12},{4,8},{8,4},{12,0},{1,13},{5,9},{9,5},{13,1},{2,14},{6,10},... | collective-permute-start | bytes 24584 | tf_op jit(solution)/shard_map/ppermute | solution.py:482
  25.4 3.7 %collective-permute-start.7 = (bf16[2,2048]{1,0:T(2,128)(2,1)S(1)}, bf16[2,2048]{1,0:T(2,128)(2,1)S(1)}, u32[]{:S(2)}, u32[]{:S(2)}) collective-permute-start(bf16[2,2048]{1,0:T(2,128)(2,1)S(1)} %get-tuple-element.26), channel_id=1, source_target_pairs={{0,8},{4,12},{8,0},{12,4},{1,9},{5,13},{9,1},{13,5},{2,10},{6,14},... | collective-permute-start | bytes 24584 | tf_op jit(solution)/shard_map/ppermute | solution.py:482
  26.0 3.0 %collective-permute-start.6 = (bf16[2,2048]{1,0:T(2,128)(2,1)S(1)}, bf16[2,2048]{1,0:T(2,128)(2,1)S(1)}, u32[]{:S(2)}, u32[]{:S(2)}) collective-permute-start(bf16[2,2048]{1,0:T(2,128)(2,1)S(1)} %get-tuple-element.26), channel_id=1, source_target_pairs={{0,4},{4,0},{8,12},{12,8},{1,5},{5,1},{9,13},{13,9},{2,6},{6,2},{1... | collective-permute-start | bytes 24584 | tf_op jit(solution)/shard_map/ppermute | solution.py:482

commit v16 on v15

--- a/solution.py
+++ b/solution.py
@@ -153,7 +153,8 @@
     return outs[:ranks], outs[ranks]
 
 
-def resident_kernel(ranks, len_ref, q_ref, k_hbm, v_hbm, out, *rest):
+def resident_kernel(ranks, len_ref, q_ref, k_hbm, v_hbm, *rest):
+    outs, rest = rest[:ranks], rest[ranks:]
     q_wide, q_all, k_buf, v_buf, o_all, m_all, l_all, s_all, sems = rest
     residents, positions, width = k_buf.shape
     copies = []
@@ -164,15 +165,20 @@
                 pltpu.make_async_copy(v_hbm.at[r], v_buf.at[r], sems.at[1, r]),
             )
         )
-    for pair in copies:
-        for copy in pair:
-            copy.start()
+    rank = lax.axis_index("tp")
+    held = [(rank == 0) | (len_ref[0, r] > rank * positions) for r in range(residents)]
+    for r in range(residents):
+
+        @pl.when(held[r])
+        def _():
+            for copy in copies[r]:
+                copy.start()
+
     heads = q_ref.shape[0]
     kv_heads = width // 128
     group = heads // kv_heads
     pair_rows = 2 * group
     heads_mine = heads // ranks
-    rank = lax.axis_index("tp")
     top_half = iota((pair_rows, 128), 0) < group
     position = rank * positions + iota((pair_rows, positions), 1)
     scale = F32(1.0) / jnp.sqrt(F32(128.0))
@@ -185,7 +191,7 @@
     q_wide[...] = q_ref[...].astype(F32)
     for r in range(residents):
         q_all[r] = q_wide[:, r, :].astype(BF16)
-    for r in range(residents):
+    def attend(r):
         valid = position < len_ref[0, r]
         copies[r][0].wait()
         weights = []
@@ -216,18 +222,30 @@
             o_all[r, p * pair_rows : (p + 1) * pair_rows, :] = jnp.where(
                 top_half, both[:, :128], both[:, 128:]
             )
+
+    for r in range(residents):
+        pl.when(held[r])(functools.partial(attend, r))
+
+        @pl.when(jnp.logical_not(held[r]))
+        def _():
+            o_all[r] = jnp.zeros((heads, 128), F32)
+            m_all[r] = jnp.full((heads, 1), ABSENT, F32)
+            l_all[r] = jnp.zeros((heads, 1), F32)
+
     for r in range(residents):
         s_all[r, 0] = to_rows(m_all[r])
         high, low = split_bf16(to_rows(l_all[r]))
         s_all[r, 1] = high.astype(F32)
         s_all[r, 2] = low.astype(F32)
     filled = residents * (heads_mine + 3)
-    for t in range(ranks):
-        parts = [o_all[r, t * heads_mine : (t + 1) * heads_mine, :] for r in range(residents)]
-        parts += [s_all[r, i, t : t + 1, :] for i in range(3) for r in range(residents)]
-        if out.shape[1] > filled:
-            parts.append(jnp.zeros((out.shape[1] - filled, 128), F32))
-        out[t] = jnp.concatenate(parts, axis=0).astype(BF16)
+    for j in range(ranks):
+        target = rank ^ j
+        first = pl.multiple_of(target * heads_mine, heads_mine)
+        parts = [o_all[r, pl.ds(first, heads_mine), :] for r in range(residents)]
+        parts += [s_all[r, i, pl.ds(target, 1), :] for i in range(3) for r in range(residents)]
+        if outs[j].shape[0] > filled:
+            parts.append(jnp.zeros((outs[j].shape[0] - filled, 128), F32))
+        outs[j][...] = jnp.concatenate(parts, axis=0).astype(BF16)
 
 
 def attend_resident(lengths, queries, k_cache, v_cache, ranks):
@@ -238,8 +256,8 @@
     return pl.pallas_call(
         functools.partial(resident_kernel, ranks),
         in_specs=[SMEM, VMEM, HBM, HBM],
-        out_specs=VMEM,
-        out_shape=jax.ShapeDtypeStruct((ranks, rows, 128), BF16),
+        out_specs=[VMEM] * ranks,
+        out_shape=[jax.ShapeDtypeStruct((rows, 128), BF16)] * ranks,
         scratch_shapes=[
             pltpu.VMEM(queries.shape, F32),
             pltpu.VMEM((residents, heads, 128), BF16),
@@ -405,10 +423,11 @@
     )(dest, count, k_gain, cos, sin, *asks, *pieces)
 
 
-def combine_kernel(residents, kv_mine, ask_ref, payload_ref, out_ref):
+def combine_kernel(residents, kv_mine, ask_ref, *rest):
+    refs, out_ref = rest[:-1], rest[-1]
     heads_mine = out_ref.shape[1] // 128
     scale = F32(1.0) / jnp.sqrt(F32(128.0))
-    payloads = [payload_ref[t].astype(F32) for t in range(payload_ref.shape[0])]
+    payloads = [ref[...].astype(F32) for ref in refs]
     at = residents * heads_mine
     ask = ask_ref[...].astype(F32)
     for r in range(residents):
@@ -439,12 +458,12 @@
 def combine_resident(ask, payloads, residents, heads_mine, kv_mine):
     return pl.pallas_call(
         functools.partial(combine_kernel, residents, kv_mine),
-        in_specs=[VMEM] * 2,
+        in_specs=[VMEM] * (1 + len(payloads)),
         out_specs=VMEM,
         out_shape=jax.ShapeDtypeStruct((residents, heads_mine * 128), F32),
         compiler_params=pltpu.CompilerParams(vmem_limit_bytes=8 * MIB),
         name="combine_resident",
-    )(ask, payloads)
+    )(ask, *payloads)
 
 
 def finish_kernel(kept_ref, place_ref, *rest):
@@ -527,7 +546,8 @@
     queries = jnp.transpose(query[0].reshape(query.shape[1], heads, head_size), (1, 0, 2))
     payloads = attend_resident(lengths, queries, k_cache[0], v_cache[0], ranks)
     asks, payloads = lax.optimization_barrier((asks, payloads))
-    received = lax.all_to_all(payloads, "tp", 0, 0, tiled=True)
+    order = sorted(range(1, ranks), key=lambda j: (j > 1, -j))
+    received = [payloads[0]] + [swapped(payloads[j], "tp", j, ranks) for j in order]
     cos, sin = rotation(slots, requests, head_size)
     moved, places = attend_moved(
         mig_dest.T,

time: 30 us -> 31.1 us (1.037)
  waiting for transfers between devices: 2.82 us -> 3.66 us
  local copies, waits for them, and re-layouts: 0.04 us -> 0.74 us
  starting transfers between devices: 13.4 us -> 12.8 us
    all_to_all x1 -> x0, starting transfers between devices: 4.2 us -> none  [per_device(): received = lax.all_to_all(payloads, 'tp', 0, 0, tiled=True)]
    ppermute x9 -> x12, starting transfers between devices: 9.17 us -> 12.8 us  [swapped(): return lax.ppermute(x, axis, [(i, i ^ j) for i in range(n)])]
    ppermute x9 -> x12, waiting for transfers between devices: 0.41 us -> 3.66 us  [swapped(): return lax.ppermute(x, axis, [(i, i ^ j) for i in range(n)])]
    all_to_all x1 -> x0, waiting for transfers between devices: 2.41 us -> none  [per_device(): received = lax.all_to_all(payloads, 'tp', 0, 0, tiled=True)]
    unnamed x14 -> x16, local copies, waits for them, and re-layouts: 0.04 us -> 0.74 us
  transfers between devices with their start and end apart: 10 -> 12, of which waited for: 2 -> 3; matrix products, arithmetic and copies ran while one was open for 0% -> 0% of each run, Pallas kernels for 29% -> 28%
where the time goes in v16:
time: 31.1 us; the launch traced here: 30.8 us
  Pallas kernels  13.4 us (43%)
  starting transfers between devices  12.8 us (41%)
  waiting for transfers between devices  3.66 us (12%)
  local copies, waits for them, and re-layouts  0.74 us (2%)
    ppermute x12, starting transfers between devices, swapped(): return lax.ppermute(x, axis, [(i, i ^ j) for i in range(n)])  12.8 us
    pallas_call x1, Pallas kernels, attend_resident(): pl.pallas_call(functools.partial(resident_kernel, ranks), in_specs=[SMEM,...  7.13 us
    pallas_call x1, Pallas kernels, project(): pl.pallas_call(functools.partial(project_kernel, ranks, group), in_specs=...  4.12 us
    ppermute x12, waiting for transfers between devices, swapped(): return lax.ppermute(x, axis, [(i, i ^ j) for i in range(n)])  3.66 us
    pallas_call x1, Pallas kernels, attend_moved(): pl.pallas_call(functools.partial(moved_kernel, insts, len(pieces), reside...  1.32 us
    unnamed x16, local copies, waits for them, and re-layouts  0.74 us
    pallas_call x1, Pallas kernels, finish(): pl.pallas_call(finish_kernel, in_specs=[VMEM] * (2 + len(moved)), out_spe...  0.67 us
  transfers between devices with their start and end apart: 12, of which 3 were waited for; matrix products, arithmetic and copies ran while one was open for 0% of the time, Pallas kernels for 28%

profile of v16, /device:TPU:0, one launch (start us, length us, event | category | flops | bytes accessed | tf_op | source)
XLA Modules:
  0.0 30.8 jit_solution(6687483538667234381)
XLA Ops:
  0.0 4.1 %project.1 = (bf16[136,512]{1,0:T(8,128)(2,1)}, bf16[136,512]{1,0:T(8,128)(2,1)}, bf16[136,512]{1,0:T(8,128)(2,1)}, bf16[136,512]{1,0:T(8,128)(2,1)}, bf16[5,2560]{1,0:T(8,128)(2,1)}) custom-call(bf16[1280]{0:T(1024)(128)(2,1)} %gain_hbm.1, bf16[64,2,1280]{2,1,0:T(2,128)(2,1)} %bitcast.19, bf16[1280,2048]{1,0:T(8,128)(2,1)} %w_hbm.1, ...), custom_call_target="tpu_custom_call" | custom-call | flops 671088640 | bytes 5242880 | tf_op jit(solution)/shard_map/project/pallas_call | solution.py:131
  4.1 4.1 %collective-permute-start.6 = (bf16[136,512]{1,0:T(8,128)(2,1)}, bf16[136,512]{1,0:T(8,128)(2,1)S(1)}, u32[]{:S(2)}, u32[]{:S(2)}) collective-permute-start(bf16[136,512]{1,0:T(8,128)(2,1)} %get-tuple-element.36), channel_id=1, source_target_pairs={{0,2},{1,3},{2,0},{3,1},{4,6},{5,7},{6,4},{7,5},{8,10},{9,11},{10,... | collective-permute-start | bytes 417800 | tf_op jit(solution)/shard_map/ppermute | solution.py:501
  8.2 1.3 %collective-permute-start.7 = (bf16[136,512]{1,0:T(8,128)(2,1)}, bf16[136,512]{1,0:T(8,128)(2,1)S(1)}, u32[]{:S(2)}, u32[]{:S(2)}) collective-permute-start(bf16[136,512]{1,0:T(8,128)(2,1)} %get-tuple-element.37), channel_id=1, source_target_pairs={{0,3},{1,2},{2,1},{3,0},{4,7},{5,6},{6,5},{7,4},{8,11},{9,10},{10,... | collective-permute-start | bytes 417800 | tf_op jit(solution)/shard_map/ppermute | solution.py:501
  9.6 0.2 collective-permute-start.8
  9.8 0.4 %collective-permute-start.2 = (bf16[5,2560]{1,0:T(8,128)(2,1)}, bf16[5,2560]{1,0:T(8,128)(2,1)S(1)}, u32[]{:S(2)}, u32[]{:S(2)}) collective-permute-start(bf16[5,2560]{1,0:T(8,128)(2,1)} %get-tuple-element.23.ask_ref), channel_id=1, source_target_pairs={{0,12},{4,8},{8,4},{12,0},{1,13},{5,9},{9,5},{13,1},{2,14},{6,10},... | collective-permute-start | bytes 76808 | tf_op jit(solution)/shard_map/ppermute | solution.py:501
  10.2 1.2 %collective-permute-start.1 = (bf16[5,2560]{1,0:T(8,128)(2,1)}, bf16[5,2560]{1,0:T(8,128)(2,1)S(1)}, u32[]{:S(2)}, u32[]{:S(2)}) collective-permute-start(bf16[5,2560]{1,0:T(8,128)(2,1)} %get-tuple-element.23.ask_ref), channel_id=1, source_target_pairs={{0,8},{4,12},{8,0},{12,4},{1,9},{5,13},{9,1},{13,5},{2,10},{6,14},... | collective-permute-start | bytes 76808 | tf_op jit(solution)/shard_map/ppermute | solution.py:501
  11.3 2.5 %collective-permute-done.2.rest_2_ = bf16[5,2560]{1,0:T(8,128)(2,1)S(1)} collective-permute-done((bf16[5,2560]{1,0:T(8,128)(2,1)}, bf16[5,2560]{1,0:T(8,128)(2,1)S(1)}, u32[]{:S(2)}, u32[]{:S(2)}) %collective-permute-start.2) | collective-permute-done | bytes 25632 | tf_op jit(solution)/shard_map/ppermute | solution.py:501
  13.8 0.2 collective-permute-start
  14.0 0.0 copy-start
  14.0 0.0 copy-start.1
  14.0 0.0 copy-start.2
  14.0 0.0 copy-start.5
  14.0 0.0 copy-start.6
  14.0 0.0 copy-start.7
  14.0 0.0 copy-start.3
  14.0 7.1 %attend_resident.1 = (bf16[64,128]{1,0:T(8,128)(2,1)}, bf16[64,128]{1,0:T(8,128)(2,1)}, bf16[64,128]{1,0:T(8,128)(2,1)}, bf16[64,128]{1,0:T(8,128)(2,1)}) custom-call(s32[1,3]{1,0:T(1,128)} %len_ref.1, bf16[64,5,128]{2,1,0:T(8,128)(2,1)} %bitcast.18, bf16[3,1024,1024]{2,1,0:T(8,128)(2,1)} %bitcast.15, bf16[3,1024,1024]{2,1,0:T(8,128)(2,1)} %bitcast.16), custom_call_target="tpu_custom_call" | custom-call | flops 100663296 | bytes 12582912 | tf_op jit(solution)/shard_map/attend_resident/pallas_call | solution.py:256
  21.2 0.0 collective-permute-done.1.rest_1_
  21.2 0.0 collective-permute-done.rest_0_
  21.2 0.1 collective-permute-start.3
  21.3 1.7 %collective-permute-start.4 = (bf16[64,128]{1,0:T(8,128)(2,1)}, bf16[64,128]{1,0:T(8,128)(2,1)S(1)}, u32[]{:S(2)}, u32[]{:S(2)}) collective-permute-start(bf16[64,128]{1,0:T(8,128)(2,1)} %get-tuple-element.30), channel_id=1, source_target_pairs={{0,3},{1,2},{2,1},{3,0},{4,7},{5,6},{6,5},{7,4},{8,11},{9,10},{10,... | collective-permute-start | bytes 49160 | tf_op jit(solution)/shard_map/ppermute | solution.py:501
  23.0 0.0 collective-permute-done.6.rest_4_
  23.0 1.7 %collective-permute-start.5 = (bf16[64,128]{1,0:T(8,128)(2,1)}, bf16[64,128]{1,0:T(8,128)(2,1)S(1)}, u32[]{:S(2)}, u32[]{:S(2)}) collective-permute-start(bf16[64,128]{1,0:T(8,128)(2,1)} %get-tuple-element.31), channel_id=1, source_target_pairs={{0,2},{1,3},{2,0},{3,1},{4,6},{5,7},{6,4},{7,5},{8,10},{9,11},{10,... | collective-permute-start | bytes 49160 | tf_op jit(solution)/shard_map/ppermute | solution.py:501
  24.8 0.0 collective-permute-done.7.rest_5_
  24.8 0.0 collective-permute-done.8.rest_6_
  24.8 0.0 copy-done
  24.8 0.0 copy-done.1
  24.8 0.0 copy-done.2
  24.8 0.0 copy-done.5
  24.8 0.0 copy-done.6
  24.8 0.0 copy-done.7
  24.8 1.3 %attend_moved.1 = (bf16[2,2048]{1,0:T(2,128)(2,1)S(1)}, s32[8,128]{1,0:T(8,128)S(1)}) custom-call(s32[2,4]{1,0:T(2,128)S(1)} %bitcast.12, s32[2,4]{1,0:T(2,128)S(1)} %bitcast.13, bf16[1,128]{1,0:T(2,128)(2,1)S(1)} %bitcast.14, f32[128,128]{1,0:T(8,128)S(1)} %copy-done.2, f32[128,128]{1,0:T(8,128)S(1)} %copy-done.1, ...), custom_call_target="tpu_custom_call" | custom-call | tf_op jit(solution)/shard_map/attend_moved/pallas_call | solution.py:407
  26.2 0.3 collective-permute-start.11
  26.4 0.9 %collective-permute-start.10 = (bf16[2,2048]{1,0:T(2,128)(2,1)S(1)}, bf16[2,2048]{1,0:T(2,128)(2,1)S(1)}, u32[]{:S(2)}, u32[]{:S(2)}) collective-permute-start(bf16[2,2048]{1,0:T(2,128)(2,1)S(1)} %get-tuple-element.40), channel_id=1, source_target_pairs={{0,8},{4,12},{8,0},{12,4},{1,9},{5,13},{9,1},{13,5},{2,10},{6,14},... | collective-permute-start | bytes 24584 | tf_op jit(solution)/shard_map/ppermute | solution.py:501
  27.4 0.0 collective-permute-done.3.rest_1_
  27.4 0.7 %collective-permute-start.9 = (bf16[2,2048]{1,0:T(2,128)(2,1)S(1)}, bf16[2,2048]{1,0:T(2,128)(2,1)S(1)}, u32[]{:S(2)}, u32[]{:S(2)}) collective-permute-start(bf16[2,2048]{1,0:T(2,128)(2,1)S(1)} %get-tuple-element.40), channel_id=1, source_target_pairs={{0,4},{4,0},{8,12},{12,8},{1,5},{5,1},{9,13},{13,9},{2,6},{6,2},{1... | collective-permute-start | bytes 24584 | tf_op jit(solution)/shard_map/ppermute | solution.py:501
  28.1 0.0 collective-permute-done.4.rest_2_
  28.1 0.0 collective-permute-done.5.rest_3_
  28.1 0.0 copy-done.3
  28.1 0.0 copy-start.4
  28.1 0.7 %copy-done.4 = bf16[64,128]{1,0:T(8,128)(2,1)S(1)} copy-done((bf16[64,128]{1,0:T(8,128)(2,1)S(1)}, bf16[64,128]{1,0:T(8,128)(2,1)}, u32[]{:S(2)}) %copy-start.4) | copy-done | bytes 16408
  28.8 0.2 combine_resident.1.kept_ref
  29.0 0.3 %collective-permute-done.11.rest_2_ = bf16[2,2048]{1,0:T(2,128)(2,1)S(1)} collective-permute-done((bf16[2,2048]{1,0:T(2,128)(2,1)S(1)}, bf16[2,2048]{1,0:T(2,128)(2,1)S(1)}, u32[]{:S(2)}, u32[]{:S(2)}) %collective-permute-start.11) | collective-permute-done | bytes 8224 | tf_op jit(solution)/shard_map/ppermute | solution.py:501
  29.3 0.8 %collective-permute-done.10.rest_1_ = bf16[2,2048]{1,0:T(2,128)(2,1)S(1)} collective-permute-done((bf16[2,2048]{1,0:T(2,128)(2,1)S(1)}, bf16[2,2048]{1,0:T(2,128)(2,1)S(1)}, u32[]{:S(2)}, u32[]{:S(2)}) %collective-permute-start.10) | collective-permute-done | bytes 8224 | tf_op jit(solution)/shard_map/ppermute | solution.py:501
  30.1 0.0 collective-permute-done.9.rest_0_
  30.1 0.7 %finish.1 = bf16[5,2048]{1,0:T(8,128)(2,1)} custom-call(f32[3,2048]{1,0:T(4,128)S(1)} %combine_resident.1.kept_ref, s32[8,128]{1,0:T(8,128)S(1)} %get-tuple-element.39.place_ref, bf16[2,2048]{1,0:T(2,128)(2,1)S(1)} %collective-permute-done.9.rest_0_, bf16[2,2048]{1,0:T(2,128)(2,1)S(1)} %collective-permute-done.10.rest_1_, ...), custom_call_target="tpu_custom_call" | custom-call | tf_op jit(solution)/shard_map/finish/pallas_call | solution.py:490
Async XLA Ops:
  4.1 18.9 %collective-permute-start.6 = (bf16[136,512]{1,0:T(8,128)(2,1)}, bf16[136,512]{1,0:T(8,128)(2,1)S(1)}, u32[]{:S(2)}, u32[]{:S(2)}) collective-permute-start(bf16[136,512]{1,0:T(8,128)(2,1)} %get-tuple-element.36), channel_id=1, source_target_pairs={{0,2},{1,3},{2,0},{3,1},{4,6},{5,7},{6,4},{7,5},{8,10},{9,11},{10,... | collective-permute-start | bytes 417800 | tf_op jit(solution)/shard_map/ppermute | solution.py:501
  8.2 16.5 %collective-permute-start.7 = (bf16[136,512]{1,0:T(8,128)(2,1)}, bf16[136,512]{1,0:T(8,128)(2,1)S(1)}, u32[]{:S(2)}, u32[]{:S(2)}) collective-permute-start(bf16[136,512]{1,0:T(8,128)(2,1)} %get-tuple-element.37), channel_id=1, source_target_pairs={{0,3},{1,2},{2,1},{3,0},{4,7},{5,6},{6,5},{7,4},{8,11},{9,10},{10,... | collective-permute-start | bytes 417800 | tf_op jit(solution)/shard_map/ppermute | solution.py:501
  9.6 15.2 %collective-permute-start.8 = (bf16[136,512]{1,0:T(8,128)(2,1)}, bf16[136,512]{1,0:T(8,128)(2,1)S(1)}, u32[]{:S(2)}, u32[]{:S(2)}) collective-permute-start(bf16[136,512]{1,0:T(8,128)(2,1)} %get-tuple-element.38), channel_id=1, source_target_pairs={{0,1},{1,0},{2,3},{3,2},{4,5},{5,4},{6,7},{7,6},{8,9},{9,8},{10,11... | collective-permute-start | bytes 417800 | tf_op jit(solution)/shard_map/ppermute | solution.py:501
  9.8 4.0 %collective-permute-start.2 = (bf16[5,2560]{1,0:T(8,128)(2,1)}, bf16[5,2560]{1,0:T(8,128)(2,1)S(1)}, u32[]{:S(2)}, u32[]{:S(2)}) collective-permute-start(bf16[5,2560]{1,0:T(8,128)(2,1)} %get-tuple-element.23.ask_ref), channel_id=1, source_target_pairs={{0,12},{4,8},{8,4},{12,0},{1,13},{5,9},{9,5},{13,1},{2,14},{6,10},... | collective-permute-start | bytes 76808 | tf_op jit(solution)/shard_map/ppermute | solution.py:501
  10.2 11.0 %collective-permute-start.1 = (bf16[5,2560]{1,0:T(8,128)(2,1)}, bf16[5,2560]{1,0:T(8,128)(2,1)S(1)}, u32[]{:S(2)}, u32[]{:S(2)}) collective-permute-start(bf16[5,2560]{1,0:T(8,128)(2,1)} %get-tuple-element.23.ask_ref), channel_id=1, source_target_pairs={{0,8},{4,12},{8,0},{12,4},{1,9},{5,13},{9,1},{13,5},{2,10},{6,14},... | collective-permute-start | bytes 76808 | tf_op jit(solution)/shard_map/ppermute | solution.py:501
  13.8 7.4 %collective-permute-start = (bf16[5,2560]{1,0:T(8,128)(2,1)}, bf16[5,2560]{1,0:T(8,128)(2,1)S(1)}, u32[]{:S(2)}, u32[]{:S(2)}) collective-permute-start(bf16[5,2560]{1,0:T(8,128)(2,1)} %get-tuple-element.23.ask_ref), channel_id=1, source_target_pairs={{0,4},{4,0},{8,12},{12,8},{1,5},{5,1},{9,13},{13,9},{2,6},{6,2},{1... | collective-permute-start | bytes 76808 | tf_op jit(solution)/shard_map/ppermute | solution.py:501
  14.0 10.8 %copy-start = (bf16[136,512]{1,0:T(8,128)(2,1)S(1)}, bf16[136,512]{1,0:T(8,128)(2,1)}, u32[]{:S(2)}) copy-start(bf16[136,512]{1,0:T(8,128)(2,1)} %get-tuple-element.35.rest_3_) | copy-start | bytes 417796
  14.0 10.8 %copy-start.1 = (f32[128,128]{1,0:T(8,128)S(1)}, f32[128,128]{1,0:T(8,128)}, u32[]{:S(2)}) copy-start(f32[128,128]{1,0:T(8,128)} %constant.5.clone.sin_ref) | copy-start | bytes 196612
  14.0 10.8 %copy-start.2 = (f32[128,128]{1,0:T(8,128)S(1)}, f32[128,128]{1,0:T(8,128)}, u32[]{:S(2)}) copy-start(f32[128,128]{1,0:T(8,128)} %constant.4.clone.cos_ref) | copy-start | bytes 196612
  14.0 10.8 %copy-start.5 = (s32[4,2]{0,1:T(2,128)S(1)}, s32[4,2]{0,1:T(2,128)}, u32[]{:S(2)}) copy-start(s32[4,2]{0,1:T(2,128)} %param.14) | copy-start | bytes 100
  14.0 10.8 %copy-start.6 = (s32[4,2]{0,1:T(2,128)S(1)}, s32[4,2]{0,1:T(2,128)}, u32[]{:S(2)}) copy-start(s32[4,2]{0,1:T(2,128)} %param.15) | copy-start | bytes 100
  14.0 10.8 %copy-start.7 = (bf16[128]{0:T(256)(128)(2,1)S(1)}, bf16[128]{0:T(256)(128)(2,1)}, u32[]{:S(2)}) copy-start(bf16[128]{0:T(256)(128)(2,1)} %param.18) | copy-start | bytes 772
  14.0 14.1 %copy-start.3 = (bf16[5,2560]{1,0:T(8,128)(2,1)S(1)}, bf16[5,2560]{1,0:T(8,128)(2,1)}, u32[]{:S(2)}) copy-start(bf16[5,2560]{1,0:T(8,128)(2,1)} %get-tuple-element.23.ask_ref) | copy-start | bytes 76804
  21.2 6.2 %collective-permute-start.3 = (bf16[64,128]{1,0:T(8,128)(2,1)}, bf16[64,128]{1,0:T(8,128)(2,1)S(1)}, u32[]{:S(2)}, u32[]{:S(2)}) collective-permute-start(bf16[64,128]{1,0:T(8,128)(2,1)} %get-tuple-element.29), channel_id=1, source_target_pairs={{0,1},{1,0},{2,3},{3,2},{4,5},{5,4},{6,7},{7,6},{8,9},{9,8},{10,11... | collective-permute-start | bytes 49160 | tf_op jit(solution)/shard_map/ppermute | solution.py:501
  21.3 6.8 %collective-permute-start.4 = (bf16[64,128]{1,0:T(8,128)(2,1)}, bf16[64,128]{1,0:T(8,128)(2,1)S(1)}, u32[]{:S(2)}, u32[]{:S(2)}) collective-permute-start(bf16[64,128]{1,0:T(8,128)(2,1)} %get-tuple-element.30), channel_id=1, source_target_pairs={{0,3},{1,2},{2,1},{3,0},{4,7},{5,6},{6,5},{7,4},{8,11},{9,10},{10,... | collective-permute-start | bytes 49160 | tf_op jit(solution)/shard_map/ppermute | solution.py:501
  23.0 5.1 %collective-permute-start.5 = (bf16[64,128]{1,0:T(8,128)(2,1)}, bf16[64,128]{1,0:T(8,128)(2,1)S(1)}, u32[]{:S(2)}, u32[]{:S(2)}) collective-permute-start(bf16[64,128]{1,0:T(8,128)(2,1)} %get-tuple-element.31), channel_id=1, source_target_pairs={{0,2},{1,3},{2,0},{3,1},{4,6},{5,7},{6,4},{7,5},{8,10},{9,11},{10,... | collective-permute-start | bytes 49160 | tf_op jit(solution)/shard_map/ppermute | solution.py:501
  26.2 3.1 %collective-permute-start.11 = (bf16[2,2048]{1,0:T(2,128)(2,1)S(1)}, bf16[2,2048]{1,0:T(2,128)(2,1)S(1)}, u32[]{:S(2)}, u32[]{:S(2)}) collective-permute-start(bf16[2,2048]{1,0:T(2,128)(2,1)S(1)} %get-tuple-element.40), channel_id=1, source_target_pairs={{0,12},{4,8},{8,4},{12,0},{1,13},{5,9},{9,5},{13,1},{2,14},{6,10},... | collective-permute-start | bytes 24584 | tf_op jit(solution)/shard_map/ppermute | solution.py:501
  26.4 3.7 %collective-permute-start.10 = (bf16[2,2048]{1,0:T(2,128)(2,1)S(1)}, bf16[2,2048]{1,0:T(2,128)(2,1)S(1)}, u32[]{:S(2)}, u32[]{:S(2)}) collective-permute-start(bf16[2,2048]{1,0:T(2,128)(2,1)S(1)} %get-tuple-element.40), channel_id=1, source_target_pairs={{0,8},{4,12},{8,0},{12,4},{1,9},{5,13},{9,1},{13,5},{2,10},{6,14},... | collective-permute-start | bytes 24584 | tf_op jit(solution)/shard_map/ppermute | solution.py:501
  27.4 2.8 %collective-permute-start.9 = (bf16[2,2048]{1,0:T(2,128)(2,1)S(1)}, bf16[2,2048]{1,0:T(2,128)(2,1)S(1)}, u32[]{:S(2)}, u32[]{:S(2)}) collective-permute-start(bf16[2,2048]{1,0:T(2,128)(2,1)S(1)} %get-tuple-element.40), channel_id=1, source_target_pairs={{0,4},{4,0},{8,12},{12,8},{1,5},{5,1},{9,13},{13,9},{2,6},{6,2},{1... | collective-permute-start | bytes 24584 | tf_op jit(solution)/shard_map/ppermute | solution.py:501
  28.1 0.7 %copy-start.4 = (bf16[64,128]{1,0:T(8,128)(2,1)S(1)}, bf16[64,128]{1,0:T(8,128)(2,1)}, u32[]{:S(2)}) copy-start(bf16[64,128]{1,0:T(8,128)(2,1)} %get-tuple-element.28.rest_0_) | copy-start | bytes 49156

commit v17 on v16

--- a/solution.py
+++ b/solution.py
@@ -539,10 +539,11 @@
     pieces, ask = project(
         mig_hidden[0], attn_gain, kv_weight, query[0], new_kv[0], ranks, group, kv_mine
     )
-    order = sorted(range(1, ranks), key=lambda j: (j == 1, abs(j - ranks // 2), j))
-    sent = {j: swapped(pieces[j], "tp", j, ranks) for j in order}
-    pieces = [pieces[0]] + [sent[j] for j in order]
+    order = sorted(range(2, ranks), key=lambda j: (abs(j - ranks // 2), j))
     asks = [swapped(ask, "inst", b, insts) for b in range(1, insts)]
+    sent = [swapped(pieces[j], "tp", j, ranks) for j in order]
+    asks[0], near = lax.optimization_barrier((asks[0], pieces[1]))
+    pieces = [pieces[0]] + sent + [swapped(near, "tp", 1, ranks)]
     queries = jnp.transpose(query[0].reshape(query.shape[1], heads, head_size), (1, 0, 2))
     payloads = attend_resident(lengths, queries, k_cache[0], v_cache[0], ranks)
     asks, payloads = lax.optimization_barrier((asks, payloads))

time: 31.1 us -> 28.9 us (0.929)
  waiting for transfers between devices: 3.66 us -> 1.55 us
    ppermute x12, waiting for transfers between devices: 3.66 us -> 1.55 us  [swapped(): return lax.ppermute(x, axis, [(i, i ^ j) for i in range(n)])]
  transfers between devices with their start and end apart: 12 -> 12, of which waited for: 3 -> 2; matrix products, arithmetic and copies ran while one was open for 0% -> 0% of each run, Pallas kernels for 28% -> 30%
where the time goes in v17:
time: 28.9 us; the launch traced here: 28.6 us
  Pallas kernels  13.4 us (46%)
  starting transfers between devices  12.8 us (44%)
  waiting for transfers between devices  1.55 us (5%)
  local copies, waits for them, and re-layouts  0.74 us (3%)
    ppermute x12, starting transfers between devices, swapped(): return lax.ppermute(x, axis, [(i, i ^ j) for i in range(n)])  12.8 us
    pallas_call x1, Pallas kernels, attend_resident(): pl.pallas_call(functools.partial(resident_kernel, ranks), in_specs=[SMEM,...  7.13 us
    pallas_call x1, Pallas kernels, project(): pl.pallas_call(functools.partial(project_kernel, ranks, group), in_specs=...  4.12 us
    ppermute x12, waiting for transfers between devices, swapped(): return lax.ppermute(x, axis, [(i, i ^ j) for i in range(n)])  1.55 us
    pallas_call x1, Pallas kernels, attend_moved(): pl.pallas_call(functools.partial(moved_kernel, insts, len(pieces), reside...  1.32 us
    unnamed x16, local copies, waits for them, and re-layouts  0.74 us
    pallas_call x1, Pallas kernels, finish(): pl.pallas_call(finish_kernel, in_specs=[VMEM] * (2 + len(moved)), out_spe...  0.67 us
  transfers between devices with their start and end apart: 12, of which 2 were waited for; matrix products, arithmetic and copies ran while one was open for 0% of the time, Pallas kernels for 30%

profile of v17, /device:TPU:0, one launch (start us, length us, event | category | flops | bytes accessed | tf_op | source)
XLA Modules:
  0.0 28.6 jit_solution(14403524594649973482)
XLA Ops:
  0.0 4.1 %project.1 = (bf16[136,512]{1,0:T(8,128)(2,1)}, bf16[136,512]{1,0:T(8,128)(2,1)}, bf16[136,512]{1,0:T(8,128)(2,1)}, bf16[136,512]{1,0:T(8,128)(2,1)}, bf16[5,2560]{1,0:T(8,128)(2,1)}) custom-call(bf16[1280]{0:T(1024)(128)(2,1)} %gain_hbm.1, bf16[64,2,1280]{2,1,0:T(2,128)(2,1)} %bitcast.19, bf16[1280,2048]{1,0:T(8,128)(2,1)} %w_hbm.1, ...), custom_call_target="tpu_custom_call" | custom-call | flops 671088640 | bytes 5242880 | tf_op jit(solution)/shard_map/project/pallas_call | solution.py:131
  4.1 0.5 %collective-permute-start = (bf16[5,2560]{1,0:T(8,128)(2,1)}, bf16[5,2560]{1,0:T(8,128)(2,1)S(1)}, u32[]{:S(2)}, u32[]{:S(2)}) collective-permute-start(bf16[5,2560]{1,0:T(8,128)(2,1)} %get-tuple-element.25.ask_ref), channel_id=1, source_target_pairs={{0,4},{4,0},{8,12},{12,8},{1,5},{5,1},{9,13},{13,9},{2,6},{6,2},{1... | collective-permute-start | bytes 76808 | tf_op jit(solution)/shard_map/ppermute | solution.py:501
  4.6 3.7 %collective-permute-start.6 = (bf16[136,512]{1,0:T(8,128)(2,1)}, bf16[136,512]{1,0:T(8,128)(2,1)S(1)}, u32[]{:S(2)}, u32[]{:S(2)}) collective-permute-start(bf16[136,512]{1,0:T(8,128)(2,1)} %get-tuple-element.40), channel_id=1, source_target_pairs={{0,2},{1,3},{2,0},{3,1},{4,6},{5,7},{6,4},{7,5},{8,10},{9,11},{10,... | collective-permute-start | bytes 417800 | tf_op jit(solution)/shard_map/ppermute | solution.py:501
  8.3 1.3 %collective-permute-start.7 = (bf16[136,512]{1,0:T(8,128)(2,1)}, bf16[136,512]{1,0:T(8,128)(2,1)S(1)}, u32[]{:S(2)}, u32[]{:S(2)}) collective-permute-start(bf16[136,512]{1,0:T(8,128)(2,1)} %get-tuple-element.41), channel_id=1, source_target_pairs={{0,3},{1,2},{2,1},{3,0},{4,7},{5,6},{6,5},{7,4},{8,11},{9,10},{10,... | collective-permute-start | bytes 417800 | tf_op jit(solution)/shard_map/ppermute | solution.py:501
  9.7 0.0 collective-permute-done.rest_0_
  9.7 0.2 collective-permute-start.8
  9.9 1.0 %collective-permute-start.2 = (bf16[5,2560]{1,0:T(8,128)(2,1)}, bf16[5,2560]{1,0:T(8,128)(2,1)S(1)}, u32[]{:S(2)}, u32[]{:S(2)}) collective-permute-start(bf16[5,2560]{1,0:T(8,128)(2,1)} %get-tuple-element.25.ask_ref), channel_id=1, source_target_pairs={{0,12},{4,8},{8,4},{12,0},{1,13},{5,9},{9,5},{13,1},{2,14},{6,10},... | collective-permute-start | bytes 76808 | tf_op jit(solution)/shard_map/ppermute | solution.py:501
  10.9 0.5 %collective-permute-start.1 = (bf16[5,2560]{1,0:T(8,128)(2,1)}, bf16[5,2560]{1,0:T(8,128)(2,1)S(1)}, u32[]{:S(2)}, u32[]{:S(2)}) collective-permute-start(bf16[5,2560]{1,0:T(8,128)(2,1)} %get-tuple-element.25.ask_ref), channel_id=1, source_target_pairs={{0,8},{4,12},{8,0},{12,4},{1,9},{5,13},{9,1},{13,5},{2,10},{6,14},... | collective-permute-start | bytes 76808 | tf_op jit(solution)/shard_map/ppermute | solution.py:501
  11.4 0.0 copy-start
  11.4 0.0 copy-start.1
  11.4 0.0 copy-start.2
  11.4 0.0 copy-start.5
  11.4 0.0 copy-start.6
  11.4 0.0 copy-start.7
  11.5 0.0 copy-start.3
  11.5 7.1 %attend_resident.1 = (bf16[64,128]{1,0:T(8,128)(2,1)}, bf16[64,128]{1,0:T(8,128)(2,1)}, bf16[64,128]{1,0:T(8,128)(2,1)}, bf16[64,128]{1,0:T(8,128)(2,1)}) custom-call(s32[1,3]{1,0:T(1,128)} %len_ref.1, bf16[64,5,128]{2,1,0:T(8,128)(2,1)} %bitcast.18, bf16[3,1024,1024]{2,1,0:T(8,128)(2,1)} %bitcast.15, bf16[3,1024,1024]{2,1,0:T(8,128)(2,1)} %bitcast.16), custom_call_target="tpu_custom_call" | custom-call | flops 100663296 | bytes 12582912 | tf_op jit(solution)/shard_map/attend_resident/pallas_call | solution.py:256
  18.6 0.0 collective-permute-done.2.rest_2_
  18.6 0.0 collective-permute-done.1.rest_1_
  18.6 0.6 %collective-permute-start.3 = (bf16[64,128]{1,0:T(8,128)(2,1)}, bf16[64,128]{1,0:T(8,128)(2,1)S(1)}, u32[]{:S(2)}, u32[]{:S(2)}) collective-permute-start(bf16[64,128]{1,0:T(8,128)(2,1)} %get-tuple-element.33), channel_id=1, source_target_pairs={{0,1},{1,0},{2,3},{3,2},{4,5},{5,4},{6,7},{7,6},{8,9},{9,8},{10,11... | collective-permute-start | bytes 49160 | tf_op jit(solution)/shard_map/ppermute | solution.py:501
  19.3 1.2 %collective-permute-start.4 = (bf16[64,128]{1,0:T(8,128)(2,1)}, bf16[64,128]{1,0:T(8,128)(2,1)S(1)}, u32[]{:S(2)}, u32[]{:S(2)}) collective-permute-start(bf16[64,128]{1,0:T(8,128)(2,1)} %get-tuple-element.34), channel_id=1, source_target_pairs={{0,3},{1,2},{2,1},{3,0},{4,7},{5,6},{6,5},{7,4},{8,11},{9,10},{10,... | collective-permute-start | bytes 49160 | tf_op jit(solution)/shard_map/ppermute | solution.py:501
  20.5 0.0 collective-permute-done.6.rest_4_
  20.5 1.7 %collective-permute-start.5 = (bf16[64,128]{1,0:T(8,128)(2,1)}, bf16[64,128]{1,0:T(8,128)(2,1)S(1)}, u32[]{:S(2)}, u32[]{:S(2)}) collective-permute-start(bf16[64,128]{1,0:T(8,128)(2,1)} %get-tuple-element.35), channel_id=1, source_target_pairs={{0,2},{1,3},{2,0},{3,1},{4,6},{5,7},{6,4},{7,5},{8,10},{9,11},{10,... | collective-permute-start | bytes 49160 | tf_op jit(solution)/shard_map/ppermute | solution.py:501
  22.2 0.0 collective-permute-done.7.rest_5_
  22.2 0.0 collective-permute-done.8.rest_6_
  22.2 0.0 copy-done
  22.2 0.0 copy-done.1
  22.2 0.0 copy-done.2
  22.2 0.0 copy-done.5
  22.2 0.0 copy-done.6
  22.2 0.0 copy-done.7
  22.2 1.3 %attend_moved.1 = (bf16[2,2048]{1,0:T(2,128)(2,1)S(1)}, s32[8,128]{1,0:T(8,128)S(1)}) custom-call(s32[2,4]{1,0:T(2,128)S(1)} %bitcast.12, s32[2,4]{1,0:T(2,128)S(1)} %bitcast.13, bf16[1,128]{1,0:T(2,128)(2,1)S(1)} %bitcast.14, f32[128,128]{1,0:T(8,128)S(1)} %copy-done.2, f32[128,128]{1,0:T(8,128)S(1)} %copy-done.1, ...), custom_call_target="tpu_custom_call" | custom-call | tf_op jit(solution)/shard_map/attend_moved/pallas_call | solution.py:407
  23.6 0.7 %collective-permute-start.11 = (bf16[2,2048]{1,0:T(2,128)(2,1)S(1)}, bf16[2,2048]{1,0:T(2,128)(2,1)S(1)}, u32[]{:S(2)}, u32[]{:S(2)}) collective-permute-start(bf16[2,2048]{1,0:T(2,128)(2,1)S(1)} %get-tuple-element.44), channel_id=1, source_target_pairs={{0,12},{4,8},{8,4},{12,0},{1,13},{5,9},{9,5},{13,1},{2,14},{6,10},... | collective-permute-start | bytes 24584 | tf_op jit(solution)/shard_map/ppermute | solution.py:501
  24.2 1.0 %collective-permute-start.10 = (bf16[2,2048]{1,0:T(2,128)(2,1)S(1)}, bf16[2,2048]{1,0:T(2,128)(2,1)S(1)}, u32[]{:S(2)}, u32[]{:S(2)}) collective-permute-start(bf16[2,2048]{1,0:T(2,128)(2,1)S(1)} %get-tuple-element.44), channel_id=1, source_target_pairs={{0,8},{4,12},{8,0},{12,4},{1,9},{5,13},{9,1},{13,5},{2,10},{6,14},... | collective-permute-start | bytes 24584 | tf_op jit(solution)/shard_map/ppermute | solution.py:501
  25.2 0.0 collective-permute-done.3.rest_1_
  25.2 0.3 %collective-permute-start.9 = (bf16[2,2048]{1,0:T(2,128)(2,1)S(1)}, bf16[2,2048]{1,0:T(2,128)(2,1)S(1)}, u32[]{:S(2)}, u32[]{:S(2)}) collective-permute-start(bf16[2,2048]{1,0:T(2,128)(2,1)S(1)} %get-tuple-element.44), channel_id=1, source_target_pairs={{0,4},{4,0},{8,12},{12,8},{1,5},{5,1},{9,13},{13,9},{2,6},{6,2},{1... | collective-permute-start | bytes 24584 | tf_op jit(solution)/shard_map/ppermute | solution.py:501
  25.5 0.0 collective-permute-done.4.rest_2_
  25.5 0.0 collective-permute-done.5.rest_3_
  25.5 0.0 copy-done.3
  25.5 0.0 copy-start.4
  25.5 0.7 %copy-done.4 = bf16[64,128]{1,0:T(8,128)(2,1)S(1)} copy-done((bf16[64,128]{1,0:T(8,128)(2,1)S(1)}, bf16[64,128]{1,0:T(8,128)(2,1)}, u32[]{:S(2)}) %copy-start.4) | copy-done | bytes 16408
  26.2 0.2 combine_resident.1.kept_ref
  26.4 0.4 %collective-permute-done.11.rest_2_ = bf16[2,2048]{1,0:T(2,128)(2,1)S(1)} collective-permute-done((bf16[2,2048]{1,0:T(2,128)(2,1)S(1)}, bf16[2,2048]{1,0:T(2,128)(2,1)S(1)}, u32[]{:S(2)}, u32[]{:S(2)}) %collective-permute-start.11) | collective-permute-done | bytes 8224 | tf_op jit(solution)/shard_map/ppermute | solution.py:501
  26.8 1.2 %collective-permute-done.10.rest_1_ = bf16[2,2048]{1,0:T(2,128)(2,1)S(1)} collective-permute-done((bf16[2,2048]{1,0:T(2,128)(2,1)S(1)}, bf16[2,2048]{1,0:T(2,128)(2,1)S(1)}, u32[]{:S(2)}, u32[]{:S(2)}) %collective-permute-start.10) | collective-permute-done | bytes 8224 | tf_op jit(solution)/shard_map/ppermute | solution.py:501
  27.9 0.0 collective-permute-done.9.rest_0_
  27.9 0.7 %finish.1 = bf16[5,2048]{1,0:T(8,128)(2,1)} custom-call(f32[3,2048]{1,0:T(4,128)S(1)} %combine_resident.1.kept_ref, s32[8,128]{1,0:T(8,128)S(1)} %get-tuple-element.43.place_ref, bf16[2,2048]{1,0:T(2,128)(2,1)S(1)} %collective-permute-done.9.rest_0_, bf16[2,2048]{1,0:T(2,128)(2,1)S(1)} %collective-permute-done.10.rest_1_, ...), custom_call_target="tpu_custom_call" | custom-call | tf_op jit(solution)/shard_map/finish/pallas_call | solution.py:490
Async XLA Ops:
  4.1 5.5 %collective-permute-start = (bf16[5,2560]{1,0:T(8,128)(2,1)}, bf16[5,2560]{1,0:T(8,128)(2,1)S(1)}, u32[]{:S(2)}, u32[]{:S(2)}) collective-permute-start(bf16[5,2560]{1,0:T(8,128)(2,1)} %get-tuple-element.25.ask_ref), channel_id=1, source_target_pairs={{0,4},{4,0},{8,12},{12,8},{1,5},{5,1},{9,13},{13,9},{2,6},{6,2},{1... | collective-permute-start | bytes 76808 | tf_op jit(solution)/shard_map/ppermute | solution.py:501
  4.6 15.8 %collective-permute-start.6 = (bf16[136,512]{1,0:T(8,128)(2,1)}, bf16[136,512]{1,0:T(8,128)(2,1)S(1)}, u32[]{:S(2)}, u32[]{:S(2)}) collective-permute-start(bf16[136,512]{1,0:T(8,128)(2,1)} %get-tuple-element.40), channel_id=1, source_target_pairs={{0,2},{1,3},{2,0},{3,1},{4,6},{5,7},{6,4},{7,5},{8,10},{9,11},{10,... | collective-permute-start | bytes 417800 | tf_op jit(solution)/shard_map/ppermute | solution.py:501
  8.3 13.9 %collective-permute-start.7 = (bf16[136,512]{1,0:T(8,128)(2,1)}, bf16[136,512]{1,0:T(8,128)(2,1)S(1)}, u32[]{:S(2)}, u32[]{:S(2)}) collective-permute-start(bf16[136,512]{1,0:T(8,128)(2,1)} %get-tuple-element.41), channel_id=1, source_target_pairs={{0,3},{1,2},{2,1},{3,0},{4,7},{5,6},{6,5},{7,4},{8,11},{9,10},{10,... | collective-permute-start | bytes 417800 | tf_op jit(solution)/shard_map/ppermute | solution.py:501
  9.7 12.5 %collective-permute-start.8 = (bf16[136,512]{1,0:T(8,128)(2,1)}, bf16[136,512]{1,0:T(8,128)(2,1)S(1)}, u32[]{:S(2)}, u32[]{:S(2)}) collective-permute-start(bf16[136,512]{1,0:T(8,128)(2,1)} %get-tuple-element.42), channel_id=1, source_target_pairs={{0,1},{1,0},{2,3},{3,2},{4,5},{5,4},{6,7},{7,6},{8,9},{9,8},{10,11... | collective-permute-start | bytes 417800 | tf_op jit(solution)/shard_map/ppermute | solution.py:501
  9.9 8.7 %collective-permute-start.2 = (bf16[5,2560]{1,0:T(8,128)(2,1)}, bf16[5,2560]{1,0:T(8,128)(2,1)S(1)}, u32[]{:S(2)}, u32[]{:S(2)}) collective-permute-start(bf16[5,2560]{1,0:T(8,128)(2,1)} %get-tuple-element.25.ask_ref), channel_id=1, source_target_pairs={{0,12},{4,8},{8,4},{12,0},{1,13},{5,9},{9,5},{13,1},{2,14},{6,10},... | collective-permute-start | bytes 76808 | tf_op jit(solution)/shard_map/ppermute | solution.py:501
  10.9 7.7 %collective-permute-start.1 = (bf16[5,2560]{1,0:T(8,128)(2,1)}, bf16[5,2560]{1,0:T(8,128)(2,1)S(1)}, u32[]{:S(2)}, u32[]{:S(2)}) collective-permute-start(bf16[5,2560]{1,0:T(8,128)(2,1)} %get-tuple-element.25.ask_ref), channel_id=1, source_target_pairs={{0,8},{4,12},{8,0},{12,4},{1,9},{5,13},{9,1},{13,5},{2,10},{6,14},... | collective-permute-start | bytes 76808 | tf_op jit(solution)/shard_map/ppermute | solution.py:501
  11.4 10.8 %copy-start = (bf16[136,512]{1,0:T(8,128)(2,1)S(1)}, bf16[136,512]{1,0:T(8,128)(2,1)}, u32[]{:S(2)}) copy-start(bf16[136,512]{1,0:T(8,128)(2,1)} %get-tuple-element.39.rest_3_) | copy-start | bytes 417796
  11.4 10.8 %copy-start.1 = (f32[128,128]{1,0:T(8,128)S(1)}, f32[128,128]{1,0:T(8,128)}, u32[]{:S(2)}) copy-start(f32[128,128]{1,0:T(8,128)} %constant.5.clone.sin_ref) | copy-start | bytes 196612
  11.4 10.8 %copy-start.2 = (f32[128,128]{1,0:T(8,128)S(1)}, f32[128,128]{1,0:T(8,128)}, u32[]{:S(2)}) copy-start(f32[128,128]{1,0:T(8,128)} %constant.4.clone.cos_ref) | copy-start | bytes 196612
  11.4 10.8 %copy-start.5 = (s32[4,2]{0,1:T(2,128)S(1)}, s32[4,2]{0,1:T(2,128)}, u32[]{:S(2)}) copy-start(s32[4,2]{0,1:T(2,128)} %param.14) | copy-start | bytes 100
  11.4 10.8 %copy-start.6 = (s32[4,2]{0,1:T(2,128)S(1)}, s32[4,2]{0,1:T(2,128)}, u32[]{:S(2)}) copy-start(s32[4,2]{0,1:T(2,128)} %param.15) | copy-start | bytes 100
  11.4 10.8 %copy-start.7 = (bf16[128]{0:T(256)(128)(2,1)S(1)}, bf16[128]{0:T(256)(128)(2,1)}, u32[]{:S(2)}) copy-start(bf16[128]{0:T(256)(128)(2,1)} %param.18) | copy-start | bytes 772
  11.5 14.1 %copy-start.3 = (bf16[5,2560]{1,0:T(8,128)(2,1)S(1)}, bf16[5,2560]{1,0:T(8,128)(2,1)}, u32[]{:S(2)}) copy-start(bf16[5,2560]{1,0:T(8,128)(2,1)} %get-tuple-element.25.ask_ref) | copy-start | bytes 76804
  18.6 6.6 %collective-permute-start.3 = (bf16[64,128]{1,0:T(8,128)(2,1)}, bf16[64,128]{1,0:T(8,128)(2,1)S(1)}, u32[]{:S(2)}, u32[]{:S(2)}) collective-permute-start(bf16[64,128]{1,0:T(8,128)(2,1)} %get-tuple-element.33), channel_id=1, source_target_pairs={{0,1},{1,0},{2,3},{3,2},{4,5},{5,4},{6,7},{7,6},{8,9},{9,8},{10,11... | collective-permute-start | bytes 49160 | tf_op jit(solution)/shard_map/ppermute | solution.py:501
  19.3 6.3 %collective-permute-start.4 = (bf16[64,128]{1,0:T(8,128)(2,1)}, bf16[64,128]{1,0:T(8,128)(2,1)S(1)}, u32[]{:S(2)}, u32[]{:S(2)}) collective-permute-start(bf16[64,128]{1,0:T(8,128)(2,1)} %get-tuple-element.34), channel_id=1, source_target_pairs={{0,3},{1,2},{2,1},{3,0},{4,7},{5,6},{6,5},{7,4},{8,11},{9,10},{10,... | collective-permute-start | bytes 49160 | tf_op jit(solution)/shard_map/ppermute | solution.py:501
  20.5 5.0 %collective-permute-start.5 = (bf16[64,128]{1,0:T(8,128)(2,1)}, bf16[64,128]{1,0:T(8,128)(2,1)S(1)}, u32[]{:S(2)}, u32[]{:S(2)}) collective-permute-start(bf16[64,128]{1,0:T(8,128)(2,1)} %get-tuple-element.35), channel_id=1, source_target_pairs={{0,2},{1,3},{2,0},{3,1},{4,6},{5,7},{6,4},{7,5},{8,10},{9,11},{10,... | collective-permute-start | bytes 49160 | tf_op jit(solution)/shard_map/ppermute | solution.py:501
  23.6 3.2 %collective-permute-start.11 = (bf16[2,2048]{1,0:T(2,128)(2,1)S(1)}, bf16[2,2048]{1,0:T(2,128)(2,1)S(1)}, u32[]{:S(2)}, u32[]{:S(2)}) collective-permute-start(bf16[2,2048]{1,0:T(2,128)(2,1)S(1)} %get-tuple-element.44), channel_id=1, source_target_pairs={{0,12},{4,8},{8,4},{12,0},{1,13},{5,9},{9,5},{13,1},{2,14},{6,10},... | collective-permute-start | bytes 24584 | tf_op jit(solution)/shard_map/ppermute | solution.py:501
  24.2 3.7 %collective-permute-start.10 = (bf16[2,2048]{1,0:T(2,128)(2,1)S(1)}, bf16[2,2048]{1,0:T(2,128)(2,1)S(1)}, u32[]{:S(2)}, u32[]{:S(2)}) collective-permute-start(bf16[2,2048]{1,0:T(2,128)(2,1)S(1)} %get-tuple-element.44), channel_id=1, source_target_pairs={{0,8},{4,12},{8,0},{12,4},{1,9},{5,13},{9,1},{13,5},{2,10},{6,14},... | collective-permute-start | bytes 24584 | tf_op jit(solution)/shard_map/ppermute | solution.py:501
  25.2 2.7 %collective-permute-start.9 = (bf16[2,2048]{1,0:T(2,128)(2,1)S(1)}, bf16[2,2048]{1,0:T(2,128)(2,1)S(1)}, u32[]{:S(2)}, u32[]{:S(2)}) collective-permute-start(bf16[2,2048]{1,0:T(2,128)(2,1)S(1)} %get-tuple-element.44), channel_id=1, source_target_pairs={{0,4},{4,0},{8,12},{12,8},{1,5},{5,1},{9,13},{13,9},{2,6},{6,2},{1... | collective-permute-start | bytes 24584 | tf_op jit(solution)/shard_map/ppermute | solution.py:501
  25.5 0.7 %copy-start.4 = (bf16[64,128]{1,0:T(8,128)(2,1)S(1)}, bf16[64,128]{1,0:T(8,128)(2,1)}, u32[]{:S(2)}) copy-start(bf16[64,128]{1,0:T(8,128)(2,1)} %get-tuple-element.32.rest_0_) | copy-start | bytes 49156

commit v18 on v17

--- a/solution.py
+++ b/solution.py
@@ -59,14 +59,6 @@
     gain_copy.start()
     x_copy = pltpu.make_async_copy(x_hbm, x_ref, in_sems.at[1])
     x_copy.start()
-    cuts = list(range(0, feats, CHUNK)) + [feats]
-    chunks = list(zip(cuts[:-1], cuts[1:]))
-    copies = []
-    for i, (low, high) in enumerate(chunks):
-        copies.append(
-            pltpu.make_async_copy(w_hbm.at[low:high, :], w_ref.at[low:high, :], w_sems.at[i])
-        )
-        copies[-1].start()
     mine = heads_mine * 128
     q_first = pl.multiple_of(rank * mine, 128)
     asking = [
@@ -84,6 +76,14 @@
         )
     for copy in asking:
         copy.start()
+    cuts = list(range(0, feats, CHUNK)) + [feats]
+    chunks = list(zip(cuts[:-1], cuts[1:]))
+    copies = []
+    for i, (low, high) in enumerate(chunks):
+        copies.append(
+            pltpu.make_async_copy(w_hbm.at[low:high, :], w_ref.at[low:high, :], w_sems.at[i])
+        )
+        copies[-1].start()
     gain_copy.wait()
     x_copy.wait()
     squares = jnp.zeros((rows, 128), F32)
@@ -100,12 +100,19 @@
             squares = squares + x
         xg = parts[0] if len(parts) == 1 else jnp.concatenate(parts, axis=1)
         copies[i].wait()
-        for n in range(0, 2 * kv_width, 512):
-            part = jnp.dot(xg, w_ref[low:high, n : n + 512], preferred_element_type=F32)
-            if i == 0:
-                acc_ref[:, n : n + 512] = part
-            else:
-                acc_ref[:, n : n + 512] += part
+        for j in range(ranks):
+            for half in range(2):
+                first = pl.multiple_of(half * kv_width + first_column(rank ^ j), 128)
+                part = jnp.dot(
+                    xg, w_ref[low:high, pl.ds(first, piece)], preferred_element_type=F32
+                )
+                at = slice(half * piece, (half + 1) * piece)
+                if i > 0:
+                    part = part + acc_ref[j, :, at]
+                if i + 1 < len(chunks):
+                    acc_ref[j, :, at] = part
+                else:
+                    outs[j][:rows, at] = part.astype(BF16)
     sq = column_to_row(jnp.sum(squares, axis=1, keepdims=True), 128)
     high, low = split_bf16(sq)
     tail = jnp.concatenate([high.astype(F32), low.astype(F32)], axis=0)
@@ -114,9 +121,6 @@
         tail = jnp.concatenate([tail, jnp.zeros((fill, 128), F32)], axis=0)
     extra = jnp.concatenate([tail.astype(BF16)] * (2 * piece // 128), axis=1)
     for j in range(ranks):
-        first = first_column(rank ^ j)
-        outs[j][:rows, :piece] = acc_ref[:, pl.ds(first, piece)].astype(BF16)
-        outs[j][:rows, piece:] = acc_ref[:, pl.ds(kv_width + first, piece)].astype(BF16)
         outs[j][rows:, :] = extra
     for copy in asking:
         copy.wait()
@@ -138,7 +142,7 @@
             pltpu.VMEM((feats,), BF16),
             pltpu.VMEM((slots, requests, feats), BF16),
             pltpu.VMEM(weight.shape, BF16),
-            pltpu.VMEM((rows, weight.shape[1]), F32),
+            pltpu.VMEM((ranks, rows, 2 * piece), F32),
             pltpu.SemaphoreType.DMA((5,)),
             pltpu.SemaphoreType.DMA((-(-feats // CHUNK),)),
         ],

time: 28.9 us -> 28.9 us (level)
  no operation moved by 1% of the time
where the time goes in v18:
time: 28.9 us; the launch traced here: 28.6 us
  Pallas kernels  13.3 us (46%)
  starting transfers between devices  12.8 us (44%)
  waiting for transfers between devices  1.62 us (6%)
  local copies, waits for them, and re-layouts  0.74 us (3%)
    ppermute x12, starting transfers between devices, swapped(): return lax.ppermute(x, axis, [(i, i ^ j) for i in range(n)])  12.8 us
    pallas_call x1, Pallas kernels, attend_resident(): pl.pallas_call(functools.partial(resident_kernel, ranks), in_specs=[SMEM,...  7.13 us
    pallas_call x1, Pallas kernels, project(): pl.pallas_call(functools.partial(project_kernel, ranks, group), in_specs=...  4.06 us
    ppermute x12, waiting for transfers between devices, swapped(): return lax.ppermute(x, axis, [(i, i ^ j) for i in range(n)])  1.62 us
    pallas_call x1, Pallas kernels, attend_moved(): pl.pallas_call(functools.partial(moved_kernel, insts, len(pieces), reside...  1.32 us
    unnamed x16, local copies, waits for them, and re-layouts  0.74 us
    pallas_call x1, Pallas kernels, finish(): pl.pallas_call(finish_kernel, in_specs=[VMEM] * (2 + len(moved)), out_spe...  0.67 us
  transfers between devices with their start and end apart: 12, of which 2 were waited for; matrix products, arithmetic and copies ran while one was open for 0% of the time, Pallas kernels for 30%

profile of v18, /device:TPU:0, one launch (start us, length us, event | category | flops | bytes accessed | tf_op | source)
XLA Modules:
  0.0 28.6 jit_solution(4245769485984852604)
XLA Ops:
  0.0 4.1 %project.1 = (bf16[136,512]{1,0:T(8,128)(2,1)}, bf16[136,512]{1,0:T(8,128)(2,1)}, bf16[136,512]{1,0:T(8,128)(2,1)}, bf16[136,512]{1,0:T(8,128)(2,1)}, bf16[5,2560]{1,0:T(8,128)(2,1)}) custom-call(bf16[1280]{0:T(1024)(128)(2,1)} %gain_hbm.1, bf16[64,2,1280]{2,1,0:T(2,128)(2,1)} %bitcast.19, bf16[1280,2048]{1,0:T(8,128)(2,1)} %w_hbm.1, ...), custom_call_target="tpu_custom_call" | custom-call | flops 671088640 | bytes 5242880 | tf_op jit(solution)/shard_map/project/pallas_call | solution.py:135
  4.1 0.5 %collective-permute-start = (bf16[5,2560]{1,0:T(8,128)(2,1)}, bf16[5,2560]{1,0:T(8,128)(2,1)S(1)}, u32[]{:S(2)}, u32[]{:S(2)}) collective-permute-start(bf16[5,2560]{1,0:T(8,128)(2,1)} %get-tuple-element.25.ask_ref), channel_id=1, source_target_pairs={{0,4},{4,0},{8,12},{12,8},{1,5},{5,1},{9,13},{13,9},{2,6},{6,2},{1... | collective-permute-start | bytes 76808 | tf_op jit(solution)/shard_map/ppermute | solution.py:505
  4.6 3.7 %collective-permute-start.6 = (bf16[136,512]{1,0:T(8,128)(2,1)}, bf16[136,512]{1,0:T(8,128)(2,1)S(1)}, u32[]{:S(2)}, u32[]{:S(2)}) collective-permute-start(bf16[136,512]{1,0:T(8,128)(2,1)} %get-tuple-element.40), channel_id=1, source_target_pairs={{0,2},{1,3},{2,0},{3,1},{4,6},{5,7},{6,4},{7,5},{8,10},{9,11},{10,... | collective-permute-start | bytes 417800 | tf_op jit(solution)/shard_map/ppermute | solution.py:505
  8.3 1.3 %collective-permute-start.7 = (bf16[136,512]{1,0:T(8,128)(2,1)}, bf16[136,512]{1,0:T(8,128)(2,1)S(1)}, u32[]{:S(2)}, u32[]{:S(2)}) collective-permute-start(bf16[136,512]{1,0:T(8,128)(2,1)} %get-tuple-element.41), channel_id=1, source_target_pairs={{0,3},{1,2},{2,1},{3,0},{4,7},{5,6},{6,5},{7,4},{8,11},{9,10},{10,... | collective-permute-start | bytes 417800 | tf_op jit(solution)/shard_map/ppermute | solution.py:505
  9.6 0.0 collective-permute-done.rest_0_
  9.6 0.2 collective-permute-start.8
  9.9 1.0 %collective-permute-start.2 = (bf16[5,2560]{1,0:T(8,128)(2,1)}, bf16[5,2560]{1,0:T(8,128)(2,1)S(1)}, u32[]{:S(2)}, u32[]{:S(2)}) collective-permute-start(bf16[5,2560]{1,0:T(8,128)(2,1)} %get-tuple-element.25.ask_ref), channel_id=1, source_target_pairs={{0,12},{4,8},{8,4},{12,0},{1,13},{5,9},{9,5},{13,1},{2,14},{6,10},... | collective-permute-start | bytes 76808 | tf_op jit(solution)/shard_map/ppermute | solution.py:505
  10.8 0.5 %collective-permute-start.1 = (bf16[5,2560]{1,0:T(8,128)(2,1)}, bf16[5,2560]{1,0:T(8,128)(2,1)S(1)}, u32[]{:S(2)}, u32[]{:S(2)}) collective-permute-start(bf16[5,2560]{1,0:T(8,128)(2,1)} %get-tuple-element.25.ask_ref), channel_id=1, source_target_pairs={{0,8},{4,12},{8,0},{12,4},{1,9},{5,13},{9,1},{13,5},{2,10},{6,14},... | collective-permute-start | bytes 76808 | tf_op jit(solution)/shard_map/ppermute | solution.py:505
  11.4 0.0 copy-start
  11.4 0.0 copy-start.1
  11.4 0.0 copy-start.2
  11.4 0.0 copy-start.5
  11.4 0.0 copy-start.6
  11.4 0.0 copy-start.7
  11.4 0.0 copy-start.3
  11.4 7.1 %attend_resident.1 = (bf16[64,128]{1,0:T(8,128)(2,1)}, bf16[64,128]{1,0:T(8,128)(2,1)}, bf16[64,128]{1,0:T(8,128)(2,1)}, bf16[64,128]{1,0:T(8,128)(2,1)}) custom-call(s32[1,3]{1,0:T(1,128)} %len_ref.1, bf16[64,5,128]{2,1,0:T(8,128)(2,1)} %bitcast.18, bf16[3,1024,1024]{2,1,0:T(8,128)(2,1)} %bitcast.15, bf16[3,1024,1024]{2,1,0:T(8,128)(2,1)} %bitcast.16), custom_call_target="tpu_custom_call" | custom-call | flops 100663296 | bytes 12582912 | tf_op jit(solution)/shard_map/attend_resident/pallas_call | solution.py:260
  18.6 0.0 collective-permute-done.2.rest_2_
  18.6 0.0 collective-permute-done.1.rest_1_
  18.6 0.6 %collective-permute-start.3 = (bf16[64,128]{1,0:T(8,128)(2,1)}, bf16[64,128]{1,0:T(8,128)(2,1)S(1)}, u32[]{:S(2)}, u32[]{:S(2)}) collective-permute-start(bf16[64,128]{1,0:T(8,128)(2,1)} %get-tuple-element.33), channel_id=1, source_target_pairs={{0,1},{1,0},{2,3},{3,2},{4,5},{5,4},{6,7},{7,6},{8,9},{9,8},{10,11... | collective-permute-start | bytes 49160 | tf_op jit(solution)/shard_map/ppermute | solution.py:505
  19.2 1.2 %collective-permute-start.4 = (bf16[64,128]{1,0:T(8,128)(2,1)}, bf16[64,128]{1,0:T(8,128)(2,1)S(1)}, u32[]{:S(2)}, u32[]{:S(2)}) collective-permute-start(bf16[64,128]{1,0:T(8,128)(2,1)} %get-tuple-element.34), channel_id=1, source_target_pairs={{0,3},{1,2},{2,1},{3,0},{4,7},{5,6},{6,5},{7,4},{8,11},{9,10},{10,... | collective-permute-start | bytes 49160 | tf_op jit(solution)/shard_map/ppermute | solution.py:505
  20.4 0.0 collective-permute-done.6.rest_4_
  20.4 1.7 %collective-permute-start.5 = (bf16[64,128]{1,0:T(8,128)(2,1)}, bf16[64,128]{1,0:T(8,128)(2,1)S(1)}, u32[]{:S(2)}, u32[]{:S(2)}) collective-permute-start(bf16[64,128]{1,0:T(8,128)(2,1)} %get-tuple-element.35), channel_id=1, source_target_pairs={{0,2},{1,3},{2,0},{3,1},{4,6},{5,7},{6,4},{7,5},{8,10},{9,11},{10,... | collective-permute-start | bytes 49160 | tf_op jit(solution)/shard_map/ppermute | solution.py:505
  22.1 0.0 collective-permute-done.7.rest_5_
  22.1 0.0 collective-permute-done.8.rest_6_
  22.2 0.0 copy-done
  22.2 0.0 copy-done.1
  22.2 0.0 copy-done.2
  22.2 0.0 copy-done.5
  22.2 0.0 copy-done.6
  22.2 0.0 copy-done.7
  22.2 1.3 %attend_moved.1 = (bf16[2,2048]{1,0:T(2,128)(2,1)S(1)}, s32[8,128]{1,0:T(8,128)S(1)}) custom-call(s32[2,4]{1,0:T(2,128)S(1)} %bitcast.12, s32[2,4]{1,0:T(2,128)S(1)} %bitcast.13, bf16[1,128]{1,0:T(2,128)(2,1)S(1)} %bitcast.14, f32[128,128]{1,0:T(8,128)S(1)} %copy-done.2, f32[128,128]{1,0:T(8,128)S(1)} %copy-done.1, ...), custom_call_target="tpu_custom_call" | custom-call | tf_op jit(solution)/shard_map/attend_moved/pallas_call | solution.py:411
  23.5 0.8 %collective-permute-start.11 = (bf16[2,2048]{1,0:T(2,128)(2,1)S(1)}, bf16[2,2048]{1,0:T(2,128)(2,1)S(1)}, u32[]{:S(2)}, u32[]{:S(2)}) collective-permute-start(bf16[2,2048]{1,0:T(2,128)(2,1)S(1)} %get-tuple-element.44), channel_id=1, source_target_pairs={{0,12},{4,8},{8,4},{12,0},{1,13},{5,9},{9,5},{13,1},{2,14},{6,10},... | collective-permute-start | bytes 24584 | tf_op jit(solution)/shard_map/ppermute | solution.py:505
  24.3 0.9 %collective-permute-start.10 = (bf16[2,2048]{1,0:T(2,128)(2,1)S(1)}, bf16[2,2048]{1,0:T(2,128)(2,1)S(1)}, u32[]{:S(2)}, u32[]{:S(2)}) collective-permute-start(bf16[2,2048]{1,0:T(2,128)(2,1)S(1)} %get-tuple-element.44), channel_id=1, source_target_pairs={{0,8},{4,12},{8,0},{12,4},{1,9},{5,13},{9,1},{13,5},{2,10},{6,14},... | collective-permute-start | bytes 24584 | tf_op jit(solution)/shard_map/ppermute | solution.py:505
  25.2 0.0 collective-permute-done.3.rest_1_
  25.2 0.3 %collective-permute-start.9 = (bf16[2,2048]{1,0:T(2,128)(2,1)S(1)}, bf16[2,2048]{1,0:T(2,128)(2,1)S(1)}, u32[]{:S(2)}, u32[]{:S(2)}) collective-permute-start(bf16[2,2048]{1,0:T(2,128)(2,1)S(1)} %get-tuple-element.44), channel_id=1, source_target_pairs={{0,4},{4,0},{8,12},{12,8},{1,5},{5,1},{9,13},{13,9},{2,6},{6,2},{1... | collective-permute-start | bytes 24584 | tf_op jit(solution)/shard_map/ppermute | solution.py:505
  25.5 0.0 collective-permute-done.4.rest_2_
  25.5 0.0 collective-permute-done.5.rest_3_
  25.5 0.0 copy-done.3
  25.5 0.0 copy-start.4
  25.5 0.7 %copy-done.4 = bf16[64,128]{1,0:T(8,128)(2,1)S(1)} copy-done((bf16[64,128]{1,0:T(8,128)(2,1)S(1)}, bf16[64,128]{1,0:T(8,128)(2,1)}, u32[]{:S(2)}) %copy-start.4) | copy-done | bytes 16408
  26.2 0.2 combine_resident.1.kept_ref
  26.4 0.4 %collective-permute-done.11.rest_2_ = bf16[2,2048]{1,0:T(2,128)(2,1)S(1)} collective-permute-done((bf16[2,2048]{1,0:T(2,128)(2,1)S(1)}, bf16[2,2048]{1,0:T(2,128)(2,1)S(1)}, u32[]{:S(2)}, u32[]{:S(2)}) %collective-permute-start.11) | collective-permute-done | bytes 8224 | tf_op jit(solution)/shard_map/ppermute | solution.py:505
  26.7 1.2 %collective-permute-done.10.rest_1_ = bf16[2,2048]{1,0:T(2,128)(2,1)S(1)} collective-permute-done((bf16[2,2048]{1,0:T(2,128)(2,1)S(1)}, bf16[2,2048]{1,0:T(2,128)(2,1)S(1)}, u32[]{:S(2)}, u32[]{:S(2)}) %collective-permute-start.10) | collective-permute-done | bytes 8224 | tf_op jit(solution)/shard_map/ppermute | solution.py:505
  28.0 0.0 collective-permute-done.9.rest_0_
  28.0 0.7 %finish.1 = bf16[5,2048]{1,0:T(8,128)(2,1)} custom-call(f32[3,2048]{1,0:T(4,128)S(1)} %combine_resident.1.kept_ref, s32[8,128]{1,0:T(8,128)S(1)} %get-tuple-element.43.place_ref, bf16[2,2048]{1,0:T(2,128)(2,1)S(1)} %collective-permute-done.9.rest_0_, bf16[2,2048]{1,0:T(2,128)(2,1)S(1)} %collective-permute-done.10.rest_1_, ...), custom_call_target="tpu_custom_call" | custom-call | tf_op jit(solution)/shard_map/finish/pallas_call | solution.py:494
Async XLA Ops:
  4.1 5.5 %collective-permute-start = (bf16[5,2560]{1,0:T(8,128)(2,1)}, bf16[5,2560]{1,0:T(8,128)(2,1)S(1)}, u32[]{:S(2)}, u32[]{:S(2)}) collective-permute-start(bf16[5,2560]{1,0:T(8,128)(2,1)} %get-tuple-element.25.ask_ref), channel_id=1, source_target_pairs={{0,4},{4,0},{8,12},{12,8},{1,5},{5,1},{9,13},{13,9},{2,6},{6,2},{1... | collective-permute-start | bytes 76808 | tf_op jit(solution)/shard_map/ppermute | solution.py:505
  4.6 15.8 %collective-permute-start.6 = (bf16[136,512]{1,0:T(8,128)(2,1)}, bf16[136,512]{1,0:T(8,128)(2,1)S(1)}, u32[]{:S(2)}, u32[]{:S(2)}) collective-permute-start(bf16[136,512]{1,0:T(8,128)(2,1)} %get-tuple-element.40), channel_id=1, source_target_pairs={{0,2},{1,3},{2,0},{3,1},{4,6},{5,7},{6,4},{7,5},{8,10},{9,11},{10,... | collective-permute-start | bytes 417800 | tf_op jit(solution)/shard_map/ppermute | solution.py:505
  8.3 13.9 %collective-permute-start.7 = (bf16[136,512]{1,0:T(8,128)(2,1)}, bf16[136,512]{1,0:T(8,128)(2,1)S(1)}, u32[]{:S(2)}, u32[]{:S(2)}) collective-permute-start(bf16[136,512]{1,0:T(8,128)(2,1)} %get-tuple-element.41), channel_id=1, source_target_pairs={{0,3},{1,2},{2,1},{3,0},{4,7},{5,6},{6,5},{7,4},{8,11},{9,10},{10,... | collective-permute-start | bytes 417800 | tf_op jit(solution)/shard_map/ppermute | solution.py:505
  9.6 12.5 %collective-permute-start.8 = (bf16[136,512]{1,0:T(8,128)(2,1)}, bf16[136,512]{1,0:T(8,128)(2,1)S(1)}, u32[]{:S(2)}, u32[]{:S(2)}) collective-permute-start(bf16[136,512]{1,0:T(8,128)(2,1)} %get-tuple-element.42), channel_id=1, source_target_pairs={{0,1},{1,0},{2,3},{3,2},{4,5},{5,4},{6,7},{7,6},{8,9},{9,8},{10,11... | collective-permute-start | bytes 417800 | tf_op jit(solution)/shard_map/ppermute | solution.py:505
  9.9 8.7 %collective-permute-start.2 = (bf16[5,2560]{1,0:T(8,128)(2,1)}, bf16[5,2560]{1,0:T(8,128)(2,1)S(1)}, u32[]{:S(2)}, u32[]{:S(2)}) collective-permute-start(bf16[5,2560]{1,0:T(8,128)(2,1)} %get-tuple-element.25.ask_ref), channel_id=1, source_target_pairs={{0,12},{4,8},{8,4},{12,0},{1,13},{5,9},{9,5},{13,1},{2,14},{6,10},... | collective-permute-start | bytes 76808 | tf_op jit(solution)/shard_map/ppermute | solution.py:505
  10.8 7.7 %collective-permute-start.1 = (bf16[5,2560]{1,0:T(8,128)(2,1)}, bf16[5,2560]{1,0:T(8,128)(2,1)S(1)}, u32[]{:S(2)}, u32[]{:S(2)}) collective-permute-start(bf16[5,2560]{1,0:T(8,128)(2,1)} %get-tuple-element.25.ask_ref), channel_id=1, source_target_pairs={{0,8},{4,12},{8,0},{12,4},{1,9},{5,13},{9,1},{13,5},{2,10},{6,14},... | collective-permute-start | bytes 76808 | tf_op jit(solution)/shard_map/ppermute | solution.py:505
  11.4 10.8 %copy-start = (bf16[136,512]{1,0:T(8,128)(2,1)S(1)}, bf16[136,512]{1,0:T(8,128)(2,1)}, u32[]{:S(2)}) copy-start(bf16[136,512]{1,0:T(8,128)(2,1)} %get-tuple-element.39.rest_3_) | copy-start | bytes 417796
  11.4 10.8 %copy-start.1 = (f32[128,128]{1,0:T(8,128)S(1)}, f32[128,128]{1,0:T(8,128)}, u32[]{:S(2)}) copy-start(f32[128,128]{1,0:T(8,128)} %constant.5.clone.sin_ref) | copy-start | bytes 196612
  11.4 10.8 %copy-start.2 = (f32[128,128]{1,0:T(8,128)S(1)}, f32[128,128]{1,0:T(8,128)}, u32[]{:S(2)}) copy-start(f32[128,128]{1,0:T(8,128)} %constant.4.clone.cos_ref) | copy-start | bytes 196612
  11.4 10.8 %copy-start.5 = (s32[4,2]{0,1:T(2,128)S(1)}, s32[4,2]{0,1:T(2,128)}, u32[]{:S(2)}) copy-start(s32[4,2]{0,1:T(2,128)} %param.14) | copy-start | bytes 100
  11.4 10.8 %copy-start.6 = (s32[4,2]{0,1:T(2,128)S(1)}, s32[4,2]{0,1:T(2,128)}, u32[]{:S(2)}) copy-start(s32[4,2]{0,1:T(2,128)} %param.15) | copy-start | bytes 100
  11.4 10.8 %copy-start.7 = (bf16[128]{0:T(256)(128)(2,1)S(1)}, bf16[128]{0:T(256)(128)(2,1)}, u32[]{:S(2)}) copy-start(bf16[128]{0:T(256)(128)(2,1)} %param.18) | copy-start | bytes 772
  11.4 14.1 %copy-start.3 = (bf16[5,2560]{1,0:T(8,128)(2,1)S(1)}, bf16[5,2560]{1,0:T(8,128)(2,1)}, u32[]{:S(2)}) copy-start(bf16[5,2560]{1,0:T(8,128)(2,1)} %get-tuple-element.25.ask_ref) | copy-start | bytes 76804
  18.6 6.6 %collective-permute-start.3 = (bf16[64,128]{1,0:T(8,128)(2,1)}, bf16[64,128]{1,0:T(8,128)(2,1)S(1)}, u32[]{:S(2)}, u32[]{:S(2)}) collective-permute-start(bf16[64,128]{1,0:T(8,128)(2,1)} %get-tuple-element.33), channel_id=1, source_target_pairs={{0,1},{1,0},{2,3},{3,2},{4,5},{5,4},{6,7},{7,6},{8,9},{9,8},{10,11... | collective-permute-start | bytes 49160 | tf_op jit(solution)/shard_map/ppermute | solution.py:505
  19.2 6.3 %collective-permute-start.4 = (bf16[64,128]{1,0:T(8,128)(2,1)}, bf16[64,128]{1,0:T(8,128)(2,1)S(1)}, u32[]{:S(2)}, u32[]{:S(2)}) collective-permute-start(bf16[64,128]{1,0:T(8,128)(2,1)} %get-tuple-element.34), channel_id=1, source_target_pairs={{0,3},{1,2},{2,1},{3,0},{4,7},{5,6},{6,5},{7,4},{8,11},{9,10},{10,... | collective-permute-start | bytes 49160 | tf_op jit(solution)/shard_map/ppermute | solution.py:505
  20.4 5.0 %collective-permute-start.5 = (bf16[64,128]{1,0:T(8,128)(2,1)}, bf16[64,128]{1,0:T(8,128)(2,1)S(1)}, u32[]{:S(2)}, u32[]{:S(2)}) collective-permute-start(bf16[64,128]{1,0:T(8,128)(2,1)} %get-tuple-element.35), channel_id=1, source_target_pairs={{0,2},{1,3},{2,0},{3,1},{4,6},{5,7},{6,4},{7,5},{8,10},{9,11},{10,... | collective-permute-start | bytes 49160 | tf_op jit(solution)/shard_map/ppermute | solution.py:505
  23.5 3.2 %collective-permute-start.11 = (bf16[2,2048]{1,0:T(2,128)(2,1)S(1)}, bf16[2,2048]{1,0:T(2,128)(2,1)S(1)}, u32[]{:S(2)}, u32[]{:S(2)}) collective-permute-start(bf16[2,2048]{1,0:T(2,128)(2,1)S(1)} %get-tuple-element.44), channel_id=1, source_target_pairs={{0,12},{4,8},{8,4},{12,0},{1,13},{5,9},{9,5},{13,1},{2,14},{6,10},... | collective-permute-start | bytes 24584 | tf_op jit(solution)/shard_map/ppermute | solution.py:505
  24.3 3.7 %collective-permute-start.10 = (bf16[2,2048]{1,0:T(2,128)(2,1)S(1)}, bf16[2,2048]{1,0:T(2,128)(2,1)S(1)}, u32[]{:S(2)}, u32[]{:S(2)}) collective-permute-start(bf16[2,2048]{1,0:T(2,128)(2,1)S(1)} %get-tuple-element.44), channel_id=1, source_target_pairs={{0,8},{4,12},{8,0},{12,4},{1,9},{5,13},{9,1},{13,5},{2,10},{6,14},... | collective-permute-start | bytes 24584 | tf_op jit(solution)/shard_map/ppermute | solution.py:505
  25.2 2.8 %collective-permute-start.9 = (bf16[2,2048]{1,0:T(2,128)(2,1)S(1)}, bf16[2,2048]{1,0:T(2,128)(2,1)S(1)}, u32[]{:S(2)}, u32[]{:S(2)}) collective-permute-start(bf16[2,2048]{1,0:T(2,128)(2,1)S(1)} %get-tuple-element.44), channel_id=1, source_target_pairs={{0,4},{4,0},{8,12},{12,8},{1,5},{5,1},{9,13},{13,9},{2,6},{6,2},{1... | collective-permute-start | bytes 24584 | tf_op jit(solution)/shard_map/ppermute | solution.py:505
  25.5 0.7 %copy-start.4 = (bf16[64,128]{1,0:T(8,128)(2,1)S(1)}, bf16[64,128]{1,0:T(8,128)(2,1)}, u32[]{:S(2)}) copy-start(bf16[64,128]{1,0:T(8,128)(2,1)} %get-tuple-element.32.rest_0_) | copy-start | bytes 49156

commit v19 on v17

--- a/solution.py
+++ b/solution.py
@@ -44,7 +44,7 @@
 
 def project_kernel(ranks, group, gain_hbm, x_hbm, w_hbm, q_hbm, own_hbm, *rest):
     outs, ask_ref = rest[:ranks], rest[ranks]
-    gain_ref, x_ref, w_ref, acc_ref, in_sems, w_sems = rest[ranks + 1 :]
+    gain_ref, x_ref, rows_ref, w_ref, acc_ref, in_sems, w_sems = rest[ranks + 1 :]
     slots, requests, feats = x_ref.shape
     rows = slots * requests
     piece = outs[0].shape[1] // 2
@@ -86,12 +86,14 @@
         copy.start()
     gain_copy.wait()
     x_copy.wait()
+    for slot in range(slots):
+        rows_ref[slot * requests : (slot + 1) * requests, :] = x_ref[slot].astype(F32)
     squares = jnp.zeros((rows, 128), F32)
     for i, (low, high) in enumerate(chunks):
         parts = []
         for c in range(low, high, 128):
             width = min(128, high - c)
-            x = x_ref[:, :, c : c + width].astype(F32).reshape(rows, width)
+            x = rows_ref[:, c : c + width]
             gain = gain_ref[c : c + width].astype(F32).reshape(1, width)
             parts.append((x * gain).astype(BF16))
             x = x * x
@@ -137,6 +139,7 @@
         scratch_shapes=[
             pltpu.VMEM((feats,), BF16),
             pltpu.VMEM((slots, requests, feats), BF16),
+            pltpu.VMEM((rows, feats), F32),
             pltpu.VMEM(weight.shape, BF16),
             pltpu.VMEM((rows, weight.shape[1]), F32),
             pltpu.SemaphoreType.DMA((5,)),

time: 28.9 us -> 28.7 us (level)
  no operation moved by 1% of the time
where the time goes in v19:
time: 28.7 us; the launch traced here: 28.5 us
  Pallas kernels  13.3 us (46%)
  starting transfers between devices  12.8 us (45%)
  waiting for transfers between devices  1.55 us (5%)
  local copies, waits for them, and re-layouts  0.74 us (3%)
    ppermute x12, starting transfers between devices, swapped(): return lax.ppermute(x, axis, [(i, i ^ j) for i in range(n)])  12.8 us
    pallas_call x1, Pallas kernels, attend_resident(): pl.pallas_call(functools.partial(resident_kernel, ranks), in_specs=[SMEM,...  7.13 us
    pallas_call x1, Pallas kernels, project(): pl.pallas_call(functools.partial(project_kernel, ranks, group), in_specs=...  3.99 us
    ppermute x12, waiting for transfers between devices, swapped(): return lax.ppermute(x, axis, [(i, i ^ j) for i in range(n)])  1.55 us
    pallas_call x1, Pallas kernels, attend_moved(): pl.pallas_call(functools.partial(moved_kernel, insts, len(pieces), reside...  1.32 us
    unnamed x16, local copies, waits for them, and re-layouts  0.74 us
    pallas_call x1, Pallas kernels, finish(): pl.pallas_call(finish_kernel, in_specs=[VMEM] * (2 + len(moved)), out_spe...  0.67 us
  transfers between devices with their start and end apart: 12, of which 2 were waited for; matrix products, arithmetic and copies ran while one was open for 0% of the time, Pallas kernels for 30%

profile of v19, /device:TPU:0, one launch (start us, length us, event | category | flops | bytes accessed | tf_op | source)
XLA Modules:
  0.0 28.5 jit_solution(16129933271387606706)
XLA Ops:
  0.0 4.0 %project.1 = (bf16[136,512]{1,0:T(8,128)(2,1)}, bf16[136,512]{1,0:T(8,128)(2,1)}, bf16[136,512]{1,0:T(8,128)(2,1)}, bf16[136,512]{1,0:T(8,128)(2,1)}, bf16[5,2560]{1,0:T(8,128)(2,1)}) custom-call(bf16[1280]{0:T(1024)(128)(2,1)} %gain_hbm.1, bf16[64,2,1280]{2,1,0:T(2,128)(2,1)} %bitcast.19, bf16[1280,2048]{1,0:T(8,128)(2,1)} %w_hbm.1, ...), custom_call_target="tpu_custom_call" | custom-call | flops 671088640 | bytes 5242880 | tf_op jit(solution)/shard_map/project/pallas_call | solution.py:133
  4.0 0.5 %collective-permute-start = (bf16[5,2560]{1,0:T(8,128)(2,1)}, bf16[5,2560]{1,0:T(8,128)(2,1)S(1)}, u32[]{:S(2)}, u32[]{:S(2)}) collective-permute-start(bf16[5,2560]{1,0:T(8,128)(2,1)} %get-tuple-element.25.ask_ref), channel_id=1, source_target_pairs={{0,4},{4,0},{8,12},{12,8},{1,5},{5,1},{9,13},{13,9},{2,6},{6,2},{1... | collective-permute-start | bytes 76808 | tf_op jit(solution)/shard_map/ppermute | solution.py:504
  4.5 3.7 %collective-permute-start.6 = (bf16[136,512]{1,0:T(8,128)(2,1)}, bf16[136,512]{1,0:T(8,128)(2,1)S(1)}, u32[]{:S(2)}, u32[]{:S(2)}) collective-permute-start(bf16[136,512]{1,0:T(8,128)(2,1)} %get-tuple-element.40), channel_id=1, source_target_pairs={{0,2},{1,3},{2,0},{3,1},{4,6},{5,7},{6,4},{7,5},{8,10},{9,11},{10,... | collective-permute-start | bytes 417800 | tf_op jit(solution)/shard_map/ppermute | solution.py:504
  8.2 1.3 %collective-permute-start.7 = (bf16[136,512]{1,0:T(8,128)(2,1)}, bf16[136,512]{1,0:T(8,128)(2,1)S(1)}, u32[]{:S(2)}, u32[]{:S(2)}) collective-permute-start(bf16[136,512]{1,0:T(8,128)(2,1)} %get-tuple-element.41), channel_id=1, source_target_pairs={{0,3},{1,2},{2,1},{3,0},{4,7},{5,6},{6,5},{7,4},{8,11},{9,10},{10,... | collective-permute-start | bytes 417800 | tf_op jit(solution)/shard_map/ppermute | solution.py:504
  9.5 0.0 collective-permute-done.rest_0_
  9.5 0.2 collective-permute-start.8
  9.8 1.0 %collective-permute-start.2 = (bf16[5,2560]{1,0:T(8,128)(2,1)}, bf16[5,2560]{1,0:T(8,128)(2,1)S(1)}, u32[]{:S(2)}, u32[]{:S(2)}) collective-permute-start(bf16[5,2560]{1,0:T(8,128)(2,1)} %get-tuple-element.25.ask_ref), channel_id=1, source_target_pairs={{0,12},{4,8},{8,4},{12,0},{1,13},{5,9},{9,5},{13,1},{2,14},{6,10},... | collective-permute-start | bytes 76808 | tf_op jit(solution)/shard_map/ppermute | solution.py:504
  10.7 0.5 %collective-permute-start.1 = (bf16[5,2560]{1,0:T(8,128)(2,1)}, bf16[5,2560]{1,0:T(8,128)(2,1)S(1)}, u32[]{:S(2)}, u32[]{:S(2)}) collective-permute-start(bf16[5,2560]{1,0:T(8,128)(2,1)} %get-tuple-element.25.ask_ref), channel_id=1, source_target_pairs={{0,8},{4,12},{8,0},{12,4},{1,9},{5,13},{9,1},{13,5},{2,10},{6,14},... | collective-permute-start | bytes 76808 | tf_op jit(solution)/shard_map/ppermute | solution.py:504
  11.3 0.0 copy-start
  11.3 0.0 copy-start.1
  11.3 0.0 copy-start.2
  11.3 0.0 copy-start.5
  11.3 0.0 copy-start.6
  11.3 0.0 copy-start.7
  11.3 0.0 copy-start.3
  11.3 7.1 %attend_resident.1 = (bf16[64,128]{1,0:T(8,128)(2,1)}, bf16[64,128]{1,0:T(8,128)(2,1)}, bf16[64,128]{1,0:T(8,128)(2,1)}, bf16[64,128]{1,0:T(8,128)(2,1)}) custom-call(s32[1,3]{1,0:T(1,128)} %len_ref.1, bf16[64,5,128]{2,1,0:T(8,128)(2,1)} %bitcast.18, bf16[3,1024,1024]{2,1,0:T(8,128)(2,1)} %bitcast.15, bf16[3,1024,1024]{2,1,0:T(8,128)(2,1)} %bitcast.16), custom_call_target="tpu_custom_call" | custom-call | flops 100663296 | bytes 12582912 | tf_op jit(solution)/shard_map/attend_resident/pallas_call | solution.py:259
  18.5 0.0 collective-permute-done.2.rest_2_
  18.5 0.0 collective-permute-done.1.rest_1_
  18.5 0.6 %collective-permute-start.3 = (bf16[64,128]{1,0:T(8,128)(2,1)}, bf16[64,128]{1,0:T(8,128)(2,1)S(1)}, u32[]{:S(2)}, u32[]{:S(2)}) collective-permute-start(bf16[64,128]{1,0:T(8,128)(2,1)} %get-tuple-element.33), channel_id=1, source_target_pairs={{0,1},{1,0},{2,3},{3,2},{4,5},{5,4},{6,7},{7,6},{8,9},{9,8},{10,11... | collective-permute-start | bytes 49160 | tf_op jit(solution)/shard_map/ppermute | solution.py:504
  19.1 1.2 %collective-permute-start.4 = (bf16[64,128]{1,0:T(8,128)(2,1)}, bf16[64,128]{1,0:T(8,128)(2,1)S(1)}, u32[]{:S(2)}, u32[]{:S(2)}) collective-permute-start(bf16[64,128]{1,0:T(8,128)(2,1)} %get-tuple-element.34), channel_id=1, source_target_pairs={{0,3},{1,2},{2,1},{3,0},{4,7},{5,6},{6,5},{7,4},{8,11},{9,10},{10,... | collective-permute-start | bytes 49160 | tf_op jit(solution)/shard_map/ppermute | solution.py:504
  20.3 0.0 collective-permute-done.6.rest_4_
  20.3 1.7 %collective-permute-start.5 = (bf16[64,128]{1,0:T(8,128)(2,1)}, bf16[64,128]{1,0:T(8,128)(2,1)S(1)}, u32[]{:S(2)}, u32[]{:S(2)}) collective-permute-start(bf16[64,128]{1,0:T(8,128)(2,1)} %get-tuple-element.35), channel_id=1, source_target_pairs={{0,2},{1,3},{2,0},{3,1},{4,6},{5,7},{6,4},{7,5},{8,10},{9,11},{10,... | collective-permute-start | bytes 49160 | tf_op jit(solution)/shard_map/ppermute | solution.py:504
  22.1 0.0 collective-permute-done.7.rest_5_
  22.1 0.0 collective-permute-done.8.rest_6_
  22.1 0.0 copy-done
  22.1 0.0 copy-done.1
  22.1 0.0 copy-done.2
  22.1 0.0 copy-done.5
  22.1 0.0 copy-done.6
  22.1 0.0 copy-done.7
  22.1 1.3 %attend_moved.1 = (bf16[2,2048]{1,0:T(2,128)(2,1)S(1)}, s32[8,128]{1,0:T(8,128)S(1)}) custom-call(s32[2,4]{1,0:T(2,128)S(1)} %bitcast.12, s32[2,4]{1,0:T(2,128)S(1)} %bitcast.13, bf16[1,128]{1,0:T(2,128)(2,1)S(1)} %bitcast.14, f32[128,128]{1,0:T(8,128)S(1)} %copy-done.2, f32[128,128]{1,0:T(8,128)S(1)} %copy-done.1, ...), custom_call_target="tpu_custom_call" | custom-call | tf_op jit(solution)/shard_map/attend_moved/pallas_call | solution.py:410
  23.4 0.7 %collective-permute-start.11 = (bf16[2,2048]{1,0:T(2,128)(2,1)S(1)}, bf16[2,2048]{1,0:T(2,128)(2,1)S(1)}, u32[]{:S(2)}, u32[]{:S(2)}) collective-permute-start(bf16[2,2048]{1,0:T(2,128)(2,1)S(1)} %get-tuple-element.44), channel_id=1, source_target_pairs={{0,12},{4,8},{8,4},{12,0},{1,13},{5,9},{9,5},{13,1},{2,14},{6,10},... | collective-permute-start | bytes 24584 | tf_op jit(solution)/shard_map/ppermute | solution.py:504
  24.1 1.0 %collective-permute-start.10 = (bf16[2,2048]{1,0:T(2,128)(2,1)S(1)}, bf16[2,2048]{1,0:T(2,128)(2,1)S(1)}, u32[]{:S(2)}, u32[]{:S(2)}) collective-permute-start(bf16[2,2048]{1,0:T(2,128)(2,1)S(1)} %get-tuple-element.44), channel_id=1, source_target_pairs={{0,8},{4,12},{8,0},{12,4},{1,9},{5,13},{9,1},{13,5},{2,10},{6,14},... | collective-permute-start | bytes 24584 | tf_op jit(solution)/shard_map/ppermute | solution.py:504
  25.1 0.0 collective-permute-done.3.rest_1_
  25.1 0.3 %collective-permute-start.9 = (bf16[2,2048]{1,0:T(2,128)(2,1)S(1)}, bf16[2,2048]{1,0:T(2,128)(2,1)S(1)}, u32[]{:S(2)}, u32[]{:S(2)}) collective-permute-start(bf16[2,2048]{1,0:T(2,128)(2,1)S(1)} %get-tuple-element.44), channel_id=1, source_target_pairs={{0,4},{4,0},{8,12},{12,8},{1,5},{5,1},{9,13},{13,9},{2,6},{6,2},{1... | collective-permute-start | bytes 24584 | tf_op jit(solution)/shard_map/ppermute | solution.py:504
  25.4 0.0 collective-permute-done.4.rest_2_
  25.4 0.0 collective-permute-done.5.rest_3_
  25.4 0.0 copy-done.3
  25.4 0.0 copy-start.4
  25.4 0.7 %copy-done.4 = bf16[64,128]{1,0:T(8,128)(2,1)S(1)} copy-done((bf16[64,128]{1,0:T(8,128)(2,1)S(1)}, bf16[64,128]{1,0:T(8,128)(2,1)}, u32[]{:S(2)}) %copy-start.4) | copy-done | bytes 16408
  26.1 0.2 combine_resident.1.kept_ref
  26.3 0.4 %collective-permute-done.11.rest_2_ = bf16[2,2048]{1,0:T(2,128)(2,1)S(1)} collective-permute-done((bf16[2,2048]{1,0:T(2,128)(2,1)S(1)}, bf16[2,2048]{1,0:T(2,128)(2,1)S(1)}, u32[]{:S(2)}, u32[]{:S(2)}) %collective-permute-start.11) | collective-permute-done | bytes 8224 | tf_op jit(solution)/shard_map/ppermute | solution.py:504
  26.6 1.2 %collective-permute-done.10.rest_1_ = bf16[2,2048]{1,0:T(2,128)(2,1)S(1)} collective-permute-done((bf16[2,2048]{1,0:T(2,128)(2,1)S(1)}, bf16[2,2048]{1,0:T(2,128)(2,1)S(1)}, u32[]{:S(2)}, u32[]{:S(2)}) %collective-permute-start.10) | collective-permute-done | bytes 8224 | tf_op jit(solution)/shard_map/ppermute | solution.py:504
  27.8 0.0 collective-permute-done.9.rest_0_
  27.8 0.7 %finish.1 = bf16[5,2048]{1,0:T(8,128)(2,1)} custom-call(f32[3,2048]{1,0:T(4,128)S(1)} %combine_resident.1.kept_ref, s32[8,128]{1,0:T(8,128)S(1)} %get-tuple-element.43.place_ref, bf16[2,2048]{1,0:T(2,128)(2,1)S(1)} %collective-permute-done.9.rest_0_, bf16[2,2048]{1,0:T(2,128)(2,1)S(1)} %collective-permute-done.10.rest_1_, ...), custom_call_target="tpu_custom_call" | custom-call | tf_op jit(solution)/shard_map/finish/pallas_call | solution.py:493
Async XLA Ops:
  4.0 5.5 %collective-permute-start = (bf16[5,2560]{1,0:T(8,128)(2,1)}, bf16[5,2560]{1,0:T(8,128)(2,1)S(1)}, u32[]{:S(2)}, u32[]{:S(2)}) collective-permute-start(bf16[5,2560]{1,0:T(8,128)(2,1)} %get-tuple-element.25.ask_ref), channel_id=1, source_target_pairs={{0,4},{4,0},{8,12},{12,8},{1,5},{5,1},{9,13},{13,9},{2,6},{6,2},{1... | collective-permute-start | bytes 76808 | tf_op jit(solution)/shard_map/ppermute | solution.py:504
  4.5 15.8 %collective-permute-start.6 = (bf16[136,512]{1,0:T(8,128)(2,1)}, bf16[136,512]{1,0:T(8,128)(2,1)S(1)}, u32[]{:S(2)}, u32[]{:S(2)}) collective-permute-start(bf16[136,512]{1,0:T(8,128)(2,1)} %get-tuple-element.40), channel_id=1, source_target_pairs={{0,2},{1,3},{2,0},{3,1},{4,6},{5,7},{6,4},{7,5},{8,10},{9,11},{10,... | collective-permute-start | bytes 417800 | tf_op jit(solution)/shard_map/ppermute | solution.py:504
  8.2 13.9 %collective-permute-start.7 = (bf16[136,512]{1,0:T(8,128)(2,1)}, bf16[136,512]{1,0:T(8,128)(2,1)S(1)}, u32[]{:S(2)}, u32[]{:S(2)}) collective-permute-start(bf16[136,512]{1,0:T(8,128)(2,1)} %get-tuple-element.41), channel_id=1, source_target_pairs={{0,3},{1,2},{2,1},{3,0},{4,7},{5,6},{6,5},{7,4},{8,11},{9,10},{10,... | collective-permute-start | bytes 417800 | tf_op jit(solution)/shard_map/ppermute | solution.py:504
  9.5 12.5 %collective-permute-start.8 = (bf16[136,512]{1,0:T(8,128)(2,1)}, bf16[136,512]{1,0:T(8,128)(2,1)S(1)}, u32[]{:S(2)}, u32[]{:S(2)}) collective-permute-start(bf16[136,512]{1,0:T(8,128)(2,1)} %get-tuple-element.42), channel_id=1, source_target_pairs={{0,1},{1,0},{2,3},{3,2},{4,5},{5,4},{6,7},{7,6},{8,9},{9,8},{10,11... | collective-permute-start | bytes 417800 | tf_op jit(solution)/shard_map/ppermute | solution.py:504
  9.8 8.7 %collective-permute-start.2 = (bf16[5,2560]{1,0:T(8,128)(2,1)}, bf16[5,2560]{1,0:T(8,128)(2,1)S(1)}, u32[]{:S(2)}, u32[]{:S(2)}) collective-permute-start(bf16[5,2560]{1,0:T(8,128)(2,1)} %get-tuple-element.25.ask_ref), channel_id=1, source_target_pairs={{0,12},{4,8},{8,4},{12,0},{1,13},{5,9},{9,5},{13,1},{2,14},{6,10},... | collective-permute-start | bytes 76808 | tf_op jit(solution)/shard_map/ppermute | solution.py:504
  10.7 7.7 %collective-permute-start.1 = (bf16[5,2560]{1,0:T(8,128)(2,1)}, bf16[5,2560]{1,0:T(8,128)(2,1)S(1)}, u32[]{:S(2)}, u32[]{:S(2)}) collective-permute-start(bf16[5,2560]{1,0:T(8,128)(2,1)} %get-tuple-element.25.ask_ref), channel_id=1, source_target_pairs={{0,8},{4,12},{8,0},{12,4},{1,9},{5,13},{9,1},{13,5},{2,10},{6,14},... | collective-permute-start | bytes 76808 | tf_op jit(solution)/shard_map/ppermute | solution.py:504
  11.3 10.8 %copy-start = (bf16[136,512]{1,0:T(8,128)(2,1)S(1)}, bf16[136,512]{1,0:T(8,128)(2,1)}, u32[]{:S(2)}) copy-start(bf16[136,512]{1,0:T(8,128)(2,1)} %get-tuple-element.39.rest_3_) | copy-start | bytes 417796
  11.3 10.8 %copy-start.1 = (f32[128,128]{1,0:T(8,128)S(1)}, f32[128,128]{1,0:T(8,128)}, u32[]{:S(2)}) copy-start(f32[128,128]{1,0:T(8,128)} %constant.5.clone.sin_ref) | copy-start | bytes 196612
  11.3 10.8 %copy-start.2 = (f32[128,128]{1,0:T(8,128)S(1)}, f32[128,128]{1,0:T(8,128)}, u32[]{:S(2)}) copy-start(f32[128,128]{1,0:T(8,128)} %constant.4.clone.cos_ref) | copy-start | bytes 196612
  11.3 10.8 %copy-start.5 = (s32[4,2]{0,1:T(2,128)S(1)}, s32[4,2]{0,1:T(2,128)}, u32[]{:S(2)}) copy-start(s32[4,2]{0,1:T(2,128)} %param.14) | copy-start | bytes 100
  11.3 10.8 %copy-start.6 = (s32[4,2]{0,1:T(2,128)S(1)}, s32[4,2]{0,1:T(2,128)}, u32[]{:S(2)}) copy-start(s32[4,2]{0,1:T(2,128)} %param.15) | copy-start | bytes 100
  11.3 10.8 %copy-start.7 = (bf16[128]{0:T(256)(128)(2,1)S(1)}, bf16[128]{0:T(256)(128)(2,1)}, u32[]{:S(2)}) copy-start(bf16[128]{0:T(256)(128)(2,1)} %param.18) | copy-start | bytes 772
  11.3 14.1 %copy-start.3 = (bf16[5,2560]{1,0:T(8,128)(2,1)S(1)}, bf16[5,2560]{1,0:T(8,128)(2,1)}, u32[]{:S(2)}) copy-start(bf16[5,2560]{1,0:T(8,128)(2,1)} %get-tuple-element.25.ask_ref) | copy-start | bytes 76804
  18.5 6.6 %collective-permute-start.3 = (bf16[64,128]{1,0:T(8,128)(2,1)}, bf16[64,128]{1,0:T(8,128)(2,1)S(1)}, u32[]{:S(2)}, u32[]{:S(2)}) collective-permute-start(bf16[64,128]{1,0:T(8,128)(2,1)} %get-tuple-element.33), channel_id=1, source_target_pairs={{0,1},{1,0},{2,3},{3,2},{4,5},{5,4},{6,7},{7,6},{8,9},{9,8},{10,11... | collective-permute-start | bytes 49160 | tf_op jit(solution)/shard_map/ppermute | solution.py:504
  19.1 6.3 %collective-permute-start.4 = (bf16[64,128]{1,0:T(8,128)(2,1)}, bf16[64,128]{1,0:T(8,128)(2,1)S(1)}, u32[]{:S(2)}, u32[]{:S(2)}) collective-permute-start(bf16[64,128]{1,0:T(8,128)(2,1)} %get-tuple-element.34), channel_id=1, source_target_pairs={{0,3},{1,2},{2,1},{3,0},{4,7},{5,6},{6,5},{7,4},{8,11},{9,10},{10,... | collective-permute-start | bytes 49160 | tf_op jit(solution)/shard_map/ppermute | solution.py:504
  20.3 5.0 %collective-permute-start.5 = (bf16[64,128]{1,0:T(8,128)(2,1)}, bf16[64,128]{1,0:T(8,128)(2,1)S(1)}, u32[]{:S(2)}, u32[]{:S(2)}) collective-permute-start(bf16[64,128]{1,0:T(8,128)(2,1)} %get-tuple-element.35), channel_id=1, source_target_pairs={{0,2},{1,3},{2,0},{3,1},{4,6},{5,7},{6,4},{7,5},{8,10},{9,11},{10,... | collective-permute-start | bytes 49160 | tf_op jit(solution)/shard_map/ppermute | solution.py:504
  23.4 3.2 %collective-permute-start.11 = (bf16[2,2048]{1,0:T(2,128)(2,1)S(1)}, bf16[2,2048]{1,0:T(2,128)(2,1)S(1)}, u32[]{:S(2)}, u32[]{:S(2)}) collective-permute-start(bf16[2,2048]{1,0:T(2,128)(2,1)S(1)} %get-tuple-element.44), channel_id=1, source_target_pairs={{0,12},{4,8},{8,4},{12,0},{1,13},{5,9},{9,5},{13,1},{2,14},{6,10},... | collective-permute-start | bytes 24584 | tf_op jit(solution)/shard_map/ppermute | solution.py:504
  24.1 3.7 %collective-permute-start.10 = (bf16[2,2048]{1,0:T(2,128)(2,1)S(1)}, bf16[2,2048]{1,0:T(2,128)(2,1)S(1)}, u32[]{:S(2)}, u32[]{:S(2)}) collective-permute-start(bf16[2,2048]{1,0:T(2,128)(2,1)S(1)} %get-tuple-element.44), channel_id=1, source_target_pairs={{0,8},{4,12},{8,0},{12,4},{1,9},{5,13},{9,1},{13,5},{2,10},{6,14},... | collective-permute-start | bytes 24584 | tf_op jit(solution)/shard_map/ppermute | solution.py:504
  25.1 2.7 %collective-permute-start.9 = (bf16[2,2048]{1,0:T(2,128)(2,1)S(1)}, bf16[2,2048]{1,0:T(2,128)(2,1)S(1)}, u32[]{:S(2)}, u32[]{:S(2)}) collective-permute-start(bf16[2,2048]{1,0:T(2,128)(2,1)S(1)} %get-tuple-element.44), channel_id=1, source_target_pairs={{0,4},{4,0},{8,12},{12,8},{1,5},{5,1},{9,13},{13,9},{2,6},{6,2},{1... | collective-permute-start | bytes 24584 | tf_op jit(solution)/shard_map/ppermute | solution.py:504
  25.4 0.7 %copy-start.4 = (bf16[64,128]{1,0:T(8,128)(2,1)S(1)}, bf16[64,128]{1,0:T(8,128)(2,1)}, u32[]{:S(2)}) copy-start(bf16[64,128]{1,0:T(8,128)(2,1)} %get-tuple-element.32.rest_0_) | copy-start | bytes 49156

commit v20 on v19

--- a/solution.py
+++ b/solution.py
@@ -14,7 +14,7 @@
 F32 = jnp.float32
 BF16 = jnp.bfloat16
 MIB = 1024 * 1024
-CHUNK = 512
+CHUNK = 256
 
 VMEM = pl.BlockSpec(memory_space=pltpu.VMEM)
 SMEM = pl.BlockSpec(memory_space=pltpu.SMEM)
@@ -25,9 +25,17 @@
     return lax.broadcasted_iota(jnp.int32, shape, dim)
 
 
+def div(x, n):
+    return lax.shift_right_logical(x, n.bit_length() - 1) if n & (n - 1) == 0 else x // n
+
+
+def mod(x, n):
+    return x & (n - 1) if n & (n - 1) == 0 else x % n
+
+
 def column_to_row(column, period):
     n = column.shape[0]
-    spread = jnp.where(iota((n, 128), 0) % period == iota((n, 128), 1), column, 0.0)
+    spread = jnp.where(mod(iota((n, 128), 0), period) == iota((n, 128), 1), column, 0.0)
     return jnp.sum(spread.reshape(n // period, period, 128), axis=1)
 
 
@@ -185,7 +193,7 @@
     top_half = iota((pair_rows, 128), 0) < group
     position = rank * positions + iota((pair_rows, positions), 1)
     scale = F32(1.0) / jnp.sqrt(F32(128.0))
-    diagonal = iota((heads, 128), 0) % heads_mine == iota((heads, 128), 1)
+    diagonal = mod(iota((heads, 128), 0), heads_mine) == iota((heads, 128), 1)
 
     def to_rows(column):
         spread = jnp.where(diagonal, column, 0.0)
@@ -283,7 +291,7 @@
 
 
 def expand(own, rows):
-    which = iota((rows, 128), 0) // (rows // own.shape[0])
+    which = div(iota((rows, 128), 0), rows // own.shape[0])
     out = jnp.broadcast_to(own[0:1], (rows, 128))
     for h in range(1, own.shape[0]):
         out = jnp.where(which == h, own[h : h + 1], out)
@@ -308,7 +316,7 @@
 ):
     asks, rest = rest[: insts - 1], rest[insts - 1 :]
     pieces, rest = rest[:ranks], rest[ranks:]
-    out_ref, place_out, ask_ref, q_ref, own_ref, line_ref = rest
+    out_ref, place_out, q_ref, own_ref, line_ref = rest
     requests = out_ref.shape[0]
     tokens = cos_ref.shape[0]
     piece = pieces[0].shape[1] // 2
@@ -318,8 +326,9 @@
     scale = F32(1.0) / jnp.sqrt(F32(128.0))
     here = lax.axis_index("inst")
 
+    arrived = [ask[...].astype(F32) for ask in asks]
     ask_row = iota(asks[0].shape, 0)
-    row_request = iota((rows, tokens), 0) // heads_mine
+    row_request = div(iota((rows, tokens), 0), heads_mine)
     limit = jnp.zeros((rows, tokens), jnp.int32)
     for r in range(requests):
         dest = dest_ref[r, here]
@@ -328,19 +337,13 @@
         for s in range(insts):
             for c in range(requests):
                 place += jnp.where((dest_ref[c, s] == dest) & (here > s), 1, 0).astype(jnp.int32)
+        line = None
         for b in range(1, insts):
-
-            @pl.when(here ^ b == dest)
-            def _():
-                ask = asks[b - 1][...].astype(F32)
-                ask_ref[r : r + 1, :] = jnp.sum(
-                    jnp.where(ask_row == place, ask, 0.0), axis=0, keepdims=True
-                )
-
+            wanted = jnp.where(here ^ b == dest, place, -1)
+            part = jnp.sum(jnp.where(ask_row == wanted, arrived[b - 1], 0.0), axis=0, keepdims=True)
+            line = part if line is None else line + part
         at = slice(r * heads_mine, (r + 1) * heads_mine)
-        q_ref[at, :], own_ref[0, at, :], own_ref[1, at, :] = heads_of(
-            ask_ref[r : r + 1, :], heads_mine, kv_mine
-        )
+        q_ref[at, :], own_ref[0, at, :], own_ref[1, at, :] = heads_of(line, heads_mine, kv_mine)
     places = jnp.full(place_out.shape, -1, jnp.int32)
     row = iota(place_out.shape, 0)
     place = jnp.int32(residents)
@@ -371,7 +374,7 @@
     gain = gain_ref[...].astype(F32)
     q = q_ref[...]
     q16 = q.astype(BF16)
-    which = iota((rows, tokens), 0) % heads_mine // (heads_mine // kv_mine)
+    which = div(mod(iota((rows, tokens), 0), heads_mine), heads_mine // kv_mine)
     scores = None
     for h in range(kv_mine):
         key = column_block(h * 128)
@@ -382,7 +385,7 @@
         )
         scores = part if scores is None else jnp.where(which == h, part, scores)
     token = iota((rows, tokens), 1)
-    valid = (token % requests == row_request) & (token // requests < limit)
+    valid = (mod(token, requests) == row_request) & (div(token, requests) < limit)
     scores = jnp.where(valid, scores * scale, ABSENT)
     own_score = jnp.sum(q * own_ref[0], axis=1, keepdims=True) * scale
     top = jnp.maximum(jnp.max(scores, axis=1, keepdims=True), own_score)
@@ -416,7 +419,6 @@
             jax.ShapeDtypeStruct((insts * requests, 128), jnp.int32),
         ],
         scratch_shapes=[
-            pltpu.VMEM((requests, asks[0].shape[1]), F32),
             pltpu.VMEM((rows, 128), F32),
             pltpu.VMEM((2, rows, 128), F32),
             pltpu.VMEM((requests, heads_mine * 128), F32),

time: 28.7 us -> 28.6 us (level)
  no operation moved by 1% of the time
where the time goes in v20:
time: 28.6 us; the launch traced here: 28.3 us
  Pallas kernels  13.1 us (46%)
  starting transfers between devices  12.8 us (45%)
  waiting for transfers between devices  1.54 us (5%)
  local copies, waits for them, and re-layouts  0.75 us (3%)
    ppermute x12, starting transfers between devices, swapped(): return lax.ppermute(x, axis, [(i, i ^ j) for i in range(n)])  12.8 us
    pallas_call x1, Pallas kernels, attend_resident(): pl.pallas_call(functools.partial(resident_kernel, ranks), in_specs=[SMEM,...  7.13 us
    pallas_call x1, Pallas kernels, project(): pl.pallas_call(functools.partial(project_kernel, ranks, group), in_specs=...  3.92 us
    ppermute x12, waiting for transfers between devices, swapped(): return lax.ppermute(x, axis, [(i, i ^ j) for i in range(n)])  1.54 us
    pallas_call x1, Pallas kernels, attend_moved(): pl.pallas_call(functools.partial(moved_kernel, insts, len(pieces), reside...  1.27 us
    unnamed x16, local copies, waits for them, and re-layouts  0.75 us
    pallas_call x1, Pallas kernels, finish(): pl.pallas_call(finish_kernel, in_specs=[VMEM] * (2 + len(moved)), out_spe...  0.67 us
  transfers between devices with their start and end apart: 12, of which 2 were waited for; matrix products, arithmetic and copies ran while one was open for 0% of the time, Pallas kernels for 30%

profile of v20, /device:TPU:0, one launch (start us, length us, event | category | flops | bytes accessed | tf_op | source)
XLA Modules:
  0.0 28.3 jit_solution(9892796490780656592)
XLA Ops:
  0.0 3.9 %project.1 = (bf16[136,512]{1,0:T(8,128)(2,1)}, bf16[136,512]{1,0:T(8,128)(2,1)}, bf16[136,512]{1,0:T(8,128)(2,1)}, bf16[136,512]{1,0:T(8,128)(2,1)}, bf16[5,2560]{1,0:T(8,128)(2,1)}) custom-call(bf16[1280]{0:T(1024)(128)(2,1)} %gain_hbm.1, bf16[64,2,1280]{2,1,0:T(2,128)(2,1)} %bitcast.19, bf16[1280,2048]{1,0:T(8,128)(2,1)} %w_hbm.1, ...), custom_call_target="tpu_custom_call" | custom-call | flops 671088640 | bytes 5242880 | tf_op jit(solution)/shard_map/project/pallas_call | solution.py:141
  3.9 0.5 %collective-permute-start = (bf16[5,2560]{1,0:T(8,128)(2,1)}, bf16[5,2560]{1,0:T(8,128)(2,1)S(1)}, u32[]{:S(2)}, u32[]{:S(2)}) collective-permute-start(bf16[5,2560]{1,0:T(8,128)(2,1)} %get-tuple-element.25.ask_ref), channel_id=1, source_target_pairs={{0,4},{4,0},{8,12},{12,8},{1,5},{5,1},{9,13},{13,9},{2,6},{6,2},{1... | collective-permute-start | bytes 76808 | tf_op jit(solution)/shard_map/ppermute | solution.py:506
  4.4 3.7 %collective-permute-start.6 = (bf16[136,512]{1,0:T(8,128)(2,1)}, bf16[136,512]{1,0:T(8,128)(2,1)S(1)}, u32[]{:S(2)}, u32[]{:S(2)}) collective-permute-start(bf16[136,512]{1,0:T(8,128)(2,1)} %get-tuple-element.40), channel_id=1, source_target_pairs={{0,2},{1,3},{2,0},{3,1},{4,6},{5,7},{6,4},{7,5},{8,10},{9,11},{10,... | collective-permute-start | bytes 417800 | tf_op jit(solution)/shard_map/ppermute | solution.py:506
  8.1 1.3 %collective-permute-start.7 = (bf16[136,512]{1,0:T(8,128)(2,1)}, bf16[136,512]{1,0:T(8,128)(2,1)S(1)}, u32[]{:S(2)}, u32[]{:S(2)}) collective-permute-start(bf16[136,512]{1,0:T(8,128)(2,1)} %get-tuple-element.41), channel_id=1, source_target_pairs={{0,3},{1,2},{2,1},{3,0},{4,7},{5,6},{6,5},{7,4},{8,11},{9,10},{10,... | collective-permute-start | bytes 417800 | tf_op jit(solution)/shard_map/ppermute | solution.py:506
  9.5 0.0 collective-permute-done.rest_0_
  9.5 0.2 collective-permute-start.8
  9.7 1.0 %collective-permute-start.2 = (bf16[5,2560]{1,0:T(8,128)(2,1)}, bf16[5,2560]{1,0:T(8,128)(2,1)S(1)}, u32[]{:S(2)}, u32[]{:S(2)}) collective-permute-start(bf16[5,2560]{1,0:T(8,128)(2,1)} %get-tuple-element.25.ask_ref), channel_id=1, source_target_pairs={{0,12},{4,8},{8,4},{12,0},{1,13},{5,9},{9,5},{13,1},{2,14},{6,10},... | collective-permute-start | bytes 76808 | tf_op jit(solution)/shard_map/ppermute | solution.py:506
  10.7 0.6 %collective-permute-start.1 = (bf16[5,2560]{1,0:T(8,128)(2,1)}, bf16[5,2560]{1,0:T(8,128)(2,1)S(1)}, u32[]{:S(2)}, u32[]{:S(2)}) collective-permute-start(bf16[5,2560]{1,0:T(8,128)(2,1)} %get-tuple-element.25.ask_ref), channel_id=1, source_target_pairs={{0,8},{4,12},{8,0},{12,4},{1,9},{5,13},{9,1},{13,5},{2,10},{6,14},... | collective-permute-start | bytes 76808 | tf_op jit(solution)/shard_map/ppermute | solution.py:506
  11.2 0.0 copy-start
  11.2 0.0 copy-start.1
  11.2 0.0 copy-start.2
  11.2 0.0 copy-start.5
  11.2 0.0 copy-start.6
  11.3 0.0 copy-start.7
  11.3 0.0 copy-start.3
  11.3 7.1 %attend_resident.1 = (bf16[64,128]{1,0:T(8,128)(2,1)}, bf16[64,128]{1,0:T(8,128)(2,1)}, bf16[64,128]{1,0:T(8,128)(2,1)}, bf16[64,128]{1,0:T(8,128)(2,1)}) custom-call(s32[1,3]{1,0:T(1,128)} %len_ref.1, bf16[64,5,128]{2,1,0:T(8,128)(2,1)} %bitcast.18, bf16[3,1024,1024]{2,1,0:T(8,128)(2,1)} %bitcast.15, bf16[3,1024,1024]{2,1,0:T(8,128)(2,1)} %bitcast.16), custom_call_target="tpu_custom_call" | custom-call | flops 100663296 | bytes 12582912 | tf_op jit(solution)/shard_map/attend_resident/pallas_call | solution.py:267
  18.4 0.0 collective-permute-done.2.rest_2_
  18.4 0.0 collective-permute-done.1.rest_1_
  18.4 0.6 %collective-permute-start.3 = (bf16[64,128]{1,0:T(8,128)(2,1)}, bf16[64,128]{1,0:T(8,128)(2,1)S(1)}, u32[]{:S(2)}, u32[]{:S(2)}) collective-permute-start(bf16[64,128]{1,0:T(8,128)(2,1)} %get-tuple-element.33), channel_id=1, source_target_pairs={{0,1},{1,0},{2,3},{3,2},{4,5},{5,4},{6,7},{7,6},{8,9},{9,8},{10,11... | collective-permute-start | bytes 49160 | tf_op jit(solution)/shard_map/ppermute | solution.py:506
  19.1 2.5 %collective-permute-start.4 = (bf16[64,128]{1,0:T(8,128)(2,1)}, bf16[64,128]{1,0:T(8,128)(2,1)S(1)}, u32[]{:S(2)}, u32[]{:S(2)}) collective-permute-start(bf16[64,128]{1,0:T(8,128)(2,1)} %get-tuple-element.34), channel_id=1, source_target_pairs={{0,3},{1,2},{2,1},{3,0},{4,7},{5,6},{6,5},{7,4},{8,11},{9,10},{10,... | collective-permute-start | bytes 49160 | tf_op jit(solution)/shard_map/ppermute | solution.py:506
  21.5 0.0 collective-permute-done.6.rest_4_
  21.5 0.5 %collective-permute-start.5 = (bf16[64,128]{1,0:T(8,128)(2,1)}, bf16[64,128]{1,0:T(8,128)(2,1)S(1)}, u32[]{:S(2)}, u32[]{:S(2)}) collective-permute-start(bf16[64,128]{1,0:T(8,128)(2,1)} %get-tuple-element.35), channel_id=1, source_target_pairs={{0,2},{1,3},{2,0},{3,1},{4,6},{5,7},{6,4},{7,5},{8,10},{9,11},{10,... | collective-permute-start | bytes 49160 | tf_op jit(solution)/shard_map/ppermute | solution.py:506
  22.0 0.0 collective-permute-done.7.rest_5_
  22.0 0.0 collective-permute-done.8.rest_6_
  22.0 0.0 copy-done
  22.0 0.0 copy-done.1
  22.0 0.0 copy-done.2
  22.0 0.0 copy-done.5
  22.0 0.0 copy-done.6
  22.0 0.0 copy-done.7
  22.1 1.3 %attend_moved.1 = (bf16[2,2048]{1,0:T(2,128)(2,1)S(1)}, s32[8,128]{1,0:T(8,128)S(1)}) custom-call(s32[2,4]{1,0:T(2,128)S(1)} %bitcast.12, s32[2,4]{1,0:T(2,128)S(1)} %bitcast.13, bf16[1,128]{1,0:T(2,128)(2,1)S(1)} %bitcast.14, f32[128,128]{1,0:T(8,128)S(1)} %copy-done.2, f32[128,128]{1,0:T(8,128)S(1)} %copy-done.1, ...), custom_call_target="tpu_custom_call" | custom-call | tf_op jit(solution)/shard_map/attend_moved/pallas_call | solution.py:413
  23.3 0.6 %collective-permute-start.11 = (bf16[2,2048]{1,0:T(2,128)(2,1)S(1)}, bf16[2,2048]{1,0:T(2,128)(2,1)S(1)}, u32[]{:S(2)}, u32[]{:S(2)}) collective-permute-start(bf16[2,2048]{1,0:T(2,128)(2,1)S(1)} %get-tuple-element.44), channel_id=1, source_target_pairs={{0,12},{4,8},{8,4},{12,0},{1,13},{5,9},{9,5},{13,1},{2,14},{6,10},... | collective-permute-start | bytes 24584 | tf_op jit(solution)/shard_map/ppermute | solution.py:506
  24.0 1.0 %collective-permute-start.10 = (bf16[2,2048]{1,0:T(2,128)(2,1)S(1)}, bf16[2,2048]{1,0:T(2,128)(2,1)S(1)}, u32[]{:S(2)}, u32[]{:S(2)}) collective-permute-start(bf16[2,2048]{1,0:T(2,128)(2,1)S(1)} %get-tuple-element.44), channel_id=1, source_target_pairs={{0,8},{4,12},{8,0},{12,4},{1,9},{5,13},{9,1},{13,5},{2,10},{6,14},... | collective-permute-start | bytes 24584 | tf_op jit(solution)/shard_map/ppermute | solution.py:506
  24.9 0.0 collective-permute-done.3.rest_1_
  24.9 0.3 %collective-permute-start.9 = (bf16[2,2048]{1,0:T(2,128)(2,1)S(1)}, bf16[2,2048]{1,0:T(2,128)(2,1)S(1)}, u32[]{:S(2)}, u32[]{:S(2)}) collective-permute-start(bf16[2,2048]{1,0:T(2,128)(2,1)S(1)} %get-tuple-element.44), channel_id=1, source_target_pairs={{0,4},{4,0},{8,12},{12,8},{1,5},{5,1},{9,13},{13,9},{2,6},{6,2},{1... | collective-permute-start | bytes 24584 | tf_op jit(solution)/shard_map/ppermute | solution.py:506
  25.3 0.0 collective-permute-done.4.rest_2_
  25.3 1.1 %collective-permute-done.5.rest_3_ = bf16[64,128]{1,0:T(8,128)(2,1)S(1)} collective-permute-done((bf16[64,128]{1,0:T(8,128)(2,1)}, bf16[64,128]{1,0:T(8,128)(2,1)S(1)}, u32[]{:S(2)}, u32[]{:S(2)}) %collective-permute-start.5) | collective-permute-done | bytes 16416 | tf_op jit(solution)/shard_map/ppermute | solution.py:506
  26.4 0.0 copy-done.3
  26.4 0.0 copy-start.4
  26.4 0.7 %copy-done.4 = bf16[64,128]{1,0:T(8,128)(2,1)S(1)} copy-done((bf16[64,128]{1,0:T(8,128)(2,1)S(1)}, bf16[64,128]{1,0:T(8,128)(2,1)}, u32[]{:S(2)}) %copy-start.4) | copy-done | bytes 16408
  27.1 0.2 combine_resident.1.kept_ref
  27.3 0.0 collective-permute-done.11.rest_2_
  27.3 0.4 %collective-permute-done.10.rest_1_ = bf16[2,2048]{1,0:T(2,128)(2,1)S(1)} collective-permute-done((bf16[2,2048]{1,0:T(2,128)(2,1)S(1)}, bf16[2,2048]{1,0:T(2,128)(2,1)S(1)}, u32[]{:S(2)}, u32[]{:S(2)}) %collective-permute-start.10) | collective-permute-done | bytes 8224 | tf_op jit(solution)/shard_map/ppermute | solution.py:506
  27.7 0.0 collective-permute-done.9.rest_0_
  27.7 0.7 %finish.1 = bf16[5,2048]{1,0:T(8,128)(2,1)} custom-call(f32[3,2048]{1,0:T(4,128)S(1)} %combine_resident.1.kept_ref, s32[8,128]{1,0:T(8,128)S(1)} %get-tuple-element.43.place_ref, bf16[2,2048]{1,0:T(2,128)(2,1)S(1)} %collective-permute-done.9.rest_0_, bf16[2,2048]{1,0:T(2,128)(2,1)S(1)} %collective-permute-done.10.rest_1_, ...), custom_call_target="tpu_custom_call" | custom-call | tf_op jit(solution)/shard_map/finish/pallas_call | solution.py:495
Async XLA Ops:
  3.9 5.5 %collective-permute-start = (bf16[5,2560]{1,0:T(8,128)(2,1)}, bf16[5,2560]{1,0:T(8,128)(2,1)S(1)}, u32[]{:S(2)}, u32[]{:S(2)}) collective-permute-start(bf16[5,2560]{1,0:T(8,128)(2,1)} %get-tuple-element.25.ask_ref), channel_id=1, source_target_pairs={{0,4},{4,0},{8,12},{12,8},{1,5},{5,1},{9,13},{13,9},{2,6},{6,2},{1... | collective-permute-start | bytes 76808 | tf_op jit(solution)/shard_map/ppermute | solution.py:506
  4.4 17.1 %collective-permute-start.6 = (bf16[136,512]{1,0:T(8,128)(2,1)}, bf16[136,512]{1,0:T(8,128)(2,1)S(1)}, u32[]{:S(2)}, u32[]{:S(2)}) collective-permute-start(bf16[136,512]{1,0:T(8,128)(2,1)} %get-tuple-element.40), channel_id=1, source_target_pairs={{0,2},{1,3},{2,0},{3,1},{4,6},{5,7},{6,4},{7,5},{8,10},{9,11},{10,... | collective-permute-start | bytes 417800 | tf_op jit(solution)/shard_map/ppermute | solution.py:506
  8.1 13.9 %collective-permute-start.7 = (bf16[136,512]{1,0:T(8,128)(2,1)}, bf16[136,512]{1,0:T(8,128)(2,1)S(1)}, u32[]{:S(2)}, u32[]{:S(2)}) collective-permute-start(bf16[136,512]{1,0:T(8,128)(2,1)} %get-tuple-element.41), channel_id=1, source_target_pairs={{0,3},{1,2},{2,1},{3,0},{4,7},{5,6},{6,5},{7,4},{8,11},{9,10},{10,... | collective-permute-start | bytes 417800 | tf_op jit(solution)/shard_map/ppermute | solution.py:506
  9.5 12.5 %collective-permute-start.8 = (bf16[136,512]{1,0:T(8,128)(2,1)}, bf16[136,512]{1,0:T(8,128)(2,1)S(1)}, u32[]{:S(2)}, u32[]{:S(2)}) collective-permute-start(bf16[136,512]{1,0:T(8,128)(2,1)} %get-tuple-element.42), channel_id=1, source_target_pairs={{0,1},{1,0},{2,3},{3,2},{4,5},{5,4},{6,7},{7,6},{8,9},{9,8},{10,11... | collective-permute-start | bytes 417800 | tf_op jit(solution)/shard_map/ppermute | solution.py:506
  9.7 8.7 %collective-permute-start.2 = (bf16[5,2560]{1,0:T(8,128)(2,1)}, bf16[5,2560]{1,0:T(8,128)(2,1)S(1)}, u32[]{:S(2)}, u32[]{:S(2)}) collective-permute-start(bf16[5,2560]{1,0:T(8,128)(2,1)} %get-tuple-element.25.ask_ref), channel_id=1, source_target_pairs={{0,12},{4,8},{8,4},{12,0},{1,13},{5,9},{9,5},{13,1},{2,14},{6,10},... | collective-permute-start | bytes 76808 | tf_op jit(solution)/shard_map/ppermute | solution.py:506
  10.7 7.8 %collective-permute-start.1 = (bf16[5,2560]{1,0:T(8,128)(2,1)}, bf16[5,2560]{1,0:T(8,128)(2,1)S(1)}, u32[]{:S(2)}, u32[]{:S(2)}) collective-permute-start(bf16[5,2560]{1,0:T(8,128)(2,1)} %get-tuple-element.25.ask_ref), channel_id=1, source_target_pairs={{0,8},{4,12},{8,0},{12,4},{1,9},{5,13},{9,1},{13,5},{2,10},{6,14},... | collective-permute-start | bytes 76808 | tf_op jit(solution)/shard_map/ppermute | solution.py:506
  11.2 10.8 %copy-start = (bf16[136,512]{1,0:T(8,128)(2,1)S(1)}, bf16[136,512]{1,0:T(8,128)(2,1)}, u32[]{:S(2)}) copy-start(bf16[136,512]{1,0:T(8,128)(2,1)} %get-tuple-element.39.rest_3_) | copy-start | bytes 417796
  11.2 10.8 %copy-start.1 = (f32[128,128]{1,0:T(8,128)S(1)}, f32[128,128]{1,0:T(8,128)}, u32[]{:S(2)}) copy-start(f32[128,128]{1,0:T(8,128)} %constant.5.clone.sin_ref) | copy-start | bytes 196612
  11.2 10.8 %copy-start.2 = (f32[128,128]{1,0:T(8,128)S(1)}, f32[128,128]{1,0:T(8,128)}, u32[]{:S(2)}) copy-start(f32[128,128]{1,0:T(8,128)} %constant.4.clone.cos_ref) | copy-start | bytes 196612
  11.2 10.8 %copy-start.5 = (s32[4,2]{0,1:T(2,128)S(1)}, s32[4,2]{0,1:T(2,128)}, u32[]{:S(2)}) copy-start(s32[4,2]{0,1:T(2,128)} %param.14) | copy-start | bytes 100
  11.2 10.8 %copy-start.6 = (s32[4,2]{0,1:T(2,128)S(1)}, s32[4,2]{0,1:T(2,128)}, u32[]{:S(2)}) copy-start(s32[4,2]{0,1:T(2,128)} %param.15) | copy-start | bytes 100
  11.3 10.8 %copy-start.7 = (bf16[128]{0:T(256)(128)(2,1)S(1)}, bf16[128]{0:T(256)(128)(2,1)}, u32[]{:S(2)}) copy-start(bf16[128]{0:T(256)(128)(2,1)} %param.18) | copy-start | bytes 772
  11.3 15.1 %copy-start.3 = (bf16[5,2560]{1,0:T(8,128)(2,1)S(1)}, bf16[5,2560]{1,0:T(8,128)(2,1)}, u32[]{:S(2)}) copy-start(bf16[5,2560]{1,0:T(8,128)(2,1)} %get-tuple-element.25.ask_ref) | copy-start | bytes 76804
  18.4 6.5 %collective-permute-start.3 = (bf16[64,128]{1,0:T(8,128)(2,1)}, bf16[64,128]{1,0:T(8,128)(2,1)S(1)}, u32[]{:S(2)}, u32[]{:S(2)}) collective-permute-start(bf16[64,128]{1,0:T(8,128)(2,1)} %get-tuple-element.33), channel_id=1, source_target_pairs={{0,1},{1,0},{2,3},{3,2},{4,5},{5,4},{6,7},{7,6},{8,9},{9,8},{10,11... | collective-permute-start | bytes 49160 | tf_op jit(solution)/shard_map/ppermute | solution.py:506
  19.1 6.2 %collective-permute-start.4 = (bf16[64,128]{1,0:T(8,128)(2,1)}, bf16[64,128]{1,0:T(8,128)(2,1)S(1)}, u32[]{:S(2)}, u32[]{:S(2)}) collective-permute-start(bf16[64,128]{1,0:T(8,128)(2,1)} %get-tuple-element.34), channel_id=1, source_target_pairs={{0,3},{1,2},{2,1},{3,0},{4,7},{5,6},{6,5},{7,4},{8,11},{9,10},{10,... | collective-permute-start | bytes 49160 | tf_op jit(solution)/shard_map/ppermute | solution.py:506
  21.5 4.8 %collective-permute-start.5 = (bf16[64,128]{1,0:T(8,128)(2,1)}, bf16[64,128]{1,0:T(8,128)(2,1)S(1)}, u32[]{:S(2)}, u32[]{:S(2)}) collective-permute-start(bf16[64,128]{1,0:T(8,128)(2,1)} %get-tuple-element.35), channel_id=1, source_target_pairs={{0,2},{1,3},{2,0},{3,1},{4,6},{5,7},{6,4},{7,5},{8,10},{9,11},{10,... | collective-permute-start | bytes 49160 | tf_op jit(solution)/shard_map/ppermute | solution.py:506
  23.3 3.9 %collective-permute-start.11 = (bf16[2,2048]{1,0:T(2,128)(2,1)S(1)}, bf16[2,2048]{1,0:T(2,128)(2,1)S(1)}, u32[]{:S(2)}, u32[]{:S(2)}) collective-permute-start(bf16[2,2048]{1,0:T(2,128)(2,1)S(1)} %get-tuple-element.44), channel_id=1, source_target_pairs={{0,12},{4,8},{8,4},{12,0},{1,13},{5,9},{9,5},{13,1},{2,14},{6,10},... | collective-permute-start | bytes 24584 | tf_op jit(solution)/shard_map/ppermute | solution.py:506
  24.0 3.7 %collective-permute-start.10 = (bf16[2,2048]{1,0:T(2,128)(2,1)S(1)}, bf16[2,2048]{1,0:T(2,128)(2,1)S(1)}, u32[]{:S(2)}, u32[]{:S(2)}) collective-permute-start(bf16[2,2048]{1,0:T(2,128)(2,1)S(1)} %get-tuple-element.44), channel_id=1, source_target_pairs={{0,8},{4,12},{8,0},{12,4},{1,9},{5,13},{9,1},{13,5},{2,10},{6,14},... | collective-permute-start | bytes 24584 | tf_op jit(solution)/shard_map/ppermute | solution.py:506
  24.9 2.7 %collective-permute-start.9 = (bf16[2,2048]{1,0:T(2,128)(2,1)S(1)}, bf16[2,2048]{1,0:T(2,128)(2,1)S(1)}, u32[]{:S(2)}, u32[]{:S(2)}) collective-permute-start(bf16[2,2048]{1,0:T(2,128)(2,1)S(1)} %get-tuple-element.44), channel_id=1, source_target_pairs={{0,4},{4,0},{8,12},{12,8},{1,5},{5,1},{9,13},{13,9},{2,6},{6,2},{1... | collective-permute-start | bytes 24584 | tf_op jit(solution)/shard_map/ppermute | solution.py:506
  26.4 0.7 %copy-start.4 = (bf16[64,128]{1,0:T(8,128)(2,1)S(1)}, bf16[64,128]{1,0:T(8,128)(2,1)}, u32[]{:S(2)}) copy-start(bf16[64,128]{1,0:T(8,128)(2,1)} %get-tuple-element.32.rest_0_) | copy-start | bytes 49156

commit v21 on v19

--- a/solution.py
+++ b/solution.py
@@ -156,9 +156,9 @@
     return outs[:ranks], outs[ranks]
 
 
-def resident_kernel(ranks, len_ref, q_ref, k_hbm, v_hbm, *rest):
+def resident_kernel(ranks, len_ref, q_hbm, k_hbm, v_hbm, *rest):
     outs, rest = rest[:ranks], rest[ranks:]
-    q_wide, q_all, k_buf, v_buf, o_all, m_all, l_all, s_all, sems = rest
+    q_ref, q_wide, q_all, k_buf, v_buf, o_all, m_all, l_all, s_all, q_sem, sems = rest
     residents, positions, width = k_buf.shape
     copies = []
     for r in range(residents):
@@ -177,6 +177,10 @@
             for copy in copies[r]:
                 copy.start()
 
+        if r == 0:
+            q_copy = pltpu.make_async_copy(q_hbm, q_ref, q_sem)
+            q_copy.start()
+
     heads = q_ref.shape[0]
     kv_heads = width // 128
     group = heads // kv_heads
@@ -191,6 +195,7 @@
         spread = jnp.where(diagonal, column, 0.0)
         return jnp.sum(spread.reshape(ranks, heads_mine, 128), axis=1)
 
+    q_copy.wait()
     q_wide[...] = q_ref[...].astype(F32)
     for r in range(residents):
         q_all[r] = q_wide[:, r, :].astype(BF16)
@@ -258,10 +263,11 @@
     rows = -(-(residents * (heads_mine + 3)) // 16) * 16
     return pl.pallas_call(
         functools.partial(resident_kernel, ranks),
-        in_specs=[SMEM, VMEM, HBM, HBM],
+        in_specs=[SMEM, HBM, HBM, HBM],
         out_specs=[VMEM] * ranks,
         out_shape=[jax.ShapeDtypeStruct((rows, 128), BF16)] * ranks,
         scratch_shapes=[
+            pltpu.VMEM(queries.shape, BF16),
             pltpu.VMEM(queries.shape, F32),
             pltpu.VMEM((residents, heads, 128), BF16),
             pltpu.VMEM((residents, positions, width), BF16),
@@ -270,6 +276,7 @@
             pltpu.VMEM((residents, heads, 1), F32),
             pltpu.VMEM((residents, heads, 1), F32),
             pltpu.VMEM((residents, 3, ranks, 128), F32),
+            pltpu.SemaphoreType.DMA,
             pltpu.SemaphoreType.DMA((2, residents)),
         ],
         compiler_params=pltpu.CompilerParams(vmem_limit_bytes=56 * MIB),

time: 28.7 us -> 31.1 us (1.084)
  Pallas kernels: 13.3 us -> 15.6 us
    pallas_call x1, Pallas kernels: 7.13 us -> 9.42 us  [attend_resident(): pl.pallas_call(functools.partial(resident_kernel, ranks), in_specs=[SMEM,...]
  transfers between devices with their start and end apart: 12 -> 12, of which waited for: 2 -> 2; matrix products, arithmetic and copies ran while one was open for 0% -> 0% of each run, Pallas kernels for 30% -> 35%
where the time goes in v21:
time: 31.1 us; the launch traced here: 30.8 us
  Pallas kernels  15.6 us (50%)
  starting transfers between devices  12.8 us (41%)
  waiting for transfers between devices  1.62 us (5%)
  local copies, waits for them, and re-layouts  0.75 us (2%)
    ppermute x12, starting transfers between devices, swapped(): return lax.ppermute(x, axis, [(i, i ^ j) for i in range(n)])  12.8 us
    pallas_call x1, Pallas kernels, attend_resident(): pl.pallas_call(functools.partial(resident_kernel, ranks), in_specs=[SMEM,...  9.42 us
    pallas_call x1, Pallas kernels, project(): pl.pallas_call(functools.partial(project_kernel, ranks, group), in_specs=...  3.99 us
    ppermute x12, waiting for transfers between devices, swapped(): return lax.ppermute(x, axis, [(i, i ^ j) for i in range(n)])  1.62 us
    pallas_call x1, Pallas kernels, attend_moved(): pl.pallas_call(functools.partial(moved_kernel, insts, len(pieces), reside...  1.32 us
    unnamed x16, local copies, waits for them, and re-layouts  0.75 us
    pallas_call x1, Pallas kernels, finish(): pl.pallas_call(finish_kernel, in_specs=[VMEM] * (2 + len(moved)), out_spe...  0.67 us
  transfers between devices with their start and end apart: 12, of which 2 were waited for; matrix products, arithmetic and copies ran while one was open for 0% of the time, Pallas kernels for 35%

profile of v21, /device:TPU:0, one launch (start us, length us, event | category | flops | bytes accessed | tf_op | source)
XLA Modules:
  0.0 30.8 jit_solution(10581679474456704939)
XLA Ops:
  0.0 4.0 %project.1 = (bf16[136,512]{1,0:T(8,128)(2,1)}, bf16[136,512]{1,0:T(8,128)(2,1)}, bf16[136,512]{1,0:T(8,128)(2,1)}, bf16[136,512]{1,0:T(8,128)(2,1)}, bf16[5,2560]{1,0:T(8,128)(2,1)}) custom-call(bf16[1280]{0:T(1024)(128)(2,1)} %gain_hbm.1, bf16[64,2,1280]{2,1,0:T(2,128)(2,1)} %bitcast.19, bf16[1280,2048]{1,0:T(8,128)(2,1)} %w_hbm.1, ...), custom_call_target="tpu_custom_call" | custom-call | flops 671088640 | bytes 5242880 | tf_op jit(solution)/shard_map/project/pallas_call | solution.py:133
  4.0 0.5 %collective-permute-start = (bf16[5,2560]{1,0:T(8,128)(2,1)}, bf16[5,2560]{1,0:T(8,128)(2,1)S(1)}, u32[]{:S(2)}, u32[]{:S(2)}) collective-permute-start(bf16[5,2560]{1,0:T(8,128)(2,1)} %get-tuple-element.25.ask_ref), channel_id=1, source_target_pairs={{0,4},{4,0},{8,12},{12,8},{1,5},{5,1},{9,13},{13,9},{2,6},{6,2},{1... | collective-permute-start | bytes 76808 | tf_op jit(solution)/shard_map/ppermute | solution.py:511
  4.5 3.7 %collective-permute-start.6 = (bf16[136,512]{1,0:T(8,128)(2,1)}, bf16[136,512]{1,0:T(8,128)(2,1)S(1)}, u32[]{:S(2)}, u32[]{:S(2)}) collective-permute-start(bf16[136,512]{1,0:T(8,128)(2,1)} %get-tuple-element.40), channel_id=1, source_target_pairs={{0,2},{1,3},{2,0},{3,1},{4,6},{5,7},{6,4},{7,5},{8,10},{9,11},{10,... | collective-permute-start | bytes 417800 | tf_op jit(solution)/shard_map/ppermute | solution.py:511
  8.2 1.3 %collective-permute-start.7 = (bf16[136,512]{1,0:T(8,128)(2,1)}, bf16[136,512]{1,0:T(8,128)(2,1)S(1)}, u32[]{:S(2)}, u32[]{:S(2)}) collective-permute-start(bf16[136,512]{1,0:T(8,128)(2,1)} %get-tuple-element.41), channel_id=1, source_target_pairs={{0,3},{1,2},{2,1},{3,0},{4,7},{5,6},{6,5},{7,4},{8,11},{9,10},{10,... | collective-permute-start | bytes 417800 | tf_op jit(solution)/shard_map/ppermute | solution.py:511
  9.5 0.0 collective-permute-done.rest_0_
  9.5 0.2 collective-permute-start.8
  9.8 1.0 %collective-permute-start.2 = (bf16[5,2560]{1,0:T(8,128)(2,1)}, bf16[5,2560]{1,0:T(8,128)(2,1)S(1)}, u32[]{:S(2)}, u32[]{:S(2)}) collective-permute-start(bf16[5,2560]{1,0:T(8,128)(2,1)} %get-tuple-element.25.ask_ref), channel_id=1, source_target_pairs={{0,12},{4,8},{8,4},{12,0},{1,13},{5,9},{9,5},{13,1},{2,14},{6,10},... | collective-permute-start | bytes 76808 | tf_op jit(solution)/shard_map/ppermute | solution.py:511
  10.7 0.5 %collective-permute-start.1 = (bf16[5,2560]{1,0:T(8,128)(2,1)}, bf16[5,2560]{1,0:T(8,128)(2,1)S(1)}, u32[]{:S(2)}, u32[]{:S(2)}) collective-permute-start(bf16[5,2560]{1,0:T(8,128)(2,1)} %get-tuple-element.25.ask_ref), channel_id=1, source_target_pairs={{0,8},{4,12},{8,0},{12,4},{1,9},{5,13},{9,1},{13,5},{2,10},{6,14},... | collective-permute-start | bytes 76808 | tf_op jit(solution)/shard_map/ppermute | solution.py:511
  11.3 0.0 copy-start
  11.3 0.0 copy-start.1
  11.3 0.0 copy-start.2
  11.3 0.0 copy-start.5
  11.3 0.0 copy-start.6
  11.3 0.0 copy-start.7
  11.3 0.0 copy-start.3
  11.3 9.4 %attend_resident.1 = (bf16[64,128]{1,0:T(8,128)(2,1)}, bf16[64,128]{1,0:T(8,128)(2,1)}, bf16[64,128]{1,0:T(8,128)(2,1)}, bf16[64,128]{1,0:T(8,128)(2,1)}) custom-call(s32[1,3]{1,0:T(1,128)} %len_ref.1, bf16[64,5,128]{2,1,0:T(8,128)(2,1)} %bitcast.18, bf16[3,1024,1024]{2,1,0:T(8,128)(2,1)} %bitcast.15, bf16[3,1024,1024]{2,1,0:T(8,128)(2,1)} %bitcast.16), custom_call_target="tpu_custom_call" | custom-call | flops 100663296 | bytes 12582912 | tf_op jit(solution)/shard_map/attend_resident/pallas_call | solution.py:264
  20.8 0.0 collective-permute-done.2.rest_2_
  20.8 0.0 collective-permute-done.1.rest_1_
  20.8 1.9 %collective-permute-start.3 = (bf16[64,128]{1,0:T(8,128)(2,1)}, bf16[64,128]{1,0:T(8,128)(2,1)S(1)}, u32[]{:S(2)}, u32[]{:S(2)}) collective-permute-start(bf16[64,128]{1,0:T(8,128)(2,1)} %get-tuple-element.33), channel_id=1, source_target_pairs={{0,1},{1,0},{2,3},{3,2},{4,5},{5,4},{6,7},{7,6},{8,9},{9,8},{10,11... | collective-permute-start | bytes 49160 | tf_op jit(solution)/shard_map/ppermute | solution.py:511
  22.6 0.7 %collective-permute-start.4 = (bf16[64,128]{1,0:T(8,128)(2,1)}, bf16[64,128]{1,0:T(8,128)(2,1)S(1)}, u32[]{:S(2)}, u32[]{:S(2)}) collective-permute-start(bf16[64,128]{1,0:T(8,128)(2,1)} %get-tuple-element.34), channel_id=1, source_target_pairs={{0,3},{1,2},{2,1},{3,0},{4,7},{5,6},{6,5},{7,4},{8,11},{9,10},{10,... | collective-permute-start | bytes 49160 | tf_op jit(solution)/shard_map/ppermute | solution.py:511
  23.3 0.0 collective-permute-done.6.rest_4_
  23.3 1.0 %collective-permute-start.5 = (bf16[64,128]{1,0:T(8,128)(2,1)}, bf16[64,128]{1,0:T(8,128)(2,1)S(1)}, u32[]{:S(2)}, u32[]{:S(2)}) collective-permute-start(bf16[64,128]{1,0:T(8,128)(2,1)} %get-tuple-element.35), channel_id=1, source_target_pairs={{0,2},{1,3},{2,0},{3,1},{4,6},{5,7},{6,4},{7,5},{8,10},{9,11},{10,... | collective-permute-start | bytes 49160 | tf_op jit(solution)/shard_map/ppermute | solution.py:511
  24.3 0.0 collective-permute-done.7.rest_5_
  24.4 0.0 collective-permute-done.8.rest_6_
  24.4 0.0 copy-done
  24.4 0.0 copy-done.1
  24.4 0.0 copy-done.2
  24.4 0.0 copy-done.5
  24.4 0.0 copy-done.6
  24.4 0.0 copy-done.7
  24.4 1.3 %attend_moved.1 = (bf16[2,2048]{1,0:T(2,128)(2,1)S(1)}, s32[8,128]{1,0:T(8,128)S(1)}) custom-call(s32[2,4]{1,0:T(2,128)S(1)} %bitcast.12, s32[2,4]{1,0:T(2,128)S(1)} %bitcast.13, bf16[1,128]{1,0:T(2,128)(2,1)S(1)} %bitcast.14, f32[128,128]{1,0:T(8,128)S(1)} %copy-done.2, f32[128,128]{1,0:T(8,128)S(1)} %copy-done.1, ...), custom_call_target="tpu_custom_call" | custom-call | tf_op jit(solution)/shard_map/attend_moved/pallas_call | solution.py:417
  25.7 0.8 %collective-permute-start.11 = (bf16[2,2048]{1,0:T(2,128)(2,1)S(1)}, bf16[2,2048]{1,0:T(2,128)(2,1)S(1)}, u32[]{:S(2)}, u32[]{:S(2)}) collective-permute-start(bf16[2,2048]{1,0:T(2,128)(2,1)S(1)} %get-tuple-element.44), channel_id=1, source_target_pairs={{0,12},{4,8},{8,4},{12,0},{1,13},{5,9},{9,5},{13,1},{2,14},{6,10},... | collective-permute-start | bytes 24584 | tf_op jit(solution)/shard_map/ppermute | solution.py:511
  26.5 0.8 %collective-permute-start.10 = (bf16[2,2048]{1,0:T(2,128)(2,1)S(1)}, bf16[2,2048]{1,0:T(2,128)(2,1)S(1)}, u32[]{:S(2)}, u32[]{:S(2)}) collective-permute-start(bf16[2,2048]{1,0:T(2,128)(2,1)S(1)} %get-tuple-element.44), channel_id=1, source_target_pairs={{0,8},{4,12},{8,0},{12,4},{1,9},{5,13},{9,1},{13,5},{2,10},{6,14},... | collective-permute-start | bytes 24584 | tf_op jit(solution)/shard_map/ppermute | solution.py:511
  27.4 0.0 collective-permute-done.3.rest_1_
  27.4 0.3 collective-permute-start.9
  27.7 0.7 %collective-permute-done.4.rest_2_ = bf16[64,128]{1,0:T(8,128)(2,1)S(1)} collective-permute-done((bf16[64,128]{1,0:T(8,128)(2,1)}, bf16[64,128]{1,0:T(8,128)(2,1)S(1)}, u32[]{:S(2)}, u32[]{:S(2)}) %collective-permute-start.4) | collective-permute-done | bytes 16416 | tf_op jit(solution)/shard_map/ppermute | solution.py:511
  28.4 0.0 collective-permute-done.5.rest_3_
  28.4 0.0 copy-done.3
  28.4 0.0 copy-start.4
  28.4 0.7 %copy-done.4 = bf16[64,128]{1,0:T(8,128)(2,1)S(1)} copy-done((bf16[64,128]{1,0:T(8,128)(2,1)S(1)}, bf16[64,128]{1,0:T(8,128)(2,1)}, u32[]{:S(2)}) %copy-start.4) | copy-done | bytes 16408
  29.1 0.2 combine_resident.1.kept_ref
  29.3 0.0 collective-permute-done.11.rest_2_
  29.3 0.9 %collective-permute-done.10.rest_1_ = bf16[2,2048]{1,0:T(2,128)(2,1)S(1)} collective-permute-done((bf16[2,2048]{1,0:T(2,128)(2,1)S(1)}, bf16[2,2048]{1,0:T(2,128)(2,1)S(1)}, u32[]{:S(2)}, u32[]{:S(2)}) %collective-permute-start.10) | collective-permute-done | bytes 8224 | tf_op jit(solution)/shard_map/ppermute | solution.py:511
  30.2 0.0 collective-permute-done.9.rest_0_
  30.2 0.7 %finish.1 = bf16[5,2048]{1,0:T(8,128)(2,1)} custom-call(f32[3,2048]{1,0:T(4,128)S(1)} %combine_resident.1.kept_ref, s32[8,128]{1,0:T(8,128)S(1)} %get-tuple-element.43.place_ref, bf16[2,2048]{1,0:T(2,128)(2,1)S(1)} %collective-permute-done.9.rest_0_, bf16[2,2048]{1,0:T(2,128)(2,1)S(1)} %collective-permute-done.10.rest_1_, ...), custom_call_target="tpu_custom_call" | custom-call | tf_op jit(solution)/shard_map/finish/pallas_call | solution.py:500
Async XLA Ops:
  4.0 5.5 %collective-permute-start = (bf16[5,2560]{1,0:T(8,128)(2,1)}, bf16[5,2560]{1,0:T(8,128)(2,1)S(1)}, u32[]{:S(2)}, u32[]{:S(2)}) collective-permute-start(bf16[5,2560]{1,0:T(8,128)(2,1)} %get-tuple-element.25.ask_ref), channel_id=1, source_target_pairs={{0,4},{4,0},{8,12},{12,8},{1,5},{5,1},{9,13},{13,9},{2,6},{6,2},{1... | collective-permute-start | bytes 76808 | tf_op jit(solution)/shard_map/ppermute | solution.py:511
  4.5 18.8 %collective-permute-start.6 = (bf16[136,512]{1,0:T(8,128)(2,1)}, bf16[136,512]{1,0:T(8,128)(2,1)S(1)}, u32[]{:S(2)}, u32[]{:S(2)}) collective-permute-start(bf16[136,512]{1,0:T(8,128)(2,1)} %get-tuple-element.40), channel_id=1, source_target_pairs={{0,2},{1,3},{2,0},{3,1},{4,6},{5,7},{6,4},{7,5},{8,10},{9,11},{10,... | collective-permute-start | bytes 417800 | tf_op jit(solution)/shard_map/ppermute | solution.py:511
  8.2 16.2 %collective-permute-start.7 = (bf16[136,512]{1,0:T(8,128)(2,1)}, bf16[136,512]{1,0:T(8,128)(2,1)S(1)}, u32[]{:S(2)}, u32[]{:S(2)}) collective-permute-start(bf16[136,512]{1,0:T(8,128)(2,1)} %get-tuple-element.41), channel_id=1, source_target_pairs={{0,3},{1,2},{2,1},{3,0},{4,7},{5,6},{6,5},{7,4},{8,11},{9,10},{10,... | collective-permute-start | bytes 417800 | tf_op jit(solution)/shard_map/ppermute | solution.py:511
  9.5 14.8 %collective-permute-start.8 = (bf16[136,512]{1,0:T(8,128)(2,1)}, bf16[136,512]{1,0:T(8,128)(2,1)S(1)}, u32[]{:S(2)}, u32[]{:S(2)}) collective-permute-start(bf16[136,512]{1,0:T(8,128)(2,1)} %get-tuple-element.42), channel_id=1, source_target_pairs={{0,1},{1,0},{2,3},{3,2},{4,5},{5,4},{6,7},{7,6},{8,9},{9,8},{10,11... | collective-permute-start | bytes 417800 | tf_op jit(solution)/shard_map/ppermute | solution.py:511
  9.8 11.0 %collective-permute-start.2 = (bf16[5,2560]{1,0:T(8,128)(2,1)}, bf16[5,2560]{1,0:T(8,128)(2,1)S(1)}, u32[]{:S(2)}, u32[]{:S(2)}) collective-permute-start(bf16[5,2560]{1,0:T(8,128)(2,1)} %get-tuple-element.25.ask_ref), channel_id=1, source_target_pairs={{0,12},{4,8},{8,4},{12,0},{1,13},{5,9},{9,5},{13,1},{2,14},{6,10},... | collective-permute-start | bytes 76808 | tf_op jit(solution)/shard_map/ppermute | solution.py:511
  10.7 10.0 %collective-permute-start.1 = (bf16[5,2560]{1,0:T(8,128)(2,1)}, bf16[5,2560]{1,0:T(8,128)(2,1)S(1)}, u32[]{:S(2)}, u32[]{:S(2)}) collective-permute-start(bf16[5,2560]{1,0:T(8,128)(2,1)} %get-tuple-element.25.ask_ref), channel_id=1, source_target_pairs={{0,8},{4,12},{8,0},{12,4},{1,9},{5,13},{9,1},{13,5},{2,10},{6,14},... | collective-permute-start | bytes 76808 | tf_op jit(solution)/shard_map/ppermute | solution.py:511
  11.3 13.1 %copy-start = (bf16[136,512]{1,0:T(8,128)(2,1)S(1)}, bf16[136,512]{1,0:T(8,128)(2,1)}, u32[]{:S(2)}) copy-start(bf16[136,512]{1,0:T(8,128)(2,1)} %get-tuple-element.39.rest_3_) | copy-start | bytes 417796
  11.3 13.1 %copy-start.1 = (f32[128,128]{1,0:T(8,128)S(1)}, f32[128,128]{1,0:T(8,128)}, u32[]{:S(2)}) copy-start(f32[128,128]{1,0:T(8,128)} %constant.5.clone.sin_ref) | copy-start | bytes 196612
  11.3 13.1 %copy-start.2 = (f32[128,128]{1,0:T(8,128)S(1)}, f32[128,128]{1,0:T(8,128)}, u32[]{:S(2)}) copy-start(f32[128,128]{1,0:T(8,128)} %constant.4.clone.cos_ref) | copy-start | bytes 196612
  11.3 13.1 %copy-start.5 = (s32[4,2]{0,1:T(2,128)S(1)}, s32[4,2]{0,1:T(2,128)}, u32[]{:S(2)}) copy-start(s32[4,2]{0,1:T(2,128)} %param.14) | copy-start | bytes 100
  11.3 13.1 %copy-start.6 = (s32[4,2]{0,1:T(2,128)S(1)}, s32[4,2]{0,1:T(2,128)}, u32[]{:S(2)}) copy-start(s32[4,2]{0,1:T(2,128)} %param.15) | copy-start | bytes 100
  11.3 13.1 %copy-start.7 = (bf16[128]{0:T(256)(128)(2,1)S(1)}, bf16[128]{0:T(256)(128)(2,1)}, u32[]{:S(2)}) copy-start(bf16[128]{0:T(256)(128)(2,1)} %param.18) | copy-start | bytes 772
  11.3 17.1 %copy-start.3 = (bf16[5,2560]{1,0:T(8,128)(2,1)S(1)}, bf16[5,2560]{1,0:T(8,128)(2,1)}, u32[]{:S(2)}) copy-start(bf16[5,2560]{1,0:T(8,128)(2,1)} %get-tuple-element.25.ask_ref) | copy-start | bytes 76804
  20.8 6.6 %collective-permute-start.3 = (bf16[64,128]{1,0:T(8,128)(2,1)}, bf16[64,128]{1,0:T(8,128)(2,1)S(1)}, u32[]{:S(2)}, u32[]{:S(2)}) collective-permute-start(bf16[64,128]{1,0:T(8,128)(2,1)} %get-tuple-element.33), channel_id=1, source_target_pairs={{0,1},{1,0},{2,3},{3,2},{4,5},{5,4},{6,7},{7,6},{8,9},{9,8},{10,11... | collective-permute-start | bytes 49160 | tf_op jit(solution)/shard_map/ppermute | solution.py:511
  22.6 5.7 %collective-permute-start.4 = (bf16[64,128]{1,0:T(8,128)(2,1)}, bf16[64,128]{1,0:T(8,128)(2,1)S(1)}, u32[]{:S(2)}, u32[]{:S(2)}) collective-permute-start(bf16[64,128]{1,0:T(8,128)(2,1)} %get-tuple-element.34), channel_id=1, source_target_pairs={{0,3},{1,2},{2,1},{3,0},{4,7},{5,6},{6,5},{7,4},{8,11},{9,10},{10,... | collective-permute-start | bytes 49160 | tf_op jit(solution)/shard_map/ppermute | solution.py:511
  23.3 5.1 %collective-permute-start.5 = (bf16[64,128]{1,0:T(8,128)(2,1)}, bf16[64,128]{1,0:T(8,128)(2,1)S(1)}, u32[]{:S(2)}, u32[]{:S(2)}) collective-permute-start(bf16[64,128]{1,0:T(8,128)(2,1)} %get-tuple-element.35), channel_id=1, source_target_pairs={{0,2},{1,3},{2,0},{3,1},{4,6},{5,7},{6,4},{7,5},{8,10},{9,11},{10,... | collective-permute-start | bytes 49160 | tf_op jit(solution)/shard_map/ppermute | solution.py:511
  25.7 3.5 %collective-permute-start.11 = (bf16[2,2048]{1,0:T(2,128)(2,1)S(1)}, bf16[2,2048]{1,0:T(2,128)(2,1)S(1)}, u32[]{:S(2)}, u32[]{:S(2)}) collective-permute-start(bf16[2,2048]{1,0:T(2,128)(2,1)S(1)} %get-tuple-element.44), channel_id=1, source_target_pairs={{0,12},{4,8},{8,4},{12,0},{1,13},{5,9},{9,5},{13,1},{2,14},{6,10},... | collective-permute-start | bytes 24584 | tf_op jit(solution)/shard_map/ppermute | solution.py:511
  26.5 3.7 %collective-permute-start.10 = (bf16[2,2048]{1,0:T(2,128)(2,1)S(1)}, bf16[2,2048]{1,0:T(2,128)(2,1)S(1)}, u32[]{:S(2)}, u32[]{:S(2)}) collective-permute-start(bf16[2,2048]{1,0:T(2,128)(2,1)S(1)} %get-tuple-element.44), channel_id=1, source_target_pairs={{0,8},{4,12},{8,0},{12,4},{1,9},{5,13},{9,1},{13,5},{2,10},{6,14},... | collective-permute-start | bytes 24584 | tf_op jit(solution)/shard_map/ppermute | solution.py:511
  27.4 2.8 %collective-permute-start.9 = (bf16[2,2048]{1,0:T(2,128)(2,1)S(1)}, bf16[2,2048]{1,0:T(2,128)(2,1)S(1)}, u32[]{:S(2)}, u32[]{:S(2)}) collective-permute-start(bf16[2,2048]{1,0:T(2,128)(2,1)S(1)} %get-tuple-element.44), channel_id=1, source_target_pairs={{0,4},{4,0},{8,12},{12,8},{1,5},{5,1},{9,13},{13,9},{2,6},{6,2},{1... | collective-permute-start | bytes 24584 | tf_op jit(solution)/shard_map/ppermute | solution.py:511
  28.4 0.7 %copy-start.4 = (bf16[64,128]{1,0:T(8,128)(2,1)S(1)}, bf16[64,128]{1,0:T(8,128)(2,1)}, u32[]{:S(2)}) copy-start(bf16[64,128]{1,0:T(8,128)(2,1)} %get-tuple-element.32.rest_0_) | copy-start | bytes 49156

commit v22 on v19

--- a/solution.py
+++ b/solution.py
@@ -165,7 +165,12 @@
         copies.append(
             (
                 pltpu.make_async_copy(k_hbm.at[r], k_buf.at[r], sems.at[0, r]),
-                pltpu.make_async_copy(v_hbm.at[r], v_buf.at[r], sems.at[1, r]),
+                pltpu.make_async_copy(
+                    v_hbm.at[r, : positions // 2, :], v_buf.at[r, : positions // 2, :], sems.at[1, r]
+                ),
+                pltpu.make_async_copy(
+                    v_hbm.at[r, positions // 2 :, :], v_buf.at[r, positions // 2 :, :], sems.at[2, r]
+                ),
             )
         )
     rank = lax.axis_index("tp")
@@ -217,14 +222,21 @@
             m_all[r, rows, :] = peak
             l_all[r, rows, :] = jnp.sum(weight, axis=1, keepdims=True)
             weights.append(weight.astype(BF16))
-        copies[r][1].wait()
-        for p in range(kv_heads // 2):
-            both = jnp.dot(
-                weights[p], v_buf[r, :, p * 256 : (p + 1) * 256], preferred_element_type=F32
-            )
-            o_all[r, p * pair_rows : (p + 1) * pair_rows, :] = jnp.where(
-                top_half, both[:, :128], both[:, 128:]
-            )
+        for i in range(2):
+            at = slice(i * positions // 2, (i + 1) * positions // 2)
+            copies[r][1 + i].wait()
+            for p in range(kv_heads // 2):
+                both = jnp.dot(
+                    weights[p][:, at],
+                    v_buf[r, at, p * 256 : (p + 1) * 256],
+                    preferred_element_type=F32,
+                )
+                rows = slice(p * pair_rows, (p + 1) * pair_rows)
+                part = jnp.where(top_half, both[:, :128], both[:, 128:])
+                if i == 0:
+                    o_all[r, rows, :] = part
+                else:
+                    o_all[r, rows, :] += part
 
     for r in range(residents):
         pl.when(held[r])(functools.partial(attend, r))
@@ -270,7 +282,7 @@
             pltpu.VMEM((residents, heads, 1), F32),
             pltpu.VMEM((residents, heads, 1), F32),
             pltpu.VMEM((residents, 3, ranks, 128), F32),
-            pltpu.SemaphoreType.DMA((2, residents)),
+            pltpu.SemaphoreType.DMA((3, residents)),
         ],
         compiler_params=pltpu.CompilerParams(vmem_limit_bytes=56 * MIB),
         cost_estimate=pl.CostEstimate(

time: 28.7 us -> 28.8 us (level)
  no operation moved by 1% of the time
where the time goes in v22:
time: 28.8 us; the launch traced here: 28.5 us
  Pallas kernels  13.3 us (46%)
  starting transfers between devices  12.8 us (44%)
  waiting for transfers between devices  1.55 us (5%)
  local copies, waits for them, and re-layouts  0.75 us (3%)
    ppermute x12, starting transfers between devices, swapped(): return lax.ppermute(x, axis, [(i, i ^ j) for i in range(n)])  12.8 us
    pallas_call x1, Pallas kernels, attend_resident(): pl.pallas_call(functools.partial(resident_kernel, ranks), in_specs=[SMEM,...  7.17 us
    pallas_call x1, Pallas kernels, project(): pl.pallas_call(functools.partial(project_kernel, ranks, group), in_specs=...  3.99 us
    ppermute x12, waiting for transfers between devices, swapped(): return lax.ppermute(x, axis, [(i, i ^ j) for i in range(n)])  1.55 us
    pallas_call x1, Pallas kernels, attend_moved(): pl.pallas_call(functools.partial(moved_kernel, insts, len(pieces), reside...  1.32 us
    unnamed x16, local copies, waits for them, and re-layouts  0.75 us
    pallas_call x1, Pallas kernels, finish(): pl.pallas_call(finish_kernel, in_specs=[VMEM] * (2 + len(moved)), out_spe...  0.67 us
  transfers between devices with their start and end apart: 12, of which 2 were waited for; matrix products, arithmetic and copies ran while one was open for 0% of the time, Pallas kernels for 30%

profile of v22, /device:TPU:0, one launch (start us, length us, event | category | flops | bytes accessed | tf_op | source)
XLA Modules:
  0.0 28.5 jit_solution(7847463030091509873)
XLA Ops:
  0.0 4.0 %project.1 = (bf16[136,512]{1,0:T(8,128)(2,1)}, bf16[136,512]{1,0:T(8,128)(2,1)}, bf16[136,512]{1,0:T(8,128)(2,1)}, bf16[136,512]{1,0:T(8,128)(2,1)}, bf16[5,2560]{1,0:T(8,128)(2,1)}) custom-call(bf16[1280]{0:T(1024)(128)(2,1)} %gain_hbm.1, bf16[64,2,1280]{2,1,0:T(2,128)(2,1)} %bitcast.19, bf16[1280,2048]{1,0:T(8,128)(2,1)} %w_hbm.1, ...), custom_call_target="tpu_custom_call" | custom-call | flops 671088640 | bytes 5242880 | tf_op jit(solution)/shard_map/project/pallas_call | solution.py:133
  4.0 0.5 %collective-permute-start = (bf16[5,2560]{1,0:T(8,128)(2,1)}, bf16[5,2560]{1,0:T(8,128)(2,1)S(1)}, u32[]{:S(2)}, u32[]{:S(2)}) collective-permute-start(bf16[5,2560]{1,0:T(8,128)(2,1)} %get-tuple-element.25.ask_ref), channel_id=1, source_target_pairs={{0,4},{4,0},{8,12},{12,8},{1,5},{5,1},{9,13},{13,9},{2,6},{6,2},{1... | collective-permute-start | bytes 76808 | tf_op jit(solution)/shard_map/ppermute | solution.py:516
  4.5 3.7 %collective-permute-start.6 = (bf16[136,512]{1,0:T(8,128)(2,1)}, bf16[136,512]{1,0:T(8,128)(2,1)S(1)}, u32[]{:S(2)}, u32[]{:S(2)}) collective-permute-start(bf16[136,512]{1,0:T(8,128)(2,1)} %get-tuple-element.40), channel_id=1, source_target_pairs={{0,2},{1,3},{2,0},{3,1},{4,6},{5,7},{6,4},{7,5},{8,10},{9,11},{10,... | collective-permute-start | bytes 417800 | tf_op jit(solution)/shard_map/ppermute | solution.py:516
  8.2 1.3 %collective-permute-start.7 = (bf16[136,512]{1,0:T(8,128)(2,1)}, bf16[136,512]{1,0:T(8,128)(2,1)S(1)}, u32[]{:S(2)}, u32[]{:S(2)}) collective-permute-start(bf16[136,512]{1,0:T(8,128)(2,1)} %get-tuple-element.41), channel_id=1, source_target_pairs={{0,3},{1,2},{2,1},{3,0},{4,7},{5,6},{6,5},{7,4},{8,11},{9,10},{10,... | collective-permute-start | bytes 417800 | tf_op jit(solution)/shard_map/ppermute | solution.py:516
  9.5 0.0 collective-permute-done.rest_0_
  9.5 0.2 collective-permute-start.8
  9.8 1.0 %collective-permute-start.2 = (bf16[5,2560]{1,0:T(8,128)(2,1)}, bf16[5,2560]{1,0:T(8,128)(2,1)S(1)}, u32[]{:S(2)}, u32[]{:S(2)}) collective-permute-start(bf16[5,2560]{1,0:T(8,128)(2,1)} %get-tuple-element.25.ask_ref), channel_id=1, source_target_pairs={{0,12},{4,8},{8,4},{12,0},{1,13},{5,9},{9,5},{13,1},{2,14},{6,10},... | collective-permute-start | bytes 76808 | tf_op jit(solution)/shard_map/ppermute | solution.py:516
  10.7 0.5 %collective-permute-start.1 = (bf16[5,2560]{1,0:T(8,128)(2,1)}, bf16[5,2560]{1,0:T(8,128)(2,1)S(1)}, u32[]{:S(2)}, u32[]{:S(2)}) collective-permute-start(bf16[5,2560]{1,0:T(8,128)(2,1)} %get-tuple-element.25.ask_ref), channel_id=1, source_target_pairs={{0,8},{4,12},{8,0},{12,4},{1,9},{5,13},{9,1},{13,5},{2,10},{6,14},... | collective-permute-start | bytes 76808 | tf_op jit(solution)/shard_map/ppermute | solution.py:516
  11.3 0.0 copy-start
  11.3 0.0 copy-start.1
  11.3 0.0 copy-start.2
  11.3 0.0 copy-start.5
  11.3 0.0 copy-start.6
  11.3 0.0 copy-start.7
  11.3 0.0 copy-start.3
  11.3 7.2 %attend_resident.1 = (bf16[64,128]{1,0:T(8,128)(2,1)}, bf16[64,128]{1,0:T(8,128)(2,1)}, bf16[64,128]{1,0:T(8,128)(2,1)}, bf16[64,128]{1,0:T(8,128)(2,1)}) custom-call(s32[1,3]{1,0:T(1,128)} %len_ref.1, bf16[64,5,128]{2,1,0:T(8,128)(2,1)} %bitcast.18, bf16[3,1024,1024]{2,1,0:T(8,128)(2,1)} %bitcast.15, bf16[3,1024,1024]{2,1,0:T(8,128)(2,1)} %bitcast.16), custom_call_target="tpu_custom_call" | custom-call | flops 100663296 | bytes 12582912 | tf_op jit(solution)/shard_map/attend_resident/pallas_call | solution.py:271
  18.5 0.0 collective-permute-done.2.rest_2_
  18.5 0.0 collective-permute-done.1.rest_1_
  18.5 1.9 %collective-permute-start.3 = (bf16[64,128]{1,0:T(8,128)(2,1)}, bf16[64,128]{1,0:T(8,128)(2,1)S(1)}, u32[]{:S(2)}, u32[]{:S(2)}) collective-permute-start(bf16[64,128]{1,0:T(8,128)(2,1)} %get-tuple-element.33), channel_id=1, source_target_pairs={{0,1},{1,0},{2,3},{3,2},{4,5},{5,4},{6,7},{7,6},{8,9},{9,8},{10,11... | collective-permute-start | bytes 49160 | tf_op jit(solution)/shard_map/ppermute | solution.py:516
  20.4 0.0 collective-permute-start.4
  20.4 0.0 collective-permute-done.6.rest_4_
  20.4 1.7 %collective-permute-start.5 = (bf16[64,128]{1,0:T(8,128)(2,1)}, bf16[64,128]{1,0:T(8,128)(2,1)S(1)}, u32[]{:S(2)}, u32[]{:S(2)}) collective-permute-start(bf16[64,128]{1,0:T(8,128)(2,1)} %get-tuple-element.35), channel_id=1, source_target_pairs={{0,2},{1,3},{2,0},{3,1},{4,6},{5,7},{6,4},{7,5},{8,10},{9,11},{10,... | collective-permute-start | bytes 49160 | tf_op jit(solution)/shard_map/ppermute | solution.py:516
  22.1 0.0 collective-permute-done.7.rest_5_
  22.1 0.0 collective-permute-done.8.rest_6_
  22.1 0.0 copy-done
  22.1 0.0 copy-done.1
  22.1 0.0 copy-done.2
  22.1 0.0 copy-done.5
  22.1 0.0 copy-done.6
  22.1 0.0 copy-done.7
  22.2 1.3 %attend_moved.1 = (bf16[2,2048]{1,0:T(2,128)(2,1)S(1)}, s32[8,128]{1,0:T(8,128)S(1)}) custom-call(s32[2,4]{1,0:T(2,128)S(1)} %bitcast.12, s32[2,4]{1,0:T(2,128)S(1)} %bitcast.13, bf16[1,128]{1,0:T(2,128)(2,1)S(1)} %bitcast.14, f32[128,128]{1,0:T(8,128)S(1)} %copy-done.2, f32[128,128]{1,0:T(8,128)S(1)} %copy-done.1, ...), custom_call_target="tpu_custom_call" | custom-call | tf_op jit(solution)/shard_map/attend_moved/pallas_call | solution.py:422
  23.5 0.7 %collective-permute-start.11 = (bf16[2,2048]{1,0:T(2,128)(2,1)S(1)}, bf16[2,2048]{1,0:T(2,128)(2,1)S(1)}, u32[]{:S(2)}, u32[]{:S(2)}) collective-permute-start(bf16[2,2048]{1,0:T(2,128)(2,1)S(1)} %get-tuple-element.44), channel_id=1, source_target_pairs={{0,12},{4,8},{8,4},{12,0},{1,13},{5,9},{9,5},{13,1},{2,14},{6,10},... | collective-permute-start | bytes 24584 | tf_op jit(solution)/shard_map/ppermute | solution.py:516
  24.1 1.0 %collective-permute-start.10 = (bf16[2,2048]{1,0:T(2,128)(2,1)S(1)}, bf16[2,2048]{1,0:T(2,128)(2,1)S(1)}, u32[]{:S(2)}, u32[]{:S(2)}) collective-permute-start(bf16[2,2048]{1,0:T(2,128)(2,1)S(1)} %get-tuple-element.44), channel_id=1, source_target_pairs={{0,8},{4,12},{8,0},{12,4},{1,9},{5,13},{9,1},{13,5},{2,10},{6,14},... | collective-permute-start | bytes 24584 | tf_op jit(solution)/shard_map/ppermute | solution.py:516
  25.1 0.0 collective-permute-done.3.rest_1_
  25.1 0.3 %collective-permute-start.9 = (bf16[2,2048]{1,0:T(2,128)(2,1)S(1)}, bf16[2,2048]{1,0:T(2,128)(2,1)S(1)}, u32[]{:S(2)}, u32[]{:S(2)}) collective-permute-start(bf16[2,2048]{1,0:T(2,128)(2,1)S(1)} %get-tuple-element.44), channel_id=1, source_target_pairs={{0,4},{4,0},{8,12},{12,8},{1,5},{5,1},{9,13},{13,9},{2,6},{6,2},{1... | collective-permute-start | bytes 24584 | tf_op jit(solution)/shard_map/ppermute | solution.py:516
  25.4 0.7 %collective-permute-done.4.rest_2_ = bf16[64,128]{1,0:T(8,128)(2,1)S(1)} collective-permute-done((bf16[64,128]{1,0:T(8,128)(2,1)}, bf16[64,128]{1,0:T(8,128)(2,1)S(1)}, u32[]{:S(2)}, u32[]{:S(2)}) %collective-permute-start.4) | collective-permute-done | bytes 16416 | tf_op jit(solution)/shard_map/ppermute | solution.py:516
  26.1 0.0 collective-permute-done.5.rest_3_
  26.1 0.0 copy-done.3
  26.1 0.0 copy-start.4
  26.1 0.7 %copy-done.4 = bf16[64,128]{1,0:T(8,128)(2,1)S(1)} copy-done((bf16[64,128]{1,0:T(8,128)(2,1)S(1)}, bf16[64,128]{1,0:T(8,128)(2,1)}, u32[]{:S(2)}) %copy-start.4) | copy-done | bytes 16408
  26.9 0.2 combine_resident.1.kept_ref
  27.0 0.0 collective-permute-done.11.rest_2_
  27.0 0.8 %collective-permute-done.10.rest_1_ = bf16[2,2048]{1,0:T(2,128)(2,1)S(1)} collective-permute-done((bf16[2,2048]{1,0:T(2,128)(2,1)S(1)}, bf16[2,2048]{1,0:T(2,128)(2,1)S(1)}, u32[]{:S(2)}, u32[]{:S(2)}) %collective-permute-start.10) | collective-permute-done | bytes 8224 | tf_op jit(solution)/shard_map/ppermute | solution.py:516
  27.8 0.0 collective-permute-done.9.rest_0_
  27.8 0.7 %finish.1 = bf16[5,2048]{1,0:T(8,128)(2,1)} custom-call(f32[3,2048]{1,0:T(4,128)S(1)} %combine_resident.1.kept_ref, s32[8,128]{1,0:T(8,128)S(1)} %get-tuple-element.43.place_ref, bf16[2,2048]{1,0:T(2,128)(2,1)S(1)} %collective-permute-done.9.rest_0_, bf16[2,2048]{1,0:T(2,128)(2,1)S(1)} %collective-permute-done.10.rest_1_, ...), custom_call_target="tpu_custom_call" | custom-call | tf_op jit(solution)/shard_map/finish/pallas_call | solution.py:505
Async XLA Ops:
  4.0 5.5 %collective-permute-start = (bf16[5,2560]{1,0:T(8,128)(2,1)}, bf16[5,2560]{1,0:T(8,128)(2,1)S(1)}, u32[]{:S(2)}, u32[]{:S(2)}) collective-permute-start(bf16[5,2560]{1,0:T(8,128)(2,1)} %get-tuple-element.25.ask_ref), channel_id=1, source_target_pairs={{0,4},{4,0},{8,12},{12,8},{1,5},{5,1},{9,13},{13,9},{2,6},{6,2},{1... | collective-permute-start | bytes 76808 | tf_op jit(solution)/shard_map/ppermute | solution.py:516
  4.5 15.9 %collective-permute-start.6 = (bf16[136,512]{1,0:T(8,128)(2,1)}, bf16[136,512]{1,0:T(8,128)(2,1)S(1)}, u32[]{:S(2)}, u32[]{:S(2)}) collective-permute-start(bf16[136,512]{1,0:T(8,128)(2,1)} %get-tuple-element.40), channel_id=1, source_target_pairs={{0,2},{1,3},{2,0},{3,1},{4,6},{5,7},{6,4},{7,5},{8,10},{9,11},{10,... | collective-permute-start | bytes 417800 | tf_op jit(solution)/shard_map/ppermute | solution.py:516
  8.2 13.9 %collective-permute-start.7 = (bf16[136,512]{1,0:T(8,128)(2,1)}, bf16[136,512]{1,0:T(8,128)(2,1)S(1)}, u32[]{:S(2)}, u32[]{:S(2)}) collective-permute-start(bf16[136,512]{1,0:T(8,128)(2,1)} %get-tuple-element.41), channel_id=1, source_target_pairs={{0,3},{1,2},{2,1},{3,0},{4,7},{5,6},{6,5},{7,4},{8,11},{9,10},{10,... | collective-permute-start | bytes 417800 | tf_op jit(solution)/shard_map/ppermute | solution.py:516
  9.5 12.6 %collective-permute-start.8 = (bf16[136,512]{1,0:T(8,128)(2,1)}, bf16[136,512]{1,0:T(8,128)(2,1)S(1)}, u32[]{:S(2)}, u32[]{:S(2)}) collective-permute-start(bf16[136,512]{1,0:T(8,128)(2,1)} %get-tuple-element.42), channel_id=1, source_target_pairs={{0,1},{1,0},{2,3},{3,2},{4,5},{5,4},{6,7},{7,6},{8,9},{9,8},{10,11... | collective-permute-start | bytes 417800 | tf_op jit(solution)/shard_map/ppermute | solution.py:516
  9.8 8.8 %collective-permute-start.2 = (bf16[5,2560]{1,0:T(8,128)(2,1)}, bf16[5,2560]{1,0:T(8,128)(2,1)S(1)}, u32[]{:S(2)}, u32[]{:S(2)}) collective-permute-start(bf16[5,2560]{1,0:T(8,128)(2,1)} %get-tuple-element.25.ask_ref), channel_id=1, source_target_pairs={{0,12},{4,8},{8,4},{12,0},{1,13},{5,9},{9,5},{13,1},{2,14},{6,10},... | collective-permute-start | bytes 76808 | tf_op jit(solution)/shard_map/ppermute | solution.py:516
  10.7 7.8 %collective-permute-start.1 = (bf16[5,2560]{1,0:T(8,128)(2,1)}, bf16[5,2560]{1,0:T(8,128)(2,1)S(1)}, u32[]{:S(2)}, u32[]{:S(2)}) collective-permute-start(bf16[5,2560]{1,0:T(8,128)(2,1)} %get-tuple-element.25.ask_ref), channel_id=1, source_target_pairs={{0,8},{4,12},{8,0},{12,4},{1,9},{5,13},{9,1},{13,5},{2,10},{6,14},... | collective-permute-start | bytes 76808 | tf_op jit(solution)/shard_map/ppermute | solution.py:516
  11.3 10.8 %copy-start = (bf16[136,512]{1,0:T(8,128)(2,1)S(1)}, bf16[136,512]{1,0:T(8,128)(2,1)}, u32[]{:S(2)}) copy-start(bf16[136,512]{1,0:T(8,128)(2,1)} %get-tuple-element.39.rest_3_) | copy-start | bytes 417796
  11.3 10.8 %copy-start.1 = (f32[128,128]{1,0:T(8,128)S(1)}, f32[128,128]{1,0:T(8,128)}, u32[]{:S(2)}) copy-start(f32[128,128]{1,0:T(8,128)} %constant.5.clone.sin_ref) | copy-start | bytes 196612
  11.3 10.8 %copy-start.2 = (f32[128,128]{1,0:T(8,128)S(1)}, f32[128,128]{1,0:T(8,128)}, u32[]{:S(2)}) copy-start(f32[128,128]{1,0:T(8,128)} %constant.4.clone.cos_ref) | copy-start | bytes 196612
  11.3 10.8 %copy-start.5 = (s32[4,2]{0,1:T(2,128)S(1)}, s32[4,2]{0,1:T(2,128)}, u32[]{:S(2)}) copy-start(s32[4,2]{0,1:T(2,128)} %param.14) | copy-start | bytes 100
  11.3 10.8 %copy-start.6 = (s32[4,2]{0,1:T(2,128)S(1)}, s32[4,2]{0,1:T(2,128)}, u32[]{:S(2)}) copy-start(s32[4,2]{0,1:T(2,128)} %param.15) | copy-start | bytes 100
  11.3 10.8 %copy-start.7 = (bf16[128]{0:T(256)(128)(2,1)S(1)}, bf16[128]{0:T(256)(128)(2,1)}, u32[]{:S(2)}) copy-start(bf16[128]{0:T(256)(128)(2,1)} %param.18) | copy-start | bytes 772
  11.3 14.8 %copy-start.3 = (bf16[5,2560]{1,0:T(8,128)(2,1)S(1)}, bf16[5,2560]{1,0:T(8,128)(2,1)}, u32[]{:S(2)}) copy-start(bf16[5,2560]{1,0:T(8,128)(2,1)} %get-tuple-element.25.ask_ref) | copy-start | bytes 76804
  18.5 6.6 %collective-permute-start.3 = (bf16[64,128]{1,0:T(8,128)(2,1)}, bf16[64,128]{1,0:T(8,128)(2,1)S(1)}, u32[]{:S(2)}, u32[]{:S(2)}) collective-permute-start(bf16[64,128]{1,0:T(8,128)(2,1)} %get-tuple-element.33), channel_id=1, source_target_pairs={{0,1},{1,0},{2,3},{3,2},{4,5},{5,4},{6,7},{7,6},{8,9},{9,8},{10,11... | collective-permute-start | bytes 49160 | tf_op jit(solution)/shard_map/ppermute | solution.py:516
  20.4 5.7 %collective-permute-start.4 = (bf16[64,128]{1,0:T(8,128)(2,1)}, bf16[64,128]{1,0:T(8,128)(2,1)S(1)}, u32[]{:S(2)}, u32[]{:S(2)}) collective-permute-start(bf16[64,128]{1,0:T(8,128)(2,1)} %get-tuple-element.34), channel_id=1, source_target_pairs={{0,3},{1,2},{2,1},{3,0},{4,7},{5,6},{6,5},{7,4},{8,11},{9,10},{10,... | collective-permute-start | bytes 49160 | tf_op jit(solution)/shard_map/ppermute | solution.py:516
  20.4 5.7 %collective-permute-start.5 = (bf16[64,128]{1,0:T(8,128)(2,1)}, bf16[64,128]{1,0:T(8,128)(2,1)S(1)}, u32[]{:S(2)}, u32[]{:S(2)}) collective-permute-start(bf16[64,128]{1,0:T(8,128)(2,1)} %get-tuple-element.35), channel_id=1, source_target_pairs={{0,2},{1,3},{2,0},{3,1},{4,6},{5,7},{6,4},{7,5},{8,10},{9,11},{10,... | collective-permute-start | bytes 49160 | tf_op jit(solution)/shard_map/ppermute | solution.py:516
  23.5 3.5 %collective-permute-start.11 = (bf16[2,2048]{1,0:T(2,128)(2,1)S(1)}, bf16[2,2048]{1,0:T(2,128)(2,1)S(1)}, u32[]{:S(2)}, u32[]{:S(2)}) collective-permute-start(bf16[2,2048]{1,0:T(2,128)(2,1)S(1)} %get-tuple-element.44), channel_id=1, source_target_pairs={{0,12},{4,8},{8,4},{12,0},{1,13},{5,9},{9,5},{13,1},{2,14},{6,10},... | collective-permute-start | bytes 24584 | tf_op jit(solution)/shard_map/ppermute | solution.py:516
  24.1 3.7 %collective-permute-start.10 = (bf16[2,2048]{1,0:T(2,128)(2,1)S(1)}, bf16[2,2048]{1,0:T(2,128)(2,1)S(1)}, u32[]{:S(2)}, u32[]{:S(2)}) collective-permute-start(bf16[2,2048]{1,0:T(2,128)(2,1)S(1)} %get-tuple-element.44), channel_id=1, source_target_pairs={{0,8},{4,12},{8,0},{12,4},{1,9},{5,13},{9,1},{13,5},{2,10},{6,14},... | collective-permute-start | bytes 24584 | tf_op jit(solution)/shard_map/ppermute | solution.py:516
  25.1 2.7 %collective-permute-start.9 = (bf16[2,2048]{1,0:T(2,128)(2,1)S(1)}, bf16[2,2048]{1,0:T(2,128)(2,1)S(1)}, u32[]{:S(2)}, u32[]{:S(2)}) collective-permute-start(bf16[2,2048]{1,0:T(2,128)(2,1)S(1)} %get-tuple-element.44), channel_id=1, source_target_pairs={{0,4},{4,0},{8,12},{12,8},{1,5},{5,1},{9,13},{13,9},{2,6},{6,2},{1... | collective-permute-start | bytes 24584 | tf_op jit(solution)/shard_map/ppermute | solution.py:516
  26.1 0.7 %copy-start.4 = (bf16[64,128]{1,0:T(8,128)(2,1)S(1)}, bf16[64,128]{1,0:T(8,128)(2,1)}, u32[]{:S(2)}) copy-start(bf16[64,128]{1,0:T(8,128)(2,1)} %get-tuple-element.32.rest_0_) | copy-start | bytes 49156

commit v23 on v19

--- a/solution.py
+++ b/solution.py
@@ -566,7 +566,9 @@
         feats * ranks,
     )
     kept = combine_resident(ask, received, residents, heads_mine, kv_mine)
-    moved = [swapped(moved, "inst", b, insts) for b in reversed(range(1, insts))][::-1]
+    order = sorted(range(1, insts), key=lambda b: (b == 1, b % 2, b))
+    results = {b: swapped(moved, "inst", b, insts) for b in order}
+    moved = [results[b] for b in range(1, insts)]
     return finish(kept, places, moved, requests)[None]
 
 

time: 28.7 us -> 28.7 us (level)
  no operation moved by 1% of the time
where the time goes in v23:
time: 28.7 us; the launch traced here: 28.5 us
  Pallas kernels  13.3 us (46%)
  starting transfers between devices  12.8 us (45%)
  waiting for transfers between devices  1.55 us (5%)
  local copies, waits for them, and re-layouts  0.75 us (3%)
    ppermute x12, starting transfers between devices, swapped(): return lax.ppermute(x, axis, [(i, i ^ j) for i in range(n)])  12.8 us
    pallas_call x1, Pallas kernels, attend_resident(): pl.pallas_call(functools.partial(resident_kernel, ranks), in_specs=[SMEM,...  7.13 us
    pallas_call x1, Pallas kernels, project(): pl.pallas_call(functools.partial(project_kernel, ranks, group), in_specs=...  3.99 us
    ppermute x12, waiting for transfers between devices, swapped(): return lax.ppermute(x, axis, [(i, i ^ j) for i in range(n)])  1.55 us
    pallas_call x1, Pallas kernels, attend_moved(): pl.pallas_call(functools.partial(moved_kernel, insts, len(pieces), reside...  1.32 us
    unnamed x16, local copies, waits for them, and re-layouts  0.75 us
    pallas_call x1, Pallas kernels, finish(): pl.pallas_call(finish_kernel, in_specs=[VMEM] * (2 + len(moved)), out_spe...  0.67 us
  transfers between devices with their start and end apart: 12, of which 2 were waited for; matrix products, arithmetic and copies ran while one was open for 0% of the time, Pallas kernels for 30%

profile of v23, /device:TPU:0, one launch (start us, length us, event | category | flops | bytes accessed | tf_op | source)
XLA Modules:
  0.0 28.5 jit_solution(16129933271387606706)
XLA Ops:
  0.0 4.0 %project.1 = (bf16[136,512]{1,0:T(8,128)(2,1)}, bf16[136,512]{1,0:T(8,128)(2,1)}, bf16[136,512]{1,0:T(8,128)(2,1)}, bf16[136,512]{1,0:T(8,128)(2,1)}, bf16[5,2560]{1,0:T(8,128)(2,1)}) custom-call(bf16[1280]{0:T(1024)(128)(2,1)} %gain_hbm.1, bf16[64,2,1280]{2,1,0:T(2,128)(2,1)} %bitcast.19, bf16[1280,2048]{1,0:T(8,128)(2,1)} %w_hbm.1, ...), custom_call_target="tpu_custom_call" | custom-call | flops 671088640 | bytes 5242880 | tf_op jit(solution)/shard_map/project/pallas_call | solution.py:133
  4.0 0.5 %collective-permute-start = (bf16[5,2560]{1,0:T(8,128)(2,1)}, bf16[5,2560]{1,0:T(8,128)(2,1)S(1)}, u32[]{:S(2)}, u32[]{:S(2)}) collective-permute-start(bf16[5,2560]{1,0:T(8,128)(2,1)} %get-tuple-element.25.ask_ref), channel_id=1, source_target_pairs={{0,4},{4,0},{8,12},{12,8},{1,5},{5,1},{9,13},{13,9},{2,6},{6,2},{1... | collective-permute-start | bytes 76808 | tf_op jit(solution)/shard_map/ppermute | solution.py:504
  4.5 3.7 %collective-permute-start.6 = (bf16[136,512]{1,0:T(8,128)(2,1)}, bf16[136,512]{1,0:T(8,128)(2,1)S(1)}, u32[]{:S(2)}, u32[]{:S(2)}) collective-permute-start(bf16[136,512]{1,0:T(8,128)(2,1)} %get-tuple-element.40), channel_id=1, source_target_pairs={{0,2},{1,3},{2,0},{3,1},{4,6},{5,7},{6,4},{7,5},{8,10},{9,11},{10,... | collective-permute-start | bytes 417800 | tf_op jit(solution)/shard_map/ppermute | solution.py:504
  8.2 1.3 %collective-permute-start.7 = (bf16[136,512]{1,0:T(8,128)(2,1)}, bf16[136,512]{1,0:T(8,128)(2,1)S(1)}, u32[]{:S(2)}, u32[]{:S(2)}) collective-permute-start(bf16[136,512]{1,0:T(8,128)(2,1)} %get-tuple-element.41), channel_id=1, source_target_pairs={{0,3},{1,2},{2,1},{3,0},{4,7},{5,6},{6,5},{7,4},{8,11},{9,10},{10,... | collective-permute-start | bytes 417800 | tf_op jit(solution)/shard_map/ppermute | solution.py:504
  9.5 0.0 collective-permute-done.rest_0_
  9.5 0.2 collective-permute-start.8
  9.8 1.0 %collective-permute-start.2 = (bf16[5,2560]{1,0:T(8,128)(2,1)}, bf16[5,2560]{1,0:T(8,128)(2,1)S(1)}, u32[]{:S(2)}, u32[]{:S(2)}) collective-permute-start(bf16[5,2560]{1,0:T(8,128)(2,1)} %get-tuple-element.25.ask_ref), channel_id=1, source_target_pairs={{0,12},{4,8},{8,4},{12,0},{1,13},{5,9},{9,5},{13,1},{2,14},{6,10},... | collective-permute-start | bytes 76808 | tf_op jit(solution)/shard_map/ppermute | solution.py:504
  10.7 0.5 %collective-permute-start.1 = (bf16[5,2560]{1,0:T(8,128)(2,1)}, bf16[5,2560]{1,0:T(8,128)(2,1)S(1)}, u32[]{:S(2)}, u32[]{:S(2)}) collective-permute-start(bf16[5,2560]{1,0:T(8,128)(2,1)} %get-tuple-element.25.ask_ref), channel_id=1, source_target_pairs={{0,8},{4,12},{8,0},{12,4},{1,9},{5,13},{9,1},{13,5},{2,10},{6,14},... | collective-permute-start | bytes 76808 | tf_op jit(solution)/shard_map/ppermute | solution.py:504
  11.3 0.0 copy-start
  11.3 0.0 copy-start.1
  11.3 0.0 copy-start.2
  11.3 0.0 copy-start.5
  11.3 0.0 copy-start.6
  11.3 0.0 copy-start.7
  11.3 0.0 copy-start.3
  11.3 7.1 %attend_resident.1 = (bf16[64,128]{1,0:T(8,128)(2,1)}, bf16[64,128]{1,0:T(8,128)(2,1)}, bf16[64,128]{1,0:T(8,128)(2,1)}, bf16[64,128]{1,0:T(8,128)(2,1)}) custom-call(s32[1,3]{1,0:T(1,128)} %len_ref.1, bf16[64,5,128]{2,1,0:T(8,128)(2,1)} %bitcast.18, bf16[3,1024,1024]{2,1,0:T(8,128)(2,1)} %bitcast.15, bf16[3,1024,1024]{2,1,0:T(8,128)(2,1)} %bitcast.16), custom_call_target="tpu_custom_call" | custom-call | flops 100663296 | bytes 12582912 | tf_op jit(solution)/shard_map/attend_resident/pallas_call | solution.py:259
  18.5 0.0 collective-permute-done.2.rest_2_
  18.5 0.0 collective-permute-done.1.rest_1_
  18.5 0.6 %collective-permute-start.3 = (bf16[64,128]{1,0:T(8,128)(2,1)}, bf16[64,128]{1,0:T(8,128)(2,1)S(1)}, u32[]{:S(2)}, u32[]{:S(2)}) collective-permute-start(bf16[64,128]{1,0:T(8,128)(2,1)} %get-tuple-element.33), channel_id=1, source_target_pairs={{0,1},{1,0},{2,3},{3,2},{4,5},{5,4},{6,7},{7,6},{8,9},{9,8},{10,11... | collective-permute-start | bytes 49160 | tf_op jit(solution)/shard_map/ppermute | solution.py:504
  19.1 2.5 %collective-permute-start.4 = (bf16[64,128]{1,0:T(8,128)(2,1)}, bf16[64,128]{1,0:T(8,128)(2,1)S(1)}, u32[]{:S(2)}, u32[]{:S(2)}) collective-permute-start(bf16[64,128]{1,0:T(8,128)(2,1)} %get-tuple-element.34), channel_id=1, source_target_pairs={{0,3},{1,2},{2,1},{3,0},{4,7},{5,6},{6,5},{7,4},{8,11},{9,10},{10,... | collective-permute-start | bytes 49160 | tf_op jit(solution)/shard_map/ppermute | solution.py:504
  21.6 0.0 collective-permute-done.6.rest_4_
  21.6 0.5 %collective-permute-start.5 = (bf16[64,128]{1,0:T(8,128)(2,1)}, bf16[64,128]{1,0:T(8,128)(2,1)S(1)}, u32[]{:S(2)}, u32[]{:S(2)}) collective-permute-start(bf16[64,128]{1,0:T(8,128)(2,1)} %get-tuple-element.35), channel_id=1, source_target_pairs={{0,2},{1,3},{2,0},{3,1},{4,6},{5,7},{6,4},{7,5},{8,10},{9,11},{10,... | collective-permute-start | bytes 49160 | tf_op jit(solution)/shard_map/ppermute | solution.py:504
  22.1 0.0 collective-permute-done.7.rest_5_
  22.1 0.0 collective-permute-done.8.rest_6_
  22.1 0.0 copy-done
  22.1 0.0 copy-done.1
  22.1 0.0 copy-done.2
  22.1 0.0 copy-done.5
  22.1 0.0 copy-done.6
  22.1 0.0 copy-done.7
  22.1 1.3 %attend_moved.1 = (bf16[2,2048]{1,0:T(2,128)(2,1)S(1)}, s32[8,128]{1,0:T(8,128)S(1)}) custom-call(s32[2,4]{1,0:T(2,128)S(1)} %bitcast.12, s32[2,4]{1,0:T(2,128)S(1)} %bitcast.13, bf16[1,128]{1,0:T(2,128)(2,1)S(1)} %bitcast.14, f32[128,128]{1,0:T(8,128)S(1)} %copy-done.2, f32[128,128]{1,0:T(8,128)S(1)} %copy-done.1, ...), custom_call_target="tpu_custom_call" | custom-call | tf_op jit(solution)/shard_map/attend_moved/pallas_call | solution.py:410
  23.4 0.7 %collective-permute-start.11 = (bf16[2,2048]{1,0:T(2,128)(2,1)S(1)}, bf16[2,2048]{1,0:T(2,128)(2,1)S(1)}, u32[]{:S(2)}, u32[]{:S(2)}) collective-permute-start(bf16[2,2048]{1,0:T(2,128)(2,1)S(1)} %get-tuple-element.44), channel_id=1, source_target_pairs={{0,12},{4,8},{8,4},{12,0},{1,13},{5,9},{9,5},{13,1},{2,14},{6,10},... | collective-permute-start | bytes 24584 | tf_op jit(solution)/shard_map/ppermute | solution.py:504
  24.1 1.0 %collective-permute-start.10 = (bf16[2,2048]{1,0:T(2,128)(2,1)S(1)}, bf16[2,2048]{1,0:T(2,128)(2,1)S(1)}, u32[]{:S(2)}, u32[]{:S(2)}) collective-permute-start(bf16[2,2048]{1,0:T(2,128)(2,1)S(1)} %get-tuple-element.44), channel_id=1, source_target_pairs={{0,8},{4,12},{8,0},{12,4},{1,9},{5,13},{9,1},{13,5},{2,10},{6,14},... | collective-permute-start | bytes 24584 | tf_op jit(solution)/shard_map/ppermute | solution.py:504
  25.1 0.0 collective-permute-done.3.rest_1_
  25.1 0.3 %collective-permute-start.9 = (bf16[2,2048]{1,0:T(2,128)(2,1)S(1)}, bf16[2,2048]{1,0:T(2,128)(2,1)S(1)}, u32[]{:S(2)}, u32[]{:S(2)}) collective-permute-start(bf16[2,2048]{1,0:T(2,128)(2,1)S(1)} %get-tuple-element.44), channel_id=1, source_target_pairs={{0,4},{4,0},{8,12},{12,8},{1,5},{5,1},{9,13},{13,9},{2,6},{6,2},{1... | collective-permute-start | bytes 24584 | tf_op jit(solution)/shard_map/ppermute | solution.py:504
  25.4 0.0 collective-permute-done.4.rest_2_
  25.4 1.1 %collective-permute-done.5.rest_3_ = bf16[64,128]{1,0:T(8,128)(2,1)S(1)} collective-permute-done((bf16[64,128]{1,0:T(8,128)(2,1)}, bf16[64,128]{1,0:T(8,128)(2,1)S(1)}, u32[]{:S(2)}, u32[]{:S(2)}) %collective-permute-start.5) | collective-permute-done | bytes 16416 | tf_op jit(solution)/shard_map/ppermute | solution.py:504
  26.5 0.0 copy-done.3
  26.5 0.0 copy-start.4
  26.5 0.7 %copy-done.4 = bf16[64,128]{1,0:T(8,128)(2,1)S(1)} copy-done((bf16[64,128]{1,0:T(8,128)(2,1)S(1)}, bf16[64,128]{1,0:T(8,128)(2,1)}, u32[]{:S(2)}) %copy-start.4) | copy-done | bytes 16408
  27.2 0.2 combine_resident.1.kept_ref
  27.3 0.0 collective-permute-done.11.rest_2_
  27.4 0.5 %collective-permute-done.10.rest_1_ = bf16[2,2048]{1,0:T(2,128)(2,1)S(1)} collective-permute-done((bf16[2,2048]{1,0:T(2,128)(2,1)S(1)}, bf16[2,2048]{1,0:T(2,128)(2,1)S(1)}, u32[]{:S(2)}, u32[]{:S(2)}) %collective-permute-start.10) | collective-permute-done | bytes 8224 | tf_op jit(solution)/shard_map/ppermute | solution.py:504
  27.8 0.0 collective-permute-done.9.rest_0_
  27.8 0.7 %finish.1 = bf16[5,2048]{1,0:T(8,128)(2,1)} custom-call(f32[3,2048]{1,0:T(4,128)S(1)} %combine_resident.1.kept_ref, s32[8,128]{1,0:T(8,128)S(1)} %get-tuple-element.43.place_ref, bf16[2,2048]{1,0:T(2,128)(2,1)S(1)} %collective-permute-done.9.rest_0_, bf16[2,2048]{1,0:T(2,128)(2,1)S(1)} %collective-permute-done.10.rest_1_, ...), custom_call_target="tpu_custom_call" | custom-call | tf_op jit(solution)/shard_map/finish/pallas_call | solution.py:493
Async XLA Ops:
  4.0 5.5 %collective-permute-start = (bf16[5,2560]{1,0:T(8,128)(2,1)}, bf16[5,2560]{1,0:T(8,128)(2,1)S(1)}, u32[]{:S(2)}, u32[]{:S(2)}) collective-permute-start(bf16[5,2560]{1,0:T(8,128)(2,1)} %get-tuple-element.25.ask_ref), channel_id=1, source_target_pairs={{0,4},{4,0},{8,12},{12,8},{1,5},{5,1},{9,13},{13,9},{2,6},{6,2},{1... | collective-permute-start | bytes 76808 | tf_op jit(solution)/shard_map/ppermute | solution.py:504
  4.5 17.1 %collective-permute-start.6 = (bf16[136,512]{1,0:T(8,128)(2,1)}, bf16[136,512]{1,0:T(8,128)(2,1)S(1)}, u32[]{:S(2)}, u32[]{:S(2)}) collective-permute-start(bf16[136,512]{1,0:T(8,128)(2,1)} %get-tuple-element.40), channel_id=1, source_target_pairs={{0,2},{1,3},{2,0},{3,1},{4,6},{5,7},{6,4},{7,5},{8,10},{9,11},{10,... | collective-permute-start | bytes 417800 | tf_op jit(solution)/shard_map/ppermute | solution.py:504
  8.2 13.9 %collective-permute-start.7 = (bf16[136,512]{1,0:T(8,128)(2,1)}, bf16[136,512]{1,0:T(8,128)(2,1)S(1)}, u32[]{:S(2)}, u32[]{:S(2)}) collective-permute-start(bf16[136,512]{1,0:T(8,128)(2,1)} %get-tuple-element.41), channel_id=1, source_target_pairs={{0,3},{1,2},{2,1},{3,0},{4,7},{5,6},{6,5},{7,4},{8,11},{9,10},{10,... | collective-permute-start | bytes 417800 | tf_op jit(solution)/shard_map/ppermute | solution.py:504
  9.5 12.5 %collective-permute-start.8 = (bf16[136,512]{1,0:T(8,128)(2,1)}, bf16[136,512]{1,0:T(8,128)(2,1)S(1)}, u32[]{:S(2)}, u32[]{:S(2)}) collective-permute-start(bf16[136,512]{1,0:T(8,128)(2,1)} %get-tuple-element.42), channel_id=1, source_target_pairs={{0,1},{1,0},{2,3},{3,2},{4,5},{5,4},{6,7},{7,6},{8,9},{9,8},{10,11... | collective-permute-start | bytes 417800 | tf_op jit(solution)/shard_map/ppermute | solution.py:504
  9.8 8.7 %collective-permute-start.2 = (bf16[5,2560]{1,0:T(8,128)(2,1)}, bf16[5,2560]{1,0:T(8,128)(2,1)S(1)}, u32[]{:S(2)}, u32[]{:S(2)}) collective-permute-start(bf16[5,2560]{1,0:T(8,128)(2,1)} %get-tuple-element.25.ask_ref), channel_id=1, source_target_pairs={{0,12},{4,8},{8,4},{12,0},{1,13},{5,9},{9,5},{13,1},{2,14},{6,10},... | collective-permute-start | bytes 76808 | tf_op jit(solution)/shard_map/ppermute | solution.py:504
  10.7 7.7 %collective-permute-start.1 = (bf16[5,2560]{1,0:T(8,128)(2,1)}, bf16[5,2560]{1,0:T(8,128)(2,1)S(1)}, u32[]{:S(2)}, u32[]{:S(2)}) collective-permute-start(bf16[5,2560]{1,0:T(8,128)(2,1)} %get-tuple-element.25.ask_ref), channel_id=1, source_target_pairs={{0,8},{4,12},{8,0},{12,4},{1,9},{5,13},{9,1},{13,5},{2,10},{6,14},... | collective-permute-start | bytes 76808 | tf_op jit(solution)/shard_map/ppermute | solution.py:504
  11.3 10.8 %copy-start = (bf16[136,512]{1,0:T(8,128)(2,1)S(1)}, bf16[136,512]{1,0:T(8,128)(2,1)}, u32[]{:S(2)}) copy-start(bf16[136,512]{1,0:T(8,128)(2,1)} %get-tuple-element.39.rest_3_) | copy-start | bytes 417796
  11.3 10.8 %copy-start.1 = (f32[128,128]{1,0:T(8,128)S(1)}, f32[128,128]{1,0:T(8,128)}, u32[]{:S(2)}) copy-start(f32[128,128]{1,0:T(8,128)} %constant.5.clone.sin_ref) | copy-start | bytes 196612
  11.3 10.8 %copy-start.2 = (f32[128,128]{1,0:T(8,128)S(1)}, f32[128,128]{1,0:T(8,128)}, u32[]{:S(2)}) copy-start(f32[128,128]{1,0:T(8,128)} %constant.4.clone.cos_ref) | copy-start | bytes 196612
  11.3 10.8 %copy-start.5 = (s32[4,2]{0,1:T(2,128)S(1)}, s32[4,2]{0,1:T(2,128)}, u32[]{:S(2)}) copy-start(s32[4,2]{0,1:T(2,128)} %param.14) | copy-start | bytes 100
  11.3 10.8 %copy-start.6 = (s32[4,2]{0,1:T(2,128)S(1)}, s32[4,2]{0,1:T(2,128)}, u32[]{:S(2)}) copy-start(s32[4,2]{0,1:T(2,128)} %param.15) | copy-start | bytes 100
  11.3 10.8 %copy-start.7 = (bf16[128]{0:T(256)(128)(2,1)S(1)}, bf16[128]{0:T(256)(128)(2,1)}, u32[]{:S(2)}) copy-start(bf16[128]{0:T(256)(128)(2,1)} %param.18) | copy-start | bytes 772
  11.3 15.1 %copy-start.3 = (bf16[5,2560]{1,0:T(8,128)(2,1)S(1)}, bf16[5,2560]{1,0:T(8,128)(2,1)}, u32[]{:S(2)}) copy-start(bf16[5,2560]{1,0:T(8,128)(2,1)} %get-tuple-element.25.ask_ref) | copy-start | bytes 76804
  18.5 6.6 %collective-permute-start.3 = (bf16[64,128]{1,0:T(8,128)(2,1)}, bf16[64,128]{1,0:T(8,128)(2,1)S(1)}, u32[]{:S(2)}, u32[]{:S(2)}) collective-permute-start(bf16[64,128]{1,0:T(8,128)(2,1)} %get-tuple-element.33), channel_id=1, source_target_pairs={{0,1},{1,0},{2,3},{3,2},{4,5},{5,4},{6,7},{7,6},{8,9},{9,8},{10,11... | collective-permute-start | bytes 49160 | tf_op jit(solution)/shard_map/ppermute | solution.py:504
  19.1 6.3 %collective-permute-start.4 = (bf16[64,128]{1,0:T(8,128)(2,1)}, bf16[64,128]{1,0:T(8,128)(2,1)S(1)}, u32[]{:S(2)}, u32[]{:S(2)}) collective-permute-start(bf16[64,128]{1,0:T(8,128)(2,1)} %get-tuple-element.34), channel_id=1, source_target_pairs={{0,3},{1,2},{2,1},{3,0},{4,7},{5,6},{6,5},{7,4},{8,11},{9,10},{10,... | collective-permute-start | bytes 49160 | tf_op jit(solution)/shard_map/ppermute | solution.py:504
  21.6 4.8 %collective-permute-start.5 = (bf16[64,128]{1,0:T(8,128)(2,1)}, bf16[64,128]{1,0:T(8,128)(2,1)S(1)}, u32[]{:S(2)}, u32[]{:S(2)}) collective-permute-start(bf16[64,128]{1,0:T(8,128)(2,1)} %get-tuple-element.35), channel_id=1, source_target_pairs={{0,2},{1,3},{2,0},{3,1},{4,6},{5,7},{6,4},{7,5},{8,10},{9,11},{10,... | collective-permute-start | bytes 49160 | tf_op jit(solution)/shard_map/ppermute | solution.py:504
  23.4 3.9 %collective-permute-start.11 = (bf16[2,2048]{1,0:T(2,128)(2,1)S(1)}, bf16[2,2048]{1,0:T(2,128)(2,1)S(1)}, u32[]{:S(2)}, u32[]{:S(2)}) collective-permute-start(bf16[2,2048]{1,0:T(2,128)(2,1)S(1)} %get-tuple-element.44), channel_id=1, source_target_pairs={{0,12},{4,8},{8,4},{12,0},{1,13},{5,9},{9,5},{13,1},{2,14},{6,10},... | collective-permute-start | bytes 24584 | tf_op jit(solution)/shard_map/ppermute | solution.py:504
  24.1 3.7 %collective-permute-start.10 = (bf16[2,2048]{1,0:T(2,128)(2,1)S(1)}, bf16[2,2048]{1,0:T(2,128)(2,1)S(1)}, u32[]{:S(2)}, u32[]{:S(2)}) collective-permute-start(bf16[2,2048]{1,0:T(2,128)(2,1)S(1)} %get-tuple-element.44), channel_id=1, source_target_pairs={{0,8},{4,12},{8,0},{12,4},{1,9},{5,13},{9,1},{13,5},{2,10},{6,14},... | collective-permute-start | bytes 24584 | tf_op jit(solution)/shard_map/ppermute | solution.py:504
  25.1 2.7 %collective-permute-start.9 = (bf16[2,2048]{1,0:T(2,128)(2,1)S(1)}, bf16[2,2048]{1,0:T(2,128)(2,1)S(1)}, u32[]{:S(2)}, u32[]{:S(2)}) collective-permute-start(bf16[2,2048]{1,0:T(2,128)(2,1)S(1)} %get-tuple-element.44), channel_id=1, source_target_pairs={{0,4},{4,0},{8,12},{12,8},{1,5},{5,1},{9,13},{13,9},{2,6},{6,2},{1... | collective-permute-start | bytes 24584 | tf_op jit(solution)/shard_map/ppermute | solution.py:504
  26.5 0.7 %copy-start.4 = (bf16[64,128]{1,0:T(8,128)(2,1)S(1)}, bf16[64,128]{1,0:T(8,128)(2,1)}, u32[]{:S(2)}) copy-start(bf16[64,128]{1,0:T(8,128)(2,1)} %get-tuple-element.32.rest_0_) | copy-start | bytes 49156
